TPU v7x, 512 devices: a whole 4x8x8 slice. The times are simulated.
512 devices in a mesh: tm: 64 (over x, z_lo, y), rows: 8 (over z_hi, core).
Axes of the slice: x: 4, y: 8, z: 8 (z_hi: 4, z_lo: 2; z = z_hi * 2 + z_lo), core: 2. Of those that a mesh axis runs over, the one named last changes fastest.
Arguments:
- activations: bfloat16 [256, 16, 32, 256], P('tm', 'rows'), may hold values from -6 to 6
- cotangent: bfloat16 [256, 16, 32, 256], P('tm', 'rows'), may hold values from -6 to 6
- gain: float32 [256], replicated, may hold values from 0.1 to 1.9
- first_weight: bfloat16 [6912, 256], P('tm'), may hold values from -0.078125 to 0.078125
- second_weight: bfloat16 [6912, 256], P('tm'), may hold values from -0.078125 to 0.078125
Outputs:
- input_grad: bfloat16 [256, 16, 32, 256], P('tm', 'rows')
- weight_grad: float32 [6912, 128], P('tm')
All inputs are finite; a program needn't handle non-finite values.
Results may differ from a plain program's by a relative error of at most 0.017.
Values may be sent and summed in bfloat16 or wider, within the bound.
No kernel may reach another device: no remote copies, remote signals or barrier semaphores. Data moves between devices by JAX's collectives and lax.ppermute only.
A program may use at most 64 MiB of HBM per device.

v0:
```python
import jax
import jax.numpy as jnp
from jax import lax
from jax.sharding import PartitionSpec as P

CH = 128


epsilon = 1e-06
kernel_taps = [
    (along_t, along_h, along_w)
    for along_t in range(3)
    for along_h in range(3)
    for along_w in range(3)
]


def from_behind(block, axis, distance):
    devices = range(lax.axis_size(axis))
    route = [(i - distance, i) for i in devices if i - distance in devices]
    return lax.ppermute(block, axis, route)


def extended(block, sides, width):
    for axis, dim in sides:
        count = lax.axis_size(axis)
        forward = [(i, i + 1) for i in range(count - 1)]
        backward = [(target, source) for source, target in forward]
        low = lax.ppermute(
            lax.slice_in_dim(block, block.shape[dim] - width, None, axis=dim), axis, forward
        )
        high = lax.ppermute(lax.slice_in_dim(block, 0, width, axis=dim), axis, backward)
        block = jnp.concatenate([low, block, high], axis=dim)
    return block


def gather_taps(padded, frames, row_count, col_count, flipped):
    pieces = []
    for along_t, along_h, along_w in kernel_taps:
        if flipped:
            along_t, along_h, along_w = (2 - along_t, 2 - along_h, 2 - along_w)
        pieces.append(
            padded[
                along_t : along_t + frames,
                along_h : along_h + row_count,
                along_w : along_w + col_count,
            ]
        )
    stacked = jnp.stack(pieces, axis=3)
    return stacked.reshape(frames * row_count * col_count, len(kernel_taps), padded.shape[3])


def forward_conv(padded, weight, frames, row_count, col_count):
    patches = gather_taps(padded, frames, row_count, col_count, False)
    flat = patches.reshape(patches.shape[0], -1)
    result = jnp.dot(flat, weight, preferred_element_type=jnp.float32)
    return result.reshape(frames, row_count, col_count, weight.shape[1])


def transpose_conv(padded, weight, frames, row_count, col_count):
    channels = padded.shape[3]
    patches = gather_taps(padded, frames, row_count, col_count, True)
    kernel = weight.reshape(len(kernel_taps), channels, channels)
    result = lax.dot_general(
        patches, kernel, (((1, 2), (0, 2)), ((), ())), preferred_element_type=jnp.float32
    )
    return result.reshape(frames, row_count, col_count, channels)


def normalize(pre, gain):
    scale = lax.rsqrt(jnp.mean(pre * pre, axis=-1, keepdims=True) + epsilon)
    normed = pre * scale
    gated = normed * gain
    sigma = jax.nn.sigmoid(gated)
    return (scale, normed, gated, sigma)


def pad_columns(field):
    return jnp.pad(field, ((0, 0), (0, 0), (1, 1), (0, 0)))


def on_device(activations, cotangent, gain, first_weight, second_weight):
    frames, row_count, col_count, channels = activations.shape
    first_full = lax.all_gather(first_weight, "tm", axis=0, tiled=True)
    second_full = lax.all_gather(second_weight, "tm", axis=0, tiled=True)
    back_frames, rim_width = (2, 1)
    earlier = from_behind(activations[frames - back_frames :], "tm", 1)
    x_ext = jnp.concatenate([earlier, activations], axis=0)
    x_pad = pad_columns(extended(x_ext, (("rows", 1),), rim_width))
    pre = forward_conv(x_pad, first_full, frames, row_count, col_count)
    scale, normed, gated, sigma = normalize(pre, gain)
    act = (gated * sigma).astype(jnp.bfloat16)
    act_before = from_behind(act[frames - 2 :], "tm", 1)
    act_ext = jnp.concatenate([act_before, act], axis=0)
    a_pad = pad_columns(extended(act_ext, (("rows", 1),), 1))
    later = from_behind(cotangent[:2], "tm", -1)
    dy_ext = jnp.concatenate([cotangent, later], axis=0)
    dy_pad = pad_columns(extended(dy_ext, (("rows", 1),), 1))
    act_grad = transpose_conv(dy_pad, second_full, frames, row_count, col_count)
    norm_grad = act_grad * sigma * (1.0 + gated * (1.0 - sigma)) * gain
    pre_grad = scale * (norm_grad - normed * jnp.mean(norm_grad * normed, axis=-1, keepdims=True))
    pre_grad = pre_grad.astype(jnp.bfloat16)
    grad_later = from_behind(pre_grad[:2], "tm", -1)
    dh_ext = jnp.concatenate([pre_grad, grad_later], axis=0)
    dh_pad = pad_columns(extended(dh_ext, (("rows", 1),), 1))
    input_grad = transpose_conv(dh_pad, first_full, frames, row_count, col_count).astype(
        jnp.bfloat16
    )
    act_patches = gather_taps(a_pad, frames, row_count, col_count, False)
    act_flat = act_patches.reshape(act_patches.shape[0], -1)
    dy_cols = cotangent.reshape(-1, channels)[:, :CH]
    grad_term = lax.dot_general(
        act_flat, dy_cols, (((0,), (0,)), ((), ())), preferred_element_type=jnp.float32
    )
    summed = lax.psum(grad_term.astype(jnp.bfloat16), "rows").astype(jnp.float32)
    weight_grad = lax.psum_scatter(summed, "tm", scatter_dimension=0, tiled=True)
    return (input_grad, weight_grad)


def solution(mesh):
    return jax.shard_map(
        on_device,
        mesh=mesh,
        in_specs=(
            P("tm", "rows", None, None),
            P("tm", "rows", None, None),
            P(),
            P("tm", None),
            P("tm", None),
        ),
        out_specs=(P("tm", "rows", None, None), P("tm", None)),
        check_vma=False,
    )
```

profile of v0, /device:TPU:78, one launch (start us, length us, event | category | flops | bytes accessed | tf_op | source)
XLA Modules:
  0.0 957.8 jit_solution(11019368241903816531)
XLA Ops:
  7.2 0.7 all-gather.5.cloned.1.call-update
  7.9 0.8 slice.456
  8.8 2.3 collective-permute-start.3
  11.1 0.8 slice.427
  12.0 3.5 collective-permute-start
  15.5 1.3 dynamic-slice.4
  17.5 0.9 constant_dynamic-update-slice_fusion.30
  18.7 0.9 constant_dynamic-update-slice_fusion
  19.6 1.3 collective-permute-start.1
  20.9 1.3 collective-permute-start.2
  22.3 7.4 collective-permute-start.4
  29.7 1.4 collective-permute-start.5
  32.5 2.7 collective-permute-done.5
  35.4 0.7 constant_dynamic-update-slice_fusion.57
  36.8 0.7 constant_dynamic-update-slice_fusion.55
  37.5 0.7 constant_dynamic-update-slice_fusion.54
  39.5 0.7 constant_dynamic-update-slice_fusion.51
  40.9 0.7 constant_dynamic-update-slice_fusion.49
  41.6 0.7 constant_dynamic-update-slice_fusion.48
  43.6 0.7 constant_dynamic-update-slice_fusion.45
  45.6 0.7 constant_dynamic-update-slice_fusion.42
  46.3 0.7 constant_dynamic-update-slice_fusion.41
  47.7 0.7 constant_dynamic-update-slice_fusion.39
  48.4 0.7 constant_dynamic-update-slice_fusion.38
  49.0 0.7 constant_dynamic-update-slice_fusion.37
  49.7 0.7 constant_dynamic-update-slice_fusion.36
  51.7 0.7 constant_dynamic-update-slice_fusion.33
  52.4 0.7 constant_dynamic-update-slice_fusion.32
  53.8 253.9 %all-gather.5.cloned.1.call-done = bf16[64,108,256]{2,1,0:T(8,128)(2,1)} async-done(((bf16[1,108,256]{2,1,0:T(8,128)(2,1)}), bf16[64,108,256]{2,1,0:T(8,128)(2,1)}) %all-gather.5.cloned.1.call-update) | async-done | bytes 3538960 | tf_op jit(solution)/shard_map/all_gather | solution.py:84
  307.7 6.1 reshape.260
  313.8 3.8 multiply_reduce_fusion.1
  317.6 294.5 %all-gather.7.cloned.1.call-done = bf16[64,108,256]{2,1,0:T(8,128)(2,1)} async-done(((bf16[1,108,256]{2,1,0:T(8,128)(2,1)}), bf16[64,108,256]{2,1,0:T(8,128)(2,1)}) %all-gather.7.cloned.1.call-update) | async-done | bytes 3538960 | tf_op jit(solution)/shard_map/all_gather | solution.py:85
  612.1 6.1 reshape.261
  618.2 4.3 multiply_convert_fusion
  622.5 6.7 collective-permute-start.9
  629.4 1.9 collective-permute-start.6
  631.3 6.1 reshape.263
  637.4 1.3 collective-permute-start.10
  638.7 1.3 collective-permute-start.11
  640.0 6.0 collective-permute-start.7
  646.0 1.5 collective-permute-start.8
  648.6 2.3 copy.89
  650.9 3.6 copy.98
  654.6 2.4 convolution_convert_fusion
  657.2 0.7 constant_dynamic-update-slice_fusion.84
  659.2 0.7 constant_dynamic-update-slice_fusion.81
  661.2 0.7 constant_dynamic-update-slice_fusion.78
  661.9 0.7 constant_dynamic-update-slice_fusion.77
  663.3 0.7 constant_dynamic-update-slice_fusion.75
  665.3 0.7 constant_dynamic-update-slice_fusion.72
  665.9 0.7 constant_dynamic-update-slice_fusion.71
  667.3 0.7 constant_dynamic-update-slice_fusion.69
  669.3 0.7 constant_dynamic-update-slice_fusion.66
  671.3 0.7 constant_dynamic-update-slice_fusion.63
  672.7 0.7 constant_dynamic-update-slice_fusion.61
  673.3 0.7 constant_dynamic-update-slice_fusion.60
  675.3 80.2 %all-reduce.8.cloned.1.call-done = bf16[6912,128]{1,0:T(8,128)(2,1)} async-done(((bf16[6912,128]{1,0:T(8,128)(2,1)}), bf16[6912,128]{1,0:T(8,128)(2,1)}) %all-reduce.8.cloned.1.call-update) | async-done | bytes 1769488 | tf_op jit(solution)/shard_map/psum | solution.py:115
  755.6 1.7 convert_element_type.24
  757.3 164.2 %fusion = f32[112,128]{1,0:T(8,128)} fusion(f32[6912,128]{1,0:T(8,128)S(1)} %convert_element_type.24), kind=kCustom, calls=%all-reduce-scatter | all-reduce-scatter fusion | flops 917505 | bytes 3598336
  921.5 4.2 collective-permute-start.12
  925.8 8.8 collective-permute-start.13
  934.6 0.7 slice.667
  935.3 9.8 %collective-permute-start.14 = (f32[28,128]{1,0:T(8,128)S(1)}, f32[28,128]{1,0:T(8,128)S(1)}, u32[]{:S(2)}, u32[]{:S(2)}) collective-permute-start(f32[28,128]{1,0:T(8,128)S(1)} %slice.667), channel_id=1, source_target_pairs={{0,24},{8,32},{16,40},{24,48},{32,56},{40,64},{48,72},{56,80},{64,... | collective-permute-start | bytes 43016
  945.1 4.2 fusion.1
  (134 shorter events, 22.9 us)
Async XLA Ops:
  7.2 300.6 %all-gather.5.cloned.1.call-start = ((), (), s32[]{:S(2)}) async-start(), calls=%async_computation.1 | async-start | bytes 3727360 | tf_op jit(solution)/shard_map/all_gather | solution.py:84
  7.9 604.2 %all-gather.7.cloned.1.call-start = ((), (), s32[]{:S(2)}) async-start(), calls=%async_computation.2 | async-start | bytes 3727360 | tf_op jit(solution)/shard_map/all_gather | solution.py:85
  8.8 13.4 %collective-permute-start.3 = (bf16[2,2,32,256]{3,2,1,0:T(8,128)(2,1)S(1)}, bf16[2,2,32,256]{3,2,1,0:T(8,128)(2,1)S(1)}, u32[]{:S(2)}, u32[]{:S(2)}) collective-permute-start(bf16[2,2,32,256]{3,2,1,0:T(8,128)(2,1)S(1)} %slice.456), channel_id=1, source_target_pairs={{8,0},{16,8},{24,16},{32,24},{40,32},{48,40},{56,48},{64,56},{72,6... | collective-permute-start | bytes 196616 | tf_op jit(solution)/shard_map/ppermute | solution.py:21
  12.0 6.7 collective-permute-start
  15.5 740.1 %all-reduce.8.cloned.1.call-start = ((), (), s32[]{:S(2)}) async-start(), calls=%async_computation | async-start | bytes 3538944 | tf_op jit(solution)/shard_map/psum | solution.py:115
  19.6 11.6 %collective-permute-start.1 = (bf16[6,1,32,256]{3,2,1,0:T(8,128)(2,1)S(1)}, bf16[6,1,32,256]{3,2,1,0:T(8,128)(2,1)S(1)}, u32[]{:S(2)}, u32[]{:S(2)}) collective-permute-start(bf16[6,1,32,256]{3,2,1,0:T(8,128)(2,1)S(1)} %get-tuple-element.14), channel_id=1, source_target_pairs={{0,1},{1,2},{2,3},{3,4},{4,5},{5,6},{6,7},{8,9},{9,10},{10,11},{11... | collective-permute-start | bytes 294920 | tf_op jit(solution)/shard_map/ppermute | solution.py:29
  20.9 10.3 %collective-permute-start.2 = (bf16[6,1,32,256]{3,2,1,0:T(8,128)(2,1)S(1)}, bf16[6,1,32,256]{3,2,1,0:T(8,128)(2,1)S(1)}, u32[]{:S(2)}, u32[]{:S(2)}) collective-permute-start(bf16[6,1,32,256]{3,2,1,0:T(8,128)(2,1)S(1)} %get-tuple-element.15), channel_id=1, source_target_pairs={{1,0},{2,1},{3,2},{4,3},{5,4},{6,5},{7,6},{9,8},{10,9},{11,10},{12... | collective-permute-start | bytes 294920 | tf_op jit(solution)/shard_map/ppermute | solution.py:32
  22.3 10.2 %collective-permute-start.4 = (bf16[6,1,32,256]{3,2,1,0:T(8,128)(2,1)S(1)}, bf16[6,1,32,256]{3,2,1,0:T(8,128)(2,1)S(1)}, u32[]{:S(2)}, u32[]{:S(2)}) collective-permute-start(bf16[6,1,32,256]{3,2,1,0:T(8,128)(2,1)S(1)} %get-tuple-element.16), channel_id=1, source_target_pairs={{0,1},{1,2},{2,3},{3,4},{4,5},{5,6},{6,7},{8,9},{9,10},{10,11},{11... | collective-permute-start | bytes 294920 | tf_op jit(solution)/shard_map/ppermute | solution.py:29
  29.7 2.3 copy-start.2
  29.7 5.5 collective-permute-start.5
  32.4 18.0 %copy-start = (bf16[4,2,32,256]{3,2,1,0:T(8,128)(2,1)S(1)}, bf16[4,2,32,256]{3,2,1,0:T(8,128)(2,1)}, u32[]{:S(2)}) copy-start(bf16[4,2,32,256]{3,2,1,0:T(8,128)(2,1)} %param.6) | copy-start | bytes 393220
  317.6 300.6 %copy-start.4 = (f32[4,2,32,256]{3,2,1,0:T(8,128)S(1)}, f32[4,2,32,256]{3,2,1,0:T(8,128)}, u32[]{:S(2)}) copy-start(f32[4,2,32,256]{3,2,1,0:T(8,128)} %get-tuple-element.19) | copy-start | bytes 786436
  317.6 300.6 %copy-start.5 = (f32[256]{0:T(256)S(1)}, f32[256]{0:T(256)}, u32[]{:S(2)}) copy-start(f32[256]{0:T(256)} %param.7) | copy-start | bytes 3076
  622.5 14.9 %collective-permute-start.9 = (bf16[2,2,32,256]{3,2,1,0:T(8,128)(2,1)S(1)}, bf16[2,2,32,256]{3,2,1,0:T(8,128)(2,1)S(1)}, u32[]{:S(2)}, u32[]{:S(2)}) collective-permute-start(bf16[2,2,32,256]{3,2,1,0:T(8,128)(2,1)S(1)} %slice.635), channel_id=1, source_target_pairs={{0,8},{8,16},{16,24},{24,32},{32,40},{40,48},{48,56},{56,64},{64,7... | collective-permute-start | bytes 196616 | tf_op jit(solution)/shard_map/ppermute | solution.py:21
  629.4 10.6 %collective-permute-start.6 = (bf16[2,2,32,256]{3,2,1,0:T(8,128)(2,1)S(1)}, bf16[2,2,32,256]{3,2,1,0:T(8,128)(2,1)S(1)}, u32[]{:S(2)}, u32[]{:S(2)}) collective-permute-start(bf16[2,2,32,256]{3,2,1,0:T(8,128)(2,1)S(1)} %slice.604), channel_id=1, source_target_pairs={{8,0},{16,8},{24,16},{32,24},{40,32},{48,40},{56,48},{64,56},{72,6... | collective-permute-start | bytes 196616 | tf_op jit(solution)/shard_map/ppermute | solution.py:21
  637.4 10.1 %collective-permute-start.10 = (bf16[6,1,32,256]{3,2,1,0:T(8,128)(2,1)S(1)}, bf16[6,1,32,256]{3,2,1,0:T(8,128)(2,1)S(1)}, u32[]{:S(2)}, u32[]{:S(2)}) collective-permute-start(bf16[6,1,32,256]{3,2,1,0:T(8,128)(2,1)S(1)} %get-tuple-element.8), channel_id=1, source_target_pairs={{0,1},{1,2},{2,3},{3,4},{4,5},{5,6},{6,7},{8,9},{9,10},{10,11},{11... | collective-permute-start | bytes 294920 | tf_op jit(solution)/shard_map/ppermute | solution.py:29
  638.7 8.8 collective-permute-start.11
  640.0 16.9 %collective-permute-start.7 = (bf16[6,1,32,256]{3,2,1,0:T(8,128)(2,1)S(1)}, bf16[6,1,32,256]{3,2,1,0:T(8,128)(2,1)S(1)}, u32[]{:S(2)}, u32[]{:S(2)}) collective-permute-start(bf16[6,1,32,256]{3,2,1,0:T(8,128)(2,1)S(1)} %get-tuple-element.12), channel_id=1, source_target_pairs={{0,1},{1,2},{2,3},{3,4},{4,5},{5,6},{6,7},{8,9},{9,10},{10,11},{11... | collective-permute-start | bytes 294920 | tf_op jit(solution)/shard_map/ppermute | solution.py:29
  646.0 10.9 %collective-permute-start.8 = (bf16[6,1,32,256]{3,2,1,0:T(8,128)(2,1)S(1)}, bf16[6,1,32,256]{3,2,1,0:T(8,128)(2,1)S(1)}, u32[]{:S(2)}, u32[]{:S(2)}) collective-permute-start(bf16[6,1,32,256]{3,2,1,0:T(8,128)(2,1)S(1)} %get-tuple-element.13), channel_id=1, source_target_pairs={{1,0},{2,1},{3,2},{4,3},{5,4},{6,5},{7,6},{9,8},{10,9},{11,10},{12... | collective-permute-start | bytes 294920 | tf_op jit(solution)/shard_map/ppermute | solution.py:32
  650.9 3.6 copy-start.1
  921.5 28.5 %collective-permute-start.12 = (f32[112,128]{1,0:T(8,128)}, f32[112,128]{1,0:T(8,128)S(1)}, u32[]{:S(2)}, u32[]{:S(2)}) collective-permute-start(f32[112,128]{1,0:T(8,128)} %fusion), channel_id=1, source_target_pairs={{0,8},{8,16},{16,24},{24,32},{32,40},{40,48},{48,56},{56,64},{64,7... | collective-permute-start | bytes 172040
  925.8 24.3 %collective-permute-start.13 = (f32[112,128]{1,0:T(8,128)}, f32[112,128]{1,0:T(8,128)S(1)}, u32[]{:S(2)}, u32[]{:S(2)}) collective-permute-start(f32[112,128]{1,0:T(8,128)} %fusion), channel_id=1, source_target_pairs={{0,16},{8,24},{16,32},{24,40},{32,48},{40,56},{48,64},{56,72},{64,... | collective-permute-start | bytes 172040
  935.3 14.7 %copy-start.3 = (f32[112,128]{1,0:T(8,128)S(1)}, f32[112,128]{1,0:T(8,128)}, u32[]{:S(2)}) copy-start(f32[112,128]{1,0:T(8,128)} %fusion) | copy-start | bytes 172036
  935.3 14.7 %collective-permute-start.14 = (f32[28,128]{1,0:T(8,128)S(1)}, f32[28,128]{1,0:T(8,128)S(1)}, u32[]{:S(2)}, u32[]{:S(2)}) collective-permute-start(f32[28,128]{1,0:T(8,128)S(1)} %slice.667), channel_id=1, source_target_pairs={{0,24},{8,32},{16,40},{24,48},{32,56},{40,64},{48,72},{56,80},{64,... | collective-permute-start | bytes 43016
Sparse Core Ops, SparseCore 0:
  10.1 297.6 all-gather.4
  309.8 302.2 all-gather.6
  657.1 98.4 all-reduce.7
where the time goes:
time: 959 us; the launch traced here: 958 us
  waiting for transfers between devices  632 us (66%)
  blocking collectives  164 us (17%)
  local copies, waits for them, and re-layouts  64 us (7%)
  starting transfers between devices  58.9 us (6%)
  between operations  15.3 us (2%)
  matrix products  14.7 us (2%)
    all_gather x1, waiting for transfers between devices, on_device(): second_full = lax.all_gather(second_weight, 'tm', axis=0, tiled=True)  294 us
    all_gather x1, waiting for transfers between devices, on_device(): first_full = lax.all_gather(first_weight, 'tm', axis=0, tiled=True)  254 us
    unnamed x1, blocking collectives  164 us
    psum x1, waiting for transfers between devices, on_device(): lax.psum(grad_term.astype(jnp.bfloat16), 'rows').astype(jnp.float32)  80.2 us
    unnamed x109, local copies, waits for them, and re-layouts  45.2 us
    unnamed x3, starting transfers between devices  22.9 us
  transfers between devices with their start and end apart: 18, of which 5 were waited for; matrix products, arithmetic and copies ran while one was open for 8% of the time, Pallas kernels for 0%

commit v1 on v0

v1 whole, which is shorter than its diff:
```python
import functools

import jax
import jax.numpy as jnp
from jax import lax
from jax.experimental import pallas as pl
from jax.experimental.pallas import tpu as pltpu
from jax.sharding import PartitionSpec as P

CH = 128
C = 256
W = 32
HALF = 128
ROWS = 6912
EPS = 1e-06
BF = jnp.bfloat16
F32 = jnp.float32

YZ_GROUPS = [[x * 16 + k for k in range(16)] for x in range(4)]
X_GROUPS = [[x * 16 + k for x in range(4)] for k in range(16)]
Y_GROUPS = [[b * 8 + k for k in range(8)] for b in range(8)]
CORE_GROUPS = [[2 * z, 2 * z + 1] for z in range(4)]


def spread(block, axis, groups):
    count = len(groups[0])
    operand = jnp.broadcast_to(block[None], (count,) + block.shape)
    return lax.all_to_all(operand, axis, 0, 0, axis_index_groups=groups, tiled=True)


def swap(block, axis, mask):
    count = lax.axis_size(axis)
    return lax.ppermute(block, axis, [(i, i ^ mask) for i in range(count)])


def in_order(blocks, low, high):
    a, b, c, d = blocks
    a, b = jnp.where(low, b, a), jnp.where(low, a, b)
    c, d = jnp.where(low, d, c), jnp.where(low, c, d)
    a, c = jnp.where(high, c, a), jnp.where(high, a, c)
    b, d = jnp.where(high, d, b), jnp.where(high, b, d)
    return jnp.stack([a, b, c, d])


def exchange(block, index, low_mask, high_mask):
    blocks = [block] + [swap(block, "tm", m) for m in (low_mask, high_mask, low_mask | high_mask)]
    return in_order(blocks, (index & low_mask) != 0, (index & high_mask) != 0)


def shift_ppermute(block, axis, distance):
    count = lax.axis_size(axis)
    route = [(i, i + distance) for i in range(count) if 0 <= i + distance < count]
    return lax.ppermute(block, axis, route)


def fill_shifts(out, piece, at, column_of):
    frames, rows = piece.shape[:2]
    flat = piece.reshape(frames * rows * W, piece.shape[3]).astype(F32)
    column = column_of(flat.shape)
    before = jnp.where(column == 0, 0.0, pltpu.roll(flat, 1, 0))
    after = jnp.where(column == W - 1, 0.0, pltpu.roll(flat, flat.shape[0] - 1, 0))
    out[1, :, at : at + rows] = piece
    out[0, :, at : at + rows] = before.astype(BF).reshape(piece.shape)
    out[2, :, at : at + rows] = after.astype(BF).reshape(piece.shape)


def column_of(shape):
    return lax.broadcasted_iota(jnp.int32, shape, 0) % W


def normalize(pre, gain):
    scale = lax.rsqrt(jnp.mean(pre * pre, axis=-1, keepdims=True) + EPS)
    normed = pre * scale
    gated = normed * gain
    sigma = 1.0 / (1.0 + jnp.exp(-gated))
    return scale, normed, gated, sigma


def forward_kernel(x_lo, x_mid, x_hi, g_lo, g_mid, g_hi, gain, w1, pre_ref, wg_ref, xs, cs):
    for n, piece in enumerate((x_lo, x_mid, x_hi)):
        for f in range(0, 8, 2):
            fill_shifts(xs.at[:, f : f + 2], piece[f : f + 2], 2 * n, column_of)
    for n, piece in enumerate((g_lo, g_mid, g_hi)):
        for f in range(0, 6, 2):
            fill_shifts(cs.at[:, f : f + 2], piece[f : f + 2, :, :, :CH], 2 * n, column_of)
    for i in range(3):
        for j in range(3):
            lhs = jnp.concatenate(
                [xs[k, i : i + 6, j : j + 4].reshape(768, C) for k in range(3)], axis=1
            )
            at = (i * 3 + j) * 3 * C
            rhs = jnp.concatenate([w1[0, at : at + 3 * C], w1[1, at : at + 3 * C]], axis=1)
            part = jnp.dot(lhs, rhs, preferred_element_type=F32).reshape(6, 4, W, C)
            if i == 0 and j == 0:
                pre_ref[...] = part
            else:
                pre_ref[...] += part
    _, _, gated, sigma = normalize(pre_ref[:4, 1:3].reshape(256, C), gain[...])
    act_t = (gated * sigma).T.astype(BF)
    for i in range(3):
        for j in range(3):
            for k in range(3):
                rhs = cs[2 - k, 2 - i : 6 - i, 3 - j : 5 - j].reshape(256, CH)
                term = jnp.dot(act_t, rhs, preferred_element_type=F32).astype(BF)
                start = ((i * 3 + j) * 3 + k) * C
                done = 0
                while done < C:
                    block, row = divmod(start + done, 864)
                    count = min(C - done, 864 - row)
                    wg_ref[block % 2, block // 2, row : row + count] = term[done : done + count]
                    done += count


def backward_kernel(flags, g_lo, g_mid, g_hi, gain, pre, w1, w2_own, w2_other, out, cs, ps, acc):
    core_one = flags[2] == 1
    for n, piece in enumerate((g_lo, g_mid, g_hi)):
        for f in range(0, 8, 2):
            here = piece[f : f + 2]
            turned = jnp.concatenate([here[..., HALF:], here[..., :HALF]], axis=-1)
            here = jnp.where(core_one, turned, here)
            fill_shifts(cs.at[:, f : f + 2], here, 2 * n, column_of)
    nt = (((1,), (1,)), ((), ()))
    for i in range(3):
        for j in range(3):
            for k in range(3):
                lhs = cs[2 - k, 2 - i : 8 - i, 2 - j : 6 - j].reshape(768, C)
                at = ((i * 3 + j) * 3 + k) * C
                rhs = jnp.concatenate([w2_own[at : at + C], w2_other[at : at + C]], axis=1)
                part = lax.dot_general(lhs, rhs, nt, preferred_element_type=F32)
                if i == 0 and j == 0 and k == 0:
                    acc[...] = part
                else:
                    acc[...] += part
    for t in range(6):
        for h in range(4):
            at = (t * 4 + h) * W
            scale, normed, gated, sigma = normalize(pre[t, h], gain[...])
            norm_grad = acc[at : at + W] * sigma * (1.0 + gated * (1.0 - sigma)) * gain[...]
            pre_grad = scale * (
                norm_grad - normed * jnp.mean(norm_grad * normed, axis=-1, keepdims=True)
            )
            if t >= 4:
                pre_grad = jnp.where(flags[0] == flags[3], 0.0, pre_grad)
            if h == 0:
                pre_grad = jnp.where(flags[1] == 0, 0.0, pre_grad)
            if h == 3:
                pre_grad = jnp.where(flags[1] == flags[4], 0.0, pre_grad)
            fill_shifts(
                ps.at[:, t : t + 1], pre_grad.astype(BF).reshape(1, 1, W, C), h, column_of
            )
    total = None
    for i in range(3):
        for j in range(3):
            for k in range(3):
                lhs = ps[2 - k, 2 - i : 6 - i, 2 - j : 4 - j].reshape(256, C)
                at = ((i * 3 + j) * 3 + k) * C
                rhs = jnp.concatenate([w1[0, at : at + C], w1[1, at : at + C]], axis=1)
                part = lax.dot_general(lhs, rhs, nt, preferred_element_type=F32)
                if i == 0 and j == 0 and k == 0:
                    acc[:256] = part
                else:
                    acc[:256] += part
    out[...] = acc[:256].reshape(4, 2, W, C).astype(BF)


VMEM = pl.BlockSpec(memory_space=pltpu.VMEM)
SMEM = pl.BlockSpec(memory_space=pltpu.SMEM)
PARAMS = pltpu.CompilerParams(vmem_limit_bytes=48 * 1024 * 1024)


def call_forward(x_parts, g_parts, gain, w1):
    return pl.pallas_call(
        forward_kernel,
        out_shape=(
            jax.ShapeDtypeStruct((6, 4, W, C), F32),
            jax.ShapeDtypeStruct((2, 4, 864, CH), BF),
        ),
        in_specs=[VMEM] * 8,
        out_specs=(VMEM, VMEM),
        scratch_shapes=[pltpu.VMEM((3, 8, 6, W, C), BF), pltpu.VMEM((3, 6, 6, W, CH), BF)],
        compiler_params=PARAMS,
        cost_estimate=pl.CostEstimate(
            flops=2 * 768 * ROWS * C + 2 * 256 * ROWS * CH, bytes_accessed=8 << 20, transcendentals=0
        ),
        name="forward_and_terms",
    )(*x_parts, *g_parts, gain, w1)


def call_backward(flags, g_parts, gain, pre, w1, w2_own, w2_other):
    return pl.pallas_call(
        backward_kernel,
        out_shape=jax.ShapeDtypeStruct((4, 2, W, C), BF),
        in_specs=[SMEM] + [VMEM] * 8,
        out_specs=VMEM,
        scratch_shapes=[
            pltpu.VMEM((3, 8, 6, W, C), BF),
            pltpu.VMEM((3, 6, 4, W, C), BF),
            pltpu.VMEM((768, C), F32),
        ],
        compiler_params=PARAMS,
        cost_estimate=pl.CostEstimate(
            flops=2 * 1024 * ROWS * C, bytes_accessed=10 << 20, transcendentals=0
        ),
        name="input_gradient",
    )(flags, *g_parts, gain, pre, w1, w2_own, w2_other)


def on_device(activations, cotangent, gain, first_weight, second_weight):
    tm, rows = lax.axis_index("tm"), lax.axis_index("rows")
    tm_count, rows_count = lax.axis_size("tm"), lax.axis_size("rows")
    core = rows % 2
    z_lo = (tm // 8) % 2
    gain = gain.reshape(1, C)

    half1 = lax.dynamic_slice_in_dim(first_weight, core * HALF, HALF, axis=1)
    half2 = lax.dynamic_slice_in_dim(second_weight, core * HALF, HALF, axis=1)

    w1 = spread(half1, "tm", YZ_GROUPS).reshape(16 * 108, HALF)
    w1 = spread(w1, "tm", X_GROUPS).reshape(ROWS, HALF)
    w1 = spread(w1, "rows", CORE_GROUPS)

    x_t = jnp.concatenate(
        [
            shift_ppermute(activations[2:], "tm", 1),
            activations,
            shift_ppermute(activations[:2], "tm", -1),
        ],
        axis=0,
    )
    x_parts = (shift_ppermute(x_t, "rows", 1), x_t, shift_ppermute(x_t, "rows", -1))
    g_t = jnp.concatenate([cotangent, shift_ppermute(cotangent, "tm", -1)], axis=0)
    g_parts = (shift_ppermute(g_t, "rows", 1), g_t, shift_ppermute(g_t, "rows", -1))

    w2 = exchange(half2, tm, 2, 4)
    w2 = exchange(w2, tm, 1, 8)
    w2 = w2.reshape(2, 2, 4, 108, HALF).transpose(0, 2, 1, 3, 4).reshape(16 * 108, HALF)
    w2 = exchange(w2, tm, 16, 32).reshape(ROWS, HALF)
    w2_other = swap(w2, "rows", 1)

    pre, terms = call_forward(x_parts, g_parts, gain, w1)

    terms = lax.all_to_all(terms, "rows", 0, 0, axis_index_groups=CORE_GROUPS, tiled=True)
    terms = terms.astype(F32).sum(0).astype(BF)
    terms = lax.all_to_all(terms, "tm", 0, 0, axis_index_groups=X_GROUPS, tiled=True)
    terms = terms.astype(F32).sum(0).astype(BF).reshape(8, 108, CH)
    terms = lax.all_to_all(terms, "tm", 0, 0, axis_index_groups=Y_GROUPS, tiled=True)
    total = terms.astype(F32).sum(0)
    total = total + swap(total, "tm", 8)
    left, right, far = (
        lax.ppermute(total, "rows", [(i, (i + d) % rows_count) for i in range(rows_count)])
        for d in (2, rows_count - 2, 4)
    )
    total = (total + far) + (left + right)
    weight_grad = jnp.where(core == z_lo, total, swap(total, "rows", 1))

    flags = jnp.stack([tm, rows, core, tm_count - 1, rows_count - 1]).astype(jnp.int32)
    input_grad = call_backward(flags, g_parts, gain, pre, w1, w2, w2_other)
    return (input_grad, weight_grad)


def solution(mesh):
    return jax.shard_map(
        on_device,
        mesh=mesh,
        in_specs=(
            P("tm", "rows", None, None),
            P("tm", "rows", None, None),
            P(),
            P("tm", None),
            P("tm", None),
        ),
        out_specs=(P("tm", "rows", None, None), P("tm", None)),
        check_vma=False,
    )
```

time: 959 us -> 207 us (0.22)
  the two profiles are of different devices: /device:TPU:78 before, /device:TPU:1 now
where the time goes in v1:
time: 207 us; the launch traced here: 205 us
  starting transfers between devices  111 us (54%)
  blocking collectives  35.2 us (17%)
  waiting for transfers between devices  26.2 us (13%)
  Pallas kernels  17 us (8%)
  local copies, waits for them, and re-layouts  10.1 us (5%)
  other arithmetic  4.58 us (2%)
    ppermute x12, starting transfers between devices, swap(): return lax.ppermute(block, axis, [(i, i ^ mask) for i in range(count)])  46 us
    ppermute x7, starting transfers between devices, shift_ppermute(): return lax.ppermute(block, axis, route)  28.9 us
    ppermute x12, waiting for transfers between devices, swap(): return lax.ppermute(block, axis, [(i, i ^ mask) for i in range(count)])  21.4 us
    all_to_all x3, starting transfers between devices, spread(): lax.all_to_all(operand, axis, 0, 0, axis_index_groups=groups, tiled=True)  19.4 us
    ppermute x3, starting transfers between devices, on_device(): lax.ppermute(total, 'rows', [(i, (i + d) % rows_count) for i in range(row...  16.7 us
    all_to_all x1, blocking collectives, on_device(): lax.all_to_all(terms, 'tm', 0, 0, axis_index_groups=X_GROUPS, tiled=True)  16.2 us
    all_to_all x1, blocking collectives, on_device(): lax.all_to_all(terms, 'tm', 0, 0, axis_index_groups=Y_GROUPS, tiled=True)  13 us
    pallas_call x1, Pallas kernels, call_backward(): pl.pallas_call(backward_kernel, out_shape=jax.ShapeDtypeStruct((4, 2, W,...  9.12 us
  transfers between devices with their start and end apart: 25, of which 7 were waited for; matrix products, arithmetic and copies ran while one was open for 5% of the time, Pallas kernels for 8%

profile of v1, /device:TPU:1, one launch (start us, length us, event | category | flops | bytes accessed | tf_op | source)
XLA Modules:
  0.0 205.4 jit_solution(9801751777541706885)
XLA Ops:
  0.6 0.0 copy-start
  0.7 0.8 constant_dynamic-slice_fusion
  1.5 6.7 %collective-permute-start.7 = (bf16[108,128]{1,0:T(8,128)(2,1)S(1)}, bf16[108,128]{1,0:T(8,128)(2,1)S(1)}, u32[]{:S(2)}, u32[]{:S(2)}) collective-permute-start(bf16[108,128]{1,0:T(8,128)(2,1)S(1)} %constant_dynamic-slice_fusion), channel_id=1, source_target_pairs={{0,48},{8,56},{16,32},{24,40},{32,16},{40,24},{48,0},{56,8},{64,11... | collective-permute-start | bytes 82952 | tf_op jit(solution)/shard_map/ppermute | solution.py:33
  8.2 3.5 %collective-permute-start.8 = (bf16[108,128]{1,0:T(8,128)(2,1)S(1)}, bf16[108,128]{1,0:T(8,128)(2,1)S(1)}, u32[]{:S(2)}, u32[]{:S(2)}) collective-permute-start(bf16[108,128]{1,0:T(8,128)(2,1)S(1)} %constant_dynamic-slice_fusion), channel_id=1, source_target_pairs={{0,32},{8,40},{16,48},{24,56},{32,0},{40,8},{48,16},{56,24},{64,96... | collective-permute-start | bytes 82952 | tf_op jit(solution)/shard_map/ppermute | solution.py:33
  11.8 2.4 %collective-permute-start.9 = (bf16[108,128]{1,0:T(8,128)(2,1)S(1)}, bf16[108,128]{1,0:T(8,128)(2,1)S(1)}, u32[]{:S(2)}, u32[]{:S(2)}) collective-permute-start(bf16[108,128]{1,0:T(8,128)(2,1)S(1)} %constant_dynamic-slice_fusion), channel_id=1, source_target_pairs={{0,16},{8,24},{16,0},{24,8},{32,48},{40,56},{48,32},{56,40},{64,80... | collective-permute-start | bytes 82952 | tf_op jit(solution)/shard_map/ppermute | solution.py:33
  14.2 0.8 broadcast_in_dim.20
  15.0 8.3 %all-to-all-start = ((bf16[16,108,128]{2,1,0:T(8,128)(2,1)}), bf16[16,108,128]{2,1,0:T(8,128)(2,1)S(1)}, u32[]{:S(2)}, u32[]{:S(2)}) async-start(bf16[16,108,128]{2,1,0:T(8,128)(2,1)} %broadcast_in_dim.20), calls=%async_computation | async-start | bytes 917504 | tf_op jit(solution)/shard_map/all_to_all | solution.py:28
  23.3 0.9 fusion
  24.2 3.3 %collective-permute-start.3 = (bf16[2,2,32,256]{3,2,1,0:T(8,128)(2,1)S(1)}, bf16[2,2,32,256]{3,2,1,0:T(8,128)(2,1)S(1)}, u32[]{:S(2)}, u32[]{:S(2)}) collective-permute-start(bf16[2,2,32,256]{3,2,1,0:T(8,128)(2,1)S(1)} %get-tuple-element.14), channel_id=1, source_target_pairs={{0,8},{8,16},{16,24},{24,32},{32,40},{40,48},{48,56},{56,64},{64,7... | collective-permute-start | bytes 196616 | tf_op jit(solution)/shard_map/ppermute | solution.py:53
  27.5 1.3 collective-permute-start
  28.8 0.0 collective-permute-done.7
  28.8 0.0 collective-permute-done.8
  28.9 4.9 %collective-permute-start.10 = (bf16[4,108,128]{2,1,0:T(8,128)(2,1)S(1)}, bf16[4,108,128]{2,1,0:T(8,128)(2,1)S(1)}, u32[]{:S(2)}, u32[]{:S(2)}) collective-permute-start(bf16[4,108,128]{2,1,0:T(8,128)(2,1)S(1)} %pad_maximum_fusion.2), channel_id=1, source_target_pairs={{0,72},{8,64},{16,88},{24,80},{32,104},{40,96},{48,120},{56,112},{... | collective-permute-start | bytes 331784 | tf_op jit(solution)/shard_map/ppermute | solution.py:33
  33.8 3.1 %collective-permute-start.11 = (bf16[4,108,128]{2,1,0:T(8,128)(2,1)S(1)}, bf16[4,108,128]{2,1,0:T(8,128)(2,1)S(1)}, u32[]{:S(2)}, u32[]{:S(2)}) collective-permute-start(bf16[4,108,128]{2,1,0:T(8,128)(2,1)S(1)} %pad_maximum_fusion.2), channel_id=1, source_target_pairs={{0,64},{8,72},{16,80},{24,88},{32,96},{40,104},{48,112},{56,120},{... | collective-permute-start | bytes 331784 | tf_op jit(solution)/shard_map/ppermute | solution.py:33
  37.0 3.1 %collective-permute-start.12 = (bf16[4,108,128]{2,1,0:T(8,128)(2,1)S(1)}, bf16[4,108,128]{2,1,0:T(8,128)(2,1)S(1)}, u32[]{:S(2)}, u32[]{:S(2)}) collective-permute-start(bf16[4,108,128]{2,1,0:T(8,128)(2,1)S(1)} %pad_maximum_fusion.2), channel_id=1, source_target_pairs={{0,8},{8,0},{16,24},{24,16},{32,40},{40,32},{48,56},{56,48},{64,72... | collective-permute-start | bytes 331784 | tf_op jit(solution)/shard_map/ppermute | solution.py:33
  40.1 0.9 collective-permute-done.10
  41.0 1.3 collective-permute-start.4
  42.3 1.0 collective-permute-done.11
  43.4 0.1 select_bitcast_fusion.7
  43.5 0.1 broadcast_in_dim.21
  43.6 1.4 broadcast_in_dim.22
  45.0 5.1 %all-to-all-start.1 = ((bf16[4,1728,128]{2,1,0:T(8,128)(2,1)}), bf16[4,1728,128]{2,1,0:T(8,128)(2,1)}, u32[]{:S(2)}, u32[]{:S(2)}) async-start(bf16[4,1728,128]{2,1,0:T(8,128)(2,1)} %broadcast_in_dim.22), calls=%async_computation.1 | async-start | bytes 3538944 | tf_op jit(solution)/shard_map/all_to_all | solution.py:28
  50.2 0.1 pad_maximum_fusion.1
  50.3 0.1 reshape.24
  50.4 5.0 %collective-permute-start.13 = (bf16[1728,128]{1,0:T(8,128)(2,1)S(1)}, bf16[1728,128]{1,0:T(8,128)(2,1)S(1)}, u32[]{:S(2)}, u32[]{:S(2)}) collective-permute-start(bf16[1728,128]{1,0:T(8,128)(2,1)S(1)} %reshape.24), channel_id=1, source_target_pairs={{0,384},{8,392},{16,400},{24,408},{32,416},{40,424},{48,432},{56,4... | collective-permute-start | bytes 1327112 | tf_op jit(solution)/shard_map/ppermute | solution.py:33
  55.4 2.0 collective-permute-start.14
  57.4 0.0 collective-permute-done.3
  57.4 2.4 %collective-permute-start.15 = (bf16[1728,128]{1,0:T(8,128)(2,1)S(1)}, bf16[1728,128]{1,0:T(8,128)(2,1)S(1)}, u32[]{:S(2)}, u32[]{:S(2)}) collective-permute-start(bf16[1728,128]{1,0:T(8,128)(2,1)S(1)} %reshape.24), channel_id=1, source_target_pairs={{0,128},{8,136},{16,144},{24,152},{32,160},{40,168},{48,176},{56,1... | collective-permute-start | bytes 1327112 | tf_op jit(solution)/shard_map/ppermute | solution.py:33
  59.9 0.0 collective-permute-done.4
  59.9 9.6 %collective-permute-start.5 = (bf16[8,2,32,256]{3,2,1,0:T(8,128)(2,1)S(1)}, bf16[8,2,32,256]{3,2,1,0:T(8,128)(2,1)S(1)}, u32[]{:S(2)}, u32[]{:S(2)}) collective-permute-start(bf16[8,2,32,256]{3,2,1,0:T(8,128)(2,1)S(1)} %constant_dynamic-update-slice_fusion.2.x_mid), channel_id=1, source_target_pairs={{0,1},{1,2},{2,3},{3,4},{4,5},{5,6},{6,7},{8,9},{9,10},{10,11},{11... | collective-permute-start | bytes 786440 | tf_op jit(solution)/shard_map/ppermute | solution.py:53
  69.5 1.9 collective-permute-start.6
  71.4 17.6 %collective-permute-done.13 = bf16[1728,128]{1,0:T(8,128)(2,1)S(1)} collective-permute-done((bf16[1728,128]{1,0:T(8,128)(2,1)S(1)}, bf16[1728,128]{1,0:T(8,128)(2,1)S(1)}, u32[]{:S(2)}, u32[]{:S(2)}) %collective-permute-start.13) | collective-permute-done | bytes 442400 | tf_op jit(solution)/shard_map/ppermute | solution.py:33
  89.0 9.7 %collective-permute-start.1 = (bf16[8,2,32,256]{3,2,1,0:T(8,128)(2,1)S(1)}, bf16[8,2,32,256]{3,2,1,0:T(8,128)(2,1)S(1)}, u32[]{:S(2)}, u32[]{:S(2)}) collective-permute-start(bf16[8,2,32,256]{3,2,1,0:T(8,128)(2,1)S(1)} %constant_dynamic-update-slice_fusion.g_mid), channel_id=1, source_target_pairs={{0,1},{1,2},{2,3},{3,4},{4,5},{5,6},{6,7},{8,9},{9,10},{10,11},{11... | collective-permute-start | bytes 786440 | tf_op jit(solution)/shard_map/ppermute | solution.py:53
  98.7 0.0 collective-permute-done.14
  98.7 1.9 collective-permute-start.2
  100.6 0.0 collective-permute-done.15
  100.6 0.2 select_bitcast_fusion.3
  100.8 0.2 pad_maximum_fusion
  101.1 1.9 collective-permute-start.16
  103.0 3.7 %broadcast_in_dim.24 = bf16[2,6912,128]{2,1,0:T(8,128)(2,1)} broadcast(bf16[6912,128]{1,0:T(8,128)(2,1)} %bitcast.4), dimensions={1,2} | broadcast | bytes 5308416 | tf_op jit(solution)/shard_map/broadcast_in_dim | solution.py:27
  106.7 6.0 %all-to-all-start.2 = ((bf16[2,6912,128]{2,1,0:T(8,128)(2,1)}), bf16[2,6912,128]{2,1,0:T(8,128)(2,1)}, u32[]{:S(2)}, u32[]{:S(2)}) async-start(bf16[2,6912,128]{2,1,0:T(8,128)(2,1)} %broadcast_in_dim.24), calls=%async_computation.2 | async-start | bytes 7077888 | tf_op jit(solution)/shard_map/all_to_all | solution.py:28
  112.7 0.0 collective-permute-done.5.x_lo
  112.7 0.0 collective-permute-done.2.g_hi
  112.7 3.6 %all-to-all-done.2.w1 = bf16[2,6912,128]{2,1,0:T(8,128)(2,1)} async-done(((bf16[2,6912,128]{2,1,0:T(8,128)(2,1)}), bf16[2,6912,128]{2,1,0:T(8,128)(2,1)}, u32[]{:S(2)}, u32[]{:S(2)}) %all-to-all-start.2) | async-done | bytes 3538976 | tf_op jit(solution)/shard_map/all_to_all | solution.py:28
  116.4 7.9 %forward_and_terms.1 = (f32[6,4,32,256]{3,2,1,0:T(8,128)S(1)}, bf16[2,4,864,128]{3,2,1,0:T(8,128)(2,1)S(1)}) custom-call(bf16[8,2,32,256]{3,2,1,0:T(8,128)(2,1)S(1)} %collective-permute-done.5.x_lo, bf16[8,2,32,256]{3,2,1,0:T(8,128)(2,1)S(1)} %constant_dynamic-update-slice_fusion.2.x_mid, bf16[8,2,32,256]{3,2,1,0:T(8,128)(2,1)S(1)} %collective-permute-done.6.x_hi, ...), custom_call_target="tpu_custom_call" | custom-call | flops 3170893824 | bytes 8388608 | tf_op jit(solution)/shard_map/forward_and_terms/pallas_call | solution.py:172
  124.3 0.9 copy-done.2
  125.2 6.0 %all_to_all.30 = bf16[2,4,864,128]{3,2,1,0:T(8,128)(2,1)} all-to-all(bf16[2,4,864,128]{3,2,1,0:T(8,128)(2,1)S(1)} %get-tuple-element.5), channel_id=1, replica_groups={{0,1},{2,3},{4,5},{6,7},{8,9},{10,11},{12,13},{14,15},{16,17},{18,19},{..., dimensions={0} | all-to-all | bytes 3538944 | tf_op jit(solution)/shard_map/all_to_all | solution.py:242
  131.2 1.9 reduce_sum.33
  133.1 16.2 %all_to_all.31 = bf16[4,864,128]{2,1,0:T(8,128)(2,1)} all-to-all(bf16[4,864,128]{2,1,0:T(8,128)(2,1)S(1)} %reduce_sum.33), channel_id=1, replica_groups={{0,128,256,384},{8,136,264,392},{16,144,272,400},{24,152,280,408},{32,1..., dimensions={0} | all-to-all | bytes 1769472 | tf_op jit(solution)/shard_map/all_to_all | solution.py:244
  149.3 1.4 reduce_sum.34
  150.7 13.0 %all_to_all.32 = bf16[8,108,128]{2,1,0:T(8,128)(2,1)S(1)} all-to-all(bf16[8,108,128]{2,1,0:T(8,128)(2,1)S(1)} %reshape.26), channel_id=1, replica_groups={{0,8,16,24,32,40,48,56},{64,72,80,88,96,104,112,120},{128,136,144,152,1..., dimensions={0} | all-to-all | bytes 442368 | tf_op jit(solution)/shard_map/all_to_all | solution.py:246
  163.7 3.1 %collective-permute-start.17 = (f32[108,128]{1,0:T(8,128)S(1)}, f32[108,128]{1,0:T(8,128)S(1)}, u32[]{:S(2)}, u32[]{:S(2)}) collective-permute-start(f32[108,128]{1,0:T(8,128)S(1)} %convert_reduce_fusion), channel_id=1, source_target_pairs={{0,64},{8,72},{16,80},{24,88},{32,96},{40,104},{48,112},{56,120},{... | collective-permute-start | bytes 165896 | tf_op jit(solution)/shard_map/ppermute | solution.py:33
  166.8 1.8 collective-permute-done.17
  168.6 9.3 %collective-permute-start.18 = (f32[108,128]{1,0:T(8,128)S(1)}, f32[108,128]{1,0:T(8,128)S(1)}, u32[]{:S(2)}, u32[]{:S(2)}) collective-permute-start(f32[108,128]{1,0:T(8,128)S(1)} %add.27), channel_id=1, source_target_pairs={{0,4},{1,5},{2,6},{3,7},{4,0},{5,1},{6,2},{7,3},{8,12},{9,13},{10,... | collective-permute-start | bytes 165896 | tf_op jit(solution)/shard_map/ppermute | solution.py:250
  177.9 2.8 %collective-permute-start.19 = (f32[108,128]{1,0:T(8,128)S(1)}, f32[108,128]{1,0:T(8,128)S(1)}, u32[]{:S(2)}, u32[]{:S(2)}) collective-permute-start(f32[108,128]{1,0:T(8,128)S(1)} %add.27), channel_id=1, source_target_pairs={{0,2},{1,3},{2,4},{3,5},{4,6},{5,7},{6,0},{7,1},{8,10},{9,11},{10,... | collective-permute-start | bytes 165896 | tf_op jit(solution)/shard_map/ppermute | solution.py:250
  180.7 4.6 %collective-permute-start.20 = (f32[108,128]{1,0:T(8,128)S(1)}, f32[108,128]{1,0:T(8,128)S(1)}, u32[]{:S(2)}, u32[]{:S(2)}) collective-permute-start(f32[108,128]{1,0:T(8,128)S(1)} %add.27), channel_id=1, source_target_pairs={{0,6},{1,7},{2,0},{3,1},{4,2},{5,3},{6,4},{7,5},{8,14},{9,15},{10,... | collective-permute-start | bytes 165896 | tf_op jit(solution)/shard_map/ppermute | solution.py:250
  185.4 0.1 stack.60.flags
  185.5 0.0 collective-permute-done.18
  185.5 0.4 collective-permute-done.19
  185.9 0.7 collective-permute-done.20
  186.6 7.8 %collective-permute-start.21 = (f32[108,128]{1,0:T(8,128)S(1)}, f32[108,128]{1,0:T(8,128)S(1)}, u32[]{:S(2)}, u32[]{:S(2)}) collective-permute-start(f32[108,128]{1,0:T(8,128)S(1)} %add_add_fusion), channel_id=1, source_target_pairs={{0,1},{1,0},{2,3},{3,2},{4,5},{5,4},{6,7},{7,6},{8,9},{9,8},{10,11... | collective-permute-start | bytes 165896 | tf_op jit(solution)/shard_map/ppermute | solution.py:33
  194.5 1.1 copy-done.3
  195.6 9.1 %input_gradient.1 = bf16[4,2,32,256]{3,2,1,0:T(8,128)(2,1)} custom-call(s32[5]{0:T(128)S(1)} %stack.60.flags, bf16[8,2,32,256]{3,2,1,0:T(8,128)(2,1)S(1)} %collective-permute-done.1.g_lo, bf16[8,2,32,256]{3,2,1,0:T(8,128)(2,1)S(1)} %constant_dynamic-update-slice_fusion.g_mid, bf16[8,2,32,256]{3,2,1,0:T(8,128)(2,1)S(1)} %collective-permute-done.2.g_hi, ...), custom_call_target="tpu_custom_call" | custom-call | flops 3623878656 | bytes 10485760 | tf_op jit(solution)/shard_map/input_gradient/pallas_call | solution.py:190
  204.7 0.6 broadcast_select_fusion.8
  (34 shorter events, 0.3 us)
Async XLA Ops:
  0.6 13.5 %copy-start = (bf16[108,256]{1,0:T(8,128)(2,1)S(1)}, bf16[108,256]{1,0:T(8,128)(2,1)}, u32[]{:S(2)}) copy-start(bf16[108,256]{1,0:T(8,128)(2,1)} %param.8) | copy-start | bytes 165892
  0.6 28.2 %copy-start.6 = (bf16[108,256]{1,0:T(8,128)(2,1)S(1)}, bf16[108,256]{1,0:T(8,128)(2,1)}, u32[]{:S(2)}) copy-start(bf16[108,256]{1,0:T(8,128)(2,1)} %param.9) | copy-start | bytes 165892
  0.7 26.8 %copy-start.5 = (bf16[4,2,32,256]{3,2,1,0:T(8,128)(2,1)S(1)}, bf16[4,2,32,256]{3,2,1,0:T(8,128)(2,1)}, u32[]{:S(2)}) copy-start(bf16[4,2,32,256]{3,2,1,0:T(8,128)(2,1)} %param.6) | copy-start | bytes 393220
  1.5 27.3 %collective-permute-start.7 = (bf16[108,128]{1,0:T(8,128)(2,1)S(1)}, bf16[108,128]{1,0:T(8,128)(2,1)S(1)}, u32[]{:S(2)}, u32[]{:S(2)}) collective-permute-start(bf16[108,128]{1,0:T(8,128)(2,1)S(1)} %constant_dynamic-slice_fusion), channel_id=1, source_target_pairs={{0,48},{8,56},{16,32},{24,40},{32,16},{40,24},{48,0},{56,8},{64,11... | collective-permute-start | bytes 82952 | tf_op jit(solution)/shard_map/ppermute | solution.py:33
  8.2 20.6 %collective-permute-start.8 = (bf16[108,128]{1,0:T(8,128)(2,1)S(1)}, bf16[108,128]{1,0:T(8,128)(2,1)S(1)}, u32[]{:S(2)}, u32[]{:S(2)}) collective-permute-start(bf16[108,128]{1,0:T(8,128)(2,1)S(1)} %constant_dynamic-slice_fusion), channel_id=1, source_target_pairs={{0,32},{8,40},{16,48},{24,56},{32,0},{40,8},{48,16},{56,24},{64,96... | collective-permute-start | bytes 82952 | tf_op jit(solution)/shard_map/ppermute | solution.py:33
  11.8 17.1 %collective-permute-start.9 = (bf16[108,128]{1,0:T(8,128)(2,1)S(1)}, bf16[108,128]{1,0:T(8,128)(2,1)S(1)}, u32[]{:S(2)}, u32[]{:S(2)}) collective-permute-start(bf16[108,128]{1,0:T(8,128)(2,1)S(1)} %constant_dynamic-slice_fusion), channel_id=1, source_target_pairs={{0,16},{8,24},{16,0},{24,8},{32,48},{40,56},{48,32},{56,40},{64,80... | collective-permute-start | bytes 82952 | tf_op jit(solution)/shard_map/ppermute | solution.py:33
  15.0 28.5 %all-to-all-start = ((bf16[16,108,128]{2,1,0:T(8,128)(2,1)}), bf16[16,108,128]{2,1,0:T(8,128)(2,1)S(1)}, u32[]{:S(2)}, u32[]{:S(2)}) async-start(bf16[16,108,128]{2,1,0:T(8,128)(2,1)} %broadcast_in_dim.20), calls=%async_computation | async-start | bytes 917504 | tf_op jit(solution)/shard_map/all_to_all | solution.py:28
  24.2 33.2 %collective-permute-start.3 = (bf16[2,2,32,256]{3,2,1,0:T(8,128)(2,1)S(1)}, bf16[2,2,32,256]{3,2,1,0:T(8,128)(2,1)S(1)}, u32[]{:S(2)}, u32[]{:S(2)}) collective-permute-start(bf16[2,2,32,256]{3,2,1,0:T(8,128)(2,1)S(1)} %get-tuple-element.14), channel_id=1, source_target_pairs={{0,8},{8,16},{16,24},{24,32},{32,40},{40,48},{48,56},{56,64},{64,7... | collective-permute-start | bytes 196616 | tf_op jit(solution)/shard_map/ppermute | solution.py:53
  27.5 42.0 %collective-permute-start = (bf16[4,2,32,256]{3,2,1,0:T(8,128)(2,1)S(1)}, bf16[4,2,32,256]{3,2,1,0:T(8,128)(2,1)S(1)}, u32[]{:S(2)}, u32[]{:S(2)}) collective-permute-start(bf16[4,2,32,256]{3,2,1,0:T(8,128)(2,1)S(1)} %copy-done.5), channel_id=1, source_target_pairs={{8,0},{16,8},{24,16},{32,24},{40,32},{48,40},{56,48},{64,56},{72,6... | collective-permute-start | bytes 393224 | tf_op jit(solution)/shard_map/ppermute | solution.py:53
  28.9 12.1 %collective-permute-start.10 = (bf16[4,108,128]{2,1,0:T(8,128)(2,1)S(1)}, bf16[4,108,128]{2,1,0:T(8,128)(2,1)S(1)}, u32[]{:S(2)}, u32[]{:S(2)}) collective-permute-start(bf16[4,108,128]{2,1,0:T(8,128)(2,1)S(1)} %pad_maximum_fusion.2), channel_id=1, source_target_pairs={{0,72},{8,64},{16,88},{24,80},{32,104},{40,96},{48,120},{56,112},{... | collective-permute-start | bytes 331784 | tf_op jit(solution)/shard_map/ppermute | solution.py:33
  33.8 9.5 %collective-permute-start.11 = (bf16[4,108,128]{2,1,0:T(8,128)(2,1)S(1)}, bf16[4,108,128]{2,1,0:T(8,128)(2,1)S(1)}, u32[]{:S(2)}, u32[]{:S(2)}) collective-permute-start(bf16[4,108,128]{2,1,0:T(8,128)(2,1)S(1)} %pad_maximum_fusion.2), channel_id=1, source_target_pairs={{0,64},{8,72},{16,80},{24,88},{32,96},{40,104},{48,112},{56,120},{... | collective-permute-start | bytes 331784 | tf_op jit(solution)/shard_map/ppermute | solution.py:33
  37.0 6.4 %collective-permute-start.12 = (bf16[4,108,128]{2,1,0:T(8,128)(2,1)S(1)}, bf16[4,108,128]{2,1,0:T(8,128)(2,1)S(1)}, u32[]{:S(2)}, u32[]{:S(2)}) collective-permute-start(bf16[4,108,128]{2,1,0:T(8,128)(2,1)S(1)} %pad_maximum_fusion.2), channel_id=1, source_target_pairs={{0,8},{8,0},{16,24},{24,16},{32,40},{40,32},{48,56},{56,48},{64,72... | collective-permute-start | bytes 331784 | tf_op jit(solution)/shard_map/ppermute | solution.py:33
  41.0 18.8 %collective-permute-start.4 = (bf16[2,2,32,256]{3,2,1,0:T(8,128)(2,1)S(1)}, bf16[2,2,32,256]{3,2,1,0:T(8,128)(2,1)S(1)}, u32[]{:S(2)}, u32[]{:S(2)}) collective-permute-start(bf16[2,2,32,256]{3,2,1,0:T(8,128)(2,1)S(1)} %get-tuple-element.13), channel_id=1, source_target_pairs={{8,0},{16,8},{24,16},{32,24},{40,32},{48,40},{56,48},{64,56},{72,6... | collective-permute-start | bytes 196616 | tf_op jit(solution)/shard_map/ppermute | solution.py:53
  45.0 58.0 %all-to-all-start.1 = ((bf16[4,1728,128]{2,1,0:T(8,128)(2,1)}), bf16[4,1728,128]{2,1,0:T(8,128)(2,1)}, u32[]{:S(2)}, u32[]{:S(2)}) async-start(bf16[4,1728,128]{2,1,0:T(8,128)(2,1)} %broadcast_in_dim.22), calls=%async_computation.1 | async-start | bytes 3538944 | tf_op jit(solution)/shard_map/all_to_all | solution.py:28
  50.2 9.7 %copy-start.4 = (bf16[4,2,32,256]{3,2,1,0:T(8,128)(2,1)S(1)}, bf16[4,2,32,256]{3,2,1,0:T(8,128)(2,1)}, u32[]{:S(2)}) copy-start(bf16[4,2,32,256]{3,2,1,0:T(8,128)(2,1)} %param.5) | copy-start | bytes 393220
  50.4 38.7 %collective-permute-start.13 = (bf16[1728,128]{1,0:T(8,128)(2,1)S(1)}, bf16[1728,128]{1,0:T(8,128)(2,1)S(1)}, u32[]{:S(2)}, u32[]{:S(2)}) collective-permute-start(bf16[1728,128]{1,0:T(8,128)(2,1)S(1)} %reshape.24), channel_id=1, source_target_pairs={{0,384},{8,392},{16,400},{24,408},{32,416},{40,424},{48,432},{56,4... | collective-permute-start | bytes 1327112 | tf_op jit(solution)/shard_map/ppermute | solution.py:33
  55.4 43.3 %collective-permute-start.14 = (bf16[1728,128]{1,0:T(8,128)(2,1)S(1)}, bf16[1728,128]{1,0:T(8,128)(2,1)S(1)}, u32[]{:S(2)}, u32[]{:S(2)}) collective-permute-start(bf16[1728,128]{1,0:T(8,128)(2,1)S(1)} %reshape.24), channel_id=1, source_target_pairs={{0,256},{8,264},{16,272},{24,280},{32,288},{40,296},{48,304},{56,3... | collective-permute-start | bytes 1327112 | tf_op jit(solution)/shard_map/ppermute | solution.py:33
  57.4 43.2 %collective-permute-start.15 = (bf16[1728,128]{1,0:T(8,128)(2,1)S(1)}, bf16[1728,128]{1,0:T(8,128)(2,1)S(1)}, u32[]{:S(2)}, u32[]{:S(2)}) collective-permute-start(bf16[1728,128]{1,0:T(8,128)(2,1)S(1)} %reshape.24), channel_id=1, source_target_pairs={{0,128},{8,136},{16,144},{24,152},{32,160},{40,168},{48,176},{56,1... | collective-permute-start | bytes 1327112 | tf_op jit(solution)/shard_map/ppermute | solution.py:33
  59.9 52.8 %collective-permute-start.5 = (bf16[8,2,32,256]{3,2,1,0:T(8,128)(2,1)S(1)}, bf16[8,2,32,256]{3,2,1,0:T(8,128)(2,1)S(1)}, u32[]{:S(2)}, u32[]{:S(2)}) collective-permute-start(bf16[8,2,32,256]{3,2,1,0:T(8,128)(2,1)S(1)} %constant_dynamic-update-slice_fusion.2.x_mid), channel_id=1, source_target_pairs={{0,1},{1,2},{2,3},{3,4},{4,5},{5,6},{6,7},{8,9},{9,10},{10,11},{11... | collective-permute-start | bytes 786440 | tf_op jit(solution)/shard_map/ppermute | solution.py:53
  69.5 43.2 %collective-permute-start.6 = (bf16[8,2,32,256]{3,2,1,0:T(8,128)(2,1)S(1)}, bf16[8,2,32,256]{3,2,1,0:T(8,128)(2,1)S(1)}, u32[]{:S(2)}, u32[]{:S(2)}) collective-permute-start(bf16[8,2,32,256]{3,2,1,0:T(8,128)(2,1)S(1)} %constant_dynamic-update-slice_fusion.2.x_mid), channel_id=1, source_target_pairs={{1,0},{2,1},{3,2},{4,3},{5,4},{6,5},{7,6},{9,8},{10,9},{11,10},{12... | collective-permute-start | bytes 786440 | tf_op jit(solution)/shard_map/ppermute | solution.py:53
  89.0 23.7 %collective-permute-start.1 = (bf16[8,2,32,256]{3,2,1,0:T(8,128)(2,1)S(1)}, bf16[8,2,32,256]{3,2,1,0:T(8,128)(2,1)S(1)}, u32[]{:S(2)}, u32[]{:S(2)}) collective-permute-start(bf16[8,2,32,256]{3,2,1,0:T(8,128)(2,1)S(1)} %constant_dynamic-update-slice_fusion.g_mid), channel_id=1, source_target_pairs={{0,1},{1,2},{2,3},{3,4},{4,5},{5,6},{6,7},{8,9},{9,10},{10,11},{11... | collective-permute-start | bytes 786440 | tf_op jit(solution)/shard_map/ppermute | solution.py:53
  98.7 14.0 %collective-permute-start.2 = (bf16[8,2,32,256]{3,2,1,0:T(8,128)(2,1)S(1)}, bf16[8,2,32,256]{3,2,1,0:T(8,128)(2,1)S(1)}, u32[]{:S(2)}, u32[]{:S(2)}) collective-permute-start(bf16[8,2,32,256]{3,2,1,0:T(8,128)(2,1)S(1)} %constant_dynamic-update-slice_fusion.g_mid), channel_id=1, source_target_pairs={{1,0},{2,1},{3,2},{4,3},{5,4},{6,5},{7,6},{9,8},{10,9},{11,10},{12... | collective-permute-start | bytes 786440 | tf_op jit(solution)/shard_map/ppermute | solution.py:53
  101.1 93.4 %collective-permute-start.16 = (bf16[6912,128]{1,0:T(8,128)(2,1)S(1)}, bf16[6912,128]{1,0:T(8,128)(2,1)}, u32[]{:S(2)}, u32[]{:S(2)}) collective-permute-start(bf16[6912,128]{1,0:T(8,128)(2,1)S(1)} %bitcast.34), channel_id=1, source_target_pairs={{0,1},{1,0},{2,3},{3,2},{4,5},{5,4},{6,7},{7,6},{8,9},{9,8},{10,11... | collective-permute-start | bytes 5308424 | tf_op jit(solution)/shard_map/ppermute | solution.py:33
  106.7 9.6 %copy-start.1 = (f32[256]{0:T(256)S(1)}, f32[256]{0:T(256)}, u32[]{:S(2)}) copy-start(f32[256]{0:T(256)} %param.7) | copy-start | bytes 3076
  106.7 9.6 %all-to-all-start.2 = ((bf16[2,6912,128]{2,1,0:T(8,128)(2,1)}), bf16[2,6912,128]{2,1,0:T(8,128)(2,1)}, u32[]{:S(2)}, u32[]{:S(2)}) async-start(bf16[2,6912,128]{2,1,0:T(8,128)(2,1)} %broadcast_in_dim.24), calls=%async_computation.2 | async-start | bytes 7077888 | tf_op jit(solution)/shard_map/all_to_all | solution.py:28
  124.3 0.9 copy-start.2
  163.7 4.9 %collective-permute-start.17 = (f32[108,128]{1,0:T(8,128)S(1)}, f32[108,128]{1,0:T(8,128)S(1)}, u32[]{:S(2)}, u32[]{:S(2)}) collective-permute-start(f32[108,128]{1,0:T(8,128)S(1)} %convert_reduce_fusion), channel_id=1, source_target_pairs={{0,64},{8,72},{16,80},{24,88},{32,96},{40,104},{48,112},{56,120},{... | collective-permute-start | bytes 165896 | tf_op jit(solution)/shard_map/ppermute | solution.py:33
  168.6 16.8 %collective-permute-start.18 = (f32[108,128]{1,0:T(8,128)S(1)}, f32[108,128]{1,0:T(8,128)S(1)}, u32[]{:S(2)}, u32[]{:S(2)}) collective-permute-start(f32[108,128]{1,0:T(8,128)S(1)} %add.27), channel_id=1, source_target_pairs={{0,4},{1,5},{2,6},{3,7},{4,0},{5,1},{6,2},{7,3},{8,12},{9,13},{10,... | collective-permute-start | bytes 165896 | tf_op jit(solution)/shard_map/ppermute | solution.py:250
  177.9 7.9 %collective-permute-start.19 = (f32[108,128]{1,0:T(8,128)S(1)}, f32[108,128]{1,0:T(8,128)S(1)}, u32[]{:S(2)}, u32[]{:S(2)}) collective-permute-start(f32[108,128]{1,0:T(8,128)S(1)} %add.27), channel_id=1, source_target_pairs={{0,2},{1,3},{2,4},{3,5},{4,6},{5,7},{6,0},{7,1},{8,10},{9,11},{10,... | collective-permute-start | bytes 165896 | tf_op jit(solution)/shard_map/ppermute | solution.py:250
  180.7 5.8 %collective-permute-start.20 = (f32[108,128]{1,0:T(8,128)S(1)}, f32[108,128]{1,0:T(8,128)S(1)}, u32[]{:S(2)}, u32[]{:S(2)}) collective-permute-start(f32[108,128]{1,0:T(8,128)S(1)} %add.27), channel_id=1, source_target_pairs={{0,6},{1,7},{2,0},{3,1},{4,2},{5,3},{6,4},{7,5},{8,14},{9,15},{10,... | collective-permute-start | bytes 165896 | tf_op jit(solution)/shard_map/ppermute | solution.py:250
  186.6 18.1 %collective-permute-start.21 = (f32[108,128]{1,0:T(8,128)S(1)}, f32[108,128]{1,0:T(8,128)S(1)}, u32[]{:S(2)}, u32[]{:S(2)}) collective-permute-start(f32[108,128]{1,0:T(8,128)S(1)} %add_add_fusion), channel_id=1, source_target_pairs={{0,1},{1,0},{2,3},{3,2},{4,5},{5,4},{6,7},{7,6},{8,9},{9,8},{10,11... | collective-permute-start | bytes 165896 | tf_op jit(solution)/shard_map/ppermute | solution.py:33
  194.5 1.1 copy-start.3

commit v2 on v0

v2 whole, which is shorter than its diff:
```python
import jax
import jax.numpy as jnp
from jax import lax
from jax.experimental import pallas as pl
from jax.experimental.pallas import tpu as pltpu
from jax.sharding import PartitionSpec as P

CH = 128
C = 256
W = 32
HALF = 128
ROWS = 6912
EPS = 1e-06
BF = jnp.bfloat16
F32 = jnp.float32

YZ_GROUPS = [[x * 16 + k for k in range(16)] for x in range(4)]
X_GROUPS = [[k, k + 16, k + 32, k + 48] for k in range(16)]
Z_GROUPS = [[c, c + 2, c + 4, c + 6] for c in range(2)]


def spread(block, axis, groups):
    count = len(groups[0])
    operand = jnp.broadcast_to(block[None], (count,) + block.shape)
    return lax.all_to_all(operand, axis, 0, 0, axis_index_groups=groups, tiled=True)


def swap_cores(block):
    return lax.ppermute(block, "rows", [(i, i ^ 1) for i in range(lax.axis_size("rows"))])


def shift(block, axis, distance):
    count = lax.axis_size(axis)
    route = [(i, i + distance) for i in range(count) if 0 <= i + distance < count]
    return lax.ppermute(block, axis, route)


def from_x(block, mask):
    return lax.ppermute(block, "tm", [(i, i ^ (mask * 16)) for i in range(lax.axis_size("tm"))])


def in_order(blocks, low, high):
    a, b, c, d = blocks
    a, b = jnp.where(low, b, a), jnp.where(low, a, b)
    c, d = jnp.where(low, d, c), jnp.where(low, c, d)
    a, c = jnp.where(high, c, a), jnp.where(high, a, c)
    b, d = jnp.where(high, d, b), jnp.where(high, b, d)
    return jnp.stack([a, b, c, d])


def beyond_chip(block):
    count = lax.axis_size("rows")
    route = [(i - 1, i) for i in range(2, count, 2)] + [(i + 1, i) for i in range(1, count - 1, 2)]
    return lax.ppermute(block, "rows", route)


def after(value, *others):
    return lax.optimization_barrier((value,) + others)[0]


def fill_shifts(out, piece, frames, at):
    count, rows = piece.shape[:2]
    flat = piece.reshape(count * rows * W, piece.shape[3]).astype(F32)
    column = lax.broadcasted_iota(jnp.int32, flat.shape, 0) % W
    before = jnp.where(column == 0, 0.0, pltpu.roll(flat, 1, 0))
    behind = jnp.where(column == W - 1, 0.0, pltpu.roll(flat, flat.shape[0] - 1, 0))
    out[1, frames, pl.ds(at, rows)] = piece
    out[0, frames, pl.ds(at, rows)] = before.astype(BF).reshape(piece.shape)
    out[2, frames, pl.ds(at, rows)] = behind.astype(BF).reshape(piece.shape)


def normalize(pre, squares, gain):
    scale = lax.rsqrt(squares * (1.0 / C) + EPS)
    normed = pre * scale
    gated = normed * gain
    sigma = 1.0 / (1.0 + jnp.exp(-gated))
    return scale, normed, gated, sigma


def shifts_kernel(flags, mid, edge, other, xs, cs):
    core = flags[2]
    for out, base in ((xs, 0), (cs, 8)):
        for f in range(0, 8, 2):
            frames = slice(f, f + 2)
            source = slice(base + f, base + f + 2)
            fill_shifts(out, mid[source], frames, 3)
            fill_shifts(out, edge[source], frames, 1 + 4 * core)
            fill_shifts(out, other[source, :2], frames, 5 - 4 * core)
            fill_shifts(out, other[source, 2:], frames, 0)
            for k in range(3):
                out[k, frames, 7:8] = out[k, frames, 0:1]


def half_kernel(flags, xs, w1, pre, squares):
    base = 2 - 2 * flags[2]
    for i in range(3):
        for j in range(3):
            lhs = jnp.concatenate(
                [xs[k, i : i + 4, pl.ds(base + j, 4)].reshape(512, C) for k in range(3)], axis=1
            )
            at = (i * 3 + j) * 3 * C
            part = jnp.dot(lhs, w1[at : at + 3 * C], preferred_element_type=F32)
            if i == 0 and j == 0:
                pre[...] = part
            else:
                pre[...] += part
    total = jnp.sum(pre[...] * pre[...], axis=1, keepdims=True)
    squares[...] = jnp.broadcast_to(total, (512, HALF))


def terms_kernel(flags, pre, own, other, gain, cs, out):
    base = 2 - 2 * flags[2]
    _, _, gated, sigma = normalize(pre[...], own[...] + other[...], gain[...])
    act = (gated * sigma).T.astype(BF)
    taps = [(i, j, k) for i in range(3) for j in range(3) for k in range(3)]

    def operand(i, j, k):
        return cs[2 - k, 2 - i : 6 - i, pl.ds(base + 2 - j, 4), :, :CH].reshape(512, CH)

    for n in range(0, 27, 2):
        pair = taps[n : n + 2]
        rhs = jnp.concatenate([operand(*tap) for tap in pair], axis=1)
        term = jnp.dot(act, rhs, preferred_element_type=F32).astype(BF)
        for m in range(len(pair)):
            out[(n + m) * HALF : (n + m + 1) * HALF] = term[:, m * CH : (m + 1) * CH]


def halves_in_order(flags, value):
    turned = jnp.concatenate([value[..., HALF:], value[..., :HALF]], axis=-1)
    return jnp.where(flags[2] == 1, turned, value)


def pre_kernel(flags, xs, own, other, pre, acc):
    for i in range(3):
        for j in range(3):
            lhs = jnp.concatenate(
                [xs[k, i : i + 6, j + 1 : j + 5].reshape(768, C) for k in range(3)], axis=1
            )
            at = (i * 3 + j) * 3 * C
            rhs = jnp.concatenate([own[at : at + 3 * C], other[at : at + 3 * C]], axis=1)
            part = jnp.dot(lhs, rhs, preferred_element_type=F32)
            if i == 0 and j == 0:
                acc[...] = part
            else:
                acc[...] += part
    pre[...] = halves_in_order(flags, acc[...])


def backward_kernel(flags, cs, gain, pre, w1_own, w1_other, w2_own, w2_other, out, ps, acc):
    nt = (((1,), (1,)), ((), ()))
    taps = [(i, j, k) for i in range(3) for j in range(3) for k in range(3)]
    for n, (i, j, k) in enumerate(taps):
        lhs = halves_in_order(flags, cs[2 - k, 2 - i : 8 - i, 3 - j : 7 - j].reshape(768, C))
        at = n * C
        rhs = jnp.concatenate([w2_own[at : at + C], w2_other[at : at + C]], axis=1)
        part = lax.dot_general(lhs, rhs, nt, preferred_element_type=F32)
        if n == 0:
            acc[...] = part
        else:
            acc[...] += part
    row = lax.broadcasted_iota(jnp.int32, (C, C), 0)
    col = lax.broadcasted_iota(jnp.int32, (C, C), 1)
    source = jnp.where(col < HALF, 2 * col, 2 * (col - HALF) + 1)
    permutation = jnp.where(row == source, 1.0, 0.0).astype(BF)
    for t in range(6):
        natural = acc[t * 128 : t * 128 + 128]
        high = natural.astype(BF)
        rest = natural - high.astype(F32)
        middle = rest.astype(BF)
        low = (rest - middle.astype(F32)).astype(BF)
        moved = [
            jnp.dot(piece, permutation, preferred_element_type=F32) for piece in (high, middle, low)
        ]
        act_grad = (moved[0] + moved[1]) + moved[2]
        here = pre[t * 128 : t * 128 + 128]
        squares = jnp.sum(here * here, axis=-1, keepdims=True)
        scale, normed, gated, sigma = normalize(here, squares, gain[...])
        norm_grad = act_grad * sigma * (1.0 + gated * (1.0 - sigma)) * gain[...]
        pre_grad = scale * (
            norm_grad - normed * jnp.mean(norm_grad * normed, axis=-1, keepdims=True)
        )
        line = lax.broadcasted_iota(jnp.int32, pre_grad.shape, 0) // W
        outside = ((line == 0) & (flags[1] == 0)) | ((line == 3) & (flags[1] == flags[4]))
        if t >= 4:
            outside = outside | (flags[0] == flags[3])
        pre_grad = jnp.where(outside, 0.0, pre_grad)
        pre_grad = halves_in_order(flags, pre_grad).astype(BF).reshape(1, 4, W, C)
        fill_shifts(ps, pre_grad, slice(t, t + 1), 0)
    for n, (i, j, k) in enumerate(taps):
        lhs = ps[2 - k, 2 - i : 6 - i, 2 - j : 4 - j].reshape(256, C)
        at = n * C
        rhs = jnp.concatenate([w1_own[at : at + C], w1_other[at : at + C]], axis=1)
        part = lax.dot_general(lhs, rhs, nt, preferred_element_type=F32)
        if n == 0:
            acc[:256] = part
        else:
            acc[:256] += part
    out[...] = acc[:256].reshape(4, 2, W, C).astype(BF)


VMEM = pl.BlockSpec(memory_space=pltpu.VMEM)
SMEM = pl.BlockSpec(memory_space=pltpu.SMEM)


def call(kernel, name, flops, out_shape, scratch, *operands):
    smem = [SMEM] if operands[0].dtype == jnp.int32 else []
    return pl.pallas_call(
        kernel,
        out_shape=out_shape,
        in_specs=smem + [VMEM] * (len(operands) - len(smem)),
        out_specs=jax.tree.map(lambda _: VMEM, out_shape),
        scratch_shapes=scratch,
        compiler_params=pltpu.CompilerParams(vmem_limit_bytes=32 * 1024 * 1024),
        cost_estimate=pl.CostEstimate(flops=flops, bytes_accessed=1 << 20, transcendentals=0),
        name=name,
    )(*operands)


def make_shifts(flags, mid, edge, other):
    shape = jax.ShapeDtypeStruct((3, 8, 8, W, C), BF)
    return call(shifts_kernel, "shifts", 1, (shape, shape), [], flags, mid, edge, other)


def forward_half(flags, xs, w1):
    shape = jax.ShapeDtypeStruct((512, HALF), F32)
    return call(half_kernel, "forward_half", 4 * 512 * ROWS * HALF, (shape, shape), [], flags, xs, w1)


def local_terms(flags, pre, own, other, gain, cs):
    shape = jax.ShapeDtypeStruct((ROWS // 2, CH), BF)
    return call(
        terms_kernel, "local_terms", 4 * 512 * ROWS * HALF, shape, [], flags, pre, own, other, gain, cs
    )


def forward_all(flags, xs, own, other):
    shape = jax.ShapeDtypeStruct((768, C), F32)
    scratch = [pltpu.VMEM((768, C), F32)]
    return call(pre_kernel, "forward_all", 2 * 768 * ROWS * C, shape, scratch, flags, xs, own, other)


def backward(flags, cs, gain, pre, w1_own, w1_other, w2_own, w2_other):
    shape = jax.ShapeDtypeStruct((4, 2, W, C), BF)
    scratch = [pltpu.VMEM((3, 6, 4, W, C), BF), pltpu.VMEM((768, C), F32)]
    return call(
        backward_kernel, "backward", 2 * 1024 * ROWS * C, shape, scratch,
        flags, cs, gain, pre, w1_own, w1_other, w2_own, w2_other,
    )


def on_device(activations, cotangent, gain, first_weight, second_weight):
    tm, rows = lax.axis_index("tm"), lax.axis_index("rows")
    core, x = rows % 2, tm // 16
    flags = jnp.stack([tm, rows, core, lax.axis_size("tm") - 1, lax.axis_size("rows") - 1])
    flags = flags.astype(jnp.int32)

    pick = lax.broadcasted_iota(jnp.int32, (C, HALF), 0) == (
        2 * lax.broadcasted_iota(jnp.int32, (C, HALF), 1) + core
    )
    half1 = jnp.dot(first_weight, pick.astype(BF), preferred_element_type=F32).astype(BF)
    half2 = lax.dynamic_slice_in_dim(second_weight, core * HALF, HALF, axis=1)
    gain_pairs = gain.reshape(HALF, 2)
    gain_half = jnp.where(core == 0, gain_pairs[:, 0], gain_pairs[:, 1]).reshape(1, HALF)
    gain_all = jnp.concatenate([gain_pairs[:, 0], gain_pairs[:, 1]]).reshape(1, C)

    w1_block = spread(half1, "tm", YZ_GROUPS).reshape(16 * 108, HALF)
    w1_blocks = [w1_block] + [from_x(w1_block, mask) for mask in (1, 2, 3)]
    w1_own = in_order(w1_blocks, x % 2 == 1, x // 2 == 1).reshape(ROWS, HALF)
    activations, cotangent, _ = lax.optimization_barrier((activations, cotangent, half1))

    nexts = shift(jnp.concatenate([activations[:2], cotangent], axis=0), "tm", -1)
    prevs = shift(activations[2:], "tm", 1)
    mid = jnp.concatenate([prevs, activations, nexts[:2], cotangent, nexts[2:]], axis=0)
    edge = beyond_chip(mid)
    next_row = jnp.where(core == 0, edge[:, 1:], edge[:, :1])
    other = swap_cores(jnp.concatenate([mid, next_row], axis=1))
    xs, cs = make_shifts(flags, mid, edge, other)

    w2_block = spread(after(half2, edge), "tm", YZ_GROUPS).reshape(16 * 108, HALF)
    xs, w2_block = lax.optimization_barrier((xs, w2_block))

    pre_half, squares = forward_half(flags, xs, w1_own)
    squares_other = swap_cores(squares)
    w2_block = after(w2_block, squares)
    w2_blocks = [w2_block] + [from_x(w2_block, mask) for mask in (1, 2, 3)]
    terms = local_terms(flags, pre_half, squares, squares_other, gain_half, cs)

    terms, w2_blocks[1] = lax.optimization_barrier((terms, w2_blocks[1]))

    total = lax.all_to_all(
        terms.reshape(4, 864, CH), "tm", 0, 0, axis_index_groups=X_GROUPS, tiled=True
    )

    w1_other = swap_cores(after(w1_own, terms))
    pre = forward_all(flags, xs, w1_own, w1_other)
    total, pre = lax.optimization_barrier((total, pre))
    w2_blocks = lax.optimization_barrier((w2_blocks, total))[0]
    w2_own = in_order(w2_blocks, x % 2 == 1, x // 2 == 1).reshape(ROWS, HALF)
    w2_other = swap_cores(w2_own)

    total = total.astype(F32).sum(0).astype(BF).reshape(16, 54, CH)
    total = lax.all_to_all(total, "tm", 0, 0, axis_index_groups=YZ_GROUPS, tiled=True)
    total = spread(total.astype(F32).sum(0), "rows", Z_GROUPS).sum(0)
    input_grad = backward(flags, cs, gain_all, pre, w1_own, w1_other, w2_own, w2_other)

    total, input_grad = lax.optimization_barrier((total, input_grad))
    other = swap_cores(total)
    even, odd = jnp.where(core == 0, total, other), jnp.where(core == 0, other, total)
    weight_grad = jnp.stack([even, odd], axis=1).reshape(108, CH)
    return (input_grad, weight_grad)


def solution(mesh):
    return jax.shard_map(
        on_device,
        mesh=mesh,
        in_specs=(
            P("tm", "rows", None, None),
            P("tm", "rows", None, None),
            P(),
            P("tm", None),
            P("tm", None),
        ),
        out_specs=(P("tm", "rows", None, None), P("tm", None)),
        check_vma=False,
    )
```

time: 959 us -> 187 us (0.19)
  the two profiles are of different devices: /device:TPU:78 before, /device:TPU:1 now
where the time goes in v2:
time: 187 us; the launch traced here: 186 us
  starting transfers between devices  77.9 us (42%)
  waiting for transfers between devices  46.5 us (25%)
  Pallas kernels  21.4 us (11%)
  local copies, waits for them, and re-layouts  16.8 us (9%)
  blocking collectives  14.9 us (8%)
  other arithmetic  7.03 us (4%)
    all_to_all x3, starting transfers between devices, spread(): lax.all_to_all(operand, axis, 0, 0, axis_index_groups=groups, tiled=True)  25 us
    pallas_call x5, Pallas kernels, call(): pl.pallas_call(kernel, out_shape=out_shape, in_specs=smem + [VMEM] * (len...  21.4 us
    ppermute x6, waiting for transfers between devices, from_x(): lax.ppermute(block, 'tm', [(i, i ^ mask * 16) for i in range(lax.axis_siz...  20 us
    ppermute x6, starting transfers between devices, from_x(): lax.ppermute(block, 'tm', [(i, i ^ mask * 16) for i in range(lax.axis_siz...  19.7 us
    ppermute x5, starting transfers between devices, swap_cores(): lax.ppermute(block, 'rows', [(i, i ^ 1) for i in range(lax.axis_size('row...  17.3 us
    all_to_all x1, blocking collectives, on_device(): lax.all_to_all(total, 'tm', 0, 0, axis_index_groups=YZ_GROUPS, tiled=True)  14.9 us
    unnamed x28, local copies, waits for them, and re-layouts  11.7 us
    all_to_all x3, waiting for transfers between devices, spread(): lax.all_to_all(operand, axis, 0, 0, axis_index_groups=groups, tiled=True)  11.4 us
  transfers between devices with their start and end apart: 18, of which 10 were waited for; matrix products, arithmetic and copies ran while one was open for 4% of the time, Pallas kernels for 5%

profile of v2, /device:TPU:1, one launch (start us, length us, event | category | flops | bytes accessed | tf_op | source)
XLA Modules:
  0.0 185.8 jit_solution(17117059430556695023)
XLA Ops:
  0.6 0.0 copy-start
  0.6 0.0 copy-start.9
  0.7 0.8 copy-done
  1.5 0.2 fusion
  1.6 0.8 broadcast_in_dim.7
  2.4 9.7 %all-to-all-start.1 = ((bf16[16,108,128]{2,1,0:T(8,128)(2,1)}), bf16[16,108,128]{2,1,0:T(8,128)(2,1)S(1)}, u32[]{:S(2)}, u32[]{:S(2)}) async-start(bf16[16,108,128]{2,1,0:T(8,128)(2,1)} %broadcast_in_dim.7), calls=%async_computation.1 | async-start | bytes 917504 | tf_op jit(solution)/shard_map/all_to_all | solution.py:25
  12.2 0.9 fusion.2
  13.0 3.3 %collective-permute-start = (bf16[2,2,32,256]{3,2,1,0:T(8,128)(2,1)S(1)}, bf16[2,2,32,256]{3,2,1,0:T(8,128)(2,1)S(1)}, u32[]{:S(2)}, u32[]{:S(2)}) collective-permute-start(bf16[2,2,32,256]{3,2,1,0:T(8,128)(2,1)S(1)} %get-tuple-element.56), channel_id=1, source_target_pairs={{0,8},{8,16},{16,24},{24,32},{32,40},{40,48},{48,56},{56,64},{64,7... | collective-permute-start | bytes 196616 | tf_op jit(solution)/shard_map/ppermute | solution.py:35
  16.4 1.3 collective-permute-start.1
  17.7 2.6 %collective-permute-done = bf16[2,2,32,256]{3,2,1,0:T(8,128)(2,1)S(1)} collective-permute-done((bf16[2,2,32,256]{3,2,1,0:T(8,128)(2,1)S(1)}, bf16[2,2,32,256]{3,2,1,0:T(8,128)(2,1)S(1)}, u32[]{:S(2)}, u32[]{:S(2)}) %collective-permute-start) | collective-permute-done | bytes 65568 | tf_op jit(solution)/shard_map/ppermute | solution.py:35
  20.2 7.7 %collective-permute-done.1 = bf16[6,2,32,256]{3,2,1,0:T(8,128)(2,1)S(1)} collective-permute-done((bf16[6,2,32,256]{3,2,1,0:T(8,128)(2,1)S(1)}, bf16[6,2,32,256]{3,2,1,0:T(8,128)(2,1)S(1)}, u32[]{:S(2)}, u32[]{:S(2)}) %collective-permute-start.1) | collective-permute-done | bytes 196640 | tf_op jit(solution)/shard_map/ppermute | solution.py:35
  28.0 7.1 %collective-permute-start.2 = (bf16[16,2,32,256]{3,2,1,0:T(8,128)(2,1)S(1)}, bf16[16,2,32,256]{3,2,1,0:T(8,128)(2,1)S(1)}, u32[]{:S(2)}, u32[]{:S(2)}) collective-permute-start(bf16[16,2,32,256]{3,2,1,0:T(8,128)(2,1)S(1)} %slice_dynamic-update-slice_fusion.mid), channel_id=1, source_target_pairs={{1,2},{3,4},{5,6},{2,1},{4,3},{6,5},{9,10},{11,12},{13,14},{10,9},... | collective-permute-start | bytes 1572872 | tf_op jit(solution)/shard_map/ppermute | solution.py:54
  35.2 0.1 stack.54.flags
  35.3 0.0 all-to-all-done.1
  35.3 0.1 reshape.55
  35.4 4.4 %collective-permute-start.4 = (bf16[1728,128]{1,0:T(8,128)(2,1)S(1)}, bf16[1728,128]{1,0:T(8,128)(2,1)S(1)}, u32[]{:S(2)}, u32[]{:S(2)}) collective-permute-start(bf16[1728,128]{1,0:T(8,128)(2,1)S(1)} %reshape.55), channel_id=1, source_target_pairs={{0,384},{8,392},{16,400},{24,408},{32,416},{40,424},{48,432},{56,4... | collective-permute-start | bytes 1327112 | tf_op jit(solution)/shard_map/ppermute | solution.py:39
  39.8 2.4 %collective-permute-start.5 = (bf16[1728,128]{1,0:T(8,128)(2,1)S(1)}, bf16[1728,128]{1,0:T(8,128)(2,1)}, u32[]{:S(2)}, u32[]{:S(2)}) collective-permute-start(bf16[1728,128]{1,0:T(8,128)(2,1)S(1)} %reshape.55), channel_id=1, source_target_pairs={{0,256},{8,264},{16,272},{24,280},{32,288},{40,296},{48,304},{56,3... | collective-permute-start | bytes 1327112 | tf_op jit(solution)/shard_map/ppermute | solution.py:39
  42.2 2.2 %collective-permute-start.6 = (bf16[1728,128]{1,0:T(8,128)(2,1)S(1)}, bf16[1728,128]{1,0:T(8,128)(2,1)}, u32[]{:S(2)}, u32[]{:S(2)}) collective-permute-start(bf16[1728,128]{1,0:T(8,128)(2,1)S(1)} %reshape.55), channel_id=1, source_target_pairs={{0,128},{8,136},{16,144},{24,152},{32,160},{40,168},{48,176},{56,1... | collective-permute-start | bytes 1327112 | tf_op jit(solution)/shard_map/ppermute | solution.py:39
  44.4 3.2 %collective-permute-done.2.edge = bf16[16,2,32,256]{3,2,1,0:T(8,128)(2,1)S(1)} collective-permute-done((bf16[16,2,32,256]{3,2,1,0:T(8,128)(2,1)S(1)}, bf16[16,2,32,256]{3,2,1,0:T(8,128)(2,1)S(1)}, u32[]{:S(2)}, u32[]{:S(2)}) %collective-permute-start.2) | collective-permute-done | bytes 524320 | tf_op jit(solution)/shard_map/ppermute | solution.py:54
  47.6 1.0 pad_maximum_fusion.2
  48.6 1.9 %collective-permute-start.3 = (bf16[16,3,32,256]{3,2,1,0:T(8,128)(2,1)}, bf16[16,3,32,256]{3,2,1,0:T(8,128)(2,1)}, u32[]{:S(2)}, u32[]{:S(2)}) collective-permute-start(bf16[16,3,32,256]{3,2,1,0:T(8,128)(2,1)} %pad_maximum_fusion.2), channel_id=1, source_target_pairs={{0,1},{1,0},{2,3},{3,2},{4,5},{5,4},{6,7},{7,6},{8,9},{9,8},{10,11... | collective-permute-start | bytes 2359304 | tf_op jit(solution)/shard_map/ppermute | solution.py:29
  50.5 0.8 broadcast_in_dim.6
  51.4 5.8 %all-to-all-start = ((bf16[16,108,128]{2,1,0:T(8,128)(2,1)}), bf16[16,108,128]{2,1,0:T(8,128)(2,1)S(1)}, u32[]{:S(2)}, u32[]{:S(2)}) async-start(bf16[16,108,128]{2,1,0:T(8,128)(2,1)} %broadcast_in_dim.6), calls=%async_computation | async-start | bytes 917504 | tf_op jit(solution)/shard_map/all_to_all | solution.py:25
  57.1 0.0 collective-permute-done.4
  57.2 1.1 collective-permute-done.6
  58.2 1.3 select_bitcast_fusion.7
  59.5 0.2 pad_maximum_fusion
  59.8 0.0 collective-permute-done.3.other
  59.8 2.1 %shifts.1 = (bf16[3,8,8,32,256]{4,3,2,1,0:T(8,128)(2,1)S(1)}, bf16[3,8,8,32,256]{4,3,2,1,0:T(8,128)(2,1)S(1)}) custom-call(s32[5]{0:T(128)S(1)} %stack.54.flags, bf16[16,2,32,256]{3,2,1,0:T(8,128)(2,1)S(1)} %slice_dynamic-update-slice_fusion.mid, bf16[16,2,32,256]{3,2,1,0:T(8,128)(2,1)S(1)} %collective-permute-done.2.edge, ...), custom_call_target="tpu_custom_call" | custom-call | flops 1 | bytes 1048576 | tf_op jit(solution)/shard_map/shifts/pallas_call | solution.py:207
  61.8 1.6 copy-done.1
  63.5 1.7 copy-done.4
  65.1 4.2 %all-to-all-done = bf16[16,108,128]{2,1,0:T(8,128)(2,1)S(1)} async-done(((bf16[16,108,128]{2,1,0:T(8,128)(2,1)}), bf16[16,108,128]{2,1,0:T(8,128)(2,1)S(1)}, u32[]{:S(2)}, u32[]{:S(2)}) %all-to-all-start) | async-done | bytes 442400 | tf_op jit(solution)/shard_map/all_to_all | solution.py:25
  69.3 0.9 reshape.54
  70.2 1.9 %copy-done.5 = bf16[3,8,8,32,256]{4,3,2,1,0:T(8,128)(2,1)S(1)} copy-done((bf16[3,8,8,32,256]{4,3,2,1,0:T(8,128)(2,1)S(1)}, bf16[3,8,8,32,256]{4,3,2,1,0:T(8,128)(2,1)}, u32[]{:S(2)}) %copy-start.5) | copy-done | bytes 3145752
  72.1 2.6 %forward_half.1 = (f32[512,128]{1,0:T(8,128)S(1)}, f32[512,128]{1,0:T(8,128)S(1)}) custom-call(s32[5]{0:T(128)S(1)} %stack.54.flags, bf16[3,8,8,32,256]{4,3,2,1,0:T(8,128)(2,1)S(1)} %copy-done.5, bf16[6912,128]{1,0:T(8,128)(2,1)S(1)} %bitcast.31), custom_call_target="tpu_custom_call" | custom-call | flops 1811939328 | bytes 1048576 | tf_op jit(solution)/shard_map/forward_half/pallas_call | solution.py:207
  74.7 3.1 %collective-permute-start.8 = (bf16[1728,128]{1,0:T(8,128)(2,1)S(1)}, bf16[1728,128]{1,0:T(8,128)(2,1)}, u32[]{:S(2)}, u32[]{:S(2)}) collective-permute-start(bf16[1728,128]{1,0:T(8,128)(2,1)S(1)} %copy-done.7), channel_id=1, source_target_pairs={{0,128},{8,136},{16,144},{24,152},{32,160},{40,168},{48,176},{56,1... | collective-permute-start | bytes 1327112 | tf_op jit(solution)/shard_map/ppermute | solution.py:39
  77.8 5.1 %collective-permute-start.7 = (f32[512,128]{1,0:T(8,128)S(1)}, f32[512,128]{1,0:T(8,128)S(1)}, u32[]{:S(2)}, u32[]{:S(2)}) collective-permute-start(f32[512,128]{1,0:T(8,128)S(1)} %get-tuple-element.29.own), channel_id=1, source_target_pairs={{0,1},{1,0},{2,3},{3,2},{4,5},{5,4},{6,7},{7,6},{8,9},{9,8},{10,11... | collective-permute-start | bytes 786440 | tf_op jit(solution)/shard_map/ppermute | solution.py:29
  83.0 0.1 reshape.57
  83.1 0.2 slice_reduce_fusion.1
  83.3 0.8 collective-permute-done.7.other
  84.1 1.9 %copy-done.2 = bf16[3,8,8,32,256]{4,3,2,1,0:T(8,128)(2,1)S(1)} copy-done((bf16[3,8,8,32,256]{4,3,2,1,0:T(8,128)(2,1)S(1)}, bf16[3,8,8,32,256]{4,3,2,1,0:T(8,128)(2,1)}, u32[]{:S(2)}) %copy-start.2) | copy-done | bytes 3145752
  86.0 2.3 %local_terms.1 = bf16[3456,128]{1,0:T(8,128)(2,1)} custom-call(s32[5]{0:T(128)S(1)} %stack.54.flags, f32[512,128]{1,0:T(8,128)S(1)} %get-tuple-element.28.pre, f32[512,128]{1,0:T(8,128)S(1)} %get-tuple-element.29.own, f32[512,128]{1,0:T(8,128)S(1)} %collective-permute-done.7.other, f32[1,128]{1,0:T(1,128)S(1)} %bitcast.36, ...), custom_call_target="tpu_custom_call" | custom-call | flops 1811939328 | bytes 1048576 | tf_op jit(solution)/shard_map/local_terms/pallas_call | solution.py:207
  88.3 2.9 %collective-permute-start.9 = (bf16[6912,128]{1,0:T(8,128)(2,1)S(1)}, bf16[6912,128]{1,0:T(8,128)(2,1)}, u32[]{:S(2)}, u32[]{:S(2)}) collective-permute-start(bf16[6912,128]{1,0:T(8,128)(2,1)S(1)} %bitcast.32), channel_id=1, source_target_pairs={{0,1},{1,0},{2,3},{3,2},{4,5},{5,4},{6,7},{7,6},{8,9},{9,8},{10,11... | collective-permute-start | bytes 5308424 | tf_op jit(solution)/shard_map/ppermute | solution.py:29
  91.2 4.2 %all-to-all-start.2 = ((bf16[4,864,128]{2,1,0:T(8,128)(2,1)}), bf16[4,864,128]{2,1,0:T(8,128)(2,1)}, u32[]{:S(2)}, u32[]{:S(2)}) async-start(bf16[4,864,128]{2,1,0:T(8,128)(2,1)} %bitcast.9), calls=%async_computation.2 | async-start | bytes 1769472 | tf_op jit(solution)/shard_map/all_to_all | solution.py:290
  95.4 4.8 %collective-permute-start.10 = (bf16[1728,128]{1,0:T(8,128)(2,1)S(1)}, bf16[1728,128]{1,0:T(8,128)(2,1)}, u32[]{:S(2)}, u32[]{:S(2)}) collective-permute-start(bf16[1728,128]{1,0:T(8,128)(2,1)S(1)} %copy-done.7), channel_id=1, source_target_pairs={{0,256},{8,264},{16,272},{24,280},{32,288},{40,296},{48,304},{56,3... | collective-permute-start | bytes 1327112 | tf_op jit(solution)/shard_map/ppermute | solution.py:39
  100.3 2.8 %collective-permute-start.11 = (bf16[1728,128]{1,0:T(8,128)(2,1)S(1)}, bf16[1728,128]{1,0:T(8,128)(2,1)}, u32[]{:S(2)}, u32[]{:S(2)}) collective-permute-start(bf16[1728,128]{1,0:T(8,128)(2,1)S(1)} %copy-done.7), channel_id=1, source_target_pairs={{0,384},{8,392},{16,400},{24,408},{32,416},{40,424},{48,432},{56,4... | collective-permute-start | bytes 1327112 | tf_op jit(solution)/shard_map/ppermute | solution.py:39
  103.1 1.9 %copy-done.6 = bf16[3,8,8,32,256]{4,3,2,1,0:T(8,128)(2,1)S(1)} copy-done((bf16[3,8,8,32,256]{4,3,2,1,0:T(8,128)(2,1)S(1)}, bf16[3,8,8,32,256]{4,3,2,1,0:T(8,128)(2,1)}, u32[]{:S(2)}) %copy-start.6) | copy-done | bytes 3145752
  105.0 4.4 %forward_all.1.pre = f32[768,256]{1,0:T(8,128)S(1)} custom-call(s32[5]{0:T(128)S(1)} %stack.54.flags, bf16[3,8,8,32,256]{4,3,2,1,0:T(8,128)(2,1)S(1)} %copy-done.6, bf16[6912,128]{1,0:T(8,128)(2,1)S(1)} %bitcast.33, bf16[6912,128]{1,0:T(8,128)(2,1)} %collective-permute-done.9.other.w1_other), custom_call_target="tpu_custom_call" | custom-call | flops 2717908992 | bytes 1048576 | tf_op jit(solution)/shard_map/forward_all/pallas_call | solution.py:207
  109.4 9.0 %collective-permute-done.10 = bf16[1728,128]{1,0:T(8,128)(2,1)} collective-permute-done((bf16[1728,128]{1,0:T(8,128)(2,1)S(1)}, bf16[1728,128]{1,0:T(8,128)(2,1)}, u32[]{:S(2)}, u32[]{:S(2)}) %collective-permute-start.10) | collective-permute-done | bytes 442400 | tf_op jit(solution)/shard_map/ppermute | solution.py:39
  118.4 9.9 %collective-permute-done.11 = bf16[1728,128]{1,0:T(8,128)(2,1)} collective-permute-done((bf16[1728,128]{1,0:T(8,128)(2,1)S(1)}, bf16[1728,128]{1,0:T(8,128)(2,1)}, u32[]{:S(2)}, u32[]{:S(2)}) %collective-permute-start.11) | collective-permute-done | bytes 442400 | tf_op jit(solution)/shard_map/ppermute | solution.py:39
  128.3 1.4 select_bitcast_fusion.3
  129.7 1.5 pad_maximum_fusion.1
  131.1 2.4 %collective-permute-start.12 = (bf16[6912,128]{1,0:T(8,128)(2,1)}, bf16[6912,128]{1,0:T(8,128)(2,1)}, u32[]{:S(2)}, u32[]{:S(2)}) collective-permute-start(bf16[6912,128]{1,0:T(8,128)(2,1)} %bitcast.15.w2_own), channel_id=1, source_target_pairs={{0,1},{1,0},{2,3},{3,2},{4,5},{5,4},{6,7},{7,6},{8,9},{9,8},{10,11... | collective-permute-start | bytes 5308424 | tf_op jit(solution)/shard_map/ppermute | solution.py:29
  133.5 1.4 reduce_sum.30
  134.9 0.1 reshape.59
  135.0 14.9 %all_to_all.25 = bf16[16,54,128]{2,1,0:T(8,128)(2,1)S(1)} all-to-all(bf16[16,54,128]{2,1,0:T(8,128)(2,1)S(1)} %reshape.59), channel_id=1, replica_groups={{0,8,16,24,32,40,48,56,64,72,80,88,96,104,112,120},{128,136,144,152,160..., dimensions={0} | all-to-all | bytes 442368 | tf_op jit(solution)/shard_map/all_to_all | solution.py:302
  149.9 0.7 broadcast_in_dim.8
  150.6 9.5 %all-to-all-start.4 = ((f32[4,54,128]{2,1,0:T(8,128)}), f32[4,54,128]{2,1,0:T(8,128)S(1)}, u32[]{:S(2)}, u32[]{:S(2)}) async-start(f32[4,54,128]{2,1,0:T(8,128)} %broadcast_in_dim.8), calls=%async_computation.4 | async-start | bytes 229376 | tf_op jit(solution)/shard_map/all_to_all | solution.py:25
  160.1 7.2 %all-to-all-done.4 = f32[4,54,128]{2,1,0:T(8,128)S(1)} async-done(((f32[4,54,128]{2,1,0:T(8,128)}), f32[4,54,128]{2,1,0:T(8,128)S(1)}, u32[]{:S(2)}, u32[]{:S(2)}) %all-to-all-start.4) | async-done | bytes 110624 | tf_op jit(solution)/shard_map/all_to_all | solution.py:25
  167.4 1.9 %copy-done.3 = bf16[3,8,8,32,256]{4,3,2,1,0:T(8,128)(2,1)S(1)} copy-done((bf16[3,8,8,32,256]{4,3,2,1,0:T(8,128)(2,1)S(1)}, bf16[3,8,8,32,256]{4,3,2,1,0:T(8,128)(2,1)}, u32[]{:S(2)}) %copy-start.3) | copy-done | bytes 3145752
  169.2 10.0 %backward.1 = bf16[4,2,32,256]{3,2,1,0:T(8,128)(2,1)} custom-call(s32[5]{0:T(128)S(1)} %stack.54.flags, bf16[3,8,8,32,256]{4,3,2,1,0:T(8,128)(2,1)S(1)} %copy-done.3, f32[1,256]{1,0:T(1,128)S(1)} %bitcast.35, f32[768,256]{1,0:T(8,128)S(1)} %forward_all.1.pre, bf16[6912,128]{1,0:T(8,128)(2,1)S(1)} %bitcast.34, ...), custom_call_target="tpu_custom_call" | custom-call | flops 3623878656 | bytes 1048576 | tf_op jit(solution)/shard_map/backward/pallas_call | solution.py:207
  179.3 4.9 %collective-permute-start.13 = (f32[54,128]{1,0:T(8,128)S(1)}, f32[54,128]{1,0:T(8,128)S(1)}, u32[]{:S(2)}, u32[]{:S(2)}) collective-permute-start(f32[54,128]{1,0:T(8,128)S(1)} %reduce_sum.32), channel_id=1, source_target_pairs={{0,1},{1,0},{2,3},{3,2},{4,5},{5,4},{6,7},{7,6},{8,9},{9,8},{10,11... | collective-permute-start | bytes 82952 | tf_op jit(solution)/shard_map/ppermute | solution.py:29
  184.2 0.8 collective-permute-done.13
  185.1 0.7 reshape.62
  (35 shorter events, 0.2 us)
Async XLA Ops:
  0.6 0.8 copy-start
  0.6 19.6 %copy-start.9 = (bf16[4,2,32,256]{3,2,1,0:T(8,128)(2,1)S(1)}, bf16[4,2,32,256]{3,2,1,0:T(8,128)(2,1)}, u32[]{:S(2)}) copy-start(bf16[4,2,32,256]{3,2,1,0:T(8,128)(2,1)} %param.5) | copy-start | bytes 393220
  0.7 15.7 %copy-start.8 = (bf16[4,2,32,256]{3,2,1,0:T(8,128)(2,1)S(1)}, bf16[4,2,32,256]{3,2,1,0:T(8,128)(2,1)}, u32[]{:S(2)}) copy-start(bf16[4,2,32,256]{3,2,1,0:T(8,128)(2,1)} %param.6) | copy-start | bytes 393220
  2.4 41.9 %copy-start.10 = (bf16[108,256]{1,0:T(8,128)(2,1)S(1)}, bf16[108,256]{1,0:T(8,128)(2,1)}, u32[]{:S(2)}) copy-start(bf16[108,256]{1,0:T(8,128)(2,1)} %param.9) | copy-start | bytes 165892
  2.4 32.8 %all-to-all-start.1 = ((bf16[16,108,128]{2,1,0:T(8,128)(2,1)}), bf16[16,108,128]{2,1,0:T(8,128)(2,1)S(1)}, u32[]{:S(2)}, u32[]{:S(2)}) async-start(bf16[16,108,128]{2,1,0:T(8,128)(2,1)} %broadcast_in_dim.7), calls=%async_computation.1 | async-start | bytes 917504 | tf_op jit(solution)/shard_map/all_to_all | solution.py:25
  13.0 7.2 %collective-permute-start = (bf16[2,2,32,256]{3,2,1,0:T(8,128)(2,1)S(1)}, bf16[2,2,32,256]{3,2,1,0:T(8,128)(2,1)S(1)}, u32[]{:S(2)}, u32[]{:S(2)}) collective-permute-start(bf16[2,2,32,256]{3,2,1,0:T(8,128)(2,1)S(1)} %get-tuple-element.56), channel_id=1, source_target_pairs={{0,8},{8,16},{16,24},{24,32},{32,40},{40,48},{48,56},{56,64},{64,7... | collective-permute-start | bytes 196616 | tf_op jit(solution)/shard_map/ppermute | solution.py:35
  16.4 11.6 %collective-permute-start.1 = (bf16[6,2,32,256]{3,2,1,0:T(8,128)(2,1)S(1)}, bf16[6,2,32,256]{3,2,1,0:T(8,128)(2,1)S(1)}, u32[]{:S(2)}, u32[]{:S(2)}) collective-permute-start(bf16[6,2,32,256]{3,2,1,0:T(8,128)(2,1)S(1)} %pad_maximum_fusion.3), channel_id=1, source_target_pairs={{8,0},{16,8},{24,16},{32,24},{40,32},{48,40},{56,48},{64,56},{72,6... | collective-permute-start | bytes 589832 | tf_op jit(solution)/shard_map/ppermute | solution.py:35
  28.0 19.6 %collective-permute-start.2 = (bf16[16,2,32,256]{3,2,1,0:T(8,128)(2,1)S(1)}, bf16[16,2,32,256]{3,2,1,0:T(8,128)(2,1)S(1)}, u32[]{:S(2)}, u32[]{:S(2)}) collective-permute-start(bf16[16,2,32,256]{3,2,1,0:T(8,128)(2,1)S(1)} %slice_dynamic-update-slice_fusion.mid), channel_id=1, source_target_pairs={{1,2},{3,4},{5,6},{2,1},{4,3},{6,5},{9,10},{11,12},{13,14},{10,9},... | collective-permute-start | bytes 1572872 | tf_op jit(solution)/shard_map/ppermute | solution.py:54
  35.4 21.8 %collective-permute-start.4 = (bf16[1728,128]{1,0:T(8,128)(2,1)S(1)}, bf16[1728,128]{1,0:T(8,128)(2,1)S(1)}, u32[]{:S(2)}, u32[]{:S(2)}) collective-permute-start(bf16[1728,128]{1,0:T(8,128)(2,1)S(1)} %reshape.55), channel_id=1, source_target_pairs={{0,384},{8,392},{16,400},{24,408},{32,416},{40,424},{48,432},{56,4... | collective-permute-start | bytes 1327112 | tf_op jit(solution)/shard_map/ppermute | solution.py:39
  39.8 17.4 %collective-permute-start.5 = (bf16[1728,128]{1,0:T(8,128)(2,1)S(1)}, bf16[1728,128]{1,0:T(8,128)(2,1)}, u32[]{:S(2)}, u32[]{:S(2)}) collective-permute-start(bf16[1728,128]{1,0:T(8,128)(2,1)S(1)} %reshape.55), channel_id=1, source_target_pairs={{0,256},{8,264},{16,272},{24,280},{32,288},{40,296},{48,304},{56,3... | collective-permute-start | bytes 1327112 | tf_op jit(solution)/shard_map/ppermute | solution.py:39
  42.2 16.0 %collective-permute-start.6 = (bf16[1728,128]{1,0:T(8,128)(2,1)S(1)}, bf16[1728,128]{1,0:T(8,128)(2,1)}, u32[]{:S(2)}, u32[]{:S(2)}) collective-permute-start(bf16[1728,128]{1,0:T(8,128)(2,1)S(1)} %reshape.55), channel_id=1, source_target_pairs={{0,128},{8,136},{16,144},{24,152},{32,160},{40,168},{48,176},{56,1... | collective-permute-start | bytes 1327112 | tf_op jit(solution)/shard_map/ppermute | solution.py:39
  48.6 11.2 %collective-permute-start.3 = (bf16[16,3,32,256]{3,2,1,0:T(8,128)(2,1)}, bf16[16,3,32,256]{3,2,1,0:T(8,128)(2,1)}, u32[]{:S(2)}, u32[]{:S(2)}) collective-permute-start(bf16[16,3,32,256]{3,2,1,0:T(8,128)(2,1)} %pad_maximum_fusion.2), channel_id=1, source_target_pairs={{0,1},{1,0},{2,3},{3,2},{4,5},{5,4},{6,7},{7,6},{8,9},{9,8},{10,11... | collective-permute-start | bytes 2359304 | tf_op jit(solution)/shard_map/ppermute | solution.py:29
  51.4 18.0 %all-to-all-start = ((bf16[16,108,128]{2,1,0:T(8,128)(2,1)}), bf16[16,108,128]{2,1,0:T(8,128)(2,1)S(1)}, u32[]{:S(2)}, u32[]{:S(2)}) async-start(bf16[16,108,128]{2,1,0:T(8,128)(2,1)} %broadcast_in_dim.6), calls=%async_computation | async-start | bytes 917504 | tf_op jit(solution)/shard_map/all_to_all | solution.py:25
  61.8 1.6 copy-start.1
  63.5 1.7 copy-start.4
  70.2 1.9 %copy-start.5 = (bf16[3,8,8,32,256]{4,3,2,1,0:T(8,128)(2,1)S(1)}, bf16[3,8,8,32,256]{4,3,2,1,0:T(8,128)(2,1)}, u32[]{:S(2)}) copy-start(bf16[3,8,8,32,256]{4,3,2,1,0:T(8,128)(2,1)} %copy-done.4) | copy-start | bytes 9437188
  72.1 2.7 %copy-start.7 = (bf16[1728,128]{1,0:T(8,128)(2,1)S(1)}, bf16[1728,128]{1,0:T(8,128)(2,1)}, u32[]{:S(2)}) copy-start(bf16[1728,128]{1,0:T(8,128)(2,1)} %reshape.54) | copy-start | bytes 1327108
  72.1 10.9 %copy-start.11 = (f32[256]{0:T(256)S(1)}, f32[256]{0:T(256)}, u32[]{:S(2)}) copy-start(f32[256]{0:T(256)} %param.7) | copy-start | bytes 3076
  74.7 13.6 %collective-permute-start.8 = (bf16[1728,128]{1,0:T(8,128)(2,1)S(1)}, bf16[1728,128]{1,0:T(8,128)(2,1)}, u32[]{:S(2)}, u32[]{:S(2)}) collective-permute-start(bf16[1728,128]{1,0:T(8,128)(2,1)S(1)} %copy-done.7), channel_id=1, source_target_pairs={{0,128},{8,136},{16,144},{24,152},{32,160},{40,168},{48,176},{56,1... | collective-permute-start | bytes 1327112 | tf_op jit(solution)/shard_map/ppermute | solution.py:39
  77.8 6.3 %collective-permute-start.7 = (f32[512,128]{1,0:T(8,128)S(1)}, f32[512,128]{1,0:T(8,128)S(1)}, u32[]{:S(2)}, u32[]{:S(2)}) collective-permute-start(f32[512,128]{1,0:T(8,128)S(1)} %get-tuple-element.29.own), channel_id=1, source_target_pairs={{0,1},{1,0},{2,3},{3,2},{4,5},{5,4},{6,7},{7,6},{8,9},{9,8},{10,11... | collective-permute-start | bytes 786440 | tf_op jit(solution)/shard_map/ppermute | solution.py:29
  84.1 1.9 %copy-start.2 = (bf16[3,8,8,32,256]{4,3,2,1,0:T(8,128)(2,1)S(1)}, bf16[3,8,8,32,256]{4,3,2,1,0:T(8,128)(2,1)}, u32[]{:S(2)}) copy-start(bf16[3,8,8,32,256]{4,3,2,1,0:T(8,128)(2,1)} %copy-done.1) | copy-start | bytes 9437188
  88.3 14.8 %collective-permute-start.9 = (bf16[6912,128]{1,0:T(8,128)(2,1)S(1)}, bf16[6912,128]{1,0:T(8,128)(2,1)}, u32[]{:S(2)}, u32[]{:S(2)}) collective-permute-start(bf16[6912,128]{1,0:T(8,128)(2,1)S(1)} %bitcast.32), channel_id=1, source_target_pairs={{0,1},{1,0},{2,3},{3,2},{4,5},{5,4},{6,7},{7,6},{8,9},{9,8},{10,11... | collective-permute-start | bytes 5308424 | tf_op jit(solution)/shard_map/ppermute | solution.py:29
  91.2 18.2 %all-to-all-start.2 = ((bf16[4,864,128]{2,1,0:T(8,128)(2,1)}), bf16[4,864,128]{2,1,0:T(8,128)(2,1)}, u32[]{:S(2)}, u32[]{:S(2)}) async-start(bf16[4,864,128]{2,1,0:T(8,128)(2,1)} %bitcast.9), calls=%async_computation.2 | async-start | bytes 1769472 | tf_op jit(solution)/shard_map/all_to_all | solution.py:290
  95.4 22.9 %collective-permute-start.10 = (bf16[1728,128]{1,0:T(8,128)(2,1)S(1)}, bf16[1728,128]{1,0:T(8,128)(2,1)}, u32[]{:S(2)}, u32[]{:S(2)}) collective-permute-start(bf16[1728,128]{1,0:T(8,128)(2,1)S(1)} %copy-done.7), channel_id=1, source_target_pairs={{0,256},{8,264},{16,272},{24,280},{32,288},{40,296},{48,304},{56,3... | collective-permute-start | bytes 1327112 | tf_op jit(solution)/shard_map/ppermute | solution.py:39
  100.3 28.0 %collective-permute-start.11 = (bf16[1728,128]{1,0:T(8,128)(2,1)S(1)}, bf16[1728,128]{1,0:T(8,128)(2,1)}, u32[]{:S(2)}, u32[]{:S(2)}) collective-permute-start(bf16[1728,128]{1,0:T(8,128)(2,1)S(1)} %copy-done.7), channel_id=1, source_target_pairs={{0,384},{8,392},{16,400},{24,408},{32,416},{40,424},{48,432},{56,4... | collective-permute-start | bytes 1327112 | tf_op jit(solution)/shard_map/ppermute | solution.py:39
  103.1 1.9 %copy-start.6 = (bf16[3,8,8,32,256]{4,3,2,1,0:T(8,128)(2,1)S(1)}, bf16[3,8,8,32,256]{4,3,2,1,0:T(8,128)(2,1)}, u32[]{:S(2)}) copy-start(bf16[3,8,8,32,256]{4,3,2,1,0:T(8,128)(2,1)} %copy-done.4) | copy-start | bytes 9437188
  131.1 36.2 %collective-permute-start.12 = (bf16[6912,128]{1,0:T(8,128)(2,1)}, bf16[6912,128]{1,0:T(8,128)(2,1)}, u32[]{:S(2)}, u32[]{:S(2)}) collective-permute-start(bf16[6912,128]{1,0:T(8,128)(2,1)} %bitcast.15.w2_own), channel_id=1, source_target_pairs={{0,1},{1,0},{2,3},{3,2},{4,5},{5,4},{6,7},{7,6},{8,9},{9,8},{10,11... | collective-permute-start | bytes 5308424 | tf_op jit(solution)/shard_map/ppermute | solution.py:29
  150.6 16.7 %all-to-all-start.4 = ((f32[4,54,128]{2,1,0:T(8,128)}), f32[4,54,128]{2,1,0:T(8,128)S(1)}, u32[]{:S(2)}, u32[]{:S(2)}) async-start(f32[4,54,128]{2,1,0:T(8,128)} %broadcast_in_dim.8), calls=%async_computation.4 | async-start | bytes 229376 | tf_op jit(solution)/shard_map/all_to_all | solution.py:25
  167.4 1.9 %copy-start.3 = (bf16[3,8,8,32,256]{4,3,2,1,0:T(8,128)(2,1)S(1)}, bf16[3,8,8,32,256]{4,3,2,1,0:T(8,128)(2,1)}, u32[]{:S(2)}) copy-start(bf16[3,8,8,32,256]{4,3,2,1,0:T(8,128)(2,1)} %copy-done.1) | copy-start | bytes 9437188
  179.3 5.8 %collective-permute-start.13 = (f32[54,128]{1,0:T(8,128)S(1)}, f32[54,128]{1,0:T(8,128)S(1)}, u32[]{:S(2)}, u32[]{:S(2)}) collective-permute-start(f32[54,128]{1,0:T(8,128)S(1)} %reduce_sum.32), channel_id=1, source_target_pairs={{0,1},{1,0},{2,3},{3,2},{4,5},{5,4},{6,7},{7,6},{8,9},{9,8},{10,11... | collective-permute-start | bytes 82952 | tf_op jit(solution)/shard_map/ppermute | solution.py:29

commit v3 on v2

--- a/solution.py
+++ b/solution.py
@@ -16,7 +16,8 @@
 
 YZ_GROUPS = [[x * 16 + k for k in range(16)] for x in range(4)]
 X_GROUPS = [[k, k + 16, k + 32, k + 48] for k in range(16)]
-Z_GROUPS = [[c, c + 2, c + 4, c + 6] for c in range(2)]
+Y_GROUPS = [[b * 8 + k for k in range(8)] for b in range(8)]
+ROW_GROUPS = [list(range(8))]
 
 
 def spread(block, axis, groups):
@@ -35,17 +36,18 @@
     return lax.ppermute(block, axis, route)
 
 
-def from_x(block, mask):
-    return lax.ppermute(block, "tm", [(i, i ^ (mask * 16)) for i in range(lax.axis_size("tm"))])
-
-
-def in_order(blocks, low, high):
-    a, b, c, d = blocks
-    a, b = jnp.where(low, b, a), jnp.where(low, a, b)
-    c, d = jnp.where(low, d, c), jnp.where(low, c, d)
-    a, c = jnp.where(high, c, a), jnp.where(high, a, c)
-    b, d = jnp.where(high, d, b), jnp.where(high, b, d)
-    return jnp.stack([a, b, c, d])
+def from_z(block, distance):
+    def device(x, y, z, c):
+        return (x * 16 + (z % 2) * 8 + y) * 8 + (z // 2) * 2 + c
+
+    route = [
+        (device(x, y, (z + distance) % 8, c), device(x, y, z, c))
+        for x in range(4)
+        for y in range(8)
+        for z in range(8)
+        for c in range(2)
+    ]
+    return lax.ppermute(block, ("tm", "rows"), route)
 
 
 def beyond_chip(block):
@@ -77,22 +79,33 @@
     return scale, normed, gated, sigma
 
 
-def shifts_kernel(flags, mid, edge, other, xs, cs):
+def fill_all(out, flags, field, base, count, far, channels=C):
+    mid, edge, other = field
     core = flags[2]
-    for out, base in ((xs, 0), (cs, 8)):
-        for f in range(0, 8, 2):
-            frames = slice(f, f + 2)
-            source = slice(base + f, base + f + 2)
-            fill_shifts(out, mid[source], frames, 3)
-            fill_shifts(out, edge[source], frames, 1 + 4 * core)
-            fill_shifts(out, other[source, :2], frames, 5 - 4 * core)
-            fill_shifts(out, other[source, 2:], frames, 0)
+    for f in range(0, count, 2):
+        frames = slice(f, f + 2)
+        source = slice(base + f, base + f + 2)
+        fill_shifts(out, mid[source, :, :, :channels], frames, 3)
+        fill_shifts(out, edge[source, :, :, :channels], frames, 1 + 4 * core)
+        fill_shifts(out, other[source, :2, :, :channels], frames, 5 - 4 * core)
+        if far:
+            fill_shifts(out, other[source, 2:, :, :channels], frames, 0)
             for k in range(3):
                 out[k, frames, 7:8] = out[k, frames, 0:1]
 
 
-def half_kernel(flags, xs, w1, pre, squares):
+def arrange(out, flags, part, more_a, more_b):
+    here, there = flags[5] * 864, 864 - flags[5] * 864
+    for n in range(4):
+        out[pl.ds(pl.multiple_of(n * 1728 + here, 32), 864)] = part[n]
+        more = more_a[n] if n < 2 else more_b[n - 2]
+        out[pl.ds(pl.multiple_of(n * 1728 + there, 32), 864)] = more
+
+
+def half_kernel(flags, mid, edge, other, part, more_a, more_b, pre, squares, w1, xs):
     base = 2 - 2 * flags[2]
+    fill_all(xs, flags, (mid, edge, other), 0, 6, True)
+    arrange(w1, flags, part, more_a, more_b)
     for i in range(3):
         for j in range(3):
             lhs = jnp.concatenate(
@@ -108,14 +121,15 @@
     squares[...] = jnp.broadcast_to(total, (512, HALF))
 
 
-def terms_kernel(flags, pre, own, other, gain, cs, out):
+def terms_kernel(flags, pre, own, others, gain, mid, edge, other, out, cs):
     base = 2 - 2 * flags[2]
-    _, _, gated, sigma = normalize(pre[...], own[...] + other[...], gain[...])
+    fill_all(cs, flags, (mid, edge, other), 8, 6, True, CH)
+    _, _, gated, sigma = normalize(pre[...], own[...] + others[...], gain[...])
     act = (gated * sigma).T.astype(BF)
     taps = [(i, j, k) for i in range(3) for j in range(3) for k in range(3)]
 
     def operand(i, j, k):
-        return cs[2 - k, 2 - i : 6 - i, pl.ds(base + 2 - j, 4), :, :CH].reshape(512, CH)
+        return cs[2 - k, 2 - i : 6 - i, pl.ds(base + 2 - j, 4)].reshape(512, CH)
 
     for n in range(0, 27, 2):
         pair = taps[n : n + 2]
@@ -130,7 +144,8 @@
     return jnp.where(flags[2] == 1, turned, value)
 
 
-def pre_kernel(flags, xs, own, other, pre, acc):
+def pre_kernel(flags, mid, edge, others, own, other, pre, acc, xs):
+    fill_all(xs, flags, (mid, edge, others), 0, 8, False)
     for i in range(3):
         for j in range(3):
             lhs = jnp.concatenate(
@@ -146,7 +161,13 @@
     pre[...] = halves_in_order(flags, acc[...])
 
 
-def backward_kernel(flags, cs, gain, pre, w1_own, w1_other, w2_own, w2_other, out, ps, acc):
+def backward_kernel(
+    flags, mid, edge, other, gain, pre, w1_own, w1_other, part, more_a, more_b,
+    far_part, far_more_a, far_more_b, out, ps, acc, cs, w2_own, w2_other,
+):
+    fill_all(cs, flags, (mid, edge, other), 8, 8, False)
+    arrange(w2_own, flags, part, more_a, more_b)
+    arrange(w2_other, flags, far_part, far_more_a, far_more_b)
     nt = (((1,), (1,)), ((), ()))
     taps = [(i, j, k) for i in range(3) for j in range(3) for k in range(3)]
     for n, (i, j, k) in enumerate(taps):
@@ -216,42 +237,52 @@
     )(*operands)
 
 
-def make_shifts(flags, mid, edge, other):
-    shape = jax.ShapeDtypeStruct((3, 8, 8, W, C), BF)
-    return call(shifts_kernel, "shifts", 1, (shape, shape), [], flags, mid, edge, other)
-
-
-def forward_half(flags, xs, w1):
+def forward_half(flags, field, part, more_a, more_b):
     shape = jax.ShapeDtypeStruct((512, HALF), F32)
-    return call(half_kernel, "forward_half", 4 * 512 * ROWS * HALF, (shape, shape), [], flags, xs, w1)
-
-
-def local_terms(flags, pre, own, other, gain, cs):
+    weight = jax.ShapeDtypeStruct((ROWS, HALF), BF)
+    scratch = [pltpu.VMEM((3, 6, 8, W, C), BF)]
+    return call(
+        half_kernel, "forward_half", 4 * 512 * ROWS * HALF, (shape, shape, weight), scratch,
+        flags, *field, part, more_a, more_b,
+    )
+
+
+def local_terms(flags, pre, own, others, gain, field):
     shape = jax.ShapeDtypeStruct((ROWS // 2, CH), BF)
+    scratch = [pltpu.VMEM((3, 6, 8, W, CH), BF)]
     return call(
-        terms_kernel, "local_terms", 4 * 512 * ROWS * HALF, shape, [], flags, pre, own, other, gain, cs
-    )
-
-
-def forward_all(flags, xs, own, other):
+        terms_kernel, "local_terms", 4 * 512 * ROWS * HALF, shape, scratch,
+        flags, pre, own, others, gain, *field,
+    )
+
+
+def forward_all(flags, field, own, other):
     shape = jax.ShapeDtypeStruct((768, C), F32)
-    scratch = [pltpu.VMEM((768, C), F32)]
-    return call(pre_kernel, "forward_all", 2 * 768 * ROWS * C, shape, scratch, flags, xs, own, other)
-
-
-def backward(flags, cs, gain, pre, w1_own, w1_other, w2_own, w2_other):
+    scratch = [pltpu.VMEM((768, C), F32), pltpu.VMEM((3, 8, 8, W, C), BF)]
+    return call(
+        pre_kernel, "forward_all", 2 * 768 * ROWS * C, shape, scratch, flags, *field, own, other
+    )
+
+
+def backward(flags, field, gain, pre, w1_own, w1_other, w2_own, w2_other):
     shape = jax.ShapeDtypeStruct((4, 2, W, C), BF)
-    scratch = [pltpu.VMEM((3, 6, 4, W, C), BF), pltpu.VMEM((768, C), F32)]
+    scratch = [
+        pltpu.VMEM((3, 6, 4, W, C), BF),
+        pltpu.VMEM((768, C), F32),
+        pltpu.VMEM((3, 8, 8, W, C), BF),
+        pltpu.VMEM((ROWS, HALF), BF),
+        pltpu.VMEM((ROWS, HALF), BF),
+    ]
     return call(
         backward_kernel, "backward", 2 * 1024 * ROWS * C, shape, scratch,
-        flags, cs, gain, pre, w1_own, w1_other, w2_own, w2_other,
+        flags, *field, gain, pre, w1_own, w1_other, *w2_own, *w2_other,
     )
 
 
 def on_device(activations, cotangent, gain, first_weight, second_weight):
     tm, rows = lax.axis_index("tm"), lax.axis_index("rows")
-    core, x = rows % 2, tm // 16
-    flags = jnp.stack([tm, rows, core, lax.axis_size("tm") - 1, lax.axis_size("rows") - 1])
+    core, z_lo = rows % 2, (tm // 8) % 2
+    flags = jnp.stack([tm, rows, core, lax.axis_size("tm") - 1, lax.axis_size("rows") - 1, z_lo])
     flags = flags.astype(jnp.int32)
 
     pick = lax.broadcasted_iota(jnp.int32, (C, HALF), 0) == (
@@ -263,9 +294,8 @@
     gain_half = jnp.where(core == 0, gain_pairs[:, 0], gain_pairs[:, 1]).reshape(1, HALF)
     gain_all = jnp.concatenate([gain_pairs[:, 0], gain_pairs[:, 1]]).reshape(1, C)
 
-    w1_block = spread(half1, "tm", YZ_GROUPS).reshape(16 * 108, HALF)
-    w1_blocks = [w1_block] + [from_x(w1_block, mask) for mask in (1, 2, 3)]
-    w1_own = in_order(w1_blocks, x % 2 == 1, x // 2 == 1).reshape(ROWS, HALF)
+    block = spread(jnp.concatenate([half1, half2]), "tm", Y_GROUPS)
+    w1_part = spread(block[:, :108].reshape(864, HALF), "tm", X_GROUPS)
     activations, cotangent, _ = lax.optimization_barrier((activations, cotangent, half1))
 
     nexts = shift(jnp.concatenate([activations[:2], cotangent], axis=0), "tm", -1)
@@ -273,40 +303,32 @@
     mid = jnp.concatenate([prevs, activations, nexts[:2], cotangent, nexts[2:]], axis=0)
     edge = beyond_chip(mid)
     next_row = jnp.where(core == 0, edge[:, 1:], edge[:, :1])
-    other = swap_cores(jnp.concatenate([mid, next_row], axis=1))
-    xs, cs = make_shifts(flags, mid, edge, other)
-
-    w2_block = spread(after(half2, edge), "tm", YZ_GROUPS).reshape(16 * 108, HALF)
-    xs, w2_block = lax.optimization_barrier((xs, w2_block))
-
-    pre_half, squares = forward_half(flags, xs, w1_own)
+    field = (mid, edge, swap_cores(jnp.concatenate([mid, next_row], axis=1)))
+
+    w1_more = from_z(w1_part[:2], 1), from_z(w1_part[2:], -1)
+    w2_part = spread(after(block[:, 108:].reshape(864, HALF), w1_part), "tm", X_GROUPS)
+    w1_more, w2_part = lax.optimization_barrier((w1_more, w2_part))
+
+    pre_half, squares, w1_own = forward_half(flags, field, w1_part, *w1_more)
     squares_other = swap_cores(squares)
-    w2_block = after(w2_block, squares)
-    w2_blocks = [w2_block] + [from_x(w2_block, mask) for mask in (1, 2, 3)]
-    terms = local_terms(flags, pre_half, squares, squares_other, gain_half, cs)
-
-    terms, w2_blocks[1] = lax.optimization_barrier((terms, w2_blocks[1]))
+    terms = local_terms(flags, pre_half, squares, squares_other, gain_half, field)
 
     total = lax.all_to_all(
         terms.reshape(4, 864, CH), "tm", 0, 0, axis_index_groups=X_GROUPS, tiled=True
     )
-
+    w2_part = after(w2_part, terms)
+    w2_own = [w2_part, from_z(w2_part[:2], 1), from_z(w2_part[2:], -1)]
     w1_other = swap_cores(after(w1_own, terms))
-    pre = forward_all(flags, xs, w1_own, w1_other)
+    pre = forward_all(flags, field, w1_own, w1_other)
     total, pre = lax.optimization_barrier((total, pre))
-    w2_blocks = lax.optimization_barrier((w2_blocks, total))[0]
-    w2_own = in_order(w2_blocks, x % 2 == 1, x // 2 == 1).reshape(ROWS, HALF)
-    w2_other = swap_cores(w2_own)
+    w2_other = [swap_cores(part) for part in w2_own]
+    input_grad = backward(flags, field, gain_all, pre, w1_own, w1_other, w2_own, w2_other)
 
     total = total.astype(F32).sum(0).astype(BF).reshape(16, 54, CH)
     total = lax.all_to_all(total, "tm", 0, 0, axis_index_groups=YZ_GROUPS, tiled=True)
-    total = spread(total.astype(F32).sum(0), "rows", Z_GROUPS).sum(0)
-    input_grad = backward(flags, cs, gain_all, pre, w1_own, w1_other, w2_own, w2_other)
-
+    total = spread(total.astype(F32).sum(0), "rows", ROW_GROUPS)
     total, input_grad = lax.optimization_barrier((total, input_grad))
-    other = swap_cores(total)
-    even, odd = jnp.where(core == 0, total, other), jnp.where(core == 0, other, total)
-    weight_grad = jnp.stack([even, odd], axis=1).reshape(108, CH)
+    weight_grad = total.reshape(4, 2, 54, CH).sum(0).transpose(1, 0, 2).reshape(108, CH)
     return (input_grad, weight_grad)
 
 

time: 187 us -> 150 us (0.80)
  waiting for transfers between devices: 46.5 us -> 24.5 us
  blocking collectives: 14.9 us -> 0 us
  starting transfers between devices: 77.9 us -> 81.4 us
  local copies, waits for them, and re-layouts: 16.8 us -> 13.4 us
  Pallas kernels: 21.4 us -> 23.9 us
  other arithmetic: 7.03 us -> 4.75 us
    all_to_all x1 -> x0, blocking collectives: 14.9 us -> none  [on_device(): lax.all_to_all(total, 'tm', 0, 0, axis_index_groups=YZ_GROUPS, tiled=True)]
    ppermute x6 -> x4, waiting for transfers between devices: 20 us -> 8.91 us  [from_z(): return lax.ppermute(block, ('tm', 'rows'), route)]
    ppermute x2, waiting for transfers between devices: 10.3 us -> 0.01 us  [shift(): return lax.ppermute(block, axis, route)]
    unnamed x28 -> x20, local copies, waits for them, and re-layouts: 11.7 us -> 4.47 us
    another operation x6 -> x0, other arithmetic: 4.41 us -> none  [the longest x4 4.4 us: in_order(): return jnp.stack([a, b, c, d])]
    all_to_all x0 -> x1, starting transfers between devices: none -> 3.53 us  [on_device(): lax.all_to_all(total, 'tm', 0, 0, axis_index_groups=YZ_GROUPS, tiled=True)]
    ppermute x5 -> x6, starting transfers between devices: 17.3 us -> 20.5 us  [swap_cores(): lax.ppermute(block, 'rows', [(i, i ^ 1) for i in range(lax.axis_size('row...]
    ppermute x1, waiting for transfers between devices: 3.2 us -> 0.3 us  [beyond_chip(): return lax.ppermute(block, 'rows', route)]
  transfers between devices with their start and end apart: 18 -> 19, of which waited for: 10 -> 7; matrix products, arithmetic and copies ran while one was open for 4% -> 8% of each run, Pallas kernels for 5% -> 11%
where the time goes in v3:
time: 150 us; the launch traced here: 149 us
  starting transfers between devices  81.4 us (54%)
  waiting for transfers between devices  24.5 us (16%)
  Pallas kernels  23.9 us (16%)
  local copies, waits for them, and re-layouts  13.4 us (9%)
  other arithmetic  4.75 us (3%)
    pallas_call x4, Pallas kernels, call(): pl.pallas_call(kernel, out_shape=out_shape, in_specs=smem + [VMEM] * (len...  23.9 us
    all_to_all x4, starting transfers between devices, spread(): lax.all_to_all(operand, axis, 0, 0, axis_index_groups=groups, tiled=True)  22.6 us
    ppermute x6, starting transfers between devices, swap_cores(): lax.ppermute(block, 'rows', [(i, i ^ 1) for i in range(lax.axis_size('row...  20.5 us
    ppermute x4, starting transfers between devices, from_z(): return lax.ppermute(block, ('tm', 'rows'), route)  17.9 us
    all_to_all x4, waiting for transfers between devices, spread(): lax.all_to_all(operand, axis, 0, 0, axis_index_groups=groups, tiled=True)  11.8 us
    ppermute x4, waiting for transfers between devices, from_z(): return lax.ppermute(block, ('tm', 'rows'), route)  8.91 us
    ppermute x1, starting transfers between devices, beyond_chip(): return lax.ppermute(block, 'rows', route)  7.21 us
    ppermute x2, starting transfers between devices, shift(): return lax.ppermute(block, axis, route)  5.33 us
  transfers between devices with their start and end apart: 19, of which 7 were waited for; matrix products, arithmetic and copies ran while one was open for 8% of the time, Pallas kernels for 11%

profile of v3, /device:TPU:1, one launch (start us, length us, event | category | flops | bytes accessed | tf_op | source)
XLA Modules:
  0.0 149.1 jit_solution(416196981565851250)
XLA Ops:
  0.6 0.0 copy-start
  0.6 0.0 copy-start.6
  0.7 0.0 copy-start.5
  0.7 0.8 copy-done
  1.5 0.1 fusion
  1.6 0.9 fusion.5
  2.5 4.0 %collective-permute-start = (bf16[2,2,32,256]{3,2,1,0:T(8,128)(2,1)S(1)}, bf16[2,2,32,256]{3,2,1,0:T(8,128)(2,1)S(1)}, u32[]{:S(2)}, u32[]{:S(2)}) collective-permute-start(bf16[2,2,32,256]{3,2,1,0:T(8,128)(2,1)S(1)} %get-tuple-element.42), channel_id=1, source_target_pairs={{0,8},{8,16},{16,24},{24,32},{32,40},{40,48},{48,56},{56,64},{64,7... | collective-permute-start | bytes 196616 | tf_op jit(solution)/shard_map/ppermute | solution.py:36
  6.5 0.9 pad_maximum_fusion.1
  7.5 1.3 collective-permute-start.1
  8.8 0.8 constant_dynamic-slice_fusion
  9.6 0.8 broadcast_in_dim.10
  10.4 8.8 %all-to-all-start = ((bf16[8,216,128]{2,1,0:T(8,128)(2,1)}), bf16[8,216,128]{2,1,0:T(8,128)(2,1)S(1)}, u32[]{:S(2)}, u32[]{:S(2)}) async-start(bf16[8,216,128]{2,1,0:T(8,128)(2,1)} %broadcast_in_dim.10), calls=%async_computation | async-start | bytes 884736 | tf_op jit(solution)/shard_map/all_to_all | solution.py:26
  19.2 0.0 collective-permute-done
  19.2 0.0 collective-permute-done.1
  19.3 7.2 %collective-permute-start.2 = (bf16[16,2,32,256]{3,2,1,0:T(8,128)(2,1)S(1)}, bf16[16,2,32,256]{3,2,1,0:T(8,128)(2,1)S(1)}, u32[]{:S(2)}, u32[]{:S(2)}) collective-permute-start(bf16[16,2,32,256]{3,2,1,0:T(8,128)(2,1)S(1)} %slice_dynamic-update-slice_fusion.mid), channel_id=1, source_target_pairs={{1,2},{3,4},{5,6},{2,1},{4,3},{6,5},{9,10},{11,12},{13,14},{10,9},... | collective-permute-start | bytes 1572872 | tf_op jit(solution)/shard_map/ppermute | solution.py:56
  26.5 7.0 %all-to-all-done = bf16[8,216,128]{2,1,0:T(8,128)(2,1)S(1)} async-done(((bf16[8,216,128]{2,1,0:T(8,128)(2,1)}), bf16[8,216,128]{2,1,0:T(8,128)(2,1)S(1)}, u32[]{:S(2)}, u32[]{:S(2)}) %all-to-all-start) | async-done | bytes 442400 | tf_op jit(solution)/shard_map/all_to_all | solution.py:26
  33.5 0.1 fusion.4
  33.7 1.0 broadcast_in_dim.12
  34.7 4.0 %all-to-all-start.1 = ((bf16[4,864,128]{2,1,0:T(8,128)(2,1)}), bf16[4,864,128]{2,1,0:T(8,128)(2,1)S(1)}, u32[]{:S(2)}, u32[]{:S(2)}) async-start(bf16[4,864,128]{2,1,0:T(8,128)(2,1)} %broadcast_in_dim.12), calls=%async_computation.1 | async-start | bytes 1769472 | tf_op jit(solution)/shard_map/all_to_all | solution.py:26
  38.7 0.3 collective-permute-done.2.edge
  39.0 1.0 pad_maximum_fusion
  40.0 4.2 %collective-permute-start.3 = (bf16[16,3,32,256]{3,2,1,0:T(8,128)(2,1)}, bf16[16,3,32,256]{3,2,1,0:T(8,128)(2,1)}, u32[]{:S(2)}, u32[]{:S(2)}) collective-permute-start(bf16[16,3,32,256]{3,2,1,0:T(8,128)(2,1)} %pad_maximum_fusion), channel_id=1, source_target_pairs={{0,1},{1,0},{2,3},{3,2},{4,5},{5,4},{6,7},{7,6},{8,9},{9,8},{10,11... | collective-permute-start | bytes 2359304 | tf_op jit(solution)/shard_map/ppermute | solution.py:30
  44.3 4.8 %all-to-all-done.1.part = bf16[4,864,128]{2,1,0:T(8,128)(2,1)S(1)} async-done(((bf16[4,864,128]{2,1,0:T(8,128)(2,1)}), bf16[4,864,128]{2,1,0:T(8,128)(2,1)S(1)}, u32[]{:S(2)}, u32[]{:S(2)}) %all-to-all-start.1) | async-done | bytes 884768 | tf_op jit(solution)/shard_map/all_to_all | solution.py:26
  49.1 1.0 broadcast_in_dim.13
  50.2 3.5 %all-to-all-start.2 = ((bf16[4,864,128]{2,1,0:T(8,128)(2,1)}), bf16[4,864,128]{2,1,0:T(8,128)(2,1)S(1)}, u32[]{:S(2)}, u32[]{:S(2)}) async-start(bf16[4,864,128]{2,1,0:T(8,128)(2,1)} %broadcast_in_dim.13), calls=%async_computation.2 | async-start | bytes 1769472 | tf_op jit(solution)/shard_map/all_to_all | solution.py:26
  53.7 1.0 fusion.3
  54.7 10.7 %collective-permute-start.4 = (bf16[2,864,128]{2,1,0:T(8,128)(2,1)}, bf16[2,864,128]{2,1,0:T(8,128)(2,1)S(1)}, u32[]{:S(2)}, u32[]{:S(2)}) collective-permute-start(bf16[2,864,128]{2,1,0:T(8,128)(2,1)} %get-tuple-element.38), channel_id=1, source_target_pairs={{64,0},{65,1},{2,64},{3,65},{66,2},{67,3},{4,66},{5,67},{68,4},{69... | collective-permute-start | bytes 1327112 | tf_op jit(solution)/shard_map/ppermute | solution.py:50
  65.3 1.9 %collective-permute-start.5 = (bf16[2,864,128]{2,1,0:T(8,128)(2,1)}, bf16[2,864,128]{2,1,0:T(8,128)(2,1)}, u32[]{:S(2)}, u32[]{:S(2)}) collective-permute-start(bf16[2,864,128]{2,1,0:T(8,128)(2,1)} %get-tuple-element.37), channel_id=1, source_target_pairs={{70,0},{71,1},{0,64},{1,65},{64,2},{65,3},{2,66},{3,67},{66,4},{67... | collective-permute-start | bytes 1327112 | tf_op jit(solution)/shard_map/ppermute | solution.py:50
  67.3 0.1 stack.19.flags
  67.4 3.9 %collective-permute-done.4.more_a = bf16[2,864,128]{2,1,0:T(8,128)(2,1)S(1)} collective-permute-done((bf16[2,864,128]{2,1,0:T(8,128)(2,1)}, bf16[2,864,128]{2,1,0:T(8,128)(2,1)S(1)}, u32[]{:S(2)}, u32[]{:S(2)}) %collective-permute-start.4) | collective-permute-done | bytes 442400 | tf_op jit(solution)/shard_map/ppermute | solution.py:50
  71.2 5.0 %collective-permute-done.5.more_b = bf16[2,864,128]{2,1,0:T(8,128)(2,1)} collective-permute-done((bf16[2,864,128]{2,1,0:T(8,128)(2,1)}, bf16[2,864,128]{2,1,0:T(8,128)(2,1)}, u32[]{:S(2)}, u32[]{:S(2)}) %collective-permute-start.5) | collective-permute-done | bytes 442400 | tf_op jit(solution)/shard_map/ppermute | solution.py:50
  76.3 0.0 all-to-all-done.2.part
  76.3 0.0 collective-permute-done.3.other.others
  76.3 4.5 %forward_half.1 = (f32[512,128]{1,0:T(8,128)S(1)}, f32[512,128]{1,0:T(8,128)}, bf16[6912,128]{1,0:T(8,128)(2,1)}) custom-call(s32[6]{0:T(128)S(1)} %stack.19.flags, bf16[16,2,32,256]{3,2,1,0:T(8,128)(2,1)S(1)} %slice_dynamic-update-slice_fusion.mid, bf16[16,2,32,256]{3,2,1,0:T(8,128)(2,1)S(1)} %collective-permute-done.2.edge, ...), custom_call_target="tpu_custom_call" | custom-call | flops 1811939328 | bytes 1048576 | tf_op jit(solution)/shard_map/forward_half/pallas_call | solution.py:228
  80.8 0.7 copy-done.3
  81.5 6.9 %collective-permute-start.6 = (f32[512,128]{1,0:T(8,128)}, f32[512,128]{1,0:T(8,128)S(1)}, u32[]{:S(2)}, u32[]{:S(2)}) collective-permute-start(f32[512,128]{1,0:T(8,128)} %get-tuple-element.23.own), channel_id=1, source_target_pairs={{0,1},{1,0},{2,3},{3,2},{4,5},{5,4},{6,7},{7,6},{8,9},{9,8},{10,11... | collective-permute-start | bytes 786440 | tf_op jit(solution)/shard_map/ppermute | solution.py:30
  88.4 0.1 reshape.50
  88.6 0.7 slice_reduce_fusion.1
  89.3 0.5 collective-permute-done.6.others
  89.8 0.9 copy-done.4
  90.7 3.2 %local_terms.1 = bf16[3456,128]{1,0:T(8,128)(2,1)} custom-call(s32[6]{0:T(128)S(1)} %stack.19.flags, f32[512,128]{1,0:T(8,128)S(1)} %copy-done.4, f32[512,128]{1,0:T(8,128)} %get-tuple-element.23.own, f32[512,128]{1,0:T(8,128)S(1)} %collective-permute-done.6.others, f32[1,128]{1,0:T(1,128)S(1)} %bitcast.13, ...), custom_call_target="tpu_custom_call" | custom-call | flops 1811939328 | bytes 1048576 | tf_op jit(solution)/shard_map/local_terms/pallas_call | solution.py:228
  93.9 2.3 %collective-permute-start.7 = (bf16[6912,128]{1,0:T(8,128)(2,1)}, bf16[6912,128]{1,0:T(8,128)(2,1)}, u32[]{:S(2)}, u32[]{:S(2)}) collective-permute-start(bf16[6912,128]{1,0:T(8,128)(2,1)} %get-tuple-element.25.own.w1_own), channel_id=1, source_target_pairs={{0,1},{1,0},{2,3},{3,2},{4,5},{5,4},{6,7},{7,6},{8,9},{9,8},{10,11... | collective-permute-start | bytes 5308424 | tf_op jit(solution)/shard_map/ppermute | solution.py:30
  96.2 4.3 %all-to-all-start.3 = ((bf16[4,864,128]{2,1,0:T(8,128)(2,1)}), bf16[4,864,128]{2,1,0:T(8,128)(2,1)}, u32[]{:S(2)}, u32[]{:S(2)}) async-start(bf16[4,864,128]{2,1,0:T(8,128)(2,1)} %bitcast.5), calls=%async_computation.3 | async-start | bytes 1769472 | tf_op jit(solution)/shard_map/all_to_all | solution.py:316
  100.5 2.3 %collective-permute-start.10 = (bf16[4,864,128]{2,1,0:T(8,128)(2,1)S(1)}, bf16[4,864,128]{2,1,0:T(8,128)(2,1)}, u32[]{:S(2)}, u32[]{:S(2)}) collective-permute-start(bf16[4,864,128]{2,1,0:T(8,128)(2,1)S(1)} %all-to-all-done.2.part), channel_id=1, source_target_pairs={{0,1},{1,0},{2,3},{3,2},{4,5},{5,4},{6,7},{7,6},{8,9},{9,8},{10,11... | collective-permute-start | bytes 2654216 | tf_op jit(solution)/shard_map/ppermute | solution.py:30
  102.8 0.9 fusion.2
  103.7 1.9 %collective-permute-start.8 = (bf16[2,864,128]{2,1,0:T(8,128)(2,1)}, bf16[2,864,128]{2,1,0:T(8,128)(2,1)S(1)}, u32[]{:S(2)}, u32[]{:S(2)}) collective-permute-start(bf16[2,864,128]{2,1,0:T(8,128)(2,1)} %get-tuple-element.36), channel_id=1, source_target_pairs={{64,0},{65,1},{2,64},{3,65},{66,2},{67,3},{4,66},{5,67},{68,4},{69... | collective-permute-start | bytes 1327112 | tf_op jit(solution)/shard_map/ppermute | solution.py:50
  105.6 3.4 %collective-permute-start.9 = (bf16[2,864,128]{2,1,0:T(8,128)(2,1)S(1)}, bf16[2,864,128]{2,1,0:T(8,128)(2,1)S(1)}, u32[]{:S(2)}, u32[]{:S(2)}) collective-permute-start(bf16[2,864,128]{2,1,0:T(8,128)(2,1)S(1)} %get-tuple-element.35), channel_id=1, source_target_pairs={{70,0},{71,1},{0,64},{1,65},{64,2},{65,3},{2,66},{3,67},{66,4},{67... | collective-permute-start | bytes 1327112 | tf_op jit(solution)/shard_map/ppermute | solution.py:50
  109.0 0.0 collective-permute-done.7.other.w1_other
  109.0 5.5 %forward_all.1.pre = f32[768,256]{1,0:T(8,128)S(1)} custom-call(s32[6]{0:T(128)S(1)} %stack.19.flags, bf16[16,2,32,256]{3,2,1,0:T(8,128)(2,1)S(1)} %slice_dynamic-update-slice_fusion.mid, bf16[16,2,32,256]{3,2,1,0:T(8,128)(2,1)S(1)} %collective-permute-done.2.edge, bf16[16,3,32,256]{3,2,1,0:T(8,128)(2,1)} %collective-permute-done.3.other.others, ...), custom_call_target="tpu_custom_call" | custom-call | flops 2717908992 | bytes 1048576 | tf_op jit(solution)/shard_map/forward_all/pallas_call | solution.py:228
  114.6 0.9 copy-done.1
  115.5 0.0 all-to-all-done.3
  115.5 1.4 reduce_sum.30
  116.8 0.8 reshape.52
  117.6 3.5 %all-to-all-start.4 = ((bf16[16,54,128]{2,1,0:T(8,128)(2,1)}), bf16[16,54,128]{2,1,0:T(8,128)(2,1)S(1)}, u32[]{:S(2)}, u32[]{:S(2)}) async-start(bf16[16,54,128]{2,1,0:T(8,128)(2,1)} %reshape.52), calls=%async_computation.4 | async-start | bytes 458752 | tf_op jit(solution)/shard_map/all_to_all | solution.py:328
  121.1 0.0 collective-permute-done.8.more_a
  121.1 2.8 %collective-permute-start.11 = (bf16[2,864,128]{2,1,0:T(8,128)(2,1)S(1)}, bf16[2,864,128]{2,1,0:T(8,128)(2,1)}, u32[]{:S(2)}, u32[]{:S(2)}) collective-permute-start(bf16[2,864,128]{2,1,0:T(8,128)(2,1)S(1)} %collective-permute-done.8.more_a), channel_id=1, source_target_pairs={{0,1},{1,0},{2,3},{3,2},{4,5},{5,4},{6,7},{7,6},{8,9},{9,8},{10,11... | collective-permute-start | bytes 1327112 | tf_op jit(solution)/shard_map/ppermute | solution.py:30
  124.0 1.9 %collective-permute-start.12 = (bf16[2,864,128]{2,1,0:T(8,128)(2,1)S(1)}, bf16[2,864,128]{2,1,0:T(8,128)(2,1)}, u32[]{:S(2)}, u32[]{:S(2)}) collective-permute-start(bf16[2,864,128]{2,1,0:T(8,128)(2,1)S(1)} %collective-permute-done.9.more_b), channel_id=1, source_target_pairs={{0,1},{1,0},{2,3},{3,2},{4,5},{5,4},{6,7},{7,6},{8,9},{9,8},{10,11... | collective-permute-start | bytes 1327112 | tf_op jit(solution)/shard_map/ppermute | solution.py:30
  125.9 2.9 %all-to-all-done.4 = bf16[16,54,128]{2,1,0:T(8,128)(2,1)S(1)} async-done(((bf16[16,54,128]{2,1,0:T(8,128)(2,1)}), bf16[16,54,128]{2,1,0:T(8,128)(2,1)S(1)}, u32[]{:S(2)}, u32[]{:S(2)}) %all-to-all-start.4) | async-done | bytes 221216 | tf_op jit(solution)/shard_map/all_to_all | solution.py:328
  128.8 0.7 broadcast_in_dim.14
  129.5 6.2 %all-to-all-start.5 = ((f32[8,54,128]{2,1,0:T(8,128)}), f32[8,54,128]{2,1,0:T(8,128)S(1)}, u32[]{:S(2)}, u32[]{:S(2)}) async-start(f32[8,54,128]{2,1,0:T(8,128)} %broadcast_in_dim.14), calls=%async_computation.5 | async-start | bytes 458752 | tf_op jit(solution)/shard_map/all_to_all | solution.py:26
  135.8 0.7 pad_maximum_fusion.3
  136.5 1.1 copy-done.2
  137.6 10.8 %backward.1 = bf16[4,2,32,256]{3,2,1,0:T(8,128)(2,1)} custom-call(s32[6]{0:T(128)S(1)} %stack.19.flags, bf16[16,2,32,256]{3,2,1,0:T(8,128)(2,1)S(1)} %slice_dynamic-update-slice_fusion.mid, bf16[16,2,32,256]{3,2,1,0:T(8,128)(2,1)S(1)} %collective-permute-done.2.edge, bf16[16,3,32,256]{3,2,1,0:T(8,128)(2,1)} %collective-permute-done.3.other.others, ...), custom_call_target="tpu_custom_call" | custom-call | flops 3623878656 | bytes 1048576 | tf_op jit(solution)/shard_map/backward/pallas_call | solution.py:228
  148.4 0.7 reshape.55
  (26 shorter events, 0.3 us)
Async XLA Ops:
  0.6 0.8 copy-start
  0.6 18.6 %copy-start.6 = (bf16[4,2,32,256]{3,2,1,0:T(8,128)(2,1)S(1)}, bf16[4,2,32,256]{3,2,1,0:T(8,128)(2,1)}, u32[]{:S(2)}) copy-start(bf16[4,2,32,256]{3,2,1,0:T(8,128)(2,1)} %param.5) | copy-start | bytes 393220
  0.7 18.6 %copy-start.5 = (bf16[4,2,32,256]{3,2,1,0:T(8,128)(2,1)S(1)}, bf16[4,2,32,256]{3,2,1,0:T(8,128)(2,1)}, u32[]{:S(2)}) copy-start(bf16[4,2,32,256]{3,2,1,0:T(8,128)(2,1)} %param.6) | copy-start | bytes 393220
  2.5 16.7 %collective-permute-start = (bf16[2,2,32,256]{3,2,1,0:T(8,128)(2,1)S(1)}, bf16[2,2,32,256]{3,2,1,0:T(8,128)(2,1)S(1)}, u32[]{:S(2)}, u32[]{:S(2)}) collective-permute-start(bf16[2,2,32,256]{3,2,1,0:T(8,128)(2,1)S(1)} %get-tuple-element.42), channel_id=1, source_target_pairs={{0,8},{8,16},{16,24},{24,32},{32,40},{40,48},{48,56},{56,64},{64,7... | collective-permute-start | bytes 196616 | tf_op jit(solution)/shard_map/ppermute | solution.py:36
  7.5 11.8 %collective-permute-start.1 = (bf16[6,2,32,256]{3,2,1,0:T(8,128)(2,1)S(1)}, bf16[6,2,32,256]{3,2,1,0:T(8,128)(2,1)S(1)}, u32[]{:S(2)}, u32[]{:S(2)}) collective-permute-start(bf16[6,2,32,256]{3,2,1,0:T(8,128)(2,1)S(1)} %pad_maximum_fusion.1), channel_id=1, source_target_pairs={{8,0},{16,8},{24,16},{32,24},{40,32},{48,40},{56,48},{64,56},{72,6... | collective-permute-start | bytes 589832 | tf_op jit(solution)/shard_map/ppermute | solution.py:36
  10.4 23.2 %all-to-all-start = ((bf16[8,216,128]{2,1,0:T(8,128)(2,1)}), bf16[8,216,128]{2,1,0:T(8,128)(2,1)S(1)}, u32[]{:S(2)}, u32[]{:S(2)}) async-start(bf16[8,216,128]{2,1,0:T(8,128)(2,1)} %broadcast_in_dim.10), calls=%async_computation | async-start | bytes 884736 | tf_op jit(solution)/shard_map/all_to_all | solution.py:26
  19.3 19.7 %collective-permute-start.2 = (bf16[16,2,32,256]{3,2,1,0:T(8,128)(2,1)S(1)}, bf16[16,2,32,256]{3,2,1,0:T(8,128)(2,1)S(1)}, u32[]{:S(2)}, u32[]{:S(2)}) collective-permute-start(bf16[16,2,32,256]{3,2,1,0:T(8,128)(2,1)S(1)} %slice_dynamic-update-slice_fusion.mid), channel_id=1, source_target_pairs={{1,2},{3,4},{5,6},{2,1},{4,3},{6,5},{9,10},{11,12},{13,14},{10,9},... | collective-permute-start | bytes 1572872 | tf_op jit(solution)/shard_map/ppermute | solution.py:56
  34.7 14.5 %all-to-all-start.1 = ((bf16[4,864,128]{2,1,0:T(8,128)(2,1)}), bf16[4,864,128]{2,1,0:T(8,128)(2,1)S(1)}, u32[]{:S(2)}, u32[]{:S(2)}) async-start(bf16[4,864,128]{2,1,0:T(8,128)(2,1)} %broadcast_in_dim.12), calls=%async_computation.1 | async-start | bytes 1769472 | tf_op jit(solution)/shard_map/all_to_all | solution.py:26
  40.0 36.3 %collective-permute-start.3 = (bf16[16,3,32,256]{3,2,1,0:T(8,128)(2,1)}, bf16[16,3,32,256]{3,2,1,0:T(8,128)(2,1)}, u32[]{:S(2)}, u32[]{:S(2)}) collective-permute-start(bf16[16,3,32,256]{3,2,1,0:T(8,128)(2,1)} %pad_maximum_fusion), channel_id=1, source_target_pairs={{0,1},{1,0},{2,3},{3,2},{4,5},{5,4},{6,7},{7,6},{8,9},{9,8},{10,11... | collective-permute-start | bytes 2359304 | tf_op jit(solution)/shard_map/ppermute | solution.py:30
  50.2 26.1 %all-to-all-start.2 = ((bf16[4,864,128]{2,1,0:T(8,128)(2,1)}), bf16[4,864,128]{2,1,0:T(8,128)(2,1)S(1)}, u32[]{:S(2)}, u32[]{:S(2)}) async-start(bf16[4,864,128]{2,1,0:T(8,128)(2,1)} %broadcast_in_dim.13), calls=%async_computation.2 | async-start | bytes 1769472 | tf_op jit(solution)/shard_map/all_to_all | solution.py:26
  54.7 16.6 %collective-permute-start.4 = (bf16[2,864,128]{2,1,0:T(8,128)(2,1)}, bf16[2,864,128]{2,1,0:T(8,128)(2,1)S(1)}, u32[]{:S(2)}, u32[]{:S(2)}) collective-permute-start(bf16[2,864,128]{2,1,0:T(8,128)(2,1)} %get-tuple-element.38), channel_id=1, source_target_pairs={{64,0},{65,1},{2,64},{3,65},{66,2},{67,3},{4,66},{5,67},{68,4},{69... | collective-permute-start | bytes 1327112 | tf_op jit(solution)/shard_map/ppermute | solution.py:50
  65.3 11.0 %collective-permute-start.5 = (bf16[2,864,128]{2,1,0:T(8,128)(2,1)}, bf16[2,864,128]{2,1,0:T(8,128)(2,1)}, u32[]{:S(2)}, u32[]{:S(2)}) collective-permute-start(bf16[2,864,128]{2,1,0:T(8,128)(2,1)} %get-tuple-element.37), channel_id=1, source_target_pairs={{70,0},{71,1},{0,64},{1,65},{64,2},{65,3},{2,66},{3,67},{66,4},{67... | collective-permute-start | bytes 1327112 | tf_op jit(solution)/shard_map/ppermute | solution.py:50
  67.4 21.0 %copy-start.7 = (f32[256]{0:T(256)S(1)}, f32[256]{0:T(256)}, u32[]{:S(2)}) copy-start(f32[256]{0:T(256)} %param.7) | copy-start | bytes 3076
  80.8 0.7 copy-start.3
  81.5 8.3 %collective-permute-start.6 = (f32[512,128]{1,0:T(8,128)}, f32[512,128]{1,0:T(8,128)S(1)}, u32[]{:S(2)}, u32[]{:S(2)}) collective-permute-start(f32[512,128]{1,0:T(8,128)} %get-tuple-element.23.own), channel_id=1, source_target_pairs={{0,1},{1,0},{2,3},{3,2},{4,5},{5,4},{6,7},{7,6},{8,9},{9,8},{10,11... | collective-permute-start | bytes 786440 | tf_op jit(solution)/shard_map/ppermute | solution.py:30
  89.8 0.9 copy-start.4
  93.9 15.2 %collective-permute-start.7 = (bf16[6912,128]{1,0:T(8,128)(2,1)}, bf16[6912,128]{1,0:T(8,128)(2,1)}, u32[]{:S(2)}, u32[]{:S(2)}) collective-permute-start(bf16[6912,128]{1,0:T(8,128)(2,1)} %get-tuple-element.25.own.w1_own), channel_id=1, source_target_pairs={{0,1},{1,0},{2,3},{3,2},{4,5},{5,4},{6,7},{7,6},{8,9},{9,8},{10,11... | collective-permute-start | bytes 5308424 | tf_op jit(solution)/shard_map/ppermute | solution.py:30
  96.2 19.3 %all-to-all-start.3 = ((bf16[4,864,128]{2,1,0:T(8,128)(2,1)}), bf16[4,864,128]{2,1,0:T(8,128)(2,1)}, u32[]{:S(2)}, u32[]{:S(2)}) async-start(bf16[4,864,128]{2,1,0:T(8,128)(2,1)} %bitcast.5), calls=%async_computation.3 | async-start | bytes 1769472 | tf_op jit(solution)/shard_map/all_to_all | solution.py:316
  100.5 35.9 %collective-permute-start.10 = (bf16[4,864,128]{2,1,0:T(8,128)(2,1)S(1)}, bf16[4,864,128]{2,1,0:T(8,128)(2,1)}, u32[]{:S(2)}, u32[]{:S(2)}) collective-permute-start(bf16[4,864,128]{2,1,0:T(8,128)(2,1)S(1)} %all-to-all-done.2.part), channel_id=1, source_target_pairs={{0,1},{1,0},{2,3},{3,2},{4,5},{5,4},{6,7},{7,6},{8,9},{9,8},{10,11... | collective-permute-start | bytes 2654216 | tf_op jit(solution)/shard_map/ppermute | solution.py:30
  103.7 17.4 %collective-permute-start.8 = (bf16[2,864,128]{2,1,0:T(8,128)(2,1)}, bf16[2,864,128]{2,1,0:T(8,128)(2,1)S(1)}, u32[]{:S(2)}, u32[]{:S(2)}) collective-permute-start(bf16[2,864,128]{2,1,0:T(8,128)(2,1)} %get-tuple-element.36), channel_id=1, source_target_pairs={{64,0},{65,1},{2,64},{3,65},{66,2},{67,3},{4,66},{5,67},{68,4},{69... | collective-permute-start | bytes 1327112 | tf_op jit(solution)/shard_map/ppermute | solution.py:50
  105.6 18.3 %collective-permute-start.9 = (bf16[2,864,128]{2,1,0:T(8,128)(2,1)S(1)}, bf16[2,864,128]{2,1,0:T(8,128)(2,1)S(1)}, u32[]{:S(2)}, u32[]{:S(2)}) collective-permute-start(bf16[2,864,128]{2,1,0:T(8,128)(2,1)S(1)} %get-tuple-element.35), channel_id=1, source_target_pairs={{70,0},{71,1},{0,64},{1,65},{64,2},{65,3},{2,66},{3,67},{66,4},{67... | collective-permute-start | bytes 1327112 | tf_op jit(solution)/shard_map/ppermute | solution.py:50
  114.6 0.9 copy-start.1
  117.6 11.2 %all-to-all-start.4 = ((bf16[16,54,128]{2,1,0:T(8,128)(2,1)}), bf16[16,54,128]{2,1,0:T(8,128)(2,1)S(1)}, u32[]{:S(2)}, u32[]{:S(2)}) async-start(bf16[16,54,128]{2,1,0:T(8,128)(2,1)} %reshape.52), calls=%async_computation.4 | async-start | bytes 458752 | tf_op jit(solution)/shard_map/all_to_all | solution.py:328
  121.1 15.3 %collective-permute-start.11 = (bf16[2,864,128]{2,1,0:T(8,128)(2,1)S(1)}, bf16[2,864,128]{2,1,0:T(8,128)(2,1)}, u32[]{:S(2)}, u32[]{:S(2)}) collective-permute-start(bf16[2,864,128]{2,1,0:T(8,128)(2,1)S(1)} %collective-permute-done.8.more_a), channel_id=1, source_target_pairs={{0,1},{1,0},{2,3},{3,2},{4,5},{5,4},{6,7},{7,6},{8,9},{9,8},{10,11... | collective-permute-start | bytes 1327112 | tf_op jit(solution)/shard_map/ppermute | solution.py:30
  124.0 12.5 %collective-permute-start.12 = (bf16[2,864,128]{2,1,0:T(8,128)(2,1)S(1)}, bf16[2,864,128]{2,1,0:T(8,128)(2,1)}, u32[]{:S(2)}, u32[]{:S(2)}) collective-permute-start(bf16[2,864,128]{2,1,0:T(8,128)(2,1)S(1)} %collective-permute-done.9.more_b), channel_id=1, source_target_pairs={{0,1},{1,0},{2,3},{3,2},{4,5},{5,4},{6,7},{7,6},{8,9},{9,8},{10,11... | collective-permute-start | bytes 1327112 | tf_op jit(solution)/shard_map/ppermute | solution.py:30
  129.5 18.8 %all-to-all-start.5 = ((f32[8,54,128]{2,1,0:T(8,128)}), f32[8,54,128]{2,1,0:T(8,128)S(1)}, u32[]{:S(2)}, u32[]{:S(2)}) async-start(f32[8,54,128]{2,1,0:T(8,128)} %broadcast_in_dim.14), calls=%async_computation.5 | async-start | bytes 458752 | tf_op jit(solution)/shard_map/all_to_all | solution.py:26
  136.5 1.1 copy-start.2

commit v4 on v3

--- a/solution.py
+++ b/solution.py
@@ -18,6 +18,10 @@
 X_GROUPS = [[k, k + 16, k + 32, k + 48] for k in range(16)]
 Y_GROUPS = [[b * 8 + k for k in range(8)] for b in range(8)]
 ROW_GROUPS = [list(range(8))]
+UNPACK_COST = 1 << 36
+SUM_COST = 1 << 20
+SPLIT_COST = 1 << 36
+GAINS_COST = 1 << 36
 
 
 def spread(block, axis, groups):
@@ -94,18 +98,64 @@
                 out[k, frames, 7:8] = out[k, frames, 0:1]
 
 
-def arrange(out, flags, part, more_a, more_b):
+def start_all(sems, pairs):
+    copies = [pltpu.make_async_copy(source, to, sems.at[n]) for n, (source, to) in enumerate(pairs)]
+    for copy in copies:
+        copy.start()
+    return copies
+
+
+def wait_all(copies):
+    for copy in copies:
+        copy.wait()
+
+
+def fetch(out, flags, weight, sems):
     here, there = flags[5] * 864, 864 - flags[5] * 864
+    pairs = []
     for n in range(4):
-        out[pl.ds(pl.multiple_of(n * 1728 + here, 32), 864)] = part[n]
-        more = more_a[n] if n < 2 else more_b[n - 2]
-        out[pl.ds(pl.multiple_of(n * 1728 + there, 32), 864)] = more
-
-
-def half_kernel(flags, mid, edge, other, part, more_a, more_b, pre, squares, w1, xs):
+        more = weight[1].at[n] if len(weight) == 2 else weight[1 + n // 2].at[n % 2]
+        pairs.append((weight[0].at[n], out.at[pl.ds(pl.multiple_of(n * 1728 + here, 32), 864)]))
+        pairs.append((more, out.at[pl.ds(pl.multiple_of(n * 1728 + there, 32), 864)]))
+    return start_all(sems, pairs)
+
+
+def gains_kernel(flags, gain, half, both):
+    row = lax.broadcasted_iota(jnp.int32, (C, HALF), 0)
+    col = lax.broadcasted_iota(jnp.int32, (C, HALF), 1)
+    wide = jnp.broadcast_to(gain[...], (HALF, C)).T
+    even = jnp.sum(jnp.where(row == 2 * col, wide, 0.0), axis=0, keepdims=True)
+    odd = jnp.sum(jnp.where(row == 2 * col + 1, wide, 0.0), axis=0, keepdims=True)
+    half[...] = jnp.where(flags[2] == 0, even, odd)
+    both[...] = jnp.concatenate([even, odd], axis=1)
+
+
+def unpack_kernel(block_in, first, second, block, sems):
+    wait_all(start_all(sems, ((block_in, block),)))
+    for out, at in ((first, 0), (second, 108)):
+        rows = [block[n, at : at + 108].astype(F32) for n in range(8)]
+        rows = jnp.concatenate(rows, axis=0).astype(BF)
+        for n in range(4):
+            out[n] = rows
+
+
+def split_kernel(part, first, second, sems):
+    wait_all(start_all(sems, ((part.at[:2], first), (part.at[2:], second))))
+
+
+def sum_kernel(terms_in, out, terms, sems):
+    wait_all(start_all(sems, ((terms_in, terms),)))
+    total = terms[0].astype(F32) + terms[1].astype(F32)
+    total = (total + terms[2].astype(F32)) + terms[3].astype(F32)
+    for n in range(16):
+        out[n] = total[n * 54 : n * 54 + 54].astype(BF)
+
+
+def half_kernel(flags, mid, edge, other, part, more_a, more_b, pre, squares, w1, xs, sems):
     base = 2 - 2 * flags[2]
+    copies = fetch(w1, flags, (part, more_a, more_b), sems)
     fill_all(xs, flags, (mid, edge, other), 0, 6, True)
-    arrange(w1, flags, part, more_a, more_b)
+    wait_all(copies)
     for i in range(3):
         for j in range(3):
             lhs = jnp.concatenate(
@@ -121,9 +171,13 @@
     squares[...] = jnp.broadcast_to(total, (512, HALF))
 
 
-def terms_kernel(flags, pre, own, others, gain, mid, edge, other, out, cs):
+def terms_kernel(
+    flags, pre_in, own_in, others_in, gain, mid, edge, other, out, cs, pre, own, others, sems
+):
     base = 2 - 2 * flags[2]
+    copies = start_all(sems, ((pre_in, pre), (own_in, own), (others_in, others)))
     fill_all(cs, flags, (mid, edge, other), 8, 6, True, CH)
+    wait_all(copies)
     _, _, gated, sigma = normalize(pre[...], own[...] + others[...], gain[...])
     act = (gated * sigma).T.astype(BF)
     taps = [(i, j, k) for i in range(3) for j in range(3) for k in range(3)]
@@ -144,8 +198,13 @@
     return jnp.where(flags[2] == 1, turned, value)
 
 
-def pre_kernel(flags, mid, edge, others, own, other, pre, acc, xs):
+def pre_kernel(
+    flags, mid, edge, others, part, more_a, more_b, far_part, far_more, pre, acc, xs, own, other, sems
+):
+    copies = fetch(own, flags, (part, more_a, more_b), sems.at[0])
+    copies += fetch(other, flags, (far_part, far_more), sems.at[1])
     fill_all(xs, flags, (mid, edge, others), 0, 8, False)
+    wait_all(copies)
     for i in range(3):
         for j in range(3):
             lhs = jnp.concatenate(
@@ -161,13 +220,15 @@
     pre[...] = halves_in_order(flags, acc[...])
 
 
-def backward_kernel(
-    flags, mid, edge, other, gain, pre, w1_own, w1_other, part, more_a, more_b,
-    far_part, far_more_a, far_more_b, out, ps, acc, cs, w2_own, w2_other,
+def middle_kernel(
+    flags, mid, edge, other, gain, pre_in, part, more_a, more_b, far_part, far_more_a, far_more_b,
+    out, pre, acc, cs, w2_own, w2_other, sems, pre_sem,
 ):
+    copies = fetch(w2_own, flags, (part, more_a, more_b), sems.at[0])
+    copies += fetch(w2_other, flags, (far_part, far_more_a, far_more_b), sems.at[1])
+    copies += start_all(pre_sem, ((pre_in, pre),))
     fill_all(cs, flags, (mid, edge, other), 8, 8, False)
-    arrange(w2_own, flags, part, more_a, more_b)
-    arrange(w2_other, flags, far_part, far_more_a, far_more_b)
+    wait_all(copies)
     nt = (((1,), (1,)), ((), ()))
     taps = [(i, j, k) for i in range(3) for j in range(3) for k in range(3)]
     for n, (i, j, k) in enumerate(taps):
@@ -205,8 +266,19 @@
         if t >= 4:
             outside = outside | (flags[0] == flags[3])
         pre_grad = jnp.where(outside, 0.0, pre_grad)
-        pre_grad = halves_in_order(flags, pre_grad).astype(BF).reshape(1, 4, W, C)
-        fill_shifts(ps, pre_grad, slice(t, t + 1), 0)
+        out[t] = halves_in_order(flags, pre_grad).astype(BF).reshape(4, W, C)
+
+
+def last_kernel(
+    flags, grad, part, more_a, more_b, far_part, far_more, out, ps, acc, w1_own, w1_other, sems
+):
+    copies = fetch(w1_own, flags, (part, more_a, more_b), sems.at[0])
+    copies += fetch(w1_other, flags, (far_part, far_more), sems.at[1])
+    for t in range(0, 6, 2):
+        fill_shifts(ps, grad[t : t + 2], slice(t, t + 2), 0)
+    wait_all(copies)
+    nt = (((1,), (1,)), ((), ()))
+    taps = [(i, j, k) for i in range(3) for j in range(3) for k in range(3)]
     for n, (i, j, k) in enumerate(taps):
         lhs = ps[2 - k, 2 - i : 6 - i, 2 - j : 4 - j].reshape(256, C)
         at = n * C
@@ -221,14 +293,16 @@
 
 VMEM = pl.BlockSpec(memory_space=pltpu.VMEM)
 SMEM = pl.BlockSpec(memory_space=pltpu.SMEM)
-
-
-def call(kernel, name, flops, out_shape, scratch, *operands):
-    smem = [SMEM] if operands[0].dtype == jnp.int32 else []
+ANY = pl.BlockSpec(memory_space=pl.ANY)
+WEIGHT = pltpu.VMEM((ROWS, HALF), BF)
+SEMS = pltpu.SemaphoreType.DMA
+
+
+def call(kernel, name, flops, out_shape, scratch, specs, *operands):
     return pl.pallas_call(
         kernel,
         out_shape=out_shape,
-        in_specs=smem + [VMEM] * (len(operands) - len(smem)),
+        in_specs=specs,
         out_specs=jax.tree.map(lambda _: VMEM, out_shape),
         scratch_shapes=scratch,
         compiler_params=pltpu.CompilerParams(vmem_limit_bytes=32 * 1024 * 1024),
@@ -237,45 +311,79 @@
     )(*operands)
 
 
-def forward_half(flags, field, part, more_a, more_b):
+def order_gains(flags, gain):
+    half = jax.ShapeDtypeStruct((1, HALF), F32)
+    both = jax.ShapeDtypeStruct((1, C), F32)
+    specs = [SMEM, VMEM]
+    return call(gains_kernel, "gains", GAINS_COST, (half, both), [], specs, flags, gain.reshape(1, C))
+
+
+def unpack(block):
+    shape = jax.ShapeDtypeStruct((4, 864, HALF), BF)
+    scratch = [pltpu.VMEM((8, 216, HALF), BF), SEMS((1,))]
+    return call(unpack_kernel, "unpack", UNPACK_COST, (shape, shape), scratch, [ANY], block)
+
+
+def split(part):
+    shape = jax.ShapeDtypeStruct((2, 864, HALF), BF)
+    return call(split_kernel, "split", SPLIT_COST, (shape, shape), [SEMS((2,))], [ANY], part)
+
+
+def sum_terms(terms):
+    shape = jax.ShapeDtypeStruct((16, 54, CH), BF)
+    scratch = [pltpu.VMEM((4, 864, CH), BF), SEMS((1,))]
+    return call(sum_kernel, "sum_terms", SUM_COST, shape, scratch, [ANY], terms)
+
+
+def forward_half(flags, field, weight):
     shape = jax.ShapeDtypeStruct((512, HALF), F32)
-    weight = jax.ShapeDtypeStruct((ROWS, HALF), BF)
-    scratch = [pltpu.VMEM((3, 6, 8, W, C), BF)]
+    scratch = [WEIGHT, pltpu.VMEM((3, 6, 8, W, C), BF), SEMS((8,))]
     return call(
-        half_kernel, "forward_half", 4 * 512 * ROWS * HALF, (shape, shape, weight), scratch,
-        flags, *field, part, more_a, more_b,
+        half_kernel, "forward_half", 4 * 512 * ROWS * HALF, (shape, shape), scratch,
+        [SMEM] + [VMEM] * 3 + [ANY] * 3, flags, *field, *weight,
     )
 
 
 def local_terms(flags, pre, own, others, gain, field):
     shape = jax.ShapeDtypeStruct((ROWS // 2, CH), BF)
-    scratch = [pltpu.VMEM((3, 6, 8, W, CH), BF)]
+    scratch = [pltpu.VMEM((3, 6, 8, W, CH), BF)] + [pltpu.VMEM((512, HALF), F32)] * 3 + [SEMS((3,))]
     return call(
         terms_kernel, "local_terms", 4 * 512 * ROWS * HALF, shape, scratch,
-        flags, pre, own, others, gain, *field,
+        [SMEM] + [ANY] * 3 + [VMEM] * 4, flags, pre, own, others, gain, *field,
     )
 
 
 def forward_all(flags, field, own, other):
     shape = jax.ShapeDtypeStruct((768, C), F32)
-    scratch = [pltpu.VMEM((768, C), F32), pltpu.VMEM((3, 8, 8, W, C), BF)]
+    scratch = [
+        pltpu.VMEM((768, C), F32), pltpu.VMEM((3, 8, 8, W, C), BF), WEIGHT, WEIGHT, SEMS((2, 8))
+    ]
     return call(
-        pre_kernel, "forward_all", 2 * 768 * ROWS * C, shape, scratch, flags, *field, own, other
-    )
-
-
-def backward(flags, field, gain, pre, w1_own, w1_other, w2_own, w2_other):
+        pre_kernel, "forward_all", 2 * 768 * ROWS * C, shape, scratch,
+        [SMEM] + [VMEM] * 3 + [ANY] * 5, flags, *field, *own, *other,
+    )
+
+
+def middle(flags, field, gain, pre, own, other):
+    shape = jax.ShapeDtypeStruct((6, 4, W, C), BF)
+    scratch = [
+        pltpu.VMEM((768, C), F32), pltpu.VMEM((768, C), F32), pltpu.VMEM((3, 8, 8, W, C), BF),
+        WEIGHT, WEIGHT, SEMS((2, 8)), SEMS((1,)),
+    ]
+    return call(
+        middle_kernel, "middle", 2 * 768 * ROWS * C, shape, scratch,
+        [SMEM] + [VMEM] * 4 + [ANY] * 7, flags, *field, gain, pre, *own, *other,
+    )
+
+
+def last(flags, grad, own, other):
     shape = jax.ShapeDtypeStruct((4, 2, W, C), BF)
     scratch = [
-        pltpu.VMEM((3, 6, 4, W, C), BF),
-        pltpu.VMEM((768, C), F32),
-        pltpu.VMEM((3, 8, 8, W, C), BF),
-        pltpu.VMEM((ROWS, HALF), BF),
-        pltpu.VMEM((ROWS, HALF), BF),
+        pltpu.VMEM((3, 6, 4, W, C), BF), pltpu.VMEM((256, C), F32), WEIGHT, WEIGHT, SEMS((2, 8))
     ]
     return call(
-        backward_kernel, "backward", 2 * 1024 * ROWS * C, shape, scratch,
-        flags, *field, gain, pre, w1_own, w1_other, *w2_own, *w2_other,
+        last_kernel, "last", 2 * 256 * ROWS * C, shape, scratch,
+        [SMEM, VMEM] + [ANY] * 5, flags, grad, *own, *other,
     )
 
 
@@ -290,43 +398,52 @@
     )
     half1 = jnp.dot(first_weight, pick.astype(BF), preferred_element_type=F32).astype(BF)
     half2 = lax.dynamic_slice_in_dim(second_weight, core * HALF, HALF, axis=1)
-    gain_pairs = gain.reshape(HALF, 2)
-    gain_half = jnp.where(core == 0, gain_pairs[:, 0], gain_pairs[:, 1]).reshape(1, HALF)
-    gain_all = jnp.concatenate([gain_pairs[:, 0], gain_pairs[:, 1]]).reshape(1, C)
-
-    block = spread(jnp.concatenate([half1, half2]), "tm", Y_GROUPS)
-    w1_part = spread(block[:, :108].reshape(864, HALF), "tm", X_GROUPS)
-    activations, cotangent, _ = lax.optimization_barrier((activations, cotangent, half1))
+
+    halves = jnp.concatenate([half1, half2])
+    halves = jnp.broadcast_to(halves[None], (8,) + halves.shape)
+    block = lax.all_to_all(halves, "tm", 0, 0, axis_index_groups=Y_GROUPS, tiled=True)
+    w1_block, w2_block = unpack(block)
+    w1_part = lax.all_to_all(w1_block, "tm", 0, 0, axis_index_groups=X_GROUPS, tiled=True)
+    activations, cotangent, _ = lax.optimization_barrier((activations, cotangent, halves))
 
     nexts = shift(jnp.concatenate([activations[:2], cotangent], axis=0), "tm", -1)
     prevs = shift(activations[2:], "tm", 1)
+    gains = order_gains(flags, gain)
+    nexts, prevs, gains = lax.optimization_barrier((nexts, prevs, gains))
+    gain_half, gain_all = gains
     mid = jnp.concatenate([prevs, activations, nexts[:2], cotangent, nexts[2:]], axis=0)
     edge = beyond_chip(mid)
     next_row = jnp.where(core == 0, edge[:, 1:], edge[:, :1])
-    field = (mid, edge, swap_cores(jnp.concatenate([mid, next_row], axis=1)))
-
-    w1_more = from_z(w1_part[:2], 1), from_z(w1_part[2:], -1)
-    w2_part = spread(after(block[:, 108:].reshape(864, HALF), w1_part), "tm", X_GROUPS)
-    w1_more, w2_part = lax.optimization_barrier((w1_more, w2_part))
-
-    pre_half, squares, w1_own = forward_half(flags, field, w1_part, *w1_more)
+    other = swap_cores(jnp.concatenate([mid, next_row], axis=1))
+    field = (mid, edge, other)
+
+    first, second = split(w1_part)
+    w1_more = [from_z(first, 1), from_z(second, -1)]
+    w1_far = [swap_cores(w1_part)]
+    w2_part = lax.all_to_all(
+        after(w2_block, w1_more[0]), "tm", 0, 0, axis_index_groups=X_GROUPS, tiled=True
+    )
+
+    w1_own = [w1_part] + w1_more
+    pre_half, squares = forward_half(flags, field, w1_own)
     squares_other = swap_cores(squares)
+    squares_other, w2_part = lax.optimization_barrier((squares_other, w2_part))
     terms = local_terms(flags, pre_half, squares, squares_other, gain_half, field)
 
     total = lax.all_to_all(
         terms.reshape(4, 864, CH), "tm", 0, 0, axis_index_groups=X_GROUPS, tiled=True
     )
+    w1_far.append(swap_cores(after(jnp.concatenate(w1_more), terms)))
     w2_part = after(w2_part, terms)
     w2_own = [w2_part, from_z(w2_part[:2], 1), from_z(w2_part[2:], -1)]
-    w1_other = swap_cores(after(w1_own, terms))
-    pre = forward_all(flags, field, w1_own, w1_other)
+    pre = forward_all(flags, field, w1_own, w1_far)
     total, pre = lax.optimization_barrier((total, pre))
-    w2_other = [swap_cores(part) for part in w2_own]
-    input_grad = backward(flags, field, gain_all, pre, w1_own, w1_other, w2_own, w2_other)
-
-    total = total.astype(F32).sum(0).astype(BF).reshape(16, 54, CH)
-    total = lax.all_to_all(total, "tm", 0, 0, axis_index_groups=YZ_GROUPS, tiled=True)
+    w2_far = [swap_cores(part) for part in w2_own]
+    pre_grad = middle(flags, field, gain_all, pre, w2_own, w2_far)
+
+    total = lax.all_to_all(sum_terms(total), "tm", 0, 0, axis_index_groups=YZ_GROUPS, tiled=True)
     total = spread(total.astype(F32).sum(0), "rows", ROW_GROUPS)
+    input_grad = last(flags, pre_grad, w1_own, w1_far)
     total, input_grad = lax.optimization_barrier((total, input_grad))
     weight_grad = total.reshape(4, 2, 54, CH).sum(0).transpose(1, 0, 2).reshape(108, CH)
     return (input_grad, weight_grad)

time: 150 us -> 161 us (1.073)
  Pallas kernels: 23.9 us -> 35.1 us
  waiting for transfers between devices: 24.5 us -> 21.9 us
  other arithmetic: 4.75 us -> 2.15 us
  local copies, waits for them, and re-layouts: 13.4 us -> 15.4 us
  starting transfers between devices: 81.4 us -> 83.2 us
    all_to_all x1 -> x4, starting transfers between devices: 3.53 us -> 24.3 us  [the longest x1 7.78 us: on_device(): lax.all_to_all(halves, 'tm', 0, 0, axis_index_groups=Y_GROUPS, tiled=True)]
    all_to_all x4 -> x1, starting transfers between devices: 22.6 us -> 8.74 us  [spread(): lax.all_to_all(operand, axis, 0, 0, axis_index_groups=groups, tiled=True)]
    all_to_all x4 -> x1, waiting for transfers between devices: 11.8 us -> 0.01 us  [spread(): lax.all_to_all(operand, axis, 0, 0, axis_index_groups=groups, tiled=True)]
    pallas_call x4 -> x9, Pallas kernels: 23.9 us -> 35.1 us  [call(): pl.pallas_call(kernel, out_shape=out_shape, in_specs=specs, out_specs=jax...]
    unnamed x20 -> x56, local copies, waits for them, and re-layouts: 4.47 us -> 12 us
    ppermute x2, waiting for transfers between devices: 0.01 us -> 6.14 us  [shift(): return lax.ppermute(block, axis, route)]
    ppermute x1, waiting for transfers between devices: 0.3 us -> 4.81 us  [beyond_chip(): return lax.ppermute(block, 'rows', route)]
    ppermute x6 -> x7, starting transfers between devices: 20.5 us -> 17.1 us  [swap_cores(): lax.ppermute(block, 'rows', [(i, i ^ 1) for i in range(lax.axis_size('row...]
  transfers between devices with their start and end apart: 19 -> 20, of which waited for: 7 -> 6; matrix products, arithmetic and copies ran while one was open for 8% -> 3% of each run, Pallas kernels for 11% -> 22%
where the time goes in v4:
time: 161 us; the launch traced here: 159 us
  starting transfers between devices  83.2 us (52%)
  Pallas kernels  35.1 us (22%)
  waiting for transfers between devices  21.9 us (14%)
  local copies, waits for them, and re-layouts  15.4 us (10%)
  other arithmetic  2.15 us (1%)
    pallas_call x9, Pallas kernels, call(): pl.pallas_call(kernel, out_shape=out_shape, in_specs=specs, out_specs=jax...  35.1 us
    ppermute x7, starting transfers between devices, swap_cores(): lax.ppermute(block, 'rows', [(i, i ^ 1) for i in range(lax.axis_size('row...  17.1 us
    ppermute x4, starting transfers between devices, from_z(): return lax.ppermute(block, ('tm', 'rows'), route)  14.5 us
    unnamed x56, local copies, waits for them, and re-layouts  12 us
    ppermute x1, starting transfers between devices, beyond_chip(): return lax.ppermute(block, 'rows', route)  8.86 us
    all_to_all x1, starting transfers between devices, spread(): lax.all_to_all(operand, axis, 0, 0, axis_index_groups=groups, tiled=True)  8.74 us
    all_to_all x1, starting transfers between devices, on_device(): lax.all_to_all(halves, 'tm', 0, 0, axis_index_groups=Y_GROUPS, tiled=True)  7.78 us
    ppermute x4, waiting for transfers between devices, from_z(): return lax.ppermute(block, ('tm', 'rows'), route)  6.46 us
  transfers between devices with their start and end apart: 20, of which 6 were waited for; matrix products, arithmetic and copies ran while one was open for 3% of the time, Pallas kernels for 22%

profile of v4, /device:TPU:1, one launch (start us, length us, event | category | flops | bytes accessed | tf_op | source)
XLA Modules:
  0.0 159.1 jit_solution(3117242437055460728)
XLA Ops:
  0.6 0.0 copy-start
  0.7 0.8 copy-done
  1.5 0.0 copy-done.25
  1.5 0.1 fusion
  1.7 0.8 broadcast_in_dim.4
  2.5 7.8 %all-to-all-start = ((bf16[8,216,128]{2,1,0:T(8,128)(2,1)}), bf16[8,216,128]{2,1,0:T(8,128)(2,1)S(1)}, u32[]{:S(2)}, u32[]{:S(2)}) async-start(bf16[8,216,128]{2,1,0:T(8,128)(2,1)} %broadcast_in_dim.4), calls=%async_computation | async-start | bytes 884736 | tf_op jit(solution)/shard_map/all_to_all | solution.py:404
  10.3 0.0 copy-start.23
  10.3 0.9 copy-done.23
  11.2 1.3 collective-permute-start
  12.5 4.0 %collective-permute-start.1 = (bf16[2,2,32,256]{3,2,1,0:T(8,128)(2,1)S(1)}, bf16[2,2,32,256]{3,2,1,0:T(8,128)(2,1)S(1)}, u32[]{:S(2)}, u32[]{:S(2)}) collective-permute-start(bf16[2,2,32,256]{3,2,1,0:T(8,128)(2,1)S(1)} %get-tuple-element.50), channel_id=1, source_target_pairs={{0,8},{8,16},{16,24},{24,32},{32,40},{40,48},{48,56},{56,64},{64,7... | collective-permute-start | bytes 196616 | tf_op jit(solution)/shard_map/ppermute | solution.py:40
  16.5 0.1 stack.19.flags
  16.6 0.7 copy-done.18
  17.3 0.7 gains.1
  18.0 2.6 %collective-permute-done.1 = bf16[2,2,32,256]{3,2,1,0:T(8,128)(2,1)S(1)} collective-permute-done((bf16[2,2,32,256]{3,2,1,0:T(8,128)(2,1)S(1)}, bf16[2,2,32,256]{3,2,1,0:T(8,128)(2,1)S(1)}, u32[]{:S(2)}, u32[]{:S(2)}) %collective-permute-start.1) | collective-permute-done | bytes 65568 | tf_op jit(solution)/shard_map/ppermute | solution.py:40
  20.6 3.5 %collective-permute-done = bf16[6,2,32,256]{3,2,1,0:T(8,128)(2,1)S(1)} collective-permute-done((bf16[6,2,32,256]{3,2,1,0:T(8,128)(2,1)S(1)}, bf16[6,2,32,256]{3,2,1,0:T(8,128)(2,1)S(1)}, u32[]{:S(2)}, u32[]{:S(2)}) %collective-permute-start) | collective-permute-done | bytes 196640 | tf_op jit(solution)/shard_map/ppermute | solution.py:40
  24.2 8.9 %collective-permute-start.2 = (bf16[16,2,32,256]{3,2,1,0:T(8,128)(2,1)S(1)}, bf16[16,2,32,256]{3,2,1,0:T(8,128)(2,1)S(1)}, u32[]{:S(2)}, u32[]{:S(2)}) collective-permute-start(bf16[16,2,32,256]{3,2,1,0:T(8,128)(2,1)S(1)} %slice_dynamic-update-slice_fusion.mid), channel_id=1, source_target_pairs={{1,2},{3,4},{5,6},{2,1},{4,3},{6,5},{9,10},{11,12},{13,14},{10,9},... | collective-permute-start | bytes 1572872 | tf_op jit(solution)/shard_map/ppermute | solution.py:60
  33.1 1.4 unpack.1
  34.5 0.9 copy-done.4
  35.4 5.6 %all-to-all-start.1 = ((bf16[4,864,128]{2,1,0:T(8,128)(2,1)}), bf16[4,864,128]{2,1,0:T(8,128)(2,1)S(1)}, u32[]{:S(2)}, u32[]{:S(2)}) async-start(bf16[4,864,128]{2,1,0:T(8,128)(2,1)} %get-tuple-element.31), calls=%async_computation.1 | async-start | bytes 1769472 | tf_op jit(solution)/shard_map/all_to_all | solution.py:406
  41.0 4.8 %collective-permute-done.2.edge = bf16[16,2,32,256]{3,2,1,0:T(8,128)(2,1)S(1)} collective-permute-done((bf16[16,2,32,256]{3,2,1,0:T(8,128)(2,1)S(1)}, bf16[16,2,32,256]{3,2,1,0:T(8,128)(2,1)S(1)}, u32[]{:S(2)}, u32[]{:S(2)}) %collective-permute-start.2) | collective-permute-done | bytes 524320 | tf_op jit(solution)/shard_map/ppermute | solution.py:60
  45.9 1.0 pad_maximum_fusion.1
  46.9 1.9 %collective-permute-start.3 = (bf16[16,3,32,256]{3,2,1,0:T(8,128)(2,1)}, bf16[16,3,32,256]{3,2,1,0:T(8,128)(2,1)}, u32[]{:S(2)}, u32[]{:S(2)}) collective-permute-start(bf16[16,3,32,256]{3,2,1,0:T(8,128)(2,1)} %pad_maximum_fusion.1), channel_id=1, source_target_pairs={{0,1},{1,0},{2,3},{3,2},{4,5},{5,4},{6,7},{7,6},{8,9},{9,8},{10,11... | collective-permute-start | bytes 2359304 | tf_op jit(solution)/shard_map/ppermute | solution.py:34
  48.8 1.6 all-to-all-done.1.part
  50.4 1.3 split.1
  51.7 6.1 %collective-permute-start.4 = (bf16[2,864,128]{2,1,0:T(8,128)(2,1)S(1)}, bf16[2,864,128]{2,1,0:T(8,128)(2,1)S(1)}, u32[]{:S(2)}, u32[]{:S(2)}) collective-permute-start(bf16[2,864,128]{2,1,0:T(8,128)(2,1)S(1)} %get-tuple-element.32), channel_id=1, source_target_pairs={{64,0},{65,1},{2,64},{3,65},{66,2},{67,3},{4,66},{5,67},{68,4},{69... | collective-permute-start | bytes 1327112 | tf_op jit(solution)/shard_map/ppermute | solution.py:54
  57.7 1.9 %collective-permute-start.5 = (bf16[2,864,128]{2,1,0:T(8,128)(2,1)}, bf16[2,864,128]{2,1,0:T(8,128)(2,1)S(1)}, u32[]{:S(2)}, u32[]{:S(2)}) collective-permute-start(bf16[2,864,128]{2,1,0:T(8,128)(2,1)} %get-tuple-element.33), channel_id=1, source_target_pairs={{70,0},{71,1},{0,64},{1,65},{64,2},{65,3},{2,66},{3,67},{66,4},{67... | collective-permute-start | bytes 1327112 | tf_op jit(solution)/shard_map/ppermute | solution.py:54
  59.7 6.5 %collective-permute-done.4.more_a = bf16[2,864,128]{2,1,0:T(8,128)(2,1)S(1)} collective-permute-done((bf16[2,864,128]{2,1,0:T(8,128)(2,1)S(1)}, bf16[2,864,128]{2,1,0:T(8,128)(2,1)S(1)}, u32[]{:S(2)}, u32[]{:S(2)}) %collective-permute-start.4) | collective-permute-done | bytes 442400 | tf_op jit(solution)/shard_map/ppermute | solution.py:54
  66.1 5.6 %all-to-all-start.2 = ((bf16[4,864,128]{2,1,0:T(8,128)(2,1)}), bf16[4,864,128]{2,1,0:T(8,128)(2,1)S(1)}, u32[]{:S(2)}, u32[]{:S(2)}) async-start(bf16[4,864,128]{2,1,0:T(8,128)(2,1)} %copy-done.4), calls=%async_computation.2 | async-start | bytes 1769472 | tf_op jit(solution)/shard_map/all_to_all | solution.py:423
  71.7 0.0 collective-permute-done.3.other.others
  71.7 0.0 collective-permute-done.5.more_b
  71.8 1.0 copy-done.10
  72.8 6.1 %forward_half.1 = (f32[512,128]{1,0:T(8,128)S(1)}, f32[512,128]{1,0:T(8,128)S(1)}) custom-call(s32[6]{0:T(128)S(1)} %stack.19.flags, bf16[16,2,32,256]{3,2,1,0:T(8,128)(2,1)S(1)} %slice_dynamic-update-slice_fusion.mid, bf16[16,2,32,256]{3,2,1,0:T(8,128)(2,1)S(1)} %copy-done.10, bf16[16,3,32,256]{3,2,1,0:T(8,128)(2,1)} %collective-permute-done.3.other.others, ...), custom_call_target="tpu_custom_call" | custom-call | flops 1811939328 | bytes 1048576 | tf_op jit(solution)/shard_map/forward_half/pallas_call | solution.py:302
  78.9 3.8 %collective-permute-start.6 = (f32[512,128]{1,0:T(8,128)S(1)}, f32[512,128]{1,0:T(8,128)S(1)}, u32[]{:S(2)}, u32[]{:S(2)}) collective-permute-start(f32[512,128]{1,0:T(8,128)S(1)} %get-tuple-element.35.own_in), channel_id=1, source_target_pairs={{0,1},{1,0},{2,3},{3,2},{4,5},{5,4},{6,7},{7,6},{8,9},{9,8},{10,11... | collective-permute-start | bytes 786440 | tf_op jit(solution)/shard_map/ppermute | solution.py:34
  82.7 1.9 %collective-permute-start.7 = (bf16[4,864,128]{2,1,0:T(8,128)(2,1)S(1)}, bf16[4,864,128]{2,1,0:T(8,128)(2,1)}, u32[]{:S(2)}, u32[]{:S(2)}) collective-permute-start(bf16[4,864,128]{2,1,0:T(8,128)(2,1)S(1)} %all-to-all-done.1.part), channel_id=1, source_target_pairs={{0,1},{1,0},{2,3},{3,2},{4,5},{5,4},{6,7},{7,6},{8,9},{9,8},{10,11... | collective-permute-start | bytes 2654216 | tf_op jit(solution)/shard_map/ppermute | solution.py:34
  84.7 1.0 pad_maximum_fusion
  85.7 0.0 collective-permute-done.6.others_in
  85.7 0.7 copy-done.16
  86.4 1.0 copy-done.11
  87.5 0.9 copy-done.15
  88.4 0.9 copy-done.17
  89.4 0.9 copy-done.22
  90.3 2.2 %local_terms.1 = bf16[3456,128]{1,0:T(8,128)(2,1)S(1)} custom-call(s32[6]{0:T(128)S(1)} %stack.19.flags, f32[512,128]{1,0:T(8,128)S(1)} %copy-done.22, f32[512,128]{1,0:T(8,128)S(1)} %copy-done.15, f32[512,128]{1,0:T(8,128)S(1)} %copy-done.17, f32[1,128]{1,0:T(1,128)S(1)} %get-tuple-element.39.gain, ...), custom_call_target="tpu_custom_call" | custom-call | flops 1811939328 | bytes 1048576 | tf_op jit(solution)/shard_map/local_terms/pallas_call | solution.py:302
  92.5 0.9 copy-done.5
  93.4 2.4 %collective-permute-start.8 = (bf16[4,864,128]{2,1,0:T(8,128)(2,1)}, bf16[4,864,128]{2,1,0:T(8,128)(2,1)}, u32[]{:S(2)}, u32[]{:S(2)}) collective-permute-start(bf16[4,864,128]{2,1,0:T(8,128)(2,1)} %pad_maximum_fusion), channel_id=1, source_target_pairs={{0,1},{1,0},{2,3},{3,2},{4,5},{5,4},{6,7},{7,6},{8,9},{9,8},{10,11... | collective-permute-start | bytes 2654216 | tf_op jit(solution)/shard_map/ppermute | solution.py:34
  95.8 4.5 %all-to-all-start.3 = ((bf16[4,864,128]{2,1,0:T(8,128)(2,1)}), bf16[4,864,128]{2,1,0:T(8,128)(2,1)S(1)}, u32[]{:S(2)}, u32[]{:S(2)}) async-start(bf16[4,864,128]{2,1,0:T(8,128)(2,1)} %bitcast.11), calls=%async_computation.3 | async-start | bytes 1769472 | tf_op jit(solution)/shard_map/all_to_all | solution.py:433
  100.3 2.3 %collective-permute-start.11 = (bf16[4,864,128]{2,1,0:T(8,128)(2,1)S(1)}, bf16[4,864,128]{2,1,0:T(8,128)(2,1)}, u32[]{:S(2)}, u32[]{:S(2)}) collective-permute-start(bf16[4,864,128]{2,1,0:T(8,128)(2,1)S(1)} %all-to-all-done.2.part), channel_id=1, source_target_pairs={{0,1},{1,0},{2,3},{3,2},{4,5},{5,4},{6,7},{7,6},{8,9},{9,8},{10,11... | collective-permute-start | bytes 2654216 | tf_op jit(solution)/shard_map/ppermute | solution.py:34
  102.6 1.0 fusion.2
  103.7 4.6 %collective-permute-start.9 = (bf16[2,864,128]{2,1,0:T(8,128)(2,1)}, bf16[2,864,128]{2,1,0:T(8,128)(2,1)}, u32[]{:S(2)}, u32[]{:S(2)}) collective-permute-start(bf16[2,864,128]{2,1,0:T(8,128)(2,1)} %get-tuple-element.49), channel_id=1, source_target_pairs={{64,0},{65,1},{2,64},{3,65},{66,2},{67,3},{4,66},{5,67},{68,4},{69... | collective-permute-start | bytes 1327112 | tf_op jit(solution)/shard_map/ppermute | solution.py:54
  108.3 1.9 %collective-permute-start.10 = (bf16[2,864,128]{2,1,0:T(8,128)(2,1)}, bf16[2,864,128]{2,1,0:T(8,128)(2,1)}, u32[]{:S(2)}, u32[]{:S(2)}) collective-permute-start(bf16[2,864,128]{2,1,0:T(8,128)(2,1)} %get-tuple-element.48), channel_id=1, source_target_pairs={{70,0},{71,1},{0,64},{1,65},{64,2},{65,3},{2,66},{3,67},{66,4},{67... | collective-permute-start | bytes 1327112 | tf_op jit(solution)/shard_map/ppermute | solution.py:54
  110.2 0.0 collective-permute-done.7.far_part
  110.3 8.2 %forward_all.1.pre_in = f32[768,256]{1,0:T(8,128)S(1)} custom-call(s32[6]{0:T(128)S(1)} %stack.19.flags, bf16[16,2,32,256]{3,2,1,0:T(8,128)(2,1)S(1)} %copy-done.7, bf16[16,2,32,256]{3,2,1,0:T(8,128)(2,1)S(1)} %copy-done.12, bf16[16,3,32,256]{3,2,1,0:T(8,128)(2,1)} %collective-permute-done.3.other.others, bf16[4,864,128]{2,1,0:T(8,128)(2,1)S(1)} %all-to-all-done.1.part, ...), custom_call_target="tpu_custom_call" | custom-call | flops 2717908992 | bytes 1048576 | tf_op jit(solution)/shard_map/forward_all/pallas_call | solution.py:302
  118.5 0.9 copy-done.19
  119.3 1.0 sum_terms.1
  120.4 5.3 %all-to-all-start.4 = ((bf16[16,54,128]{2,1,0:T(8,128)(2,1)}), bf16[16,54,128]{2,1,0:T(8,128)(2,1)S(1)}, u32[]{:S(2)}, u32[]{:S(2)}) async-start(bf16[16,54,128]{2,1,0:T(8,128)(2,1)} %sum_terms.1), calls=%async_computation.4 | async-start | bytes 458752 | tf_op jit(solution)/shard_map/all_to_all | solution.py:444
  125.7 2.8 %collective-permute-start.12 = (bf16[2,864,128]{2,1,0:T(8,128)(2,1)}, bf16[2,864,128]{2,1,0:T(8,128)(2,1)}, u32[]{:S(2)}, u32[]{:S(2)}) collective-permute-start(bf16[2,864,128]{2,1,0:T(8,128)(2,1)} %collective-permute-done.9.more_a), channel_id=1, source_target_pairs={{0,1},{1,0},{2,3},{3,2},{4,5},{5,4},{6,7},{7,6},{8,9},{9,8},{10,11... | collective-permute-start | bytes 1327112 | tf_op jit(solution)/shard_map/ppermute | solution.py:34
  128.5 0.0 collective-permute-done.10.more_b
  128.6 1.9 %collective-permute-start.13 = (bf16[2,864,128]{2,1,0:T(8,128)(2,1)}, bf16[2,864,128]{2,1,0:T(8,128)(2,1)}, u32[]{:S(2)}, u32[]{:S(2)}) collective-permute-start(bf16[2,864,128]{2,1,0:T(8,128)(2,1)} %collective-permute-done.10.more_b), channel_id=1, source_target_pairs={{0,1},{1,0},{2,3},{3,2},{4,5},{5,4},{6,7},{7,6},{8,9},{9,8},{10,11... | collective-permute-start | bytes 1327112 | tf_op jit(solution)/shard_map/ppermute | solution.py:34
  130.5 2.9 %all-to-all-done.4 = bf16[16,54,128]{2,1,0:T(8,128)(2,1)S(1)} async-done(((bf16[16,54,128]{2,1,0:T(8,128)(2,1)}), bf16[16,54,128]{2,1,0:T(8,128)(2,1)S(1)}, u32[]{:S(2)}, u32[]{:S(2)}) %all-to-all-start.4) | async-done | bytes 221216 | tf_op jit(solution)/shard_map/all_to_all | solution.py:444
  133.5 0.7 broadcast_in_dim.5
  134.2 8.7 %all-to-all-start.5 = ((f32[8,54,128]{2,1,0:T(8,128)}), f32[8,54,128]{2,1,0:T(8,128)S(1)}, u32[]{:S(2)}, u32[]{:S(2)}) async-start(f32[8,54,128]{2,1,0:T(8,128)} %broadcast_in_dim.5), calls=%async_computation.5 | async-start | bytes 458752 | tf_op jit(solution)/shard_map/all_to_all | solution.py:30
  143.0 1.2 copy-done.20
  144.1 7.9 %middle.1.grad = bf16[6,4,32,256]{3,2,1,0:T(8,128)(2,1)S(1)} custom-call(s32[6]{0:T(128)S(1)} %stack.19.flags, bf16[16,2,32,256]{3,2,1,0:T(8,128)(2,1)S(1)} %copy-done.8, bf16[16,2,32,256]{3,2,1,0:T(8,128)(2,1)S(1)} %copy-done.13, bf16[16,3,32,256]{3,2,1,0:T(8,128)(2,1)} %collective-permute-done.3.other.others, f32[1,256]{1,0:T(1,128)S(1)} %get-tuple-element.42.gain, ...), custom_call_target="tpu_custom_call" | custom-call | flops 2717908992 | bytes 1048576 | tf_op jit(solution)/shard_map/middle/pallas_call | solution.py:302
  152.1 6.3 %last.1 = bf16[4,2,32,256]{3,2,1,0:T(8,128)(2,1)} custom-call(s32[6]{0:T(128)S(1)} %stack.19.flags, bf16[6,4,32,256]{3,2,1,0:T(8,128)(2,1)S(1)} %middle.1.grad, bf16[4,864,128]{2,1,0:T(8,128)(2,1)S(1)} %all-to-all-done.1.part, bf16[2,864,128]{2,1,0:T(8,128)(2,1)S(1)} %collective-permute-done.4.more_a, bf16[2,864,128]{2,1,0:T(8,128)(2,1)S(1)} %copy-done.3, ...), custom_call_target="tpu_custom_call" | custom-call | flops 905969664 | bytes 1048576 | tf_op jit(solution)/shard_map/last/pallas_call | solution.py:302
  158.5 0.7 reshape.21
  (59 shorter events, 0.3 us)
Async XLA Ops:
  0.6 0.8 copy-start
  0.6 0.8 copy-start.25
  2.5 7.8 %copy-start.24 = (bf16[4,2,32,256]{3,2,1,0:T(8,128)(2,1)S(1)}, bf16[4,2,32,256]{3,2,1,0:T(8,128)(2,1)}, u32[]{:S(2)}) copy-start(bf16[4,2,32,256]{3,2,1,0:T(8,128)(2,1)} %param.5) | copy-start | bytes 393220
  2.5 30.6 %all-to-all-start = ((bf16[8,216,128]{2,1,0:T(8,128)(2,1)}), bf16[8,216,128]{2,1,0:T(8,128)(2,1)S(1)}, u32[]{:S(2)}, u32[]{:S(2)}) async-start(bf16[8,216,128]{2,1,0:T(8,128)(2,1)} %broadcast_in_dim.4), calls=%async_computation | async-start | bytes 884736 | tf_op jit(solution)/shard_map/all_to_all | solution.py:404
  10.3 0.9 copy-start.23
  11.2 12.9 %collective-permute-start = (bf16[6,2,32,256]{3,2,1,0:T(8,128)(2,1)S(1)}, bf16[6,2,32,256]{3,2,1,0:T(8,128)(2,1)S(1)}, u32[]{:S(2)}, u32[]{:S(2)}) collective-permute-start(bf16[6,2,32,256]{3,2,1,0:T(8,128)(2,1)S(1)} %pad_maximum_fusion.2), channel_id=1, source_target_pairs={{8,0},{16,8},{24,16},{32,24},{40,32},{48,40},{56,48},{64,56},{72,6... | collective-permute-start | bytes 589832 | tf_op jit(solution)/shard_map/ppermute | solution.py:40
  12.5 8.1 %collective-permute-start.1 = (bf16[2,2,32,256]{3,2,1,0:T(8,128)(2,1)S(1)}, bf16[2,2,32,256]{3,2,1,0:T(8,128)(2,1)S(1)}, u32[]{:S(2)}, u32[]{:S(2)}) collective-permute-start(bf16[2,2,32,256]{3,2,1,0:T(8,128)(2,1)S(1)} %get-tuple-element.50), channel_id=1, source_target_pairs={{0,8},{8,16},{16,24},{24,32},{32,40},{40,48},{48,56},{56,64},{64,7... | collective-permute-start | bytes 196616 | tf_op jit(solution)/shard_map/ppermute | solution.py:40
  16.6 0.7 copy-start.18
  24.2 62.2 %copy-start.6 = (bf16[16,2,32,256]{3,2,1,0:T(8,128)(2,1)}, bf16[16,2,32,256]{3,2,1,0:T(8,128)(2,1)S(1)}, u32[]{:S(2)}) copy-start(bf16[16,2,32,256]{3,2,1,0:T(8,128)(2,1)S(1)} %slice_dynamic-update-slice_fusion.mid) | copy-start | bytes 1572868
  24.2 21.6 %collective-permute-start.2 = (bf16[16,2,32,256]{3,2,1,0:T(8,128)(2,1)S(1)}, bf16[16,2,32,256]{3,2,1,0:T(8,128)(2,1)S(1)}, u32[]{:S(2)}, u32[]{:S(2)}) collective-permute-start(bf16[16,2,32,256]{3,2,1,0:T(8,128)(2,1)S(1)} %slice_dynamic-update-slice_fusion.mid), channel_id=1, source_target_pairs={{1,2},{3,4},{5,6},{2,1},{4,3},{6,5},{9,10},{11,12},{13,14},{10,9},... | collective-permute-start | bytes 1572872 | tf_op jit(solution)/shard_map/ppermute | solution.py:60
  34.4 0.9 copy-start.4
  35.4 15.0 %all-to-all-start.1 = ((bf16[4,864,128]{2,1,0:T(8,128)(2,1)}), bf16[4,864,128]{2,1,0:T(8,128)(2,1)S(1)}, u32[]{:S(2)}, u32[]{:S(2)}) async-start(bf16[4,864,128]{2,1,0:T(8,128)(2,1)} %get-tuple-element.31), calls=%async_computation.1 | async-start | bytes 1769472 | tf_op jit(solution)/shard_map/all_to_all | solution.py:406
  45.8 1.0 copy-start.9
  46.9 24.9 %collective-permute-start.3 = (bf16[16,3,32,256]{3,2,1,0:T(8,128)(2,1)}, bf16[16,3,32,256]{3,2,1,0:T(8,128)(2,1)}, u32[]{:S(2)}, u32[]{:S(2)}) collective-permute-start(bf16[16,3,32,256]{3,2,1,0:T(8,128)(2,1)} %pad_maximum_fusion.1), channel_id=1, source_target_pairs={{0,1},{1,0},{2,3},{3,2},{4,5},{5,4},{6,7},{7,6},{8,9},{9,8},{10,11... | collective-permute-start | bytes 2359304 | tf_op jit(solution)/shard_map/ppermute | solution.py:34
  51.7 14.4 %collective-permute-start.4 = (bf16[2,864,128]{2,1,0:T(8,128)(2,1)S(1)}, bf16[2,864,128]{2,1,0:T(8,128)(2,1)S(1)}, u32[]{:S(2)}, u32[]{:S(2)}) collective-permute-start(bf16[2,864,128]{2,1,0:T(8,128)(2,1)S(1)} %get-tuple-element.32), channel_id=1, source_target_pairs={{64,0},{65,1},{2,64},{3,65},{66,2},{67,3},{4,66},{5,67},{68,4},{69... | collective-permute-start | bytes 1327112 | tf_op jit(solution)/shard_map/ppermute | solution.py:54
  57.7 14.0 %collective-permute-start.5 = (bf16[2,864,128]{2,1,0:T(8,128)(2,1)}, bf16[2,864,128]{2,1,0:T(8,128)(2,1)S(1)}, u32[]{:S(2)}, u32[]{:S(2)}) collective-permute-start(bf16[2,864,128]{2,1,0:T(8,128)(2,1)} %get-tuple-element.33), channel_id=1, source_target_pairs={{70,0},{71,1},{0,64},{1,65},{64,2},{65,3},{2,66},{3,67},{66,4},{67... | collective-permute-start | bytes 1327112 | tf_op jit(solution)/shard_map/ppermute | solution.py:54
  66.1 20.3 %all-to-all-start.2 = ((bf16[4,864,128]{2,1,0:T(8,128)(2,1)}), bf16[4,864,128]{2,1,0:T(8,128)(2,1)S(1)}, u32[]{:S(2)}, u32[]{:S(2)}) async-start(bf16[4,864,128]{2,1,0:T(8,128)(2,1)} %copy-done.4), calls=%async_computation.2 | async-start | bytes 1769472 | tf_op jit(solution)/shard_map/all_to_all | solution.py:423
  71.7 1.0 copy-start.10
  72.8 11.9 %copy-start.1 = (bf16[2,864,128]{2,1,0:T(8,128)(2,1)}, bf16[2,864,128]{2,1,0:T(8,128)(2,1)S(1)}, u32[]{:S(2)}) copy-start(bf16[2,864,128]{2,1,0:T(8,128)(2,1)S(1)} %collective-permute-done.5.more_b) | copy-start | bytes 1327108
  78.9 6.8 %copy-start.14 = (f32[512,128]{1,0:T(8,128)}, f32[512,128]{1,0:T(8,128)S(1)}, u32[]{:S(2)}) copy-start(f32[512,128]{1,0:T(8,128)S(1)} %get-tuple-element.35.own_in) | copy-start | bytes 786436
  78.9 6.8 %copy-start.21 = (f32[512,128]{1,0:T(8,128)}, f32[512,128]{1,0:T(8,128)S(1)}, u32[]{:S(2)}) copy-start(f32[512,128]{1,0:T(8,128)S(1)} %get-tuple-element.34.pre_in) | copy-start | bytes 786436
  78.9 6.8 %collective-permute-start.6 = (f32[512,128]{1,0:T(8,128)S(1)}, f32[512,128]{1,0:T(8,128)S(1)}, u32[]{:S(2)}, u32[]{:S(2)}) collective-permute-start(f32[512,128]{1,0:T(8,128)S(1)} %get-tuple-element.35.own_in), channel_id=1, source_target_pairs={{0,1},{1,0},{2,3},{3,2},{4,5},{5,4},{6,7},{7,6},{8,9},{9,8},{10,11... | collective-permute-start | bytes 786440 | tf_op jit(solution)/shard_map/ppermute | solution.py:34
  82.7 27.5 %collective-permute-start.7 = (bf16[4,864,128]{2,1,0:T(8,128)(2,1)S(1)}, bf16[4,864,128]{2,1,0:T(8,128)(2,1)}, u32[]{:S(2)}, u32[]{:S(2)}) collective-permute-start(bf16[4,864,128]{2,1,0:T(8,128)(2,1)S(1)} %all-to-all-done.1.part), channel_id=1, source_target_pairs={{0,1},{1,0},{2,3},{3,2},{4,5},{5,4},{6,7},{7,6},{8,9},{9,8},{10,11... | collective-permute-start | bytes 2654216 | tf_op jit(solution)/shard_map/ppermute | solution.py:34
  85.7 0.7 copy-start.16
  86.4 1.0 copy-start.11
  87.5 0.9 copy-start.15
  88.4 0.9 copy-start.17
  89.4 0.9 copy-start.22
  92.5 0.9 copy-start.5
  93.4 16.8 %collective-permute-start.8 = (bf16[4,864,128]{2,1,0:T(8,128)(2,1)}, bf16[4,864,128]{2,1,0:T(8,128)(2,1)}, u32[]{:S(2)}, u32[]{:S(2)}) collective-permute-start(bf16[4,864,128]{2,1,0:T(8,128)(2,1)} %pad_maximum_fusion), channel_id=1, source_target_pairs={{0,1},{1,0},{2,3},{3,2},{4,5},{5,4},{6,7},{7,6},{8,9},{9,8},{10,11... | collective-permute-start | bytes 2654216 | tf_op jit(solution)/shard_map/ppermute | solution.py:34
  95.8 23.5 %all-to-all-start.3 = ((bf16[4,864,128]{2,1,0:T(8,128)(2,1)}), bf16[4,864,128]{2,1,0:T(8,128)(2,1)S(1)}, u32[]{:S(2)}, u32[]{:S(2)}) async-start(bf16[4,864,128]{2,1,0:T(8,128)(2,1)} %bitcast.11), calls=%async_computation.3 | async-start | bytes 1769472 | tf_op jit(solution)/shard_map/all_to_all | solution.py:433
  100.3 9.9 %copy-start.2 = (bf16[2,864,128]{2,1,0:T(8,128)(2,1)S(1)}, bf16[2,864,128]{2,1,0:T(8,128)(2,1)}, u32[]{:S(2)}) copy-start(bf16[2,864,128]{2,1,0:T(8,128)(2,1)} %copy-done.1) | copy-start | bytes 1327108
  100.3 9.9 %copy-start.7 = (bf16[16,2,32,256]{3,2,1,0:T(8,128)(2,1)S(1)}, bf16[16,2,32,256]{3,2,1,0:T(8,128)(2,1)}, u32[]{:S(2)}) copy-start(bf16[16,2,32,256]{3,2,1,0:T(8,128)(2,1)} %copy-done.6) | copy-start | bytes 1572868
  100.3 9.9 %copy-start.12 = (bf16[16,2,32,256]{3,2,1,0:T(8,128)(2,1)S(1)}, bf16[16,2,32,256]{3,2,1,0:T(8,128)(2,1)}, u32[]{:S(2)}) copy-start(bf16[16,2,32,256]{3,2,1,0:T(8,128)(2,1)} %copy-done.9) | copy-start | bytes 1572868
  100.3 42.6 %collective-permute-start.11 = (bf16[4,864,128]{2,1,0:T(8,128)(2,1)S(1)}, bf16[4,864,128]{2,1,0:T(8,128)(2,1)}, u32[]{:S(2)}, u32[]{:S(2)}) collective-permute-start(bf16[4,864,128]{2,1,0:T(8,128)(2,1)S(1)} %all-to-all-done.2.part), channel_id=1, source_target_pairs={{0,1},{1,0},{2,3},{3,2},{4,5},{5,4},{6,7},{7,6},{8,9},{9,8},{10,11... | collective-permute-start | bytes 2654216 | tf_op jit(solution)/shard_map/ppermute | solution.py:34
  103.7 22.0 %collective-permute-start.9 = (bf16[2,864,128]{2,1,0:T(8,128)(2,1)}, bf16[2,864,128]{2,1,0:T(8,128)(2,1)}, u32[]{:S(2)}, u32[]{:S(2)}) collective-permute-start(bf16[2,864,128]{2,1,0:T(8,128)(2,1)} %get-tuple-element.49), channel_id=1, source_target_pairs={{64,0},{65,1},{2,64},{3,65},{66,2},{67,3},{4,66},{5,67},{68,4},{69... | collective-permute-start | bytes 1327112 | tf_op jit(solution)/shard_map/ppermute | solution.py:54
  108.3 20.3 %collective-permute-start.10 = (bf16[2,864,128]{2,1,0:T(8,128)(2,1)}, bf16[2,864,128]{2,1,0:T(8,128)(2,1)}, u32[]{:S(2)}, u32[]{:S(2)}) collective-permute-start(bf16[2,864,128]{2,1,0:T(8,128)(2,1)} %get-tuple-element.48), channel_id=1, source_target_pairs={{70,0},{71,1},{0,64},{1,65},{64,2},{65,3},{2,66},{3,67},{66,4},{67... | collective-permute-start | bytes 1327112 | tf_op jit(solution)/shard_map/ppermute | solution.py:54
  118.4 0.9 copy-start.19
  120.4 22.6 %copy-start.13 = (bf16[16,2,32,256]{3,2,1,0:T(8,128)(2,1)S(1)}, bf16[16,2,32,256]{3,2,1,0:T(8,128)(2,1)}, u32[]{:S(2)}) copy-start(bf16[16,2,32,256]{3,2,1,0:T(8,128)(2,1)} %copy-done.9) | copy-start | bytes 1572868
  120.4 13.0 %all-to-all-start.4 = ((bf16[16,54,128]{2,1,0:T(8,128)(2,1)}), bf16[16,54,128]{2,1,0:T(8,128)(2,1)S(1)}, u32[]{:S(2)}, u32[]{:S(2)}) async-start(bf16[16,54,128]{2,1,0:T(8,128)(2,1)} %sum_terms.1), calls=%async_computation.4 | async-start | bytes 458752 | tf_op jit(solution)/shard_map/all_to_all | solution.py:444
  125.7 17.3 %copy-start.8 = (bf16[16,2,32,256]{3,2,1,0:T(8,128)(2,1)S(1)}, bf16[16,2,32,256]{3,2,1,0:T(8,128)(2,1)}, u32[]{:S(2)}) copy-start(bf16[16,2,32,256]{3,2,1,0:T(8,128)(2,1)} %copy-done.6) | copy-start | bytes 1572868
  125.7 17.2 %collective-permute-start.12 = (bf16[2,864,128]{2,1,0:T(8,128)(2,1)}, bf16[2,864,128]{2,1,0:T(8,128)(2,1)}, u32[]{:S(2)}, u32[]{:S(2)}) collective-permute-start(bf16[2,864,128]{2,1,0:T(8,128)(2,1)} %collective-permute-done.9.more_a), channel_id=1, source_target_pairs={{0,1},{1,0},{2,3},{3,2},{4,5},{5,4},{6,7},{7,6},{8,9},{9,8},{10,11... | collective-permute-start | bytes 1327112 | tf_op jit(solution)/shard_map/ppermute | solution.py:34
  128.6 14.4 %collective-permute-start.13 = (bf16[2,864,128]{2,1,0:T(8,128)(2,1)}, bf16[2,864,128]{2,1,0:T(8,128)(2,1)}, u32[]{:S(2)}, u32[]{:S(2)}) collective-permute-start(bf16[2,864,128]{2,1,0:T(8,128)(2,1)} %collective-permute-done.10.more_b), channel_id=1, source_target_pairs={{0,1},{1,0},{2,3},{3,2},{4,5},{5,4},{6,7},{7,6},{8,9},{9,8},{10,11... | collective-permute-start | bytes 1327112 | tf_op jit(solution)/shard_map/ppermute | solution.py:34
  134.2 24.2 %all-to-all-start.5 = ((f32[8,54,128]{2,1,0:T(8,128)}), f32[8,54,128]{2,1,0:T(8,128)S(1)}, u32[]{:S(2)}, u32[]{:S(2)}) async-start(f32[8,54,128]{2,1,0:T(8,128)} %broadcast_in_dim.5), calls=%async_computation.5 | async-start | bytes 458752 | tf_op jit(solution)/shard_map/all_to_all | solution.py:30
  142.9 9.2 %copy-start.3 = (bf16[2,864,128]{2,1,0:T(8,128)(2,1)S(1)}, bf16[2,864,128]{2,1,0:T(8,128)(2,1)}, u32[]{:S(2)}) copy-start(bf16[2,864,128]{2,1,0:T(8,128)(2,1)} %copy-done.1) | copy-start | bytes 1327108
  143.0 1.2 copy-start.20

commit v5 on v3

--- a/solution.py
+++ b/solution.py
@@ -16,8 +16,10 @@
 
 YZ_GROUPS = [[x * 16 + k for k in range(16)] for x in range(4)]
 X_GROUPS = [[k, k + 16, k + 32, k + 48] for k in range(16)]
-Y_GROUPS = [[b * 8 + k for k in range(8)] for b in range(8)]
 ROW_GROUPS = [list(range(8))]
+GAINS_COST = 1 << 36
+UNPACK_COST = 1 << 36
+ASSEMBLE_COST = 1 << 36
 
 
 def spread(block, axis, groups):
@@ -36,18 +38,10 @@
     return lax.ppermute(block, axis, route)
 
 
-def from_z(block, distance):
-    def device(x, y, z, c):
-        return (x * 16 + (z % 2) * 8 + y) * 8 + (z // 2) * 2 + c
-
-    route = [
-        (device(x, y, (z + distance) % 8, c), device(x, y, z, c))
-        for x in range(4)
-        for y in range(8)
-        for z in range(8)
-        for c in range(2)
-    ]
-    return lax.ppermute(block, ("tm", "rows"), route)
+def along_x(block):
+    count = lax.axis_size("tm")
+    routes = [[(i, i ^ (mask * 16)) for i in range(count)] for mask in (1, 2, 3)]
+    return [block] + [lax.ppermute(block, "tm", route) for route in routes]
 
 
 def beyond_chip(block):
@@ -94,18 +88,33 @@
                 out[k, frames, 7:8] = out[k, frames, 0:1]
 
 
-def arrange(out, flags, part, more_a, more_b):
-    here, there = flags[5] * 864, 864 - flags[5] * 864
-    for n in range(4):
-        out[pl.ds(pl.multiple_of(n * 1728 + here, 32), 864)] = part[n]
-        more = more_a[n] if n < 2 else more_b[n - 2]
-        out[pl.ds(pl.multiple_of(n * 1728 + there, 32), 864)] = more
-
-
-def half_kernel(flags, mid, edge, other, part, more_a, more_b, pre, squares, w1, xs):
+def place(flags, mask):
+    return pl.ds(pl.multiple_of(flags[5 + mask] * 1728, 64), 1728)
+
+
+def assemble_kernel(flags, a, b, c, d, out):
+    for mask, block in enumerate((a, b, c, d)):
+        out[place(flags, mask)] = block[...]
+
+
+def gains_kernel(flags, gain, half, both):
+    row = lax.broadcasted_iota(jnp.int32, (C, HALF), 0)
+    col = lax.broadcasted_iota(jnp.int32, (C, HALF), 1)
+    wide = jnp.broadcast_to(gain[...], (HALF, C)).T
+    even = jnp.sum(jnp.where(row == 2 * col, wide, 0.0), axis=0, keepdims=True)
+    odd = jnp.sum(jnp.where(row == 2 * col + 1, wide, 0.0), axis=0, keepdims=True)
+    half[...] = jnp.where(flags[2] == 0, even, odd)
+    both[...] = jnp.concatenate([even, odd], axis=1)
+
+
+def unpack_kernel(block, out):
+    rows = [block[n].astype(F32) for n in range(16)]
+    out[...] = jnp.concatenate(rows, axis=0).astype(BF)
+
+
+def half_kernel(flags, mid, edge, other, w1, pre, squares, xs):
     base = 2 - 2 * flags[2]
     fill_all(xs, flags, (mid, edge, other), 0, 6, True)
-    arrange(w1, flags, part, more_a, more_b)
     for i in range(3):
         for j in range(3):
             lhs = jnp.concatenate(
@@ -162,12 +171,12 @@
 
 
 def backward_kernel(
-    flags, mid, edge, other, gain, pre, w1_own, w1_other, part, more_a, more_b,
-    far_part, far_more_a, far_more_b, out, ps, acc, cs, w2_own, w2_other,
+    flags, mid, edge, other, gain, pre, w1_own, w1_other, a, b, c, d, far_a, far_b, far_c, far_d,
+    out, ps, acc, cs, w2_own, w2_other,
 ):
     fill_all(cs, flags, (mid, edge, other), 8, 8, False)
-    arrange(w2_own, flags, part, more_a, more_b)
-    arrange(w2_other, flags, far_part, far_more_a, far_more_b)
+    assemble_kernel(flags, a, b, c, d, w2_own)
+    assemble_kernel(flags, far_a, far_b, far_c, far_d, w2_other)
     nt = (((1,), (1,)), ((), ()))
     taps = [(i, j, k) for i in range(3) for j in range(3) for k in range(3)]
     for n, (i, j, k) in enumerate(taps):
@@ -231,19 +240,34 @@
         in_specs=smem + [VMEM] * (len(operands) - len(smem)),
         out_specs=jax.tree.map(lambda _: VMEM, out_shape),
         scratch_shapes=scratch,
-        compiler_params=pltpu.CompilerParams(vmem_limit_bytes=32 * 1024 * 1024),
+        compiler_params=pltpu.CompilerParams(vmem_limit_bytes=24 * 1024 * 1024),
         cost_estimate=pl.CostEstimate(flops=flops, bytes_accessed=1 << 20, transcendentals=0),
         name=name,
     )(*operands)
 
 
-def forward_half(flags, field, part, more_a, more_b):
+def order_gains(flags, gain):
+    half = jax.ShapeDtypeStruct((1, HALF), F32)
+    both = jax.ShapeDtypeStruct((1, C), F32)
+    return call(gains_kernel, "gains", GAINS_COST, (half, both), [], flags, gain.reshape(1, C))
+
+
+def unpack(block, cost=1):
+    shape = jax.ShapeDtypeStruct((1728, HALF), BF)
+    return call(unpack_kernel, "unpack", cost, shape, [], block)
+
+
+def assemble(flags, blocks, cost=1):
+    shape = jax.ShapeDtypeStruct((ROWS, HALF), BF)
+    return call(assemble_kernel, "assemble", cost, shape, [], flags, *blocks)
+
+
+def forward_half(flags, field, w1):
     shape = jax.ShapeDtypeStruct((512, HALF), F32)
-    weight = jax.ShapeDtypeStruct((ROWS, HALF), BF)
     scratch = [pltpu.VMEM((3, 6, 8, W, C), BF)]
     return call(
-        half_kernel, "forward_half", 4 * 512 * ROWS * HALF, (shape, shape, weight), scratch,
-        flags, *field, part, more_a, more_b,
+        half_kernel, "forward_half", 4 * 512 * ROWS * HALF, (shape, shape), scratch,
+        flags, *field, w1,
     )
 
 
@@ -281,51 +305,50 @@
 
 def on_device(activations, cotangent, gain, first_weight, second_weight):
     tm, rows = lax.axis_index("tm"), lax.axis_index("rows")
-    core, z_lo = rows % 2, (tm // 8) % 2
-    flags = jnp.stack([tm, rows, core, lax.axis_size("tm") - 1, lax.axis_size("rows") - 1, z_lo])
-    flags = flags.astype(jnp.int32)
+    core, x = rows % 2, tm // 16
+    flags = [tm, rows, core, lax.axis_size("tm") - 1, lax.axis_size("rows") - 1]
+    flags = jnp.stack(flags + [x ^ mask for mask in range(4)]).astype(jnp.int32)
 
     pick = lax.broadcasted_iota(jnp.int32, (C, HALF), 0) == (
         2 * lax.broadcasted_iota(jnp.int32, (C, HALF), 1) + core
     )
     half1 = jnp.dot(first_weight, pick.astype(BF), preferred_element_type=F32).astype(BF)
     half2 = lax.dynamic_slice_in_dim(second_weight, core * HALF, HALF, axis=1)
-    gain_pairs = gain.reshape(HALF, 2)
-    gain_half = jnp.where(core == 0, gain_pairs[:, 0], gain_pairs[:, 1]).reshape(1, HALF)
-    gain_all = jnp.concatenate([gain_pairs[:, 0], gain_pairs[:, 1]]).reshape(1, C)
-
-    block = spread(jnp.concatenate([half1, half2]), "tm", Y_GROUPS)
-    w1_part = spread(block[:, :108].reshape(864, HALF), "tm", X_GROUPS)
-    activations, cotangent, _ = lax.optimization_barrier((activations, cotangent, half1))
+
+    operand = jnp.broadcast_to(half1[None], (16,) + half1.shape)
+    w1_block = lax.all_to_all(operand, "tm", 0, 0, axis_index_groups=YZ_GROUPS, tiled=True)
+    w1_blocks = along_x(unpack(w1_block, UNPACK_COST))
+    activations, cotangent, _ = lax.optimization_barrier((activations, cotangent, operand))
 
     nexts = shift(jnp.concatenate([activations[:2], cotangent], axis=0), "tm", -1)
     prevs = shift(activations[2:], "tm", 1)
+    gain_half, gain_all = order_gains(flags, gain)
+    nexts, prevs = lax.optimization_barrier((nexts, prevs, gain_half))[:2]
     mid = jnp.concatenate([prevs, activations, nexts[:2], cotangent, nexts[2:]], axis=0)
     edge = beyond_chip(mid)
     next_row = jnp.where(core == 0, edge[:, 1:], edge[:, :1])
     field = (mid, edge, swap_cores(jnp.concatenate([mid, next_row], axis=1)))
 
-    w1_more = from_z(w1_part[:2], 1), from_z(w1_part[2:], -1)
-    w2_part = spread(after(block[:, 108:].reshape(864, HALF), w1_part), "tm", X_GROUPS)
-    w1_more, w2_part = lax.optimization_barrier((w1_more, w2_part))
-
-    pre_half, squares, w1_own = forward_half(flags, field, w1_part, *w1_more)
+    w2_block = unpack(spread(after(half2, edge), "tm", YZ_GROUPS))
+
+    w1_own = assemble(flags, w1_blocks, ASSEMBLE_COST)
+    pre_half, squares = forward_half(flags, field, w1_own)
     squares_other = swap_cores(squares)
+    squares_other, w2_block = lax.optimization_barrier((squares_other, w2_block))
     terms = local_terms(flags, pre_half, squares, squares_other, gain_half, field)
 
     total = lax.all_to_all(
         terms.reshape(4, 864, CH), "tm", 0, 0, axis_index_groups=X_GROUPS, tiled=True
     )
-    w2_part = after(w2_part, terms)
-    w2_own = [w2_part, from_z(w2_part[:2], 1), from_z(w2_part[2:], -1)]
     w1_other = swap_cores(after(w1_own, terms))
+    w2_blocks = along_x(after(w2_block, terms))
     pre = forward_all(flags, field, w1_own, w1_other)
     total, pre = lax.optimization_barrier((total, pre))
-    w2_other = [swap_cores(part) for part in w2_own]
-    input_grad = backward(flags, field, gain_all, pre, w1_own, w1_other, w2_own, w2_other)
 
     total = total.astype(F32).sum(0).astype(BF).reshape(16, 54, CH)
     total = lax.all_to_all(total, "tm", 0, 0, axis_index_groups=YZ_GROUPS, tiled=True)
+    w2_far = [swap_cores(block) for block in w2_blocks]
+    input_grad = backward(flags, field, gain_all, pre, w1_own, w1_other, w2_blocks, w2_far)
     total = spread(total.astype(F32).sum(0), "rows", ROW_GROUPS)
     total, input_grad = lax.optimization_barrier((total, input_grad))
     weight_grad = total.reshape(4, 2, 54, CH).sum(0).transpose(1, 0, 2).reshape(108, CH)

time: 150 us -> 147 us (0.980)
  starting transfers between devices: 81.4 us -> 86.3 us
  local copies, waits for them, and re-layouts: 13.4 us -> 9.29 us
  waiting for transfers between devices: 24.5 us -> 20.6 us
  other arithmetic: 4.75 us -> 2.43 us
  Pallas kernels: 23.9 us -> 25.6 us
    all_to_all x4 -> x2, waiting for transfers between devices: 11.8 us -> 0.01 us  [spread(): lax.all_to_all(operand, axis, 0, 0, axis_index_groups=groups, tiled=True)]
    all_to_all x0 -> x1, starting transfers between devices: none -> 9.56 us  [on_device(): lax.all_to_all(operand, 'tm', 0, 0, axis_index_groups=YZ_GROUPS, tiled=True)]
    ppermute x2, waiting for transfers between devices: 0.01 us -> 8.78 us  [shift(): return lax.ppermute(block, axis, route)]
    all_to_all x4 -> x2, starting transfers between devices: 22.6 us -> 18 us  [spread(): lax.all_to_all(operand, axis, 0, 0, axis_index_groups=groups, tiled=True)]
    ppermute x6 -> x7, starting transfers between devices: 20.5 us -> 16.3 us  [swap_cores(): lax.ppermute(block, 'rows', [(i, i ^ 1) for i in range(lax.axis_size('row...]
    all_to_all x1, starting transfers between devices: 3.53 us -> 6.53 us  [on_device(): lax.all_to_all(total, 'tm', 0, 0, axis_index_groups=YZ_GROUPS, tiled=True)]
    all_to_all x1, waiting for transfers between devices: 2.9 us -> 0.01 us  [on_device(): lax.all_to_all(total, 'tm', 0, 0, axis_index_groups=YZ_GROUPS, tiled=True)]
    ppermute x1, waiting for transfers between devices: 0.3 us -> 3.15 us  [beyond_chip(): return lax.ppermute(block, 'rows', route)]
  transfers between devices with their start and end apart: 19 -> 21, of which waited for: 7 -> 6; matrix products, arithmetic and copies ran while one was open for 8% -> 4% of each run, Pallas kernels for 11% -> 16%
where the time goes in v5:
time: 147 us; the launch traced here: 145 us
  starting transfers between devices  86.3 us (59%)
  Pallas kernels  25.6 us (17%)
  waiting for transfers between devices  20.6 us (14%)
  local copies, waits for them, and re-layouts  9.29 us (6%)
  other arithmetic  2.43 us (2%)
    pallas_call x8, Pallas kernels, call(): pl.pallas_call(kernel, out_shape=out_shape, in_specs=smem + [VMEM] * (len...  25.6 us
    ppermute x6, starting transfers between devices, along_x(): return [block] + [lax.ppermute(block, 'tm', route) for route in routes]  19.2 us
    all_to_all x2, starting transfers between devices, spread(): lax.all_to_all(operand, axis, 0, 0, axis_index_groups=groups, tiled=True)  18 us
    ppermute x7, starting transfers between devices, swap_cores(): lax.ppermute(block, 'rows', [(i, i ^ 1) for i in range(lax.axis_size('row...  16.3 us
    all_to_all x1, starting transfers between devices, on_device(): lax.all_to_all(operand, 'tm', 0, 0, axis_index_groups=YZ_GROUPS, tiled=True)  9.56 us
    ppermute x2, waiting for transfers between devices, shift(): return lax.ppermute(block, axis, route)  8.78 us
    ppermute x1, starting transfers between devices, beyond_chip(): return lax.ppermute(block, 'rows', route)  7.28 us
    ppermute x6, waiting for transfers between devices, along_x(): return [block] + [lax.ppermute(block, 'tm', route) for route in routes]  7.24 us
  transfers between devices with their start and end apart: 21, of which 6 were waited for; matrix products, arithmetic and copies ran while one was open for 4% of the time, Pallas kernels for 16%

profile of v5, /device:TPU:1, one launch (start us, length us, event | category | flops | bytes accessed | tf_op | source)
XLA Modules:
  0.0 145.5 jit_solution(1299886819747305918)
XLA Ops:
  0.6 0.0 copy-start
  0.7 0.8 copy-done
  1.5 0.1 fusion
  1.6 0.8 broadcast_in_dim.6
  2.4 9.6 %all-to-all-start = ((bf16[16,108,128]{2,1,0:T(8,128)(2,1)}), bf16[16,108,128]{2,1,0:T(8,128)(2,1)S(1)}, u32[]{:S(2)}, u32[]{:S(2)}) async-start(bf16[16,108,128]{2,1,0:T(8,128)(2,1)} %broadcast_in_dim.6), calls=%async_computation | async-start | bytes 917504 | tf_op jit(solution)/shard_map/all_to_all | solution.py:319
  12.0 0.9 fusion.2
  12.9 1.3 collective-permute-start
  14.2 4.0 %collective-permute-start.1 = (bf16[2,2,32,256]{3,2,1,0:T(8,128)(2,1)S(1)}, bf16[2,2,32,256]{3,2,1,0:T(8,128)(2,1)S(1)}, u32[]{:S(2)}, u32[]{:S(2)}) collective-permute-start(bf16[2,2,32,256]{3,2,1,0:T(8,128)(2,1)S(1)} %get-tuple-element.36), channel_id=1, source_target_pairs={{0,8},{8,16},{16,24},{24,32},{32,40},{40,48},{48,56},{56,64},{64,7... | collective-permute-start | bytes 196616 | tf_op jit(solution)/shard_map/ppermute | solution.py:38
  18.3 0.1 stack.31.flags
  18.3 0.0 copy-start.7
  18.4 0.7 gains.1
  19.0 1.5 %collective-permute-done.1 = bf16[2,2,32,256]{3,2,1,0:T(8,128)(2,1)S(1)} collective-permute-done((bf16[2,2,32,256]{3,2,1,0:T(8,128)(2,1)S(1)}, bf16[2,2,32,256]{3,2,1,0:T(8,128)(2,1)S(1)}, u32[]{:S(2)}, u32[]{:S(2)}) %collective-permute-start.1) | collective-permute-done | bytes 65568 | tf_op jit(solution)/shard_map/ppermute | solution.py:38
  20.6 7.2 %collective-permute-done = bf16[6,2,32,256]{3,2,1,0:T(8,128)(2,1)S(1)} collective-permute-done((bf16[6,2,32,256]{3,2,1,0:T(8,128)(2,1)S(1)}, bf16[6,2,32,256]{3,2,1,0:T(8,128)(2,1)S(1)}, u32[]{:S(2)}, u32[]{:S(2)}) %collective-permute-start) | collective-permute-done | bytes 196640 | tf_op jit(solution)/shard_map/ppermute | solution.py:38
  27.9 0.0 copy-start.8
  27.9 7.3 %collective-permute-start.2 = (bf16[16,2,32,256]{3,2,1,0:T(8,128)(2,1)S(1)}, bf16[16,2,32,256]{3,2,1,0:T(8,128)(2,1)S(1)}, u32[]{:S(2)}, u32[]{:S(2)}) collective-permute-start(bf16[16,2,32,256]{3,2,1,0:T(8,128)(2,1)S(1)} %slice_dynamic-update-slice_fusion.mid), channel_id=1, source_target_pairs={{1,2},{3,4},{5,6},{2,1},{4,3},{6,5},{9,10},{11,12},{13,14},{10,9},... | collective-permute-start | bytes 1572872 | tf_op jit(solution)/shard_map/ppermute | solution.py:50
  35.2 0.0 all-to-all-done.block
  35.2 0.1 unpack.2.a
  35.3 3.1 %collective-permute-start.4 = (bf16[1728,128]{1,0:T(8,128)(2,1)S(1)}, bf16[1728,128]{1,0:T(8,128)(2,1)S(1)}, u32[]{:S(2)}, u32[]{:S(2)}) collective-permute-start(bf16[1728,128]{1,0:T(8,128)(2,1)S(1)} %unpack.2.a), channel_id=1, source_target_pairs={{0,128},{8,136},{16,144},{24,152},{32,160},{40,168},{48,176},{56,1... | collective-permute-start | bytes 1327112 | tf_op jit(solution)/shard_map/ppermute | solution.py:44
  38.4 4.5 %collective-permute-start.5 = (bf16[1728,128]{1,0:T(8,128)(2,1)S(1)}, bf16[1728,128]{1,0:T(8,128)(2,1)}, u32[]{:S(2)}, u32[]{:S(2)}) collective-permute-start(bf16[1728,128]{1,0:T(8,128)(2,1)S(1)} %unpack.2.a), channel_id=1, source_target_pairs={{0,256},{8,264},{16,272},{24,280},{32,288},{40,296},{48,304},{56,3... | collective-permute-start | bytes 1327112 | tf_op jit(solution)/shard_map/ppermute | solution.py:44
  42.9 2.0 %collective-permute-start.6 = (bf16[1728,128]{1,0:T(8,128)(2,1)S(1)}, bf16[1728,128]{1,0:T(8,128)(2,1)}, u32[]{:S(2)}, u32[]{:S(2)}) collective-permute-start(bf16[1728,128]{1,0:T(8,128)(2,1)S(1)} %unpack.2.a), channel_id=1, source_target_pairs={{0,384},{8,392},{16,400},{24,408},{32,416},{40,424},{48,432},{56,4... | collective-permute-start | bytes 1327112 | tf_op jit(solution)/shard_map/ppermute | solution.py:44
  44.9 3.1 %collective-permute-done.2.edge = bf16[16,2,32,256]{3,2,1,0:T(8,128)(2,1)S(1)} collective-permute-done((bf16[16,2,32,256]{3,2,1,0:T(8,128)(2,1)S(1)}, bf16[16,2,32,256]{3,2,1,0:T(8,128)(2,1)S(1)}, u32[]{:S(2)}, u32[]{:S(2)}) %collective-permute-start.2) | collective-permute-done | bytes 524320 | tf_op jit(solution)/shard_map/ppermute | solution.py:50
  48.1 1.0 pad_maximum_fusion
  49.1 1.9 %collective-permute-start.3 = (bf16[16,3,32,256]{3,2,1,0:T(8,128)(2,1)}, bf16[16,3,32,256]{3,2,1,0:T(8,128)(2,1)S(1)}, u32[]{:S(2)}, u32[]{:S(2)}) collective-permute-start(bf16[16,3,32,256]{3,2,1,0:T(8,128)(2,1)} %pad_maximum_fusion), channel_id=1, source_target_pairs={{0,1},{1,0},{2,3},{3,2},{4,5},{5,4},{6,7},{7,6},{8,9},{9,8},{10,11... | collective-permute-start | bytes 2359304 | tf_op jit(solution)/shard_map/ppermute | solution.py:32
  51.0 0.8 broadcast_in_dim.7
  51.8 5.6 %all-to-all-start.1 = ((bf16[16,108,128]{2,1,0:T(8,128)(2,1)}), bf16[16,108,128]{2,1,0:T(8,128)(2,1)S(1)}, u32[]{:S(2)}, u32[]{:S(2)}) async-start(bf16[16,108,128]{2,1,0:T(8,128)(2,1)} %broadcast_in_dim.7), calls=%async_computation.1 | async-start | bytes 917504 | tf_op jit(solution)/shard_map/all_to_all | solution.py:28
  57.4 0.0 collective-permute-done.4.b
  57.4 0.0 collective-permute-done.5.c
  57.4 5.0 %collective-permute-done.6.d = bf16[1728,128]{1,0:T(8,128)(2,1)} collective-permute-done((bf16[1728,128]{1,0:T(8,128)(2,1)S(1)}, bf16[1728,128]{1,0:T(8,128)(2,1)}, u32[]{:S(2)}, u32[]{:S(2)}) %collective-permute-start.6) | collective-permute-done | bytes 442400 | tf_op jit(solution)/shard_map/ppermute | solution.py:44
  62.4 2.5 %assemble.1.w1.own.w1_own = bf16[6912,128]{1,0:T(8,128)(2,1)} custom-call(s32[9]{0:T(128)S(1)} %stack.31.flags, bf16[1728,128]{1,0:T(8,128)(2,1)S(1)} %unpack.2.a, bf16[1728,128]{1,0:T(8,128)(2,1)S(1)} %collective-permute-done.4.b, bf16[1728,128]{1,0:T(8,128)(2,1)} %collective-permute-done.5.c, bf16[1728,128]{1,0:T(8,128)(2,1)} %collective-permute-done.6.d), custom_call_target="tpu_custom_call" | custom-call | flops 68719476736 | bytes 1048576 | tf_op jit(solution)/shard_map/assemble/pallas_call | solution.py:237
  64.9 0.0 collective-permute-done.3.other.others
  64.9 3.9 %forward_half.1 = (f32[512,128]{1,0:T(8,128)S(1)}, f32[512,128]{1,0:T(8,128)S(1)}) custom-call(s32[9]{0:T(128)S(1)} %stack.31.flags, bf16[16,2,32,256]{3,2,1,0:T(8,128)(2,1)S(1)} %slice_dynamic-update-slice_fusion.mid, bf16[16,2,32,256]{3,2,1,0:T(8,128)(2,1)S(1)} %collective-permute-done.2.edge, ...), custom_call_target="tpu_custom_call" | custom-call | flops 1811939328 | bytes 1048576 | tf_op jit(solution)/shard_map/forward_half/pallas_call | solution.py:237
  68.8 0.7 copy-done.4
  69.5 1.9 %collective-permute-start.7 = (f32[512,128]{1,0:T(8,128)S(1)}, f32[512,128]{1,0:T(8,128)S(1)}, u32[]{:S(2)}, u32[]{:S(2)}) collective-permute-start(f32[512,128]{1,0:T(8,128)S(1)} %get-tuple-element.25.own), channel_id=1, source_target_pairs={{0,1},{1,0},{2,3},{3,2},{4,5},{5,4},{6,7},{7,6},{8,9},{9,8},{10,11... | collective-permute-start | bytes 786440 | tf_op jit(solution)/shard_map/ppermute | solution.py:32
  71.4 0.0 all-to-all-done.1.block
  71.5 0.1 unpack.3.a
  71.5 1.4 collective-permute-done.7.others
  72.9 0.9 copy-done.5
  73.9 2.4 %local_terms.1 = bf16[3456,128]{1,0:T(8,128)(2,1)} custom-call(s32[9]{0:T(128)S(1)} %stack.31.flags, f32[512,128]{1,0:T(8,128)S(1)} %copy-done.5, f32[512,128]{1,0:T(8,128)S(1)} %get-tuple-element.25.own, f32[512,128]{1,0:T(8,128)S(1)} %collective-permute-done.7.others, f32[1,128]{1,0:T(1,128)S(1)} %get-tuple-element.21.gain, ...), custom_call_target="tpu_custom_call" | custom-call | flops 1811939328 | bytes 1048576 | tf_op jit(solution)/shard_map/local_terms/pallas_call | solution.py:237
  76.3 2.0 %collective-permute-start.8 = (bf16[6912,128]{1,0:T(8,128)(2,1)}, bf16[6912,128]{1,0:T(8,128)(2,1)}, u32[]{:S(2)}, u32[]{:S(2)}) collective-permute-start(bf16[6912,128]{1,0:T(8,128)(2,1)} %assemble.1.w1.own.w1_own), channel_id=1, source_target_pairs={{0,1},{1,0},{2,3},{3,2},{4,5},{5,4},{6,7},{7,6},{8,9},{9,8},{10,11... | collective-permute-start | bytes 5308424 | tf_op jit(solution)/shard_map/ppermute | solution.py:32
  78.4 4.2 %all-to-all-start.2 = ((bf16[4,864,128]{2,1,0:T(8,128)(2,1)}), bf16[4,864,128]{2,1,0:T(8,128)(2,1)}, u32[]{:S(2)}, u32[]{:S(2)}) async-start(bf16[4,864,128]{2,1,0:T(8,128)(2,1)} %bitcast.9), calls=%async_computation.2 | async-start | bytes 1769472 | tf_op jit(solution)/shard_map/all_to_all | solution.py:340
  82.6 3.3 %collective-permute-start.9 = (bf16[1728,128]{1,0:T(8,128)(2,1)S(1)}, bf16[1728,128]{1,0:T(8,128)(2,1)S(1)}, u32[]{:S(2)}, u32[]{:S(2)}) collective-permute-start(bf16[1728,128]{1,0:T(8,128)(2,1)S(1)} %unpack.3.a), channel_id=1, source_target_pairs={{0,128},{8,136},{16,144},{24,152},{32,160},{40,168},{48,176},{56,1... | collective-permute-start | bytes 1327112 | tf_op jit(solution)/shard_map/ppermute | solution.py:44
  85.9 4.3 %collective-permute-start.10 = (bf16[1728,128]{1,0:T(8,128)(2,1)S(1)}, bf16[1728,128]{1,0:T(8,128)(2,1)S(1)}, u32[]{:S(2)}, u32[]{:S(2)}) collective-permute-start(bf16[1728,128]{1,0:T(8,128)(2,1)S(1)} %unpack.3.a), channel_id=1, source_target_pairs={{0,256},{8,264},{16,272},{24,280},{32,288},{40,296},{48,304},{56,3... | collective-permute-start | bytes 1327112 | tf_op jit(solution)/shard_map/ppermute | solution.py:44
  90.2 2.0 %collective-permute-start.11 = (bf16[1728,128]{1,0:T(8,128)(2,1)S(1)}, bf16[1728,128]{1,0:T(8,128)(2,1)}, u32[]{:S(2)}, u32[]{:S(2)}) collective-permute-start(bf16[1728,128]{1,0:T(8,128)(2,1)S(1)} %unpack.3.a), channel_id=1, source_target_pairs={{0,384},{8,392},{16,400},{24,408},{32,416},{40,424},{48,432},{56,4... | collective-permute-start | bytes 1327112 | tf_op jit(solution)/shard_map/ppermute | solution.py:44
  92.2 0.0 collective-permute-done.8.other.w1_other
  92.2 5.3 %forward_all.1.pre = f32[768,256]{1,0:T(8,128)S(1)} custom-call(s32[9]{0:T(128)S(1)} %stack.31.flags, bf16[16,2,32,256]{3,2,1,0:T(8,128)(2,1)S(1)} %slice_dynamic-update-slice_fusion.mid, bf16[16,2,32,256]{3,2,1,0:T(8,128)(2,1)S(1)} %collective-permute-done.2.edge, bf16[16,3,32,256]{3,2,1,0:T(8,128)(2,1)S(1)} %collective-permute-done.3.other.others, ...), custom_call_target="tpu_custom_call" | custom-call | flops 2717908992 | bytes 1048576 | tf_op jit(solution)/shard_map/forward_all/pallas_call | solution.py:237
  97.5 0.9 copy-done.2
  98.4 0.0 all-to-all-done.2
  98.4 1.4 reduce_sum.30
  99.8 0.7 reshape.24
  100.5 6.5 %all-to-all-start.3 = ((bf16[16,54,128]{2,1,0:T(8,128)(2,1)}), bf16[16,54,128]{2,1,0:T(8,128)(2,1)S(1)}, u32[]{:S(2)}, u32[]{:S(2)}) async-start(bf16[16,54,128]{2,1,0:T(8,128)(2,1)} %reshape.24), calls=%async_computation.3 | async-start | bytes 458752 | tf_op jit(solution)/shard_map/all_to_all | solution.py:349
  107.1 3.4 %collective-permute-start.12 = (bf16[1728,128]{1,0:T(8,128)(2,1)S(1)}, bf16[1728,128]{1,0:T(8,128)(2,1)}, u32[]{:S(2)}, u32[]{:S(2)}) collective-permute-start(bf16[1728,128]{1,0:T(8,128)(2,1)S(1)} %unpack.3.a), channel_id=1, source_target_pairs={{0,1},{1,0},{2,3},{3,2},{4,5},{5,4},{6,7},{7,6},{8,9},{9,8},{10,11... | collective-permute-start | bytes 1327112 | tf_op jit(solution)/shard_map/ppermute | solution.py:32
  110.5 0.0 collective-permute-done.9.b
  110.5 1.9 %collective-permute-start.13 = (bf16[1728,128]{1,0:T(8,128)(2,1)S(1)}, bf16[1728,128]{1,0:T(8,128)(2,1)}, u32[]{:S(2)}, u32[]{:S(2)}) collective-permute-start(bf16[1728,128]{1,0:T(8,128)(2,1)S(1)} %collective-permute-done.9.b), channel_id=1, source_target_pairs={{0,1},{1,0},{2,3},{3,2},{4,5},{5,4},{6,7},{7,6},{8,9},{9,8},{10,11... | collective-permute-start | bytes 1327112 | tf_op jit(solution)/shard_map/ppermute | solution.py:32
  112.4 2.2 %collective-permute-done.10.c = bf16[1728,128]{1,0:T(8,128)(2,1)S(1)} collective-permute-done((bf16[1728,128]{1,0:T(8,128)(2,1)S(1)}, bf16[1728,128]{1,0:T(8,128)(2,1)S(1)}, u32[]{:S(2)}, u32[]{:S(2)}) %collective-permute-start.10) | collective-permute-done | bytes 442400 | tf_op jit(solution)/shard_map/ppermute | solution.py:44
  114.7 3.2 %collective-permute-start.14 = (bf16[1728,128]{1,0:T(8,128)(2,1)S(1)}, bf16[1728,128]{1,0:T(8,128)(2,1)}, u32[]{:S(2)}, u32[]{:S(2)}) collective-permute-start(bf16[1728,128]{1,0:T(8,128)(2,1)S(1)} %collective-permute-done.10.c), channel_id=1, source_target_pairs={{0,1},{1,0},{2,3},{3,2},{4,5},{5,4},{6,7},{7,6},{8,9},{9,8},{10,11... | collective-permute-start | bytes 1327112 | tf_op jit(solution)/shard_map/ppermute | solution.py:32
  117.8 0.0 collective-permute-done.11.d
  117.8 1.9 %collective-permute-start.15 = (bf16[1728,128]{1,0:T(8,128)(2,1)}, bf16[1728,128]{1,0:T(8,128)(2,1)}, u32[]{:S(2)}, u32[]{:S(2)}) collective-permute-start(bf16[1728,128]{1,0:T(8,128)(2,1)} %collective-permute-done.11.d), channel_id=1, source_target_pairs={{0,1},{1,0},{2,3},{3,2},{4,5},{5,4},{6,7},{7,6},{8,9},{9,8},{10,11... | collective-permute-start | bytes 1327112 | tf_op jit(solution)/shard_map/ppermute | solution.py:32
  119.8 0.7 broadcast_in_dim.8
  120.5 12.4 %all-to-all-start.4 = ((f32[8,54,128]{2,1,0:T(8,128)}), f32[8,54,128]{2,1,0:T(8,128)S(1)}, u32[]{:S(2)}, u32[]{:S(2)}) async-start(f32[8,54,128]{2,1,0:T(8,128)} %broadcast_in_dim.8), calls=%async_computation.4 | async-start | bytes 458752 | tf_op jit(solution)/shard_map/all_to_all | solution.py:28
  132.9 0.0 collective-permute-done.14.far_c
  132.9 0.0 collective-permute-done.15.far_d
  133.0 1.1 copy-done.3
  134.1 10.7 %backward.1 = bf16[4,2,32,256]{3,2,1,0:T(8,128)(2,1)} custom-call(s32[9]{0:T(128)S(1)} %stack.31.flags, bf16[16,2,32,256]{3,2,1,0:T(8,128)(2,1)S(1)} %slice_dynamic-update-slice_fusion.mid, bf16[16,2,32,256]{3,2,1,0:T(8,128)(2,1)S(1)} %collective-permute-done.2.edge, bf16[16,3,32,256]{3,2,1,0:T(8,128)(2,1)S(1)} %collective-permute-done.3.other.others, ...), custom_call_target="tpu_custom_call" | custom-call | flops 3623878656 | bytes 1048576 | tf_op jit(solution)/shard_map/backward/pallas_call | solution.py:237
  144.8 0.7 reshape.26
  (26 shorter events, 0.2 us)
Async XLA Ops:
  0.6 0.8 copy-start
  0.6 12.3 %copy-start.6 = (bf16[4,2,32,256]{3,2,1,0:T(8,128)(2,1)S(1)}, bf16[4,2,32,256]{3,2,1,0:T(8,128)(2,1)}, u32[]{:S(2)}) copy-start(bf16[4,2,32,256]{3,2,1,0:T(8,128)(2,1)} %param.6) | copy-start | bytes 393220
  0.7 17.7 %copy-start.1 = (f32[256]{0:T(256)S(1)}, f32[256]{0:T(256)}, u32[]{:S(2)}) copy-start(f32[256]{0:T(256)} %param.7) | copy-start | bytes 3076
  2.4 32.8 %all-to-all-start = ((bf16[16,108,128]{2,1,0:T(8,128)(2,1)}), bf16[16,108,128]{2,1,0:T(8,128)(2,1)S(1)}, u32[]{:S(2)}, u32[]{:S(2)}) async-start(bf16[16,108,128]{2,1,0:T(8,128)(2,1)} %broadcast_in_dim.6), calls=%async_computation | async-start | bytes 917504 | tf_op jit(solution)/shard_map/all_to_all | solution.py:319
  12.9 14.9 %collective-permute-start = (bf16[6,2,32,256]{3,2,1,0:T(8,128)(2,1)S(1)}, bf16[6,2,32,256]{3,2,1,0:T(8,128)(2,1)S(1)}, u32[]{:S(2)}, u32[]{:S(2)}) collective-permute-start(bf16[6,2,32,256]{3,2,1,0:T(8,128)(2,1)S(1)} %pad_maximum_fusion.1), channel_id=1, source_target_pairs={{8,0},{16,8},{24,16},{32,24},{40,32},{48,40},{56,48},{64,56},{72,6... | collective-permute-start | bytes 589832 | tf_op jit(solution)/shard_map/ppermute | solution.py:38
  14.2 6.3 %collective-permute-start.1 = (bf16[2,2,32,256]{3,2,1,0:T(8,128)(2,1)S(1)}, bf16[2,2,32,256]{3,2,1,0:T(8,128)(2,1)S(1)}, u32[]{:S(2)}, u32[]{:S(2)}) collective-permute-start(bf16[2,2,32,256]{3,2,1,0:T(8,128)(2,1)S(1)} %get-tuple-element.36), channel_id=1, source_target_pairs={{0,8},{8,16},{16,24},{24,32},{32,40},{40,48},{48,56},{56,64},{64,7... | collective-permute-start | bytes 196616 | tf_op jit(solution)/shard_map/ppermute | solution.py:38
  18.3 9.5 %copy-start.7 = (bf16[4,2,32,256]{3,2,1,0:T(8,128)(2,1)S(1)}, bf16[4,2,32,256]{3,2,1,0:T(8,128)(2,1)}, u32[]{:S(2)}) copy-start(bf16[4,2,32,256]{3,2,1,0:T(8,128)(2,1)} %param.5) | copy-start | bytes 393220
  27.9 17.0 %copy-start.8 = (bf16[108,256]{1,0:T(8,128)(2,1)S(1)}, bf16[108,256]{1,0:T(8,128)(2,1)}, u32[]{:S(2)}) copy-start(bf16[108,256]{1,0:T(8,128)(2,1)} %param.9) | copy-start | bytes 165892
  27.9 20.2 %collective-permute-start.2 = (bf16[16,2,32,256]{3,2,1,0:T(8,128)(2,1)S(1)}, bf16[16,2,32,256]{3,2,1,0:T(8,128)(2,1)S(1)}, u32[]{:S(2)}, u32[]{:S(2)}) collective-permute-start(bf16[16,2,32,256]{3,2,1,0:T(8,128)(2,1)S(1)} %slice_dynamic-update-slice_fusion.mid), channel_id=1, source_target_pairs={{1,2},{3,4},{5,6},{2,1},{4,3},{6,5},{9,10},{11,12},{13,14},{10,9},... | collective-permute-start | bytes 1572872 | tf_op jit(solution)/shard_map/ppermute | solution.py:50
  35.3 22.1 %collective-permute-start.4 = (bf16[1728,128]{1,0:T(8,128)(2,1)S(1)}, bf16[1728,128]{1,0:T(8,128)(2,1)S(1)}, u32[]{:S(2)}, u32[]{:S(2)}) collective-permute-start(bf16[1728,128]{1,0:T(8,128)(2,1)S(1)} %unpack.2.a), channel_id=1, source_target_pairs={{0,128},{8,136},{16,144},{24,152},{32,160},{40,168},{48,176},{56,1... | collective-permute-start | bytes 1327112 | tf_op jit(solution)/shard_map/ppermute | solution.py:44
  38.4 19.0 %collective-permute-start.5 = (bf16[1728,128]{1,0:T(8,128)(2,1)S(1)}, bf16[1728,128]{1,0:T(8,128)(2,1)}, u32[]{:S(2)}, u32[]{:S(2)}) collective-permute-start(bf16[1728,128]{1,0:T(8,128)(2,1)S(1)} %unpack.2.a), channel_id=1, source_target_pairs={{0,256},{8,264},{16,272},{24,280},{32,288},{40,296},{48,304},{56,3... | collective-permute-start | bytes 1327112 | tf_op jit(solution)/shard_map/ppermute | solution.py:44
  42.9 19.5 %collective-permute-start.6 = (bf16[1728,128]{1,0:T(8,128)(2,1)S(1)}, bf16[1728,128]{1,0:T(8,128)(2,1)}, u32[]{:S(2)}, u32[]{:S(2)}) collective-permute-start(bf16[1728,128]{1,0:T(8,128)(2,1)S(1)} %unpack.2.a), channel_id=1, source_target_pairs={{0,384},{8,392},{16,400},{24,408},{32,416},{40,424},{48,432},{56,4... | collective-permute-start | bytes 1327112 | tf_op jit(solution)/shard_map/ppermute | solution.py:44
  49.1 15.9 %collective-permute-start.3 = (bf16[16,3,32,256]{3,2,1,0:T(8,128)(2,1)}, bf16[16,3,32,256]{3,2,1,0:T(8,128)(2,1)S(1)}, u32[]{:S(2)}, u32[]{:S(2)}) collective-permute-start(bf16[16,3,32,256]{3,2,1,0:T(8,128)(2,1)} %pad_maximum_fusion), channel_id=1, source_target_pairs={{0,1},{1,0},{2,3},{3,2},{4,5},{5,4},{6,7},{7,6},{8,9},{9,8},{10,11... | collective-permute-start | bytes 2359304 | tf_op jit(solution)/shard_map/ppermute | solution.py:32
  51.8 19.6 %all-to-all-start.1 = ((bf16[16,108,128]{2,1,0:T(8,128)(2,1)}), bf16[16,108,128]{2,1,0:T(8,128)(2,1)S(1)}, u32[]{:S(2)}, u32[]{:S(2)}) async-start(bf16[16,108,128]{2,1,0:T(8,128)(2,1)} %broadcast_in_dim.7), calls=%async_computation.1 | async-start | bytes 917504 | tf_op jit(solution)/shard_map/all_to_all | solution.py:28
  68.8 0.7 copy-start.4
  69.5 3.4 %collective-permute-start.7 = (f32[512,128]{1,0:T(8,128)S(1)}, f32[512,128]{1,0:T(8,128)S(1)}, u32[]{:S(2)}, u32[]{:S(2)}) collective-permute-start(f32[512,128]{1,0:T(8,128)S(1)} %get-tuple-element.25.own), channel_id=1, source_target_pairs={{0,1},{1,0},{2,3},{3,2},{4,5},{5,4},{6,7},{7,6},{8,9},{9,8},{10,11... | collective-permute-start | bytes 786440 | tf_op jit(solution)/shard_map/ppermute | solution.py:32
  72.9 1.0 copy-start.5
  76.3 15.9 %collective-permute-start.8 = (bf16[6912,128]{1,0:T(8,128)(2,1)}, bf16[6912,128]{1,0:T(8,128)(2,1)}, u32[]{:S(2)}, u32[]{:S(2)}) collective-permute-start(bf16[6912,128]{1,0:T(8,128)(2,1)} %assemble.1.w1.own.w1_own), channel_id=1, source_target_pairs={{0,1},{1,0},{2,3},{3,2},{4,5},{5,4},{6,7},{7,6},{8,9},{9,8},{10,11... | collective-permute-start | bytes 5308424 | tf_op jit(solution)/shard_map/ppermute | solution.py:32
  78.4 20.1 %all-to-all-start.2 = ((bf16[4,864,128]{2,1,0:T(8,128)(2,1)}), bf16[4,864,128]{2,1,0:T(8,128)(2,1)}, u32[]{:S(2)}, u32[]{:S(2)}) async-start(bf16[4,864,128]{2,1,0:T(8,128)(2,1)} %bitcast.9), calls=%async_computation.2 | async-start | bytes 1769472 | tf_op jit(solution)/shard_map/all_to_all | solution.py:340
  82.6 27.9 %collective-permute-start.9 = (bf16[1728,128]{1,0:T(8,128)(2,1)S(1)}, bf16[1728,128]{1,0:T(8,128)(2,1)S(1)}, u32[]{:S(2)}, u32[]{:S(2)}) collective-permute-start(bf16[1728,128]{1,0:T(8,128)(2,1)S(1)} %unpack.3.a), channel_id=1, source_target_pairs={{0,128},{8,136},{16,144},{24,152},{32,160},{40,168},{48,176},{56,1... | collective-permute-start | bytes 1327112 | tf_op jit(solution)/shard_map/ppermute | solution.py:44
  85.9 28.7 %collective-permute-start.10 = (bf16[1728,128]{1,0:T(8,128)(2,1)S(1)}, bf16[1728,128]{1,0:T(8,128)(2,1)S(1)}, u32[]{:S(2)}, u32[]{:S(2)}) collective-permute-start(bf16[1728,128]{1,0:T(8,128)(2,1)S(1)} %unpack.3.a), channel_id=1, source_target_pairs={{0,256},{8,264},{16,272},{24,280},{32,288},{40,296},{48,304},{56,3... | collective-permute-start | bytes 1327112 | tf_op jit(solution)/shard_map/ppermute | solution.py:44
  90.2 27.6 %collective-permute-start.11 = (bf16[1728,128]{1,0:T(8,128)(2,1)S(1)}, bf16[1728,128]{1,0:T(8,128)(2,1)}, u32[]{:S(2)}, u32[]{:S(2)}) collective-permute-start(bf16[1728,128]{1,0:T(8,128)(2,1)S(1)} %unpack.3.a), channel_id=1, source_target_pairs={{0,384},{8,392},{16,400},{24,408},{32,416},{40,424},{48,432},{56,4... | collective-permute-start | bytes 1327112 | tf_op jit(solution)/shard_map/ppermute | solution.py:44
  97.5 0.9 copy-start.2
  100.5 19.2 %all-to-all-start.3 = ((bf16[16,54,128]{2,1,0:T(8,128)(2,1)}), bf16[16,54,128]{2,1,0:T(8,128)(2,1)S(1)}, u32[]{:S(2)}, u32[]{:S(2)}) async-start(bf16[16,54,128]{2,1,0:T(8,128)(2,1)} %reshape.24), calls=%async_computation.3 | async-start | bytes 458752 | tf_op jit(solution)/shard_map/all_to_all | solution.py:349
  107.1 25.8 %collective-permute-start.12 = (bf16[1728,128]{1,0:T(8,128)(2,1)S(1)}, bf16[1728,128]{1,0:T(8,128)(2,1)}, u32[]{:S(2)}, u32[]{:S(2)}) collective-permute-start(bf16[1728,128]{1,0:T(8,128)(2,1)S(1)} %unpack.3.a), channel_id=1, source_target_pairs={{0,1},{1,0},{2,3},{3,2},{4,5},{5,4},{6,7},{7,6},{8,9},{9,8},{10,11... | collective-permute-start | bytes 1327112 | tf_op jit(solution)/shard_map/ppermute | solution.py:32
  110.5 22.4 %collective-permute-start.13 = (bf16[1728,128]{1,0:T(8,128)(2,1)S(1)}, bf16[1728,128]{1,0:T(8,128)(2,1)}, u32[]{:S(2)}, u32[]{:S(2)}) collective-permute-start(bf16[1728,128]{1,0:T(8,128)(2,1)S(1)} %collective-permute-done.9.b), channel_id=1, source_target_pairs={{0,1},{1,0},{2,3},{3,2},{4,5},{5,4},{6,7},{7,6},{8,9},{9,8},{10,11... | collective-permute-start | bytes 1327112 | tf_op jit(solution)/shard_map/ppermute | solution.py:32
  114.7 18.3 %collective-permute-start.14 = (bf16[1728,128]{1,0:T(8,128)(2,1)S(1)}, bf16[1728,128]{1,0:T(8,128)(2,1)}, u32[]{:S(2)}, u32[]{:S(2)}) collective-permute-start(bf16[1728,128]{1,0:T(8,128)(2,1)S(1)} %collective-permute-done.10.c), channel_id=1, source_target_pairs={{0,1},{1,0},{2,3},{3,2},{4,5},{5,4},{6,7},{7,6},{8,9},{9,8},{10,11... | collective-permute-start | bytes 1327112 | tf_op jit(solution)/shard_map/ppermute | solution.py:32
  117.8 15.1 %collective-permute-start.15 = (bf16[1728,128]{1,0:T(8,128)(2,1)}, bf16[1728,128]{1,0:T(8,128)(2,1)}, u32[]{:S(2)}, u32[]{:S(2)}) collective-permute-start(bf16[1728,128]{1,0:T(8,128)(2,1)} %collective-permute-done.11.d), channel_id=1, source_target_pairs={{0,1},{1,0},{2,3},{3,2},{4,5},{5,4},{6,7},{7,6},{8,9},{9,8},{10,11... | collective-permute-start | bytes 1327112 | tf_op jit(solution)/shard_map/ppermute | solution.py:32
  120.5 24.2 %all-to-all-start.4 = ((f32[8,54,128]{2,1,0:T(8,128)}), f32[8,54,128]{2,1,0:T(8,128)S(1)}, u32[]{:S(2)}, u32[]{:S(2)}) async-start(f32[8,54,128]{2,1,0:T(8,128)} %broadcast_in_dim.8), calls=%async_computation.4 | async-start | bytes 458752 | tf_op jit(solution)/shard_map/all_to_all | solution.py:28
  132.9 1.1 copy-start.3

commit v6 on v5

--- a/solution.py
+++ b/solution.py
@@ -19,7 +19,7 @@
 ROW_GROUPS = [list(range(8))]
 GAINS_COST = 1 << 36
 UNPACK_COST = 1 << 36
-ASSEMBLE_COST = 1 << 36
+GATE_COST = 1 << 36
 
 
 def spread(block, axis, groups):
@@ -40,7 +40,7 @@
 
 def along_x(block):
     count = lax.axis_size("tm")
-    routes = [[(i, i ^ (mask * 16)) for i in range(count)] for mask in (1, 2, 3)]
+    routes = [[(i, i ^ (mask * 16)) for i in range(count)] for mask in (1, 3, 2)]
     return [block] + [lax.ppermute(block, "tm", route) for route in routes]
 
 
@@ -88,13 +88,13 @@
                 out[k, frames, 7:8] = out[k, frames, 0:1]
 
 
-def place(flags, mask):
-    return pl.ds(pl.multiple_of(flags[5 + mask] * 1728, 64), 1728)
+def place(flags, n):
+    return pl.ds(pl.multiple_of(flags[5 + n] * 1728, 64), 1728)
 
 
 def assemble_kernel(flags, a, b, c, d, out):
-    for mask, block in enumerate((a, b, c, d)):
-        out[place(flags, mask)] = block[...]
+    for n, block in enumerate((a, b, c, d)):
+        out[place(flags, n)] = block[...]
 
 
 def gains_kernel(flags, gain, half, both):
@@ -112,9 +112,10 @@
     out[...] = jnp.concatenate(rows, axis=0).astype(BF)
 
 
-def half_kernel(flags, mid, edge, other, w1, pre, squares, xs):
+def half_kernel(flags, mid, edge, other, a, b, c, d, pre, squares, w1, xs):
     base = 2 - 2 * flags[2]
     fill_all(xs, flags, (mid, edge, other), 0, 6, True)
+    assemble_kernel(flags, a, b, c, d, w1)
     for i in range(3):
         for j in range(3):
             lhs = jnp.concatenate(
@@ -171,9 +172,13 @@
 
 
 def backward_kernel(
-    flags, mid, edge, other, gain, pre, w1_own, w1_other, a, b, c, d, far_a, far_b, far_c, far_d,
-    out, ps, acc, cs, w2_own, w2_other,
+    flags, mid, edge, other, gain, pre, own_in, other_in, a, b, c, d, far_a, far_b, far_c, far_d,
+    out, ps, acc, cs, w2_own, w2_other, w1_own, w1_other, sems,
 ):
+    pairs = ((own_in, w1_own), (other_in, w1_other))
+    copies = [pltpu.make_async_copy(source, to, sems.at[n]) for n, (source, to) in enumerate(pairs)]
+    for copy in copies:
+        copy.start()
     fill_all(cs, flags, (mid, edge, other), 8, 8, False)
     assemble_kernel(flags, a, b, c, d, w2_own)
     assemble_kernel(flags, far_a, far_b, far_c, far_d, w2_other)
@@ -216,6 +221,8 @@
         pre_grad = jnp.where(outside, 0.0, pre_grad)
         pre_grad = halves_in_order(flags, pre_grad).astype(BF).reshape(1, 4, W, C)
         fill_shifts(ps, pre_grad, slice(t, t + 1), 0)
+    for copy in copies:
+        copy.wait()
     for n, (i, j, k) in enumerate(taps):
         lhs = ps[2 - k, 2 - i : 6 - i, 2 - j : 4 - j].reshape(256, C)
         at = n * C
@@ -257,17 +264,29 @@
     return call(unpack_kernel, "unpack", cost, shape, [], block)
 
 
-def assemble(flags, blocks, cost=1):
-    shape = jax.ShapeDtypeStruct((ROWS, HALF), BF)
-    return call(assemble_kernel, "assemble", cost, shape, [], flags, *blocks)
-
-
-def forward_half(flags, field, w1):
+def gate_kernel(flags, out):
+    for n in range(9):
+        out[n] = flags[n]
+
+
+def gate(flags):
+    return pl.pallas_call(
+        gate_kernel,
+        out_shape=jax.ShapeDtypeStruct((9,), jnp.int32),
+        in_specs=[SMEM],
+        out_specs=SMEM,
+        cost_estimate=pl.CostEstimate(flops=GATE_COST, bytes_accessed=1, transcendentals=0),
+        name="gate",
+    )(flags)
+
+
+def forward_half(flags, field, blocks):
     shape = jax.ShapeDtypeStruct((512, HALF), F32)
+    weight = jax.ShapeDtypeStruct((ROWS, HALF), BF)
     scratch = [pltpu.VMEM((3, 6, 8, W, C), BF)]
     return call(
-        half_kernel, "forward_half", 4 * 512 * ROWS * HALF, (shape, shape), scratch,
-        flags, *field, w1,
+        half_kernel, "forward_half", 4 * 512 * ROWS * HALF, (shape, shape, weight), scratch,
+        flags, *field, *blocks,
     )
 
 
@@ -289,25 +308,36 @@
 
 
 def backward(flags, field, gain, pre, w1_own, w1_other, w2_own, w2_other):
-    shape = jax.ShapeDtypeStruct((4, 2, W, C), BF)
-    scratch = [
-        pltpu.VMEM((3, 6, 4, W, C), BF),
-        pltpu.VMEM((768, C), F32),
-        pltpu.VMEM((3, 8, 8, W, C), BF),
-        pltpu.VMEM((ROWS, HALF), BF),
-        pltpu.VMEM((ROWS, HALF), BF),
-    ]
-    return call(
-        backward_kernel, "backward", 2 * 1024 * ROWS * C, shape, scratch,
-        flags, *field, gain, pre, w1_own, w1_other, *w2_own, *w2_other,
-    )
+    weight = pltpu.VMEM((ROWS, HALF), BF)
+    kept = pl.BlockSpec(memory_space=pl.ANY)
+    return pl.pallas_call(
+        backward_kernel,
+        out_shape=jax.ShapeDtypeStruct((4, 2, W, C), BF),
+        in_specs=[SMEM] + [VMEM] * 5 + [kept] * 2 + [VMEM] * 8,
+        out_specs=VMEM,
+        scratch_shapes=[
+            pltpu.VMEM((3, 6, 4, W, C), BF),
+            pltpu.VMEM((768, C), F32),
+            pltpu.VMEM((3, 8, 8, W, C), BF),
+            weight,
+            weight,
+            weight,
+            weight,
+            pltpu.SemaphoreType.DMA((2,)),
+        ],
+        compiler_params=pltpu.CompilerParams(vmem_limit_bytes=32 * 1024 * 1024),
+        cost_estimate=pl.CostEstimate(
+            flops=2 * 1024 * ROWS * C, bytes_accessed=10 << 20, transcendentals=0
+        ),
+        name="backward",
+    )(flags, *field, gain, pre, w1_own, w1_other, *w2_own, *w2_other)
 
 
 def on_device(activations, cotangent, gain, first_weight, second_weight):
     tm, rows = lax.axis_index("tm"), lax.axis_index("rows")
     core, x = rows % 2, tm // 16
     flags = [tm, rows, core, lax.axis_size("tm") - 1, lax.axis_size("rows") - 1]
-    flags = jnp.stack(flags + [x ^ mask for mask in range(4)]).astype(jnp.int32)
+    flags = jnp.stack(flags + [x ^ mask for mask in (0, 1, 3, 2)]).astype(jnp.int32)
 
     pick = lax.broadcasted_iota(jnp.int32, (C, HALF), 0) == (
         2 * lax.broadcasted_iota(jnp.int32, (C, HALF), 1) + core
@@ -331,8 +361,8 @@
 
     w2_block = unpack(spread(after(half2, edge), "tm", YZ_GROUPS))
 
-    w1_own = assemble(flags, w1_blocks, ASSEMBLE_COST)
-    pre_half, squares = forward_half(flags, field, w1_own)
+    behind = gate(after(flags, *w1_blocks))
+    pre_half, squares, w1_own = forward_half(behind, field, w1_blocks)
     squares_other = swap_cores(squares)
     squares_other, w2_block = lax.optimization_barrier((squares_other, w2_block))
     terms = local_terms(flags, pre_half, squares, squares_other, gain_half, field)

time: 147 us -> 142 us (0.966)
  starting transfers between devices: 86.3 us -> 83.5 us
  waiting for transfers between devices: 20.6 us -> 18.6 us
    pallas_call x8 -> x6, Pallas kernels: 25.6 us -> 12.2 us  [call(): pl.pallas_call(kernel, out_shape=out_shape, in_specs=smem + [VMEM] * (len...]
    pallas_call x0 -> x2, Pallas kernels: none -> 12.6 us  [the longest x1 11.4 us: backward(): pl.pallas_call(backward_kernel, out_shape=jax.ShapeDtypeStruct((4, 2, W,...]
    ppermute x6, waiting for transfers between devices: 7.24 us -> 3.97 us  [along_x(): return [block] + [lax.ppermute(block, 'tm', route) for route in routes]]
    all_to_all x2, starting transfers between devices: 18 us -> 14.7 us  [spread(): lax.all_to_all(operand, axis, 0, 0, axis_index_groups=groups, tiled=True)]
    all_to_all x2, waiting for transfers between devices: 0.01 us -> 2.69 us  [spread(): lax.all_to_all(operand, axis, 0, 0, axis_index_groups=groups, tiled=True)]
    ppermute x7, starting transfers between devices: 16.3 us -> 18.9 us  [swap_cores(): lax.ppermute(block, 'rows', [(i, i ^ 1) for i in range(lax.axis_size('row...]
    all_to_all x1, starting transfers between devices: 6.53 us -> 4.41 us  [on_device(): lax.all_to_all(total, 'tm', 0, 0, axis_index_groups=YZ_GROUPS, tiled=True)]
    unnamed x22 -> x28, local copies, waits for them, and re-layouts: 4.49 us -> 5.15 us
where the time goes in v6:
time: 142 us; the launch traced here: 141 us
  starting transfers between devices  83.5 us (59%)
  Pallas kernels  24.8 us (17%)
  waiting for transfers between devices  18.6 us (13%)
  local copies, waits for them, and re-layouts  9.98 us (7%)
  other arithmetic  2.45 us (2%)
    ppermute x6, starting transfers between devices, along_x(): return [block] + [lax.ppermute(block, 'tm', route) for route in routes]  19.1 us
    ppermute x7, starting transfers between devices, swap_cores(): lax.ppermute(block, 'rows', [(i, i ^ 1) for i in range(lax.axis_size('row...  18.9 us
    all_to_all x2, starting transfers between devices, spread(): lax.all_to_all(operand, axis, 0, 0, axis_index_groups=groups, tiled=True)  14.7 us
    pallas_call x6, Pallas kernels, call(): pl.pallas_call(kernel, out_shape=out_shape, in_specs=smem + [VMEM] * (len...  12.2 us
    pallas_call x1, Pallas kernels, backward(): pl.pallas_call(backward_kernel, out_shape=jax.ShapeDtypeStruct((4, 2, W,...  11.4 us
    all_to_all x1, starting transfers between devices, on_device(): lax.all_to_all(operand, 'tm', 0, 0, axis_index_groups=YZ_GROUPS, tiled=True)  9.56 us
    ppermute x2, waiting for transfers between devices, shift(): return lax.ppermute(block, axis, route)  8.77 us
    ppermute x1, starting transfers between devices, beyond_chip(): return lax.ppermute(block, 'rows', route)  7.28 us
  transfers between devices with their start and end apart: 21, of which 6 were waited for; matrix products, arithmetic and copies ran while one was open for 4% of the time, Pallas kernels for 16%

profile of v6, /device:TPU:1, one launch (start us, length us, event | category | flops | bytes accessed | tf_op | source)
XLA Modules:
  0.0 140.7 jit_solution(9484829510567561707)
XLA Ops:
  0.6 0.0 copy-start
  0.7 0.8 copy-done
  1.5 0.1 fusion
  1.6 0.8 broadcast_in_dim.6
  2.4 9.6 %all-to-all-start = ((bf16[16,108,128]{2,1,0:T(8,128)(2,1)}), bf16[16,108,128]{2,1,0:T(8,128)(2,1)S(1)}, u32[]{:S(2)}, u32[]{:S(2)}) async-start(bf16[16,108,128]{2,1,0:T(8,128)(2,1)} %broadcast_in_dim.6), calls=%async_computation | async-start | bytes 917504 | tf_op jit(solution)/shard_map/all_to_all | solution.py:349
  12.0 0.9 fusion.2
  12.9 1.3 collective-permute-start.3
  14.2 4.0 %collective-permute-start.4 = (bf16[2,2,32,256]{3,2,1,0:T(8,128)(2,1)S(1)}, bf16[2,2,32,256]{3,2,1,0:T(8,128)(2,1)S(1)}, u32[]{:S(2)}, u32[]{:S(2)}) collective-permute-start(bf16[2,2,32,256]{3,2,1,0:T(8,128)(2,1)S(1)} %get-tuple-element.40), channel_id=1, source_target_pairs={{0,8},{8,16},{16,24},{24,32},{32,40},{40,48},{48,56},{56,64},{64,7... | collective-permute-start | bytes 196616 | tf_op jit(solution)/shard_map/ppermute | solution.py:38
  18.3 0.1 stack.31.flags
  18.4 0.0 copy-start.10
  18.4 0.7 gains.1
  19.0 1.5 %collective-permute-done.4 = bf16[2,2,32,256]{3,2,1,0:T(8,128)(2,1)S(1)} collective-permute-done((bf16[2,2,32,256]{3,2,1,0:T(8,128)(2,1)S(1)}, bf16[2,2,32,256]{3,2,1,0:T(8,128)(2,1)S(1)}, u32[]{:S(2)}, u32[]{:S(2)}) %collective-permute-start.4) | collective-permute-done | bytes 65568 | tf_op jit(solution)/shard_map/ppermute | solution.py:38
  20.6 7.2 %collective-permute-done.3 = bf16[6,2,32,256]{3,2,1,0:T(8,128)(2,1)S(1)} collective-permute-done((bf16[6,2,32,256]{3,2,1,0:T(8,128)(2,1)S(1)}, bf16[6,2,32,256]{3,2,1,0:T(8,128)(2,1)S(1)}, u32[]{:S(2)}, u32[]{:S(2)}) %collective-permute-start.3) | collective-permute-done | bytes 196640 | tf_op jit(solution)/shard_map/ppermute | solution.py:38
  27.9 0.0 copy-start.11
  27.9 7.3 %collective-permute-start.5 = (bf16[16,2,32,256]{3,2,1,0:T(8,128)(2,1)S(1)}, bf16[16,2,32,256]{3,2,1,0:T(8,128)(2,1)S(1)}, u32[]{:S(2)}, u32[]{:S(2)}) collective-permute-start(bf16[16,2,32,256]{3,2,1,0:T(8,128)(2,1)S(1)} %slice_dynamic-update-slice_fusion.mid), channel_id=1, source_target_pairs={{1,2},{3,4},{5,6},{2,1},{4,3},{6,5},{9,10},{11,12},{13,14},{10,9},... | collective-permute-start | bytes 1572872 | tf_op jit(solution)/shard_map/ppermute | solution.py:50
  35.2 0.1 unpack.2.a
  35.3 3.1 %collective-permute-start = (bf16[1728,128]{1,0:T(8,128)(2,1)S(1)}, bf16[1728,128]{1,0:T(8,128)(2,1)S(1)}, u32[]{:S(2)}, u32[]{:S(2)}) collective-permute-start(bf16[1728,128]{1,0:T(8,128)(2,1)S(1)} %unpack.2.a), channel_id=1, source_target_pairs={{0,128},{8,136},{16,144},{24,152},{32,160},{40,168},{48,176},{56,1... | collective-permute-start | bytes 1327112 | tf_op jit(solution)/shard_map/ppermute | solution.py:44
  38.4 3.7 %collective-permute-start.1 = (bf16[1728,128]{1,0:T(8,128)(2,1)S(1)}, bf16[1728,128]{1,0:T(8,128)(2,1)}, u32[]{:S(2)}, u32[]{:S(2)}) collective-permute-start(bf16[1728,128]{1,0:T(8,128)(2,1)S(1)} %unpack.2.a), channel_id=1, source_target_pairs={{0,384},{8,392},{16,400},{24,408},{32,416},{40,424},{48,432},{56,4... | collective-permute-start | bytes 1327112 | tf_op jit(solution)/shard_map/ppermute | solution.py:44
  42.1 2.7 %collective-permute-start.2 = (bf16[1728,128]{1,0:T(8,128)(2,1)S(1)}, bf16[1728,128]{1,0:T(8,128)(2,1)}, u32[]{:S(2)}, u32[]{:S(2)}) collective-permute-start(bf16[1728,128]{1,0:T(8,128)(2,1)S(1)} %unpack.2.a), channel_id=1, source_target_pairs={{0,256},{8,264},{16,272},{24,280},{32,288},{40,296},{48,304},{56,3... | collective-permute-start | bytes 1327112 | tf_op jit(solution)/shard_map/ppermute | solution.py:44
  44.9 3.2 %collective-permute-done.5.edge = bf16[16,2,32,256]{3,2,1,0:T(8,128)(2,1)S(1)} collective-permute-done((bf16[16,2,32,256]{3,2,1,0:T(8,128)(2,1)S(1)}, bf16[16,2,32,256]{3,2,1,0:T(8,128)(2,1)S(1)}, u32[]{:S(2)}, u32[]{:S(2)}) %collective-permute-start.5) | collective-permute-done | bytes 524320 | tf_op jit(solution)/shard_map/ppermute | solution.py:50
  48.1 1.0 pad_maximum_fusion
  49.1 1.9 %collective-permute-start.6 = (bf16[16,3,32,256]{3,2,1,0:T(8,128)(2,1)}, bf16[16,3,32,256]{3,2,1,0:T(8,128)(2,1)S(1)}, u32[]{:S(2)}, u32[]{:S(2)}) collective-permute-start(bf16[16,3,32,256]{3,2,1,0:T(8,128)(2,1)} %pad_maximum_fusion), channel_id=1, source_target_pairs={{0,1},{1,0},{2,3},{3,2},{4,5},{5,4},{6,7},{7,6},{8,9},{9,8},{10,11... | collective-permute-start | bytes 2359304 | tf_op jit(solution)/shard_map/ppermute | solution.py:32
  51.0 0.8 broadcast_in_dim.7
  51.8 5.6 %all-to-all-start.1 = ((bf16[16,108,128]{2,1,0:T(8,128)(2,1)}), bf16[16,108,128]{2,1,0:T(8,128)(2,1)S(1)}, u32[]{:S(2)}, u32[]{:S(2)}) async-start(bf16[16,108,128]{2,1,0:T(8,128)(2,1)} %broadcast_in_dim.7), calls=%async_computation.1 | async-start | bytes 917504 | tf_op jit(solution)/shard_map/all_to_all | solution.py:28
  57.4 0.0 collective-permute-done.b
  57.4 1.3 collective-permute-done.1.c
  58.7 0.0 collective-permute-done.2.d
  58.7 1.2 gate.1.flags
  59.9 0.0 copy-start.2
  59.9 0.0 collective-permute-done.6.other.others
  60.0 0.0 copy-start.8
  60.0 0.6 copy-done.8
  60.6 3.7 %forward_half.1 = (f32[512,128]{1,0:T(8,128)S(1)}, f32[512,128]{1,0:T(8,128)S(1)}, bf16[6912,128]{1,0:T(8,128)(2,1)}) custom-call(s32[9]{0:T(128)S(1)} %copy-done.8, bf16[16,2,32,256]{3,2,1,0:T(8,128)(2,1)S(1)} %slice_dynamic-update-slice_fusion.mid, bf16[16,2,32,256]{3,2,1,0:T(8,128)(2,1)S(1)} %collective-permute-done.5.edge, ...), custom_call_target="tpu_custom_call" | custom-call | flops 1811939328 | bytes 1048576 | tf_op jit(solution)/shard_map/forward_half/pallas_call | solution.py:244
  64.3 0.7 copy-done.6
  65.0 1.9 %collective-permute-start.7 = (f32[512,128]{1,0:T(8,128)S(1)}, f32[512,128]{1,0:T(8,128)S(1)}, u32[]{:S(2)}, u32[]{:S(2)}) collective-permute-start(f32[512,128]{1,0:T(8,128)S(1)} %get-tuple-element.28.own), channel_id=1, source_target_pairs={{0,1},{1,0},{2,3},{3,2},{4,5},{5,4},{6,7},{7,6},{8,9},{9,8},{10,11... | collective-permute-start | bytes 786440 | tf_op jit(solution)/shard_map/ppermute | solution.py:32
  66.9 2.7 %all-to-all-done.1.block = bf16[16,108,128]{2,1,0:T(8,128)(2,1)S(1)} async-done(((bf16[16,108,128]{2,1,0:T(8,128)(2,1)}), bf16[16,108,128]{2,1,0:T(8,128)(2,1)S(1)}, u32[]{:S(2)}, u32[]{:S(2)}) %all-to-all-start.1) | async-done | bytes 442400 | tf_op jit(solution)/shard_map/all_to_all | solution.py:28
  69.6 0.1 unpack.3.a
  69.6 0.0 collective-permute-done.7.others
  69.7 0.9 copy-done.7
  70.6 2.4 %local_terms.1 = bf16[3456,128]{1,0:T(8,128)(2,1)} custom-call(s32[9]{0:T(128)S(1)} %copy-done.2, f32[512,128]{1,0:T(8,128)S(1)} %copy-done.7, f32[512,128]{1,0:T(8,128)S(1)} %get-tuple-element.28.own, f32[512,128]{1,0:T(8,128)S(1)} %collective-permute-done.7.others, f32[1,128]{1,0:T(1,128)S(1)} %get-tuple-element.24.gain, ...), custom_call_target="tpu_custom_call" | custom-call | flops 1811939328 | bytes 1048576 | tf_op jit(solution)/shard_map/local_terms/pallas_call | solution.py:244
  73.1 4.8 %collective-permute-start.8 = (bf16[6912,128]{1,0:T(8,128)(2,1)}, bf16[6912,128]{1,0:T(8,128)(2,1)}, u32[]{:S(2)}, u32[]{:S(2)}) collective-permute-start(bf16[6912,128]{1,0:T(8,128)(2,1)} %get-tuple-element.32.own.own_in), channel_id=1, source_target_pairs={{0,1},{1,0},{2,3},{3,2},{4,5},{5,4},{6,7},{7,6},{8,9},{9,8},{10,11... | collective-permute-start | bytes 5308424 | tf_op jit(solution)/shard_map/ppermute | solution.py:32
  77.9 4.2 %all-to-all-start.2 = ((bf16[4,864,128]{2,1,0:T(8,128)(2,1)}), bf16[4,864,128]{2,1,0:T(8,128)(2,1)}, u32[]{:S(2)}, u32[]{:S(2)}) async-start(bf16[4,864,128]{2,1,0:T(8,128)(2,1)} %bitcast.9), calls=%async_computation.2 | async-start | bytes 1769472 | tf_op jit(solution)/shard_map/all_to_all | solution.py:370
  82.1 3.3 %collective-permute-start.9 = (bf16[1728,128]{1,0:T(8,128)(2,1)S(1)}, bf16[1728,128]{1,0:T(8,128)(2,1)S(1)}, u32[]{:S(2)}, u32[]{:S(2)}) collective-permute-start(bf16[1728,128]{1,0:T(8,128)(2,1)S(1)} %unpack.3.a), channel_id=1, source_target_pairs={{0,128},{8,136},{16,144},{24,152},{32,160},{40,168},{48,176},{56,1... | collective-permute-start | bytes 1327112 | tf_op jit(solution)/shard_map/ppermute | solution.py:44
  85.5 3.7 %collective-permute-start.10 = (bf16[1728,128]{1,0:T(8,128)(2,1)S(1)}, bf16[1728,128]{1,0:T(8,128)(2,1)S(1)}, u32[]{:S(2)}, u32[]{:S(2)}) collective-permute-start(bf16[1728,128]{1,0:T(8,128)(2,1)S(1)} %unpack.3.a), channel_id=1, source_target_pairs={{0,384},{8,392},{16,400},{24,408},{32,416},{40,424},{48,432},{56,4... | collective-permute-start | bytes 1327112 | tf_op jit(solution)/shard_map/ppermute | solution.py:44
  89.2 2.5 %collective-permute-start.11 = (bf16[1728,128]{1,0:T(8,128)(2,1)S(1)}, bf16[1728,128]{1,0:T(8,128)(2,1)}, u32[]{:S(2)}, u32[]{:S(2)}) collective-permute-start(bf16[1728,128]{1,0:T(8,128)(2,1)S(1)} %unpack.3.a), channel_id=1, source_target_pairs={{0,256},{8,264},{16,272},{24,280},{32,288},{40,296},{48,304},{56,3... | collective-permute-start | bytes 1327112 | tf_op jit(solution)/shard_map/ppermute | solution.py:44
  91.7 0.0 collective-permute-done.8.other.other_in
  91.7 5.3 %forward_all.1.pre = f32[768,256]{1,0:T(8,128)S(1)} custom-call(s32[9]{0:T(128)S(1)} %copy-done.2, bf16[16,2,32,256]{3,2,1,0:T(8,128)(2,1)S(1)} %slice_dynamic-update-slice_fusion.mid, bf16[16,2,32,256]{3,2,1,0:T(8,128)(2,1)S(1)} %collective-permute-done.5.edge, bf16[16,3,32,256]{3,2,1,0:T(8,128)(2,1)S(1)} %collective-permute-done.6.other.others, ...), custom_call_target="tpu_custom_call" | custom-call | flops 2717908992 | bytes 1048576 | tf_op jit(solution)/shard_map/forward_all/pallas_call | solution.py:244
  97.1 0.9 copy-done.4
  98.0 0.0 all-to-all-done.2
  98.0 1.4 reduce_sum.30
  99.3 0.8 reshape.24
  100.1 4.4 %all-to-all-start.3 = ((bf16[16,54,128]{2,1,0:T(8,128)(2,1)}), bf16[16,54,128]{2,1,0:T(8,128)(2,1)S(1)}, u32[]{:S(2)}, u32[]{:S(2)}) async-start(bf16[16,54,128]{2,1,0:T(8,128)(2,1)} %reshape.24), calls=%async_computation.3 | async-start | bytes 458752 | tf_op jit(solution)/shard_map/all_to_all | solution.py:379
  104.5 3.1 %collective-permute-start.12 = (bf16[1728,128]{1,0:T(8,128)(2,1)S(1)}, bf16[1728,128]{1,0:T(8,128)(2,1)}, u32[]{:S(2)}, u32[]{:S(2)}) collective-permute-start(bf16[1728,128]{1,0:T(8,128)(2,1)S(1)} %unpack.3.a), channel_id=1, source_target_pairs={{0,1},{1,0},{2,3},{3,2},{4,5},{5,4},{6,7},{7,6},{8,9},{9,8},{10,11... | collective-permute-start | bytes 1327112 | tf_op jit(solution)/shard_map/ppermute | solution.py:32
  107.7 1.9 %collective-permute-start.13 = (bf16[1728,128]{1,0:T(8,128)(2,1)S(1)}, bf16[1728,128]{1,0:T(8,128)(2,1)}, u32[]{:S(2)}, u32[]{:S(2)}) collective-permute-start(bf16[1728,128]{1,0:T(8,128)(2,1)S(1)} %collective-permute-done.9.b), channel_id=1, source_target_pairs={{0,1},{1,0},{2,3},{3,2},{4,5},{5,4},{6,7},{7,6},{8,9},{9,8},{10,11... | collective-permute-start | bytes 1327112 | tf_op jit(solution)/shard_map/ppermute | solution.py:32
  109.6 2.4 %collective-permute-start.14 = (bf16[1728,128]{1,0:T(8,128)(2,1)S(1)}, bf16[1728,128]{1,0:T(8,128)(2,1)}, u32[]{:S(2)}, u32[]{:S(2)}) collective-permute-start(bf16[1728,128]{1,0:T(8,128)(2,1)S(1)} %collective-permute-done.10.c), channel_id=1, source_target_pairs={{0,1},{1,0},{2,3},{3,2},{4,5},{5,4},{6,7},{7,6},{8,9},{9,8},{10,11... | collective-permute-start | bytes 1327112 | tf_op jit(solution)/shard_map/ppermute | solution.py:32
  112.0 2.6 %collective-permute-done.11.d = bf16[1728,128]{1,0:T(8,128)(2,1)} collective-permute-done((bf16[1728,128]{1,0:T(8,128)(2,1)S(1)}, bf16[1728,128]{1,0:T(8,128)(2,1)}, u32[]{:S(2)}, u32[]{:S(2)}) %collective-permute-start.11) | collective-permute-done | bytes 442400 | tf_op jit(solution)/shard_map/ppermute | solution.py:44
  114.7 2.8 %collective-permute-start.15 = (bf16[1728,128]{1,0:T(8,128)(2,1)}, bf16[1728,128]{1,0:T(8,128)(2,1)}, u32[]{:S(2)}, u32[]{:S(2)}) collective-permute-start(bf16[1728,128]{1,0:T(8,128)(2,1)} %collective-permute-done.11.d), channel_id=1, source_target_pairs={{0,1},{1,0},{2,3},{3,2},{4,5},{5,4},{6,7},{7,6},{8,9},{9,8},{10,11... | collective-permute-start | bytes 1327112 | tf_op jit(solution)/shard_map/ppermute | solution.py:32
  117.4 0.0 all-to-all-done.3
  117.5 0.7 broadcast_in_dim.8
  118.2 9.2 %all-to-all-start.4 = ((f32[8,54,128]{2,1,0:T(8,128)}), f32[8,54,128]{2,1,0:T(8,128)S(1)}, u32[]{:S(2)}, u32[]{:S(2)}) async-start(f32[8,54,128]{2,1,0:T(8,128)} %broadcast_in_dim.8), calls=%async_computation.4 | async-start | bytes 458752 | tf_op jit(solution)/shard_map/all_to_all | solution.py:28
  127.4 0.0 collective-permute-done.12.far_a
  127.4 1.1 copy-done.5
  128.5 11.4 %backward.1 = bf16[4,2,32,256]{3,2,1,0:T(8,128)(2,1)} custom-call(s32[9]{0:T(128)S(1)} %copy-done.2, bf16[16,2,32,256]{3,2,1,0:T(8,128)(2,1)S(1)} %slice_dynamic-update-slice_fusion.mid, bf16[16,2,32,256]{3,2,1,0:T(8,128)(2,1)S(1)} %collective-permute-done.5.edge, bf16[16,3,32,256]{3,2,1,0:T(8,128)(2,1)S(1)} %collective-permute-done.6.other.others, ...), custom_call_target="tpu_custom_call" | custom-call | flops 3623878656 | bytes 10485760 | tf_op jit(solution)/shard_map/backward/pallas_call | solution.py:313
  140.0 0.7 reshape.26
  (32 shorter events, 0.2 us)
Async XLA Ops:
  0.6 0.8 copy-start
  0.6 12.3 %copy-start.9 = (bf16[4,2,32,256]{3,2,1,0:T(8,128)(2,1)S(1)}, bf16[4,2,32,256]{3,2,1,0:T(8,128)(2,1)}, u32[]{:S(2)}) copy-start(bf16[4,2,32,256]{3,2,1,0:T(8,128)(2,1)} %param.6) | copy-start | bytes 393220
  0.7 17.7 %copy-start.3 = (f32[256]{0:T(256)S(1)}, f32[256]{0:T(256)}, u32[]{:S(2)}) copy-start(f32[256]{0:T(256)} %param.7) | copy-start | bytes 3076
  2.4 32.8 %all-to-all-start = ((bf16[16,108,128]{2,1,0:T(8,128)(2,1)}), bf16[16,108,128]{2,1,0:T(8,128)(2,1)S(1)}, u32[]{:S(2)}, u32[]{:S(2)}) async-start(bf16[16,108,128]{2,1,0:T(8,128)(2,1)} %broadcast_in_dim.6), calls=%async_computation | async-start | bytes 917504 | tf_op jit(solution)/shard_map/all_to_all | solution.py:349
  12.9 14.9 %collective-permute-start.3 = (bf16[6,2,32,256]{3,2,1,0:T(8,128)(2,1)S(1)}, bf16[6,2,32,256]{3,2,1,0:T(8,128)(2,1)S(1)}, u32[]{:S(2)}, u32[]{:S(2)}) collective-permute-start(bf16[6,2,32,256]{3,2,1,0:T(8,128)(2,1)S(1)} %pad_maximum_fusion.1), channel_id=1, source_target_pairs={{8,0},{16,8},{24,16},{32,24},{40,32},{48,40},{56,48},{64,56},{72,6... | collective-permute-start | bytes 589832 | tf_op jit(solution)/shard_map/ppermute | solution.py:38
  14.2 6.3 %collective-permute-start.4 = (bf16[2,2,32,256]{3,2,1,0:T(8,128)(2,1)S(1)}, bf16[2,2,32,256]{3,2,1,0:T(8,128)(2,1)S(1)}, u32[]{:S(2)}, u32[]{:S(2)}) collective-permute-start(bf16[2,2,32,256]{3,2,1,0:T(8,128)(2,1)S(1)} %get-tuple-element.40), channel_id=1, source_target_pairs={{0,8},{8,16},{16,24},{24,32},{32,40},{40,48},{48,56},{56,64},{64,7... | collective-permute-start | bytes 196616 | tf_op jit(solution)/shard_map/ppermute | solution.py:38
  18.3 0.7 copy-start.1
  18.4 9.5 %copy-start.10 = (bf16[4,2,32,256]{3,2,1,0:T(8,128)(2,1)S(1)}, bf16[4,2,32,256]{3,2,1,0:T(8,128)(2,1)}, u32[]{:S(2)}) copy-start(bf16[4,2,32,256]{3,2,1,0:T(8,128)(2,1)} %param.5) | copy-start | bytes 393220
  27.9 17.0 %copy-start.11 = (bf16[108,256]{1,0:T(8,128)(2,1)S(1)}, bf16[108,256]{1,0:T(8,128)(2,1)}, u32[]{:S(2)}) copy-start(bf16[108,256]{1,0:T(8,128)(2,1)} %param.9) | copy-start | bytes 165892
  27.9 20.2 %collective-permute-start.5 = (bf16[16,2,32,256]{3,2,1,0:T(8,128)(2,1)S(1)}, bf16[16,2,32,256]{3,2,1,0:T(8,128)(2,1)S(1)}, u32[]{:S(2)}, u32[]{:S(2)}) collective-permute-start(bf16[16,2,32,256]{3,2,1,0:T(8,128)(2,1)S(1)} %slice_dynamic-update-slice_fusion.mid), channel_id=1, source_target_pairs={{1,2},{3,4},{5,6},{2,1},{4,3},{6,5},{9,10},{11,12},{13,14},{10,9},... | collective-permute-start | bytes 1572872 | tf_op jit(solution)/shard_map/ppermute | solution.py:50
  35.3 22.1 %collective-permute-start = (bf16[1728,128]{1,0:T(8,128)(2,1)S(1)}, bf16[1728,128]{1,0:T(8,128)(2,1)S(1)}, u32[]{:S(2)}, u32[]{:S(2)}) collective-permute-start(bf16[1728,128]{1,0:T(8,128)(2,1)S(1)} %unpack.2.a), channel_id=1, source_target_pairs={{0,128},{8,136},{16,144},{24,152},{32,160},{40,168},{48,176},{56,1... | collective-permute-start | bytes 1327112 | tf_op jit(solution)/shard_map/ppermute | solution.py:44
  38.4 20.3 %collective-permute-start.1 = (bf16[1728,128]{1,0:T(8,128)(2,1)S(1)}, bf16[1728,128]{1,0:T(8,128)(2,1)}, u32[]{:S(2)}, u32[]{:S(2)}) collective-permute-start(bf16[1728,128]{1,0:T(8,128)(2,1)S(1)} %unpack.2.a), channel_id=1, source_target_pairs={{0,384},{8,392},{16,400},{24,408},{32,416},{40,424},{48,432},{56,4... | collective-permute-start | bytes 1327112 | tf_op jit(solution)/shard_map/ppermute | solution.py:44
  42.1 16.6 %collective-permute-start.2 = (bf16[1728,128]{1,0:T(8,128)(2,1)S(1)}, bf16[1728,128]{1,0:T(8,128)(2,1)}, u32[]{:S(2)}, u32[]{:S(2)}) collective-permute-start(bf16[1728,128]{1,0:T(8,128)(2,1)S(1)} %unpack.2.a), channel_id=1, source_target_pairs={{0,256},{8,264},{16,272},{24,280},{32,288},{40,296},{48,304},{56,3... | collective-permute-start | bytes 1327112 | tf_op jit(solution)/shard_map/ppermute | solution.py:44
  49.1 10.9 %collective-permute-start.6 = (bf16[16,3,32,256]{3,2,1,0:T(8,128)(2,1)}, bf16[16,3,32,256]{3,2,1,0:T(8,128)(2,1)S(1)}, u32[]{:S(2)}, u32[]{:S(2)}) collective-permute-start(bf16[16,3,32,256]{3,2,1,0:T(8,128)(2,1)} %pad_maximum_fusion), channel_id=1, source_target_pairs={{0,1},{1,0},{2,3},{3,2},{4,5},{5,4},{6,7},{7,6},{8,9},{9,8},{10,11... | collective-permute-start | bytes 2359304 | tf_op jit(solution)/shard_map/ppermute | solution.py:32
  51.8 17.8 %all-to-all-start.1 = ((bf16[16,108,128]{2,1,0:T(8,128)(2,1)}), bf16[16,108,128]{2,1,0:T(8,128)(2,1)S(1)}, u32[]{:S(2)}, u32[]{:S(2)}) async-start(bf16[16,108,128]{2,1,0:T(8,128)(2,1)} %broadcast_in_dim.7), calls=%async_computation.1 | async-start | bytes 917504 | tf_op jit(solution)/shard_map/all_to_all | solution.py:28
  59.9 9.7 %copy-start.2 = (s32[9]{0:T(128)S(1)}, s32[9]{0:T(128)}, u32[]{:S(2)}) copy-start(s32[9]{0:T(128)} %copy-done.1) | copy-start | bytes 112
  60.0 0.7 copy-start.8
  64.3 0.7 copy-start.6
  65.0 4.7 %collective-permute-start.7 = (f32[512,128]{1,0:T(8,128)S(1)}, f32[512,128]{1,0:T(8,128)S(1)}, u32[]{:S(2)}, u32[]{:S(2)}) collective-permute-start(f32[512,128]{1,0:T(8,128)S(1)} %get-tuple-element.28.own), channel_id=1, source_target_pairs={{0,1},{1,0},{2,3},{3,2},{4,5},{5,4},{6,7},{7,6},{8,9},{9,8},{10,11... | collective-permute-start | bytes 786440 | tf_op jit(solution)/shard_map/ppermute | solution.py:32
  69.7 1.0 copy-start.7
  73.1 18.7 %collective-permute-start.8 = (bf16[6912,128]{1,0:T(8,128)(2,1)}, bf16[6912,128]{1,0:T(8,128)(2,1)}, u32[]{:S(2)}, u32[]{:S(2)}) collective-permute-start(bf16[6912,128]{1,0:T(8,128)(2,1)} %get-tuple-element.32.own.own_in), channel_id=1, source_target_pairs={{0,1},{1,0},{2,3},{3,2},{4,5},{5,4},{6,7},{7,6},{8,9},{9,8},{10,11... | collective-permute-start | bytes 5308424 | tf_op jit(solution)/shard_map/ppermute | solution.py:32
  77.9 20.1 %all-to-all-start.2 = ((bf16[4,864,128]{2,1,0:T(8,128)(2,1)}), bf16[4,864,128]{2,1,0:T(8,128)(2,1)}, u32[]{:S(2)}, u32[]{:S(2)}) async-start(bf16[4,864,128]{2,1,0:T(8,128)(2,1)} %bitcast.9), calls=%async_computation.2 | async-start | bytes 1769472 | tf_op jit(solution)/shard_map/all_to_all | solution.py:370
  82.1 25.5 %collective-permute-start.9 = (bf16[1728,128]{1,0:T(8,128)(2,1)S(1)}, bf16[1728,128]{1,0:T(8,128)(2,1)S(1)}, u32[]{:S(2)}, u32[]{:S(2)}) collective-permute-start(bf16[1728,128]{1,0:T(8,128)(2,1)S(1)} %unpack.3.a), channel_id=1, source_target_pairs={{0,128},{8,136},{16,144},{24,152},{32,160},{40,168},{48,176},{56,1... | collective-permute-start | bytes 1327112 | tf_op jit(solution)/shard_map/ppermute | solution.py:44
  85.5 24.1 %collective-permute-start.10 = (bf16[1728,128]{1,0:T(8,128)(2,1)S(1)}, bf16[1728,128]{1,0:T(8,128)(2,1)S(1)}, u32[]{:S(2)}, u32[]{:S(2)}) collective-permute-start(bf16[1728,128]{1,0:T(8,128)(2,1)S(1)} %unpack.3.a), channel_id=1, source_target_pairs={{0,384},{8,392},{16,400},{24,408},{32,416},{40,424},{48,432},{56,4... | collective-permute-start | bytes 1327112 | tf_op jit(solution)/shard_map/ppermute | solution.py:44
  89.2 25.5 %collective-permute-start.11 = (bf16[1728,128]{1,0:T(8,128)(2,1)S(1)}, bf16[1728,128]{1,0:T(8,128)(2,1)}, u32[]{:S(2)}, u32[]{:S(2)}) collective-permute-start(bf16[1728,128]{1,0:T(8,128)(2,1)S(1)} %unpack.3.a), channel_id=1, source_target_pairs={{0,256},{8,264},{16,272},{24,280},{32,288},{40,296},{48,304},{56,3... | collective-permute-start | bytes 1327112 | tf_op jit(solution)/shard_map/ppermute | solution.py:44
  97.1 0.9 copy-start.4
  100.1 17.4 %all-to-all-start.3 = ((bf16[16,54,128]{2,1,0:T(8,128)(2,1)}), bf16[16,54,128]{2,1,0:T(8,128)(2,1)S(1)}, u32[]{:S(2)}, u32[]{:S(2)}) async-start(bf16[16,54,128]{2,1,0:T(8,128)(2,1)} %reshape.24), calls=%async_computation.3 | async-start | bytes 458752 | tf_op jit(solution)/shard_map/all_to_all | solution.py:379
  104.5 22.9 %collective-permute-start.12 = (bf16[1728,128]{1,0:T(8,128)(2,1)S(1)}, bf16[1728,128]{1,0:T(8,128)(2,1)}, u32[]{:S(2)}, u32[]{:S(2)}) collective-permute-start(bf16[1728,128]{1,0:T(8,128)(2,1)S(1)} %unpack.3.a), channel_id=1, source_target_pairs={{0,1},{1,0},{2,3},{3,2},{4,5},{5,4},{6,7},{7,6},{8,9},{9,8},{10,11... | collective-permute-start | bytes 1327112 | tf_op jit(solution)/shard_map/ppermute | solution.py:32
  107.7 19.7 %collective-permute-start.13 = (bf16[1728,128]{1,0:T(8,128)(2,1)S(1)}, bf16[1728,128]{1,0:T(8,128)(2,1)}, u32[]{:S(2)}, u32[]{:S(2)}) collective-permute-start(bf16[1728,128]{1,0:T(8,128)(2,1)S(1)} %collective-permute-done.9.b), channel_id=1, source_target_pairs={{0,1},{1,0},{2,3},{3,2},{4,5},{5,4},{6,7},{7,6},{8,9},{9,8},{10,11... | collective-permute-start | bytes 1327112 | tf_op jit(solution)/shard_map/ppermute | solution.py:32
  109.6 17.8 %collective-permute-start.14 = (bf16[1728,128]{1,0:T(8,128)(2,1)S(1)}, bf16[1728,128]{1,0:T(8,128)(2,1)}, u32[]{:S(2)}, u32[]{:S(2)}) collective-permute-start(bf16[1728,128]{1,0:T(8,128)(2,1)S(1)} %collective-permute-done.10.c), channel_id=1, source_target_pairs={{0,1},{1,0},{2,3},{3,2},{4,5},{5,4},{6,7},{7,6},{8,9},{9,8},{10,11... | collective-permute-start | bytes 1327112 | tf_op jit(solution)/shard_map/ppermute | solution.py:32
  114.7 12.7 %collective-permute-start.15 = (bf16[1728,128]{1,0:T(8,128)(2,1)}, bf16[1728,128]{1,0:T(8,128)(2,1)}, u32[]{:S(2)}, u32[]{:S(2)}) collective-permute-start(bf16[1728,128]{1,0:T(8,128)(2,1)} %collective-permute-done.11.d), channel_id=1, source_target_pairs={{0,1},{1,0},{2,3},{3,2},{4,5},{5,4},{6,7},{7,6},{8,9},{9,8},{10,11... | collective-permute-start | bytes 1327112 | tf_op jit(solution)/shard_map/ppermute | solution.py:32
  118.2 21.7 %all-to-all-start.4 = ((f32[8,54,128]{2,1,0:T(8,128)}), f32[8,54,128]{2,1,0:T(8,128)S(1)}, u32[]{:S(2)}, u32[]{:S(2)}) async-start(f32[8,54,128]{2,1,0:T(8,128)} %broadcast_in_dim.8), calls=%async_computation.4 | async-start | bytes 458752 | tf_op jit(solution)/shard_map/all_to_all | solution.py:28
  127.4 1.1 copy-start.5

commit v7 on v6

--- a/solution.py
+++ b/solution.py
@@ -112,7 +112,14 @@
     out[...] = jnp.concatenate(rows, axis=0).astype(BF)
 
 
-def half_kernel(flags, mid, edge, other, a, b, c, d, pre, squares, w1, xs):
+def sum_kernel(terms, out):
+    total = terms[0].astype(F32) + terms[1].astype(F32)
+    total = (total + terms[2].astype(F32)) + terms[3].astype(F32)
+    for n in range(16):
+        out[n] = total[n * 54 : n * 54 + 54].astype(BF)
+
+
+def half_kernel(flags, gated, mid, edge, other, a, b, c, d, pre, squares, w1, xs):
     base = 2 - 2 * flags[2]
     fill_all(xs, flags, (mid, edge, other), 0, 6, True)
     assemble_kernel(flags, a, b, c, d, w1)
@@ -172,13 +179,11 @@
 
 
 def backward_kernel(
-    flags, mid, edge, other, gain, pre, own_in, other_in, a, b, c, d, far_a, far_b, far_c, far_d,
-    out, ps, acc, cs, w2_own, w2_other, w1_own, w1_other, sems,
+    flags, mid, edge, other, gain, pre_in, w1_own, w1_other, a, b, c, d, far_a, far_b, far_c, far_d,
+    out, ps, acc, cs, w2_own, w2_other, pre, sem,
 ):
-    pairs = ((own_in, w1_own), (other_in, w1_other))
-    copies = [pltpu.make_async_copy(source, to, sems.at[n]) for n, (source, to) in enumerate(pairs)]
-    for copy in copies:
-        copy.start()
+    copy = pltpu.make_async_copy(pre_in, pre, sem)
+    copy.start()
     fill_all(cs, flags, (mid, edge, other), 8, 8, False)
     assemble_kernel(flags, a, b, c, d, w2_own)
     assemble_kernel(flags, far_a, far_b, far_c, far_d, w2_other)
@@ -193,6 +198,7 @@
             acc[...] = part
         else:
             acc[...] += part
+    copy.wait()
     row = lax.broadcasted_iota(jnp.int32, (C, C), 0)
     col = lax.broadcasted_iota(jnp.int32, (C, C), 1)
     source = jnp.where(col < HALF, 2 * col, 2 * (col - HALF) + 1)
@@ -221,8 +227,6 @@
         pre_grad = jnp.where(outside, 0.0, pre_grad)
         pre_grad = halves_in_order(flags, pre_grad).astype(BF).reshape(1, 4, W, C)
         fill_shifts(ps, pre_grad, slice(t, t + 1), 0)
-    for copy in copies:
-        copy.wait()
     for n, (i, j, k) in enumerate(taps):
         lhs = ps[2 - k, 2 - i : 6 - i, 2 - j : 4 - j].reshape(256, C)
         at = n * C
@@ -264,29 +268,27 @@
     return call(unpack_kernel, "unpack", cost, shape, [], block)
 
 
-def gate_kernel(flags, out):
-    for n in range(9):
-        out[n] = flags[n]
-
-
-def gate(flags):
-    return pl.pallas_call(
-        gate_kernel,
-        out_shape=jax.ShapeDtypeStruct((9,), jnp.int32),
-        in_specs=[SMEM],
-        out_specs=SMEM,
-        cost_estimate=pl.CostEstimate(flops=GATE_COST, bytes_accessed=1, transcendentals=0),
-        name="gate",
-    )(flags)
-
-
-def forward_half(flags, field, blocks):
+def gate_kernel(value, out):
+    out[...] = value[...]
+
+
+def gate(value):
+    shape = jax.ShapeDtypeStruct(value.shape, value.dtype)
+    return call(gate_kernel, "gate", GATE_COST, shape, [], value)
+
+
+def sum_terms(terms):
+    shape = jax.ShapeDtypeStruct((16, 54, CH), BF)
+    return call(sum_kernel, "sum_terms", 1 << 20, shape, [], terms)
+
+
+def forward_half(flags, gated, field, blocks):
     shape = jax.ShapeDtypeStruct((512, HALF), F32)
     weight = jax.ShapeDtypeStruct((ROWS, HALF), BF)
     scratch = [pltpu.VMEM((3, 6, 8, W, C), BF)]
     return call(
         half_kernel, "forward_half", 4 * 512 * ROWS * HALF, (shape, shape, weight), scratch,
-        flags, *field, *blocks,
+        flags, gated, *field, *blocks,
     )
 
 
@@ -313,7 +315,7 @@
     return pl.pallas_call(
         backward_kernel,
         out_shape=jax.ShapeDtypeStruct((4, 2, W, C), BF),
-        in_specs=[SMEM] + [VMEM] * 5 + [kept] * 2 + [VMEM] * 8,
+        in_specs=[SMEM] + [VMEM] * 4 + [kept] + [VMEM] * 10,
         out_specs=VMEM,
         scratch_shapes=[
             pltpu.VMEM((3, 6, 4, W, C), BF),
@@ -321,9 +323,8 @@
             pltpu.VMEM((3, 8, 8, W, C), BF),
             weight,
             weight,
-            weight,
-            weight,
-            pltpu.SemaphoreType.DMA((2,)),
+            pltpu.VMEM((768, C), F32),
+            pltpu.SemaphoreType.DMA,
         ],
         compiler_params=pltpu.CompilerParams(vmem_limit_bytes=32 * 1024 * 1024),
         cost_estimate=pl.CostEstimate(
@@ -361,8 +362,8 @@
 
     w2_block = unpack(spread(after(half2, edge), "tm", YZ_GROUPS))
 
-    behind = gate(after(flags, *w1_blocks))
-    pre_half, squares, w1_own = forward_half(behind, field, w1_blocks)
+    gated = gate(after(gain_all, *w1_blocks))
+    pre_half, squares, w1_own = forward_half(flags, gated, field, w1_blocks)
     squares_other = swap_cores(squares)
     squares_other, w2_block = lax.optimization_barrier((squares_other, w2_block))
     terms = local_terms(flags, pre_half, squares, squares_other, gain_half, field)
@@ -375,8 +376,7 @@
     pre = forward_all(flags, field, w1_own, w1_other)
     total, pre = lax.optimization_barrier((total, pre))
 
-    total = total.astype(F32).sum(0).astype(BF).reshape(16, 54, CH)
-    total = lax.all_to_all(total, "tm", 0, 0, axis_index_groups=YZ_GROUPS, tiled=True)
+    total = lax.all_to_all(sum_terms(total), "tm", 0, 0, axis_index_groups=YZ_GROUPS, tiled=True)
     w2_far = [swap_cores(block) for block in w2_blocks]
     input_grad = backward(flags, field, gain_all, pre, w1_own, w1_other, w2_blocks, w2_far)
     total = spread(total.astype(F32).sum(0), "rows", ROW_GROUPS)

time: 142 us -> 141 us (level)
  waiting for transfers between devices: 18.6 us -> 21.2 us
  local copies, waits for them, and re-layouts: 9.98 us -> 8.56 us
    all_to_all x2, waiting for transfers between devices: 2.69 us -> 4.42 us  [spread(): lax.all_to_all(operand, axis, 0, 0, axis_index_groups=groups, tiled=True)]
    pallas_call x6 -> x8, Pallas kernels: 12.2 us -> 13.2 us  [call(): pl.pallas_call(kernel, out_shape=out_shape, in_specs=smem + [VMEM] * (len...]
    unnamed x28 -> x22, local copies, waits for them, and re-layouts: 5.15 us -> 4.49 us
  transfers between devices with their start and end apart: 21 -> 21, of which waited for: 6 -> 6; matrix products, arithmetic and copies ran while one was open for 4% -> 3% of each run, Pallas kernels for 16% -> 15%
where the time goes in v7:
time: 141 us; the launch traced here: 140 us
  starting transfers between devices  83.8 us (59%)
  Pallas kernels  24.1 us (17%)
  waiting for transfers between devices  21.2 us (15%)
  local copies, waits for them, and re-layouts  8.56 us (6%)
    ppermute x7, starting transfers between devices, swap_cores(): lax.ppermute(block, 'rows', [(i, i ^ 1) for i in range(lax.axis_size('row...  19.3 us
    ppermute x6, starting transfers between devices, along_x(): return [block] + [lax.ppermute(block, 'tm', route) for route in routes]  19.1 us
    all_to_all x2, starting transfers between devices, spread(): lax.all_to_all(operand, axis, 0, 0, axis_index_groups=groups, tiled=True)  14.8 us
    pallas_call x8, Pallas kernels, call(): pl.pallas_call(kernel, out_shape=out_shape, in_specs=smem + [VMEM] * (len...  13.2 us
    pallas_call x1, Pallas kernels, backward(): pl.pallas_call(backward_kernel, out_shape=jax.ShapeDtypeStruct((4, 2, W,...  10.9 us
    all_to_all x1, starting transfers between devices, on_device(): lax.all_to_all(operand, 'tm', 0, 0, axis_index_groups=YZ_GROUPS, tiled=True)  9.56 us
    ppermute x2, waiting for transfers between devices, shift(): return lax.ppermute(block, axis, route)  8.78 us
    ppermute x1, starting transfers between devices, beyond_chip(): return lax.ppermute(block, 'rows', route)  7.28 us
  transfers between devices with their start and end apart: 21, of which 6 were waited for; matrix products, arithmetic and copies ran while one was open for 3% of the time, Pallas kernels for 15%

profile of v7, /device:TPU:1, one launch (start us, length us, event | category | flops | bytes accessed | tf_op | source)
XLA Modules:
  0.0 140.0 jit_solution(12475026166014401029)
XLA Ops:
  0.6 0.0 copy-start
  0.7 0.8 copy-done
  1.5 0.1 fusion
  1.6 0.8 broadcast_in_dim.6
  2.4 9.6 %all-to-all-start = ((bf16[16,108,128]{2,1,0:T(8,128)(2,1)}), bf16[16,108,128]{2,1,0:T(8,128)(2,1)S(1)}, u32[]{:S(2)}, u32[]{:S(2)}) async-start(bf16[16,108,128]{2,1,0:T(8,128)(2,1)} %broadcast_in_dim.6), calls=%async_computation | async-start | bytes 917504 | tf_op jit(solution)/shard_map/all_to_all | solution.py:350
  12.0 0.9 fusion.2
  12.9 1.3 collective-permute-start.3
  14.2 4.0 %collective-permute-start.4 = (bf16[2,2,32,256]{3,2,1,0:T(8,128)(2,1)S(1)}, bf16[2,2,32,256]{3,2,1,0:T(8,128)(2,1)S(1)}, u32[]{:S(2)}, u32[]{:S(2)}) collective-permute-start(bf16[2,2,32,256]{3,2,1,0:T(8,128)(2,1)S(1)} %get-tuple-element.40), channel_id=1, source_target_pairs={{0,8},{8,16},{16,24},{24,32},{32,40},{40,48},{48,56},{56,64},{64,7... | collective-permute-start | bytes 196616 | tf_op jit(solution)/shard_map/ppermute | solution.py:38
  18.3 0.1 stack.31.flags
  18.3 0.0 copy-start.7
  18.4 0.7 gains.1
  19.0 1.5 %collective-permute-done.4 = bf16[2,2,32,256]{3,2,1,0:T(8,128)(2,1)S(1)} collective-permute-done((bf16[2,2,32,256]{3,2,1,0:T(8,128)(2,1)S(1)}, bf16[2,2,32,256]{3,2,1,0:T(8,128)(2,1)S(1)}, u32[]{:S(2)}, u32[]{:S(2)}) %collective-permute-start.4) | collective-permute-done | bytes 65568 | tf_op jit(solution)/shard_map/ppermute | solution.py:38
  20.6 7.2 %collective-permute-done.3 = bf16[6,2,32,256]{3,2,1,0:T(8,128)(2,1)S(1)} collective-permute-done((bf16[6,2,32,256]{3,2,1,0:T(8,128)(2,1)S(1)}, bf16[6,2,32,256]{3,2,1,0:T(8,128)(2,1)S(1)}, u32[]{:S(2)}, u32[]{:S(2)}) %collective-permute-start.3) | collective-permute-done | bytes 196640 | tf_op jit(solution)/shard_map/ppermute | solution.py:38
  27.9 0.0 copy-start.8
  27.9 7.3 %collective-permute-start.5 = (bf16[16,2,32,256]{3,2,1,0:T(8,128)(2,1)S(1)}, bf16[16,2,32,256]{3,2,1,0:T(8,128)(2,1)S(1)}, u32[]{:S(2)}, u32[]{:S(2)}) collective-permute-start(bf16[16,2,32,256]{3,2,1,0:T(8,128)(2,1)S(1)} %slice_dynamic-update-slice_fusion.mid), channel_id=1, source_target_pairs={{1,2},{3,4},{5,6},{2,1},{4,3},{6,5},{9,10},{11,12},{13,14},{10,9},... | collective-permute-start | bytes 1572872 | tf_op jit(solution)/shard_map/ppermute | solution.py:50
  35.2 0.0 all-to-all-done.block
  35.2 0.1 unpack.2.a
  35.3 3.1 %collective-permute-start = (bf16[1728,128]{1,0:T(8,128)(2,1)S(1)}, bf16[1728,128]{1,0:T(8,128)(2,1)}, u32[]{:S(2)}, u32[]{:S(2)}) collective-permute-start(bf16[1728,128]{1,0:T(8,128)(2,1)S(1)} %unpack.2.a), channel_id=1, source_target_pairs={{0,128},{8,136},{16,144},{24,152},{32,160},{40,168},{48,176},{56,1... | collective-permute-start | bytes 1327112 | tf_op jit(solution)/shard_map/ppermute | solution.py:44
  38.4 3.7 %collective-permute-start.1 = (bf16[1728,128]{1,0:T(8,128)(2,1)S(1)}, bf16[1728,128]{1,0:T(8,128)(2,1)}, u32[]{:S(2)}, u32[]{:S(2)}) collective-permute-start(bf16[1728,128]{1,0:T(8,128)(2,1)S(1)} %unpack.2.a), channel_id=1, source_target_pairs={{0,384},{8,392},{16,400},{24,408},{32,416},{40,424},{48,432},{56,4... | collective-permute-start | bytes 1327112 | tf_op jit(solution)/shard_map/ppermute | solution.py:44
  42.1 2.7 %collective-permute-start.2 = (bf16[1728,128]{1,0:T(8,128)(2,1)S(1)}, bf16[1728,128]{1,0:T(8,128)(2,1)}, u32[]{:S(2)}, u32[]{:S(2)}) collective-permute-start(bf16[1728,128]{1,0:T(8,128)(2,1)S(1)} %unpack.2.a), channel_id=1, source_target_pairs={{0,256},{8,264},{16,272},{24,280},{32,288},{40,296},{48,304},{56,3... | collective-permute-start | bytes 1327112 | tf_op jit(solution)/shard_map/ppermute | solution.py:44
  44.9 3.2 %collective-permute-done.5.edge = bf16[16,2,32,256]{3,2,1,0:T(8,128)(2,1)S(1)} collective-permute-done((bf16[16,2,32,256]{3,2,1,0:T(8,128)(2,1)S(1)}, bf16[16,2,32,256]{3,2,1,0:T(8,128)(2,1)S(1)}, u32[]{:S(2)}, u32[]{:S(2)}) %collective-permute-start.5) | collective-permute-done | bytes 524320 | tf_op jit(solution)/shard_map/ppermute | solution.py:50
  48.1 1.0 pad_maximum_fusion
  49.1 1.9 %collective-permute-start.6 = (bf16[16,3,32,256]{3,2,1,0:T(8,128)(2,1)}, bf16[16,3,32,256]{3,2,1,0:T(8,128)(2,1)S(1)}, u32[]{:S(2)}, u32[]{:S(2)}) collective-permute-start(bf16[16,3,32,256]{3,2,1,0:T(8,128)(2,1)} %pad_maximum_fusion), channel_id=1, source_target_pairs={{0,1},{1,0},{2,3},{3,2},{4,5},{5,4},{6,7},{7,6},{8,9},{9,8},{10,11... | collective-permute-start | bytes 2359304 | tf_op jit(solution)/shard_map/ppermute | solution.py:32
  51.0 0.8 broadcast_in_dim.7
  51.8 5.6 %all-to-all-start.1 = ((bf16[16,108,128]{2,1,0:T(8,128)(2,1)}), bf16[16,108,128]{2,1,0:T(8,128)(2,1)S(1)}, u32[]{:S(2)}, u32[]{:S(2)}) async-start(bf16[16,108,128]{2,1,0:T(8,128)(2,1)} %broadcast_in_dim.7), calls=%async_computation.1 | async-start | bytes 917504 | tf_op jit(solution)/shard_map/all_to_all | solution.py:28
  57.4 0.0 collective-permute-done.b
  57.4 1.3 collective-permute-done.1.c
  58.7 0.0 collective-permute-done.2.d
  58.7 0.0 collective-permute-done.6.other.others
  58.7 3.8 %forward_half.1 = (f32[512,128]{1,0:T(8,128)S(1)}, f32[512,128]{1,0:T(8,128)S(1)}, bf16[6912,128]{1,0:T(8,128)(2,1)}) custom-call(s32[9]{0:T(128)S(1)} %stack.31.flags, f32[1,256]{1,0:T(1,128)S(1)} %gate.1.gated, bf16[16,2,32,256]{3,2,1,0:T(8,128)(2,1)S(1)} %slice_dynamic-update-slice_fusion.mid, bf16[16,2,32,256]{3,2,1,0:T(8,128)(2,1)S(1)} %collective-permute-done.5.edge, ...), custom_call_target="tpu_custom_call" | custom-call | flops 1811939328 | bytes 1048576 | tf_op jit(solution)/shard_map/forward_half/pallas_call | solution.py:248
  62.5 0.7 copy-done.4
  63.2 1.9 %collective-permute-start.7 = (f32[512,128]{1,0:T(8,128)S(1)}, f32[512,128]{1,0:T(8,128)S(1)}, u32[]{:S(2)}, u32[]{:S(2)}) collective-permute-start(f32[512,128]{1,0:T(8,128)S(1)} %get-tuple-element.29.own), channel_id=1, source_target_pairs={{0,1},{1,0},{2,3},{3,2},{4,5},{5,4},{6,7},{7,6},{8,9},{9,8},{10,11... | collective-permute-start | bytes 786440 | tf_op jit(solution)/shard_map/ppermute | solution.py:32
  65.2 4.4 %all-to-all-done.1.block = bf16[16,108,128]{2,1,0:T(8,128)(2,1)S(1)} async-done(((bf16[16,108,128]{2,1,0:T(8,128)(2,1)}), bf16[16,108,128]{2,1,0:T(8,128)(2,1)S(1)}, u32[]{:S(2)}, u32[]{:S(2)}) %all-to-all-start.1) | async-done | bytes 442400 | tf_op jit(solution)/shard_map/all_to_all | solution.py:28
  69.6 0.1 unpack.3.a
  69.6 0.0 collective-permute-done.7.others
  69.7 0.9 copy-done.5
  70.6 2.4 %local_terms.1 = bf16[3456,128]{1,0:T(8,128)(2,1)} custom-call(s32[9]{0:T(128)S(1)} %stack.31.flags, f32[512,128]{1,0:T(8,128)S(1)} %copy-done.5, f32[512,128]{1,0:T(8,128)S(1)} %get-tuple-element.29.own, f32[512,128]{1,0:T(8,128)S(1)} %collective-permute-done.7.others, f32[1,128]{1,0:T(1,128)S(1)} %get-tuple-element.25.gain, ...), custom_call_target="tpu_custom_call" | custom-call | flops 1811939328 | bytes 1048576 | tf_op jit(solution)/shard_map/local_terms/pallas_call | solution.py:248
  73.0 4.8 %collective-permute-start.8 = (bf16[6912,128]{1,0:T(8,128)(2,1)}, bf16[6912,128]{1,0:T(8,128)(2,1)}, u32[]{:S(2)}, u32[]{:S(2)}) collective-permute-start(bf16[6912,128]{1,0:T(8,128)(2,1)} %get-tuple-element.33.own.w1_own), channel_id=1, source_target_pairs={{0,1},{1,0},{2,3},{3,2},{4,5},{5,4},{6,7},{7,6},{8,9},{9,8},{10,11... | collective-permute-start | bytes 5308424 | tf_op jit(solution)/shard_map/ppermute | solution.py:32
  77.9 4.0 %all-to-all-start.2 = ((bf16[4,864,128]{2,1,0:T(8,128)(2,1)}), bf16[4,864,128]{2,1,0:T(8,128)(2,1)S(1)}, u32[]{:S(2)}, u32[]{:S(2)}) async-start(bf16[4,864,128]{2,1,0:T(8,128)(2,1)} %bitcast.9), calls=%async_computation.2 | async-start | bytes 1769472 | tf_op jit(solution)/shard_map/all_to_all | solution.py:371
  81.9 3.4 %collective-permute-start.9 = (bf16[1728,128]{1,0:T(8,128)(2,1)S(1)}, bf16[1728,128]{1,0:T(8,128)(2,1)}, u32[]{:S(2)}, u32[]{:S(2)}) collective-permute-start(bf16[1728,128]{1,0:T(8,128)(2,1)S(1)} %unpack.3.a), channel_id=1, source_target_pairs={{0,128},{8,136},{16,144},{24,152},{32,160},{40,168},{48,176},{56,1... | collective-permute-start | bytes 1327112 | tf_op jit(solution)/shard_map/ppermute | solution.py:44
  85.3 3.7 %collective-permute-start.10 = (bf16[1728,128]{1,0:T(8,128)(2,1)S(1)}, bf16[1728,128]{1,0:T(8,128)(2,1)}, u32[]{:S(2)}, u32[]{:S(2)}) collective-permute-start(bf16[1728,128]{1,0:T(8,128)(2,1)S(1)} %unpack.3.a), channel_id=1, source_target_pairs={{0,384},{8,392},{16,400},{24,408},{32,416},{40,424},{48,432},{56,4... | collective-permute-start | bytes 1327112 | tf_op jit(solution)/shard_map/ppermute | solution.py:44
  89.0 2.5 %collective-permute-start.11 = (bf16[1728,128]{1,0:T(8,128)(2,1)S(1)}, bf16[1728,128]{1,0:T(8,128)(2,1)}, u32[]{:S(2)}, u32[]{:S(2)}) collective-permute-start(bf16[1728,128]{1,0:T(8,128)(2,1)S(1)} %unpack.3.a), channel_id=1, source_target_pairs={{0,256},{8,264},{16,272},{24,280},{32,288},{40,296},{48,304},{56,3... | collective-permute-start | bytes 1327112 | tf_op jit(solution)/shard_map/ppermute | solution.py:44
  91.5 0.0 collective-permute-done.8.other.w1_other
  91.5 5.3 %forward_all.1.pre_in = f32[768,256]{1,0:T(8,128)S(1)} custom-call(s32[9]{0:T(128)S(1)} %stack.31.flags, bf16[16,2,32,256]{3,2,1,0:T(8,128)(2,1)S(1)} %slice_dynamic-update-slice_fusion.mid, bf16[16,2,32,256]{3,2,1,0:T(8,128)(2,1)S(1)} %collective-permute-done.5.edge, bf16[16,3,32,256]{3,2,1,0:T(8,128)(2,1)S(1)} %collective-permute-done.6.other.others, ...), custom_call_target="tpu_custom_call" | custom-call | flops 2717908992 | bytes 1048576 | tf_op jit(solution)/shard_map/forward_all/pallas_call | solution.py:248
  96.9 0.9 copy-done.2
  97.7 0.0 all-to-all-done.2.terms
  97.8 0.9 sum_terms.1
  98.6 4.4 %all-to-all-start.3 = ((bf16[16,54,128]{2,1,0:T(8,128)(2,1)}), bf16[16,54,128]{2,1,0:T(8,128)(2,1)S(1)}, u32[]{:S(2)}, u32[]{:S(2)}) async-start(bf16[16,54,128]{2,1,0:T(8,128)(2,1)} %sum_terms.1), calls=%async_computation.3 | async-start | bytes 458752 | tf_op jit(solution)/shard_map/all_to_all | solution.py:379
  103.0 3.3 %collective-permute-start.12 = (bf16[1728,128]{1,0:T(8,128)(2,1)S(1)}, bf16[1728,128]{1,0:T(8,128)(2,1)S(1)}, u32[]{:S(2)}, u32[]{:S(2)}) collective-permute-start(bf16[1728,128]{1,0:T(8,128)(2,1)S(1)} %unpack.3.a), channel_id=1, source_target_pairs={{0,1},{1,0},{2,3},{3,2},{4,5},{5,4},{6,7},{7,6},{8,9},{9,8},{10,11... | collective-permute-start | bytes 1327112 | tf_op jit(solution)/shard_map/ppermute | solution.py:32
  106.4 0.0 collective-permute-done.9.b
  106.4 1.9 %collective-permute-start.13 = (bf16[1728,128]{1,0:T(8,128)(2,1)}, bf16[1728,128]{1,0:T(8,128)(2,1)S(1)}, u32[]{:S(2)}, u32[]{:S(2)}) collective-permute-start(bf16[1728,128]{1,0:T(8,128)(2,1)} %collective-permute-done.9.b), channel_id=1, source_target_pairs={{0,1},{1,0},{2,3},{3,2},{4,5},{5,4},{6,7},{7,6},{8,9},{9,8},{10,11... | collective-permute-start | bytes 1327112 | tf_op jit(solution)/shard_map/ppermute | solution.py:32
  108.3 0.0 collective-permute-done.10.c
  108.3 2.4 %collective-permute-start.14 = (bf16[1728,128]{1,0:T(8,128)(2,1)}, bf16[1728,128]{1,0:T(8,128)(2,1)}, u32[]{:S(2)}, u32[]{:S(2)}) collective-permute-start(bf16[1728,128]{1,0:T(8,128)(2,1)} %collective-permute-done.10.c), channel_id=1, source_target_pairs={{0,1},{1,0},{2,3},{3,2},{4,5},{5,4},{6,7},{7,6},{8,9},{9,8},{10,11... | collective-permute-start | bytes 1327112 | tf_op jit(solution)/shard_map/ppermute | solution.py:32
  110.7 3.5 %collective-permute-done.11.d = bf16[1728,128]{1,0:T(8,128)(2,1)} collective-permute-done((bf16[1728,128]{1,0:T(8,128)(2,1)S(1)}, bf16[1728,128]{1,0:T(8,128)(2,1)}, u32[]{:S(2)}, u32[]{:S(2)}) %collective-permute-start.11) | collective-permute-done | bytes 442400 | tf_op jit(solution)/shard_map/ppermute | solution.py:44
  114.2 3.0 %collective-permute-start.15 = (bf16[1728,128]{1,0:T(8,128)(2,1)}, bf16[1728,128]{1,0:T(8,128)(2,1)}, u32[]{:S(2)}, u32[]{:S(2)}) collective-permute-start(bf16[1728,128]{1,0:T(8,128)(2,1)} %collective-permute-done.11.d), channel_id=1, source_target_pairs={{0,1},{1,0},{2,3},{3,2},{4,5},{5,4},{6,7},{7,6},{8,9},{9,8},{10,11... | collective-permute-start | bytes 1327112 | tf_op jit(solution)/shard_map/ppermute | solution.py:32
  117.2 0.0 all-to-all-done.3
  117.3 0.7 broadcast_in_dim.8
  118.0 9.2 %all-to-all-start.4 = ((f32[8,54,128]{2,1,0:T(8,128)}), f32[8,54,128]{2,1,0:T(8,128)S(1)}, u32[]{:S(2)}, u32[]{:S(2)}) async-start(f32[8,54,128]{2,1,0:T(8,128)} %broadcast_in_dim.8), calls=%async_computation.4 | async-start | bytes 458752 | tf_op jit(solution)/shard_map/all_to_all | solution.py:28
  127.2 0.0 collective-permute-done.12.far_a
  127.2 0.0 collective-permute-done.14.far_c
  127.2 0.0 collective-permute-done.15.far_d
  127.2 1.1 copy-done.3
  128.4 10.9 %backward.1 = bf16[4,2,32,256]{3,2,1,0:T(8,128)(2,1)} custom-call(s32[9]{0:T(128)S(1)} %stack.31.flags, bf16[16,2,32,256]{3,2,1,0:T(8,128)(2,1)S(1)} %slice_dynamic-update-slice_fusion.mid, bf16[16,2,32,256]{3,2,1,0:T(8,128)(2,1)S(1)} %collective-permute-done.5.edge, bf16[16,3,32,256]{3,2,1,0:T(8,128)(2,1)S(1)} %collective-permute-done.6.other.others, ...), custom_call_target="tpu_custom_call" | custom-call | flops 3623878656 | bytes 10485760 | tf_op jit(solution)/shard_map/backward/pallas_call | solution.py:315
  139.4 0.7 reshape.22
  (25 shorter events, 0.2 us)
Async XLA Ops:
  0.6 0.8 copy-start
  0.6 12.3 %copy-start.6 = (bf16[4,2,32,256]{3,2,1,0:T(8,128)(2,1)S(1)}, bf16[4,2,32,256]{3,2,1,0:T(8,128)(2,1)}, u32[]{:S(2)}) copy-start(bf16[4,2,32,256]{3,2,1,0:T(8,128)(2,1)} %param.6) | copy-start | bytes 393220
  0.7 17.7 %copy-start.1 = (f32[256]{0:T(256)S(1)}, f32[256]{0:T(256)}, u32[]{:S(2)}) copy-start(f32[256]{0:T(256)} %param.7) | copy-start | bytes 3076
  2.4 32.8 %all-to-all-start = ((bf16[16,108,128]{2,1,0:T(8,128)(2,1)}), bf16[16,108,128]{2,1,0:T(8,128)(2,1)S(1)}, u32[]{:S(2)}, u32[]{:S(2)}) async-start(bf16[16,108,128]{2,1,0:T(8,128)(2,1)} %broadcast_in_dim.6), calls=%async_computation | async-start | bytes 917504 | tf_op jit(solution)/shard_map/all_to_all | solution.py:350
  12.9 14.9 %collective-permute-start.3 = (bf16[6,2,32,256]{3,2,1,0:T(8,128)(2,1)S(1)}, bf16[6,2,32,256]{3,2,1,0:T(8,128)(2,1)S(1)}, u32[]{:S(2)}, u32[]{:S(2)}) collective-permute-start(bf16[6,2,32,256]{3,2,1,0:T(8,128)(2,1)S(1)} %pad_maximum_fusion.1), channel_id=1, source_target_pairs={{8,0},{16,8},{24,16},{32,24},{40,32},{48,40},{56,48},{64,56},{72,6... | collective-permute-start | bytes 589832 | tf_op jit(solution)/shard_map/ppermute | solution.py:38
  14.2 6.3 %collective-permute-start.4 = (bf16[2,2,32,256]{3,2,1,0:T(8,128)(2,1)S(1)}, bf16[2,2,32,256]{3,2,1,0:T(8,128)(2,1)S(1)}, u32[]{:S(2)}, u32[]{:S(2)}) collective-permute-start(bf16[2,2,32,256]{3,2,1,0:T(8,128)(2,1)S(1)} %get-tuple-element.40), channel_id=1, source_target_pairs={{0,8},{8,16},{16,24},{24,32},{32,40},{40,48},{48,56},{56,64},{64,7... | collective-permute-start | bytes 196616 | tf_op jit(solution)/shard_map/ppermute | solution.py:38
  18.3 9.5 %copy-start.7 = (bf16[4,2,32,256]{3,2,1,0:T(8,128)(2,1)S(1)}, bf16[4,2,32,256]{3,2,1,0:T(8,128)(2,1)}, u32[]{:S(2)}) copy-start(bf16[4,2,32,256]{3,2,1,0:T(8,128)(2,1)} %param.5) | copy-start | bytes 393220
  27.9 17.0 %copy-start.8 = (bf16[108,256]{1,0:T(8,128)(2,1)S(1)}, bf16[108,256]{1,0:T(8,128)(2,1)}, u32[]{:S(2)}) copy-start(bf16[108,256]{1,0:T(8,128)(2,1)} %param.9) | copy-start | bytes 165892
  27.9 20.2 %collective-permute-start.5 = (bf16[16,2,32,256]{3,2,1,0:T(8,128)(2,1)S(1)}, bf16[16,2,32,256]{3,2,1,0:T(8,128)(2,1)S(1)}, u32[]{:S(2)}, u32[]{:S(2)}) collective-permute-start(bf16[16,2,32,256]{3,2,1,0:T(8,128)(2,1)S(1)} %slice_dynamic-update-slice_fusion.mid), channel_id=1, source_target_pairs={{1,2},{3,4},{5,6},{2,1},{4,3},{6,5},{9,10},{11,12},{13,14},{10,9},... | collective-permute-start | bytes 1572872 | tf_op jit(solution)/shard_map/ppermute | solution.py:50
  35.3 22.1 %collective-permute-start = (bf16[1728,128]{1,0:T(8,128)(2,1)S(1)}, bf16[1728,128]{1,0:T(8,128)(2,1)}, u32[]{:S(2)}, u32[]{:S(2)}) collective-permute-start(bf16[1728,128]{1,0:T(8,128)(2,1)S(1)} %unpack.2.a), channel_id=1, source_target_pairs={{0,128},{8,136},{16,144},{24,152},{32,160},{40,168},{48,176},{56,1... | collective-permute-start | bytes 1327112 | tf_op jit(solution)/shard_map/ppermute | solution.py:44
  38.4 20.3 %collective-permute-start.1 = (bf16[1728,128]{1,0:T(8,128)(2,1)S(1)}, bf16[1728,128]{1,0:T(8,128)(2,1)}, u32[]{:S(2)}, u32[]{:S(2)}) collective-permute-start(bf16[1728,128]{1,0:T(8,128)(2,1)S(1)} %unpack.2.a), channel_id=1, source_target_pairs={{0,384},{8,392},{16,400},{24,408},{32,416},{40,424},{48,432},{56,4... | collective-permute-start | bytes 1327112 | tf_op jit(solution)/shard_map/ppermute | solution.py:44
  42.1 16.6 %collective-permute-start.2 = (bf16[1728,128]{1,0:T(8,128)(2,1)S(1)}, bf16[1728,128]{1,0:T(8,128)(2,1)}, u32[]{:S(2)}, u32[]{:S(2)}) collective-permute-start(bf16[1728,128]{1,0:T(8,128)(2,1)S(1)} %unpack.2.a), channel_id=1, source_target_pairs={{0,256},{8,264},{16,272},{24,280},{32,288},{40,296},{48,304},{56,3... | collective-permute-start | bytes 1327112 | tf_op jit(solution)/shard_map/ppermute | solution.py:44
  49.1 9.7 %collective-permute-start.6 = (bf16[16,3,32,256]{3,2,1,0:T(8,128)(2,1)}, bf16[16,3,32,256]{3,2,1,0:T(8,128)(2,1)S(1)}, u32[]{:S(2)}, u32[]{:S(2)}) collective-permute-start(bf16[16,3,32,256]{3,2,1,0:T(8,128)(2,1)} %pad_maximum_fusion), channel_id=1, source_target_pairs={{0,1},{1,0},{2,3},{3,2},{4,5},{5,4},{6,7},{7,6},{8,9},{9,8},{10,11... | collective-permute-start | bytes 2359304 | tf_op jit(solution)/shard_map/ppermute | solution.py:32
  51.8 17.8 %all-to-all-start.1 = ((bf16[16,108,128]{2,1,0:T(8,128)(2,1)}), bf16[16,108,128]{2,1,0:T(8,128)(2,1)S(1)}, u32[]{:S(2)}, u32[]{:S(2)}) async-start(bf16[16,108,128]{2,1,0:T(8,128)(2,1)} %broadcast_in_dim.7), calls=%async_computation.1 | async-start | bytes 917504 | tf_op jit(solution)/shard_map/all_to_all | solution.py:28
  62.5 0.7 copy-start.4
  63.2 6.4 %collective-permute-start.7 = (f32[512,128]{1,0:T(8,128)S(1)}, f32[512,128]{1,0:T(8,128)S(1)}, u32[]{:S(2)}, u32[]{:S(2)}) collective-permute-start(f32[512,128]{1,0:T(8,128)S(1)} %get-tuple-element.29.own), channel_id=1, source_target_pairs={{0,1},{1,0},{2,3},{3,2},{4,5},{5,4},{6,7},{7,6},{8,9},{9,8},{10,11... | collective-permute-start | bytes 786440 | tf_op jit(solution)/shard_map/ppermute | solution.py:32
  69.7 1.0 copy-start.5
  73.0 18.5 %collective-permute-start.8 = (bf16[6912,128]{1,0:T(8,128)(2,1)}, bf16[6912,128]{1,0:T(8,128)(2,1)}, u32[]{:S(2)}, u32[]{:S(2)}) collective-permute-start(bf16[6912,128]{1,0:T(8,128)(2,1)} %get-tuple-element.33.own.w1_own), channel_id=1, source_target_pairs={{0,1},{1,0},{2,3},{3,2},{4,5},{5,4},{6,7},{7,6},{8,9},{9,8},{10,11... | collective-permute-start | bytes 5308424 | tf_op jit(solution)/shard_map/ppermute | solution.py:32
  77.9 19.9 %all-to-all-start.2 = ((bf16[4,864,128]{2,1,0:T(8,128)(2,1)}), bf16[4,864,128]{2,1,0:T(8,128)(2,1)S(1)}, u32[]{:S(2)}, u32[]{:S(2)}) async-start(bf16[4,864,128]{2,1,0:T(8,128)(2,1)} %bitcast.9), calls=%async_computation.2 | async-start | bytes 1769472 | tf_op jit(solution)/shard_map/all_to_all | solution.py:371
  81.9 24.4 %collective-permute-start.9 = (bf16[1728,128]{1,0:T(8,128)(2,1)S(1)}, bf16[1728,128]{1,0:T(8,128)(2,1)}, u32[]{:S(2)}, u32[]{:S(2)}) collective-permute-start(bf16[1728,128]{1,0:T(8,128)(2,1)S(1)} %unpack.3.a), channel_id=1, source_target_pairs={{0,128},{8,136},{16,144},{24,152},{32,160},{40,168},{48,176},{56,1... | collective-permute-start | bytes 1327112 | tf_op jit(solution)/shard_map/ppermute | solution.py:44
  85.3 23.0 %collective-permute-start.10 = (bf16[1728,128]{1,0:T(8,128)(2,1)S(1)}, bf16[1728,128]{1,0:T(8,128)(2,1)}, u32[]{:S(2)}, u32[]{:S(2)}) collective-permute-start(bf16[1728,128]{1,0:T(8,128)(2,1)S(1)} %unpack.3.a), channel_id=1, source_target_pairs={{0,384},{8,392},{16,400},{24,408},{32,416},{40,424},{48,432},{56,4... | collective-permute-start | bytes 1327112 | tf_op jit(solution)/shard_map/ppermute | solution.py:44
  89.0 25.2 %collective-permute-start.11 = (bf16[1728,128]{1,0:T(8,128)(2,1)S(1)}, bf16[1728,128]{1,0:T(8,128)(2,1)}, u32[]{:S(2)}, u32[]{:S(2)}) collective-permute-start(bf16[1728,128]{1,0:T(8,128)(2,1)S(1)} %unpack.3.a), channel_id=1, source_target_pairs={{0,256},{8,264},{16,272},{24,280},{32,288},{40,296},{48,304},{56,3... | collective-permute-start | bytes 1327112 | tf_op jit(solution)/shard_map/ppermute | solution.py:44
  96.8 0.9 copy-start.2
  98.6 18.6 %all-to-all-start.3 = ((bf16[16,54,128]{2,1,0:T(8,128)(2,1)}), bf16[16,54,128]{2,1,0:T(8,128)(2,1)S(1)}, u32[]{:S(2)}, u32[]{:S(2)}) async-start(bf16[16,54,128]{2,1,0:T(8,128)(2,1)} %sum_terms.1), calls=%async_computation.3 | async-start | bytes 458752 | tf_op jit(solution)/shard_map/all_to_all | solution.py:379
  103.0 24.2 %collective-permute-start.12 = (bf16[1728,128]{1,0:T(8,128)(2,1)S(1)}, bf16[1728,128]{1,0:T(8,128)(2,1)S(1)}, u32[]{:S(2)}, u32[]{:S(2)}) collective-permute-start(bf16[1728,128]{1,0:T(8,128)(2,1)S(1)} %unpack.3.a), channel_id=1, source_target_pairs={{0,1},{1,0},{2,3},{3,2},{4,5},{5,4},{6,7},{7,6},{8,9},{9,8},{10,11... | collective-permute-start | bytes 1327112 | tf_op jit(solution)/shard_map/ppermute | solution.py:32
  106.4 20.8 %collective-permute-start.13 = (bf16[1728,128]{1,0:T(8,128)(2,1)}, bf16[1728,128]{1,0:T(8,128)(2,1)S(1)}, u32[]{:S(2)}, u32[]{:S(2)}) collective-permute-start(bf16[1728,128]{1,0:T(8,128)(2,1)} %collective-permute-done.9.b), channel_id=1, source_target_pairs={{0,1},{1,0},{2,3},{3,2},{4,5},{5,4},{6,7},{7,6},{8,9},{9,8},{10,11... | collective-permute-start | bytes 1327112 | tf_op jit(solution)/shard_map/ppermute | solution.py:32
  108.3 18.9 %collective-permute-start.14 = (bf16[1728,128]{1,0:T(8,128)(2,1)}, bf16[1728,128]{1,0:T(8,128)(2,1)}, u32[]{:S(2)}, u32[]{:S(2)}) collective-permute-start(bf16[1728,128]{1,0:T(8,128)(2,1)} %collective-permute-done.10.c), channel_id=1, source_target_pairs={{0,1},{1,0},{2,3},{3,2},{4,5},{5,4},{6,7},{7,6},{8,9},{9,8},{10,11... | collective-permute-start | bytes 1327112 | tf_op jit(solution)/shard_map/ppermute | solution.py:32
  114.2 13.0 %collective-permute-start.15 = (bf16[1728,128]{1,0:T(8,128)(2,1)}, bf16[1728,128]{1,0:T(8,128)(2,1)}, u32[]{:S(2)}, u32[]{:S(2)}) collective-permute-start(bf16[1728,128]{1,0:T(8,128)(2,1)} %collective-permute-done.11.d), channel_id=1, source_target_pairs={{0,1},{1,0},{2,3},{3,2},{4,5},{5,4},{6,7},{7,6},{8,9},{9,8},{10,11... | collective-permute-start | bytes 1327112 | tf_op jit(solution)/shard_map/ppermute | solution.py:32
  118.0 21.3 %all-to-all-start.4 = ((f32[8,54,128]{2,1,0:T(8,128)}), f32[8,54,128]{2,1,0:T(8,128)S(1)}, u32[]{:S(2)}, u32[]{:S(2)}) async-start(f32[8,54,128]{2,1,0:T(8,128)} %broadcast_in_dim.8), calls=%async_computation.4 | async-start | bytes 458752 | tf_op jit(solution)/shard_map/all_to_all | solution.py:28
  127.2 1.1 copy-start.3

commit v8 on v7

--- a/solution.py
+++ b/solution.py
@@ -360,18 +360,17 @@
     next_row = jnp.where(core == 0, edge[:, 1:], edge[:, :1])
     field = (mid, edge, swap_cores(jnp.concatenate([mid, next_row], axis=1)))
 
-    w2_block = unpack(spread(after(half2, edge), "tm", YZ_GROUPS))
-
-    gated = gate(after(gain_all, *w1_blocks))
+    w2_block = unpack(spread(after(half2, mid, w1_blocks[0]), "tm", YZ_GROUPS))
+
+    gated = gate(after(gain_all, w2_block, *w1_blocks))
     pre_half, squares, w1_own = forward_half(flags, gated, field, w1_blocks)
     squares_other = swap_cores(squares)
-    squares_other, w2_block = lax.optimization_barrier((squares_other, w2_block))
     terms = local_terms(flags, pre_half, squares, squares_other, gain_half, field)
 
     total = lax.all_to_all(
         terms.reshape(4, 864, CH), "tm", 0, 0, axis_index_groups=X_GROUPS, tiled=True
     )
-    w1_other = swap_cores(after(w1_own, terms))
+    w1_other = swap_cores(after(w1_own, squares))
     w2_blocks = along_x(after(w2_block, terms))
     pre = forward_all(flags, field, w1_own, w1_other)
     total, pre = lax.optimization_barrier((total, pre))

time: 141 us -> 144 us (1.021)
  starting transfers between devices: 83.8 us -> 86.1 us
  local copies, waits for them, and re-layouts: 8.56 us -> 7.06 us
    ppermute x6, waiting for transfers between devices: 4.82 us -> 11.9 us  [along_x(): return [block] + [lax.ppermute(block, 'tm', route) for route in routes]]
    all_to_all x2, waiting for transfers between devices: 4.42 us -> 0.01 us  [spread(): lax.all_to_all(operand, axis, 0, 0, axis_index_groups=groups, tiled=True)]
    all_to_all x1, starting transfers between devices: 4.41 us -> 7.83 us  [on_device(): lax.all_to_all(sum_terms(total), 'tm', 0, 0, axis_index_groups=YZ_GROUPS,...]
    ppermute x1, waiting for transfers between devices: 3.19 us -> 0.01 us  [beyond_chip(): return lax.ppermute(block, 'rows', route)]
    ppermute x7, starting transfers between devices: 19.3 us -> 16.6 us  [swap_cores(): lax.ppermute(block, 'rows', [(i, i ^ 1) for i in range(lax.axis_size('row...]
    all_to_all x2, starting transfers between devices: 14.8 us -> 17.2 us  [spread(): lax.all_to_all(operand, axis, 0, 0, axis_index_groups=groups, tiled=True)]
    ppermute x7, waiting for transfers between devices: 0.02 us -> 1.63 us  [swap_cores(): lax.ppermute(block, 'rows', [(i, i ^ 1) for i in range(lax.axis_size('row...]
    unnamed x22 -> x18, local copies, waits for them, and re-layouts: 4.49 us -> 2.99 us
  transfers between devices with their start and end apart: 21 -> 21, of which waited for: 6 -> 5; matrix products, arithmetic and copies ran while one was open for 3% -> 3% of each run, Pallas kernels for 15% -> 15%
where the time goes in v8:
time: 144 us; the launch traced here: 143 us
  starting transfers between devices  86.1 us (60%)
  Pallas kernels  25 us (17%)
  waiting for transfers between devices  22.1 us (15%)
  local copies, waits for them, and re-layouts  7.06 us (5%)
    ppermute x6, starting transfers between devices, along_x(): return [block] + [lax.ppermute(block, 'tm', route) for route in routes]  19 us
    all_to_all x2, starting transfers between devices, spread(): lax.all_to_all(operand, axis, 0, 0, axis_index_groups=groups, tiled=True)  17.2 us
    ppermute x7, starting transfers between devices, swap_cores(): lax.ppermute(block, 'rows', [(i, i ^ 1) for i in range(lax.axis_size('row...  16.6 us
    pallas_call x8, Pallas kernels, call(): pl.pallas_call(kernel, out_shape=out_shape, in_specs=smem + [VMEM] * (len...  14.1 us
    ppermute x6, waiting for transfers between devices, along_x(): return [block] + [lax.ppermute(block, 'tm', route) for route in routes]  11.9 us
    pallas_call x1, Pallas kernels, backward(): pl.pallas_call(backward_kernel, out_shape=jax.ShapeDtypeStruct((4, 2, W,...  10.9 us
    all_to_all x1, starting transfers between devices, on_device(): lax.all_to_all(operand, 'tm', 0, 0, axis_index_groups=YZ_GROUPS, tiled=True)  9.56 us
    ppermute x2, waiting for transfers between devices, shift(): return lax.ppermute(block, axis, route)  8.64 us
  transfers between devices with their start and end apart: 21, of which 5 were waited for; matrix products, arithmetic and copies ran while one was open for 3% of the time, Pallas kernels for 15%

profile of v8, /device:TPU:1, one launch (start us, length us, event | category | flops | bytes accessed | tf_op | source)
XLA Modules:
  0.0 142.6 jit_solution(17035784980072436927)
XLA Ops:
  0.6 0.0 copy-start
  0.7 0.8 copy-done
  1.5 0.1 fusion
  1.6 0.8 broadcast_in_dim.6
  2.4 9.6 %all-to-all-start = ((bf16[16,108,128]{2,1,0:T(8,128)(2,1)}), bf16[16,108,128]{2,1,0:T(8,128)(2,1)S(1)}, u32[]{:S(2)}, u32[]{:S(2)}) async-start(bf16[16,108,128]{2,1,0:T(8,128)(2,1)} %broadcast_in_dim.6), calls=%async_computation | async-start | bytes 917504 | tf_op jit(solution)/shard_map/all_to_all | solution.py:350
  12.0 0.9 fusion.2
  12.9 1.3 collective-permute-start
  14.2 4.0 %collective-permute-start.1 = (bf16[2,2,32,256]{3,2,1,0:T(8,128)(2,1)S(1)}, bf16[2,2,32,256]{3,2,1,0:T(8,128)(2,1)S(1)}, u32[]{:S(2)}, u32[]{:S(2)}) collective-permute-start(bf16[2,2,32,256]{3,2,1,0:T(8,128)(2,1)S(1)} %get-tuple-element.36), channel_id=1, source_target_pairs={{0,8},{8,16},{16,24},{24,32},{32,40},{40,48},{48,56},{56,64},{64,7... | collective-permute-start | bytes 196616 | tf_op jit(solution)/shard_map/ppermute | solution.py:38
  18.3 0.1 stack.31.flags
  18.3 0.0 copy-start.6
  18.4 0.0 copy-start.5
  18.4 0.7 gains.1
  19.0 0.1 copy-done.6
  19.2 1.4 collective-permute-done.1
  20.6 7.2 %collective-permute-done = bf16[6,2,32,256]{3,2,1,0:T(8,128)(2,1)S(1)} collective-permute-done((bf16[6,2,32,256]{3,2,1,0:T(8,128)(2,1)S(1)}, bf16[6,2,32,256]{3,2,1,0:T(8,128)(2,1)S(1)}, u32[]{:S(2)}, u32[]{:S(2)}) %collective-permute-start) | collective-permute-done | bytes 196640 | tf_op jit(solution)/shard_map/ppermute | solution.py:38
  27.9 7.1 %collective-permute-start.5 = (bf16[16,2,32,256]{3,2,1,0:T(8,128)(2,1)S(1)}, bf16[16,2,32,256]{3,2,1,0:T(8,128)(2,1)S(1)}, u32[]{:S(2)}, u32[]{:S(2)}) collective-permute-start(bf16[16,2,32,256]{3,2,1,0:T(8,128)(2,1)S(1)} %slice_dynamic-update-slice_fusion.mid), channel_id=1, source_target_pairs={{1,2},{3,4},{5,6},{2,1},{4,3},{6,5},{9,10},{11,12},{13,14},{10,9},... | collective-permute-start | bytes 1572872 | tf_op jit(solution)/shard_map/ppermute | solution.py:50
  35.1 0.0 all-to-all-done.block
  35.1 0.8 unpack.2.a
  35.9 0.9 broadcast_in_dim.7
  36.8 6.5 %all-to-all-start.1 = ((bf16[16,108,128]{2,1,0:T(8,128)(2,1)}), bf16[16,108,128]{2,1,0:T(8,128)(2,1)S(1)}, u32[]{:S(2)}, u32[]{:S(2)}) async-start(bf16[16,108,128]{2,1,0:T(8,128)(2,1)} %broadcast_in_dim.7), calls=%async_computation.1 | async-start | bytes 917504 | tf_op jit(solution)/shard_map/all_to_all | solution.py:28
  43.2 3.1 %collective-permute-start.2 = (bf16[1728,128]{1,0:T(8,128)(2,1)}, bf16[1728,128]{1,0:T(8,128)(2,1)}, u32[]{:S(2)}, u32[]{:S(2)}) collective-permute-start(bf16[1728,128]{1,0:T(8,128)(2,1)} %unpack.2.a), channel_id=1, source_target_pairs={{0,128},{8,136},{16,144},{24,152},{32,160},{40,168},{48,176},{56,1... | collective-permute-start | bytes 1327112 | tf_op jit(solution)/shard_map/ppermute | solution.py:44
  46.4 3.7 %collective-permute-start.3 = (bf16[1728,128]{1,0:T(8,128)(2,1)}, bf16[1728,128]{1,0:T(8,128)(2,1)}, u32[]{:S(2)}, u32[]{:S(2)}) collective-permute-start(bf16[1728,128]{1,0:T(8,128)(2,1)} %unpack.2.a), channel_id=1, source_target_pairs={{0,384},{8,392},{16,400},{24,408},{32,416},{40,424},{48,432},{56,4... | collective-permute-start | bytes 1327112 | tf_op jit(solution)/shard_map/ppermute | solution.py:44
  50.1 2.6 %collective-permute-start.4 = (bf16[1728,128]{1,0:T(8,128)(2,1)}, bf16[1728,128]{1,0:T(8,128)(2,1)}, u32[]{:S(2)}, u32[]{:S(2)}) collective-permute-start(bf16[1728,128]{1,0:T(8,128)(2,1)} %unpack.2.a), channel_id=1, source_target_pairs={{0,256},{8,264},{16,272},{24,280},{32,288},{40,296},{48,304},{56,3... | collective-permute-start | bytes 1327112 | tf_op jit(solution)/shard_map/ppermute | solution.py:44
  52.7 0.0 collective-permute-done.5.edge
  52.7 1.0 pad_maximum_fusion
  53.7 1.9 %collective-permute-start.6 = (bf16[16,3,32,256]{3,2,1,0:T(8,128)(2,1)}, bf16[16,3,32,256]{3,2,1,0:T(8,128)(2,1)S(1)}, u32[]{:S(2)}, u32[]{:S(2)}) collective-permute-start(bf16[16,3,32,256]{3,2,1,0:T(8,128)(2,1)} %pad_maximum_fusion), channel_id=1, source_target_pairs={{0,1},{1,0},{2,3},{3,2},{4,5},{5,4},{6,7},{7,6},{8,9},{9,8},{10,11... | collective-permute-start | bytes 2359304 | tf_op jit(solution)/shard_map/ppermute | solution.py:32
  55.6 0.0 all-to-all-done.1.block
  55.6 0.1 unpack.3.a
  55.7 0.0 collective-permute-done.2.b
  55.7 11.5 %collective-permute-done.3.c = bf16[1728,128]{1,0:T(8,128)(2,1)} collective-permute-done((bf16[1728,128]{1,0:T(8,128)(2,1)}, bf16[1728,128]{1,0:T(8,128)(2,1)}, u32[]{:S(2)}, u32[]{:S(2)}) %collective-permute-start.3) | collective-permute-done | bytes 442400 | tf_op jit(solution)/shard_map/ppermute | solution.py:44
  67.2 0.0 collective-permute-done.4.d
  67.2 0.0 collective-permute-done.6.other.others
  67.2 3.9 %forward_half.1 = (f32[512,128]{1,0:T(8,128)S(1)}, f32[512,128]{1,0:T(8,128)S(1)}, bf16[6912,128]{1,0:T(8,128)(2,1)}) custom-call(s32[9]{0:T(128)S(1)} %stack.31.flags, f32[1,256]{1,0:T(1,128)S(1)} %gate.1.gated, bf16[16,2,32,256]{3,2,1,0:T(8,128)(2,1)S(1)} %slice_dynamic-update-slice_fusion.mid, bf16[16,2,32,256]{3,2,1,0:T(8,128)(2,1)S(1)} %collective-permute-done.5.edge, ...), custom_call_target="tpu_custom_call" | custom-call | flops 1811939328 | bytes 1048576 | tf_op jit(solution)/shard_map/forward_half/pallas_call | solution.py:248
  71.1 1.9 %collective-permute-start.8 = (bf16[6912,128]{1,0:T(8,128)(2,1)}, bf16[6912,128]{1,0:T(8,128)(2,1)}, u32[]{:S(2)}, u32[]{:S(2)}) collective-permute-start(bf16[6912,128]{1,0:T(8,128)(2,1)} %get-tuple-element.30.own.w1_own), channel_id=1, source_target_pairs={{0,1},{1,0},{2,3},{3,2},{4,5},{5,4},{6,7},{7,6},{8,9},{9,8},{10,11... | collective-permute-start | bytes 5308424 | tf_op jit(solution)/shard_map/ppermute | solution.py:32
  73.1 2.4 %collective-permute-start.7 = (f32[512,128]{1,0:T(8,128)S(1)}, f32[512,128]{1,0:T(8,128)S(1)}, u32[]{:S(2)}, u32[]{:S(2)}) collective-permute-start(f32[512,128]{1,0:T(8,128)S(1)} %get-tuple-element.28.own), channel_id=1, source_target_pairs={{0,1},{1,0},{2,3},{3,2},{4,5},{5,4},{6,7},{7,6},{8,9},{9,8},{10,11... | collective-permute-start | bytes 786440 | tf_op jit(solution)/shard_map/ppermute | solution.py:32
  75.5 1.6 %collective-permute-done.7.others = f32[512,128]{1,0:T(8,128)S(1)} collective-permute-done((f32[512,128]{1,0:T(8,128)S(1)}, f32[512,128]{1,0:T(8,128)S(1)}, u32[]{:S(2)}, u32[]{:S(2)}) %collective-permute-start.7) | collective-permute-done | bytes 262176 | tf_op jit(solution)/shard_map/ppermute | solution.py:32
  77.1 2.4 %local_terms.1 = bf16[3456,128]{1,0:T(8,128)(2,1)} custom-call(s32[9]{0:T(128)S(1)} %stack.31.flags, f32[512,128]{1,0:T(8,128)S(1)} %get-tuple-element.27.pre, f32[512,128]{1,0:T(8,128)S(1)} %get-tuple-element.28.own, f32[512,128]{1,0:T(8,128)S(1)} %collective-permute-done.7.others, f32[1,128]{1,0:T(1,128)S(1)} %get-tuple-element.22.gain, ...), custom_call_target="tpu_custom_call" | custom-call | flops 1811939328 | bytes 1048576 | tf_op jit(solution)/shard_map/local_terms/pallas_call | solution.py:248
  79.5 3.5 %all-to-all-start.2 = ((bf16[4,864,128]{2,1,0:T(8,128)(2,1)}), bf16[4,864,128]{2,1,0:T(8,128)(2,1)S(1)}, u32[]{:S(2)}, u32[]{:S(2)}) async-start(bf16[4,864,128]{2,1,0:T(8,128)(2,1)} %bitcast.9), calls=%async_computation.2 | async-start | bytes 1769472 | tf_op jit(solution)/shard_map/all_to_all | solution.py:370
  83.0 3.3 %collective-permute-start.9 = (bf16[1728,128]{1,0:T(8,128)(2,1)S(1)}, bf16[1728,128]{1,0:T(8,128)(2,1)}, u32[]{:S(2)}, u32[]{:S(2)}) collective-permute-start(bf16[1728,128]{1,0:T(8,128)(2,1)S(1)} %unpack.3.a), channel_id=1, source_target_pairs={{0,128},{8,136},{16,144},{24,152},{32,160},{40,168},{48,176},{56,1... | collective-permute-start | bytes 1327112 | tf_op jit(solution)/shard_map/ppermute | solution.py:44
  86.4 3.7 %collective-permute-start.10 = (bf16[1728,128]{1,0:T(8,128)(2,1)S(1)}, bf16[1728,128]{1,0:T(8,128)(2,1)}, u32[]{:S(2)}, u32[]{:S(2)}) collective-permute-start(bf16[1728,128]{1,0:T(8,128)(2,1)S(1)} %unpack.3.a), channel_id=1, source_target_pairs={{0,384},{8,392},{16,400},{24,408},{32,416},{40,424},{48,432},{56,4... | collective-permute-start | bytes 1327112 | tf_op jit(solution)/shard_map/ppermute | solution.py:44
  90.1 2.5 %collective-permute-start.11 = (bf16[1728,128]{1,0:T(8,128)(2,1)S(1)}, bf16[1728,128]{1,0:T(8,128)(2,1)}, u32[]{:S(2)}, u32[]{:S(2)}) collective-permute-start(bf16[1728,128]{1,0:T(8,128)(2,1)S(1)} %unpack.3.a), channel_id=1, source_target_pairs={{0,256},{8,264},{16,272},{24,280},{32,288},{40,296},{48,304},{56,3... | collective-permute-start | bytes 1327112 | tf_op jit(solution)/shard_map/ppermute | solution.py:44
  92.6 0.0 collective-permute-done.8.other.w1_other
  92.6 5.3 %forward_all.1.pre_in = f32[768,256]{1,0:T(8,128)S(1)} custom-call(s32[9]{0:T(128)S(1)} %stack.31.flags, bf16[16,2,32,256]{3,2,1,0:T(8,128)(2,1)S(1)} %slice_dynamic-update-slice_fusion.mid, bf16[16,2,32,256]{3,2,1,0:T(8,128)(2,1)S(1)} %collective-permute-done.5.edge, bf16[16,3,32,256]{3,2,1,0:T(8,128)(2,1)S(1)} %collective-permute-done.6.other.others, ...), custom_call_target="tpu_custom_call" | custom-call | flops 2717908992 | bytes 1048576 | tf_op jit(solution)/shard_map/forward_all/pallas_call | solution.py:248
  97.9 0.9 copy-done.2
  98.8 0.0 all-to-all-done.2.terms
  98.8 0.9 sum_terms.1
  99.7 7.8 %all-to-all-start.3 = ((bf16[16,54,128]{2,1,0:T(8,128)(2,1)}), bf16[16,54,128]{2,1,0:T(8,128)(2,1)S(1)}, u32[]{:S(2)}, u32[]{:S(2)}) async-start(bf16[16,54,128]{2,1,0:T(8,128)(2,1)} %sum_terms.1), calls=%async_computation.3 | async-start | bytes 458752 | tf_op jit(solution)/shard_map/all_to_all | solution.py:378
  107.5 3.2 %collective-permute-start.12 = (bf16[1728,128]{1,0:T(8,128)(2,1)S(1)}, bf16[1728,128]{1,0:T(8,128)(2,1)S(1)}, u32[]{:S(2)}, u32[]{:S(2)}) collective-permute-start(bf16[1728,128]{1,0:T(8,128)(2,1)S(1)} %unpack.3.a), channel_id=1, source_target_pairs={{0,1},{1,0},{2,3},{3,2},{4,5},{5,4},{6,7},{7,6},{8,9},{9,8},{10,11... | collective-permute-start | bytes 1327112 | tf_op jit(solution)/shard_map/ppermute | solution.py:32
  110.7 0.0 collective-permute-done.9.b
  110.7 1.9 %collective-permute-start.13 = (bf16[1728,128]{1,0:T(8,128)(2,1)}, bf16[1728,128]{1,0:T(8,128)(2,1)S(1)}, u32[]{:S(2)}, u32[]{:S(2)}) collective-permute-start(bf16[1728,128]{1,0:T(8,128)(2,1)} %collective-permute-done.9.b), channel_id=1, source_target_pairs={{0,1},{1,0},{2,3},{3,2},{4,5},{5,4},{6,7},{7,6},{8,9},{9,8},{10,11... | collective-permute-start | bytes 1327112 | tf_op jit(solution)/shard_map/ppermute | solution.py:32
  112.7 0.0 collective-permute-done.10.c
  112.7 2.4 %collective-permute-start.14 = (bf16[1728,128]{1,0:T(8,128)(2,1)}, bf16[1728,128]{1,0:T(8,128)(2,1)}, u32[]{:S(2)}, u32[]{:S(2)}) collective-permute-start(bf16[1728,128]{1,0:T(8,128)(2,1)} %collective-permute-done.10.c), channel_id=1, source_target_pairs={{0,1},{1,0},{2,3},{3,2},{4,5},{5,4},{6,7},{7,6},{8,9},{9,8},{10,11... | collective-permute-start | bytes 1327112 | tf_op jit(solution)/shard_map/ppermute | solution.py:32
  115.1 0.4 collective-permute-done.11.d
  115.4 2.8 %collective-permute-start.15 = (bf16[1728,128]{1,0:T(8,128)(2,1)}, bf16[1728,128]{1,0:T(8,128)(2,1)}, u32[]{:S(2)}, u32[]{:S(2)}) collective-permute-start(bf16[1728,128]{1,0:T(8,128)(2,1)} %collective-permute-done.11.d), channel_id=1, source_target_pairs={{0,1},{1,0},{2,3},{3,2},{4,5},{5,4},{6,7},{7,6},{8,9},{9,8},{10,11... | collective-permute-start | bytes 1327112 | tf_op jit(solution)/shard_map/ppermute | solution.py:32
  118.3 0.0 all-to-all-done.3
  118.4 0.7 broadcast_in_dim.8
  119.1 10.7 %all-to-all-start.4 = ((f32[8,54,128]{2,1,0:T(8,128)}), f32[8,54,128]{2,1,0:T(8,128)S(1)}, u32[]{:S(2)}, u32[]{:S(2)}) async-start(f32[8,54,128]{2,1,0:T(8,128)} %broadcast_in_dim.8), calls=%async_computation.4 | async-start | bytes 458752 | tf_op jit(solution)/shard_map/all_to_all | solution.py:28
  129.8 0.0 collective-permute-done.12.far_a
  129.8 0.0 collective-permute-done.13.far_b
  129.8 0.0 collective-permute-done.14.far_c
  129.8 0.0 collective-permute-done.15.far_d
  129.8 1.1 copy-done.3
  130.9 10.9 %backward.1 = bf16[4,2,32,256]{3,2,1,0:T(8,128)(2,1)} custom-call(s32[9]{0:T(128)S(1)} %stack.31.flags, bf16[16,2,32,256]{3,2,1,0:T(8,128)(2,1)S(1)} %slice_dynamic-update-slice_fusion.mid, bf16[16,2,32,256]{3,2,1,0:T(8,128)(2,1)S(1)} %collective-permute-done.5.edge, bf16[16,3,32,256]{3,2,1,0:T(8,128)(2,1)S(1)} %collective-permute-done.6.other.others, ...), custom_call_target="tpu_custom_call" | custom-call | flops 3623878656 | bytes 10485760 | tf_op jit(solution)/shard_map/backward/pallas_call | solution.py:315
  141.9 0.7 reshape.22
  (21 shorter events, 0.2 us)
Async XLA Ops:
  0.6 0.8 copy-start
  0.6 12.3 %copy-start.4 = (bf16[4,2,32,256]{3,2,1,0:T(8,128)(2,1)S(1)}, bf16[4,2,32,256]{3,2,1,0:T(8,128)(2,1)}, u32[]{:S(2)}) copy-start(bf16[4,2,32,256]{3,2,1,0:T(8,128)(2,1)} %param.6) | copy-start | bytes 393220
  0.7 17.7 %copy-start.1 = (f32[256]{0:T(256)S(1)}, f32[256]{0:T(256)}, u32[]{:S(2)}) copy-start(f32[256]{0:T(256)} %param.7) | copy-start | bytes 3076
  2.4 32.6 %all-to-all-start = ((bf16[16,108,128]{2,1,0:T(8,128)(2,1)}), bf16[16,108,128]{2,1,0:T(8,128)(2,1)S(1)}, u32[]{:S(2)}, u32[]{:S(2)}) async-start(bf16[16,108,128]{2,1,0:T(8,128)(2,1)} %broadcast_in_dim.6), calls=%async_computation | async-start | bytes 917504 | tf_op jit(solution)/shard_map/all_to_all | solution.py:350
  12.9 14.9 %collective-permute-start = (bf16[6,2,32,256]{3,2,1,0:T(8,128)(2,1)S(1)}, bf16[6,2,32,256]{3,2,1,0:T(8,128)(2,1)S(1)}, u32[]{:S(2)}, u32[]{:S(2)}) collective-permute-start(bf16[6,2,32,256]{3,2,1,0:T(8,128)(2,1)S(1)} %pad_maximum_fusion.1), channel_id=1, source_target_pairs={{8,0},{16,8},{24,16},{32,24},{40,32},{48,40},{56,48},{64,56},{72,6... | collective-permute-start | bytes 589832 | tf_op jit(solution)/shard_map/ppermute | solution.py:38
  14.2 6.3 %collective-permute-start.1 = (bf16[2,2,32,256]{3,2,1,0:T(8,128)(2,1)S(1)}, bf16[2,2,32,256]{3,2,1,0:T(8,128)(2,1)S(1)}, u32[]{:S(2)}, u32[]{:S(2)}) collective-permute-start(bf16[2,2,32,256]{3,2,1,0:T(8,128)(2,1)S(1)} %get-tuple-element.36), channel_id=1, source_target_pairs={{0,8},{8,16},{16,24},{24,32},{32,40},{40,48},{48,56},{56,64},{64,7... | collective-permute-start | bytes 196616 | tf_op jit(solution)/shard_map/ppermute | solution.py:38
  18.3 0.8 copy-start.6
  18.4 9.5 %copy-start.5 = (bf16[4,2,32,256]{3,2,1,0:T(8,128)(2,1)S(1)}, bf16[4,2,32,256]{3,2,1,0:T(8,128)(2,1)}, u32[]{:S(2)}) copy-start(bf16[4,2,32,256]{3,2,1,0:T(8,128)(2,1)} %param.5) | copy-start | bytes 393220
  27.9 24.8 %collective-permute-start.5 = (bf16[16,2,32,256]{3,2,1,0:T(8,128)(2,1)S(1)}, bf16[16,2,32,256]{3,2,1,0:T(8,128)(2,1)S(1)}, u32[]{:S(2)}, u32[]{:S(2)}) collective-permute-start(bf16[16,2,32,256]{3,2,1,0:T(8,128)(2,1)S(1)} %slice_dynamic-update-slice_fusion.mid), channel_id=1, source_target_pairs={{1,2},{3,4},{5,6},{2,1},{4,3},{6,5},{9,10},{11,12},{13,14},{10,9},... | collective-permute-start | bytes 1572872 | tf_op jit(solution)/shard_map/ppermute | solution.py:50
  36.8 18.9 %all-to-all-start.1 = ((bf16[16,108,128]{2,1,0:T(8,128)(2,1)}), bf16[16,108,128]{2,1,0:T(8,128)(2,1)S(1)}, u32[]{:S(2)}, u32[]{:S(2)}) async-start(bf16[16,108,128]{2,1,0:T(8,128)(2,1)} %broadcast_in_dim.7), calls=%async_computation.1 | async-start | bytes 917504 | tf_op jit(solution)/shard_map/all_to_all | solution.py:28
  43.2 12.5 %collective-permute-start.2 = (bf16[1728,128]{1,0:T(8,128)(2,1)}, bf16[1728,128]{1,0:T(8,128)(2,1)}, u32[]{:S(2)}, u32[]{:S(2)}) collective-permute-start(bf16[1728,128]{1,0:T(8,128)(2,1)} %unpack.2.a), channel_id=1, source_target_pairs={{0,128},{8,136},{16,144},{24,152},{32,160},{40,168},{48,176},{56,1... | collective-permute-start | bytes 1327112 | tf_op jit(solution)/shard_map/ppermute | solution.py:44
  46.4 20.8 %collective-permute-start.3 = (bf16[1728,128]{1,0:T(8,128)(2,1)}, bf16[1728,128]{1,0:T(8,128)(2,1)}, u32[]{:S(2)}, u32[]{:S(2)}) collective-permute-start(bf16[1728,128]{1,0:T(8,128)(2,1)} %unpack.2.a), channel_id=1, source_target_pairs={{0,384},{8,392},{16,400},{24,408},{32,416},{40,424},{48,432},{56,4... | collective-permute-start | bytes 1327112 | tf_op jit(solution)/shard_map/ppermute | solution.py:44
  50.1 17.1 %collective-permute-start.4 = (bf16[1728,128]{1,0:T(8,128)(2,1)}, bf16[1728,128]{1,0:T(8,128)(2,1)}, u32[]{:S(2)}, u32[]{:S(2)}) collective-permute-start(bf16[1728,128]{1,0:T(8,128)(2,1)} %unpack.2.a), channel_id=1, source_target_pairs={{0,256},{8,264},{16,272},{24,280},{32,288},{40,296},{48,304},{56,3... | collective-permute-start | bytes 1327112 | tf_op jit(solution)/shard_map/ppermute | solution.py:44
  53.7 13.5 %collective-permute-start.6 = (bf16[16,3,32,256]{3,2,1,0:T(8,128)(2,1)}, bf16[16,3,32,256]{3,2,1,0:T(8,128)(2,1)S(1)}, u32[]{:S(2)}, u32[]{:S(2)}) collective-permute-start(bf16[16,3,32,256]{3,2,1,0:T(8,128)(2,1)} %pad_maximum_fusion), channel_id=1, source_target_pairs={{0,1},{1,0},{2,3},{3,2},{4,5},{5,4},{6,7},{7,6},{8,9},{9,8},{10,11... | collective-permute-start | bytes 2359304 | tf_op jit(solution)/shard_map/ppermute | solution.py:32
  71.1 21.5 %collective-permute-start.8 = (bf16[6912,128]{1,0:T(8,128)(2,1)}, bf16[6912,128]{1,0:T(8,128)(2,1)}, u32[]{:S(2)}, u32[]{:S(2)}) collective-permute-start(bf16[6912,128]{1,0:T(8,128)(2,1)} %get-tuple-element.30.own.w1_own), channel_id=1, source_target_pairs={{0,1},{1,0},{2,3},{3,2},{4,5},{5,4},{6,7},{7,6},{8,9},{9,8},{10,11... | collective-permute-start | bytes 5308424 | tf_op jit(solution)/shard_map/ppermute | solution.py:32
  73.1 4.0 %collective-permute-start.7 = (f32[512,128]{1,0:T(8,128)S(1)}, f32[512,128]{1,0:T(8,128)S(1)}, u32[]{:S(2)}, u32[]{:S(2)}) collective-permute-start(f32[512,128]{1,0:T(8,128)S(1)} %get-tuple-element.28.own), channel_id=1, source_target_pairs={{0,1},{1,0},{2,3},{3,2},{4,5},{5,4},{6,7},{7,6},{8,9},{9,8},{10,11... | collective-permute-start | bytes 786440 | tf_op jit(solution)/shard_map/ppermute | solution.py:32
  79.5 19.3 %all-to-all-start.2 = ((bf16[4,864,128]{2,1,0:T(8,128)(2,1)}), bf16[4,864,128]{2,1,0:T(8,128)(2,1)S(1)}, u32[]{:S(2)}, u32[]{:S(2)}) async-start(bf16[4,864,128]{2,1,0:T(8,128)(2,1)} %bitcast.9), calls=%async_computation.2 | async-start | bytes 1769472 | tf_op jit(solution)/shard_map/all_to_all | solution.py:370
  83.0 27.7 %collective-permute-start.9 = (bf16[1728,128]{1,0:T(8,128)(2,1)S(1)}, bf16[1728,128]{1,0:T(8,128)(2,1)}, u32[]{:S(2)}, u32[]{:S(2)}) collective-permute-start(bf16[1728,128]{1,0:T(8,128)(2,1)S(1)} %unpack.3.a), channel_id=1, source_target_pairs={{0,128},{8,136},{16,144},{24,152},{32,160},{40,168},{48,176},{56,1... | collective-permute-start | bytes 1327112 | tf_op jit(solution)/shard_map/ppermute | solution.py:44
  86.4 26.3 %collective-permute-start.10 = (bf16[1728,128]{1,0:T(8,128)(2,1)S(1)}, bf16[1728,128]{1,0:T(8,128)(2,1)}, u32[]{:S(2)}, u32[]{:S(2)}) collective-permute-start(bf16[1728,128]{1,0:T(8,128)(2,1)S(1)} %unpack.3.a), channel_id=1, source_target_pairs={{0,384},{8,392},{16,400},{24,408},{32,416},{40,424},{48,432},{56,4... | collective-permute-start | bytes 1327112 | tf_op jit(solution)/shard_map/ppermute | solution.py:44
  90.1 25.4 %collective-permute-start.11 = (bf16[1728,128]{1,0:T(8,128)(2,1)S(1)}, bf16[1728,128]{1,0:T(8,128)(2,1)}, u32[]{:S(2)}, u32[]{:S(2)}) collective-permute-start(bf16[1728,128]{1,0:T(8,128)(2,1)S(1)} %unpack.3.a), channel_id=1, source_target_pairs={{0,256},{8,264},{16,272},{24,280},{32,288},{40,296},{48,304},{56,3... | collective-permute-start | bytes 1327112 | tf_op jit(solution)/shard_map/ppermute | solution.py:44
  97.9 0.9 copy-start.2
  99.7 18.6 %all-to-all-start.3 = ((bf16[16,54,128]{2,1,0:T(8,128)(2,1)}), bf16[16,54,128]{2,1,0:T(8,128)(2,1)S(1)}, u32[]{:S(2)}, u32[]{:S(2)}) async-start(bf16[16,54,128]{2,1,0:T(8,128)(2,1)} %sum_terms.1), calls=%async_computation.3 | async-start | bytes 458752 | tf_op jit(solution)/shard_map/all_to_all | solution.py:378
  107.5 22.2 %collective-permute-start.12 = (bf16[1728,128]{1,0:T(8,128)(2,1)S(1)}, bf16[1728,128]{1,0:T(8,128)(2,1)S(1)}, u32[]{:S(2)}, u32[]{:S(2)}) collective-permute-start(bf16[1728,128]{1,0:T(8,128)(2,1)S(1)} %unpack.3.a), channel_id=1, source_target_pairs={{0,1},{1,0},{2,3},{3,2},{4,5},{5,4},{6,7},{7,6},{8,9},{9,8},{10,11... | collective-permute-start | bytes 1327112 | tf_op jit(solution)/shard_map/ppermute | solution.py:32
  110.7 19.1 %collective-permute-start.13 = (bf16[1728,128]{1,0:T(8,128)(2,1)}, bf16[1728,128]{1,0:T(8,128)(2,1)S(1)}, u32[]{:S(2)}, u32[]{:S(2)}) collective-permute-start(bf16[1728,128]{1,0:T(8,128)(2,1)} %collective-permute-done.9.b), channel_id=1, source_target_pairs={{0,1},{1,0},{2,3},{3,2},{4,5},{5,4},{6,7},{7,6},{8,9},{9,8},{10,11... | collective-permute-start | bytes 1327112 | tf_op jit(solution)/shard_map/ppermute | solution.py:32
  112.7 17.1 %collective-permute-start.14 = (bf16[1728,128]{1,0:T(8,128)(2,1)}, bf16[1728,128]{1,0:T(8,128)(2,1)}, u32[]{:S(2)}, u32[]{:S(2)}) collective-permute-start(bf16[1728,128]{1,0:T(8,128)(2,1)} %collective-permute-done.10.c), channel_id=1, source_target_pairs={{0,1},{1,0},{2,3},{3,2},{4,5},{5,4},{6,7},{7,6},{8,9},{9,8},{10,11... | collective-permute-start | bytes 1327112 | tf_op jit(solution)/shard_map/ppermute | solution.py:32
  115.4 14.3 %collective-permute-start.15 = (bf16[1728,128]{1,0:T(8,128)(2,1)}, bf16[1728,128]{1,0:T(8,128)(2,1)}, u32[]{:S(2)}, u32[]{:S(2)}) collective-permute-start(bf16[1728,128]{1,0:T(8,128)(2,1)} %collective-permute-done.11.d), channel_id=1, source_target_pairs={{0,1},{1,0},{2,3},{3,2},{4,5},{5,4},{6,7},{7,6},{8,9},{9,8},{10,11... | collective-permute-start | bytes 1327112 | tf_op jit(solution)/shard_map/ppermute | solution.py:32
  119.1 22.8 %all-to-all-start.4 = ((f32[8,54,128]{2,1,0:T(8,128)}), f32[8,54,128]{2,1,0:T(8,128)S(1)}, u32[]{:S(2)}, u32[]{:S(2)}) async-start(f32[8,54,128]{2,1,0:T(8,128)} %broadcast_in_dim.8), calls=%async_computation.4 | async-start | bytes 458752 | tf_op jit(solution)/shard_map/all_to_all | solution.py:28
  129.8 1.1 copy-start.3

commit v9 on v7

--- a/solution.py
+++ b/solution.py
@@ -357,10 +357,14 @@
     nexts, prevs = lax.optimization_barrier((nexts, prevs, gain_half))[:2]
     mid = jnp.concatenate([prevs, activations, nexts[:2], cotangent, nexts[2:]], axis=0)
     edge = beyond_chip(mid)
+    operand2 = jnp.broadcast_to(after(half2, edge)[None], (16,) + half2.shape)
+    edge = after(edge, operand2)
     next_row = jnp.where(core == 0, edge[:, 1:], edge[:, :1])
     field = (mid, edge, swap_cores(jnp.concatenate([mid, next_row], axis=1)))
 
-    w2_block = unpack(spread(after(half2, edge), "tm", YZ_GROUPS))
+    w2_block = unpack(
+        lax.all_to_all(operand2, "tm", 0, 0, axis_index_groups=YZ_GROUPS, tiled=True)
+    )
 
     gated = gate(after(gain_all, *w1_blocks))
     pre_half, squares, w1_own = forward_half(flags, gated, field, w1_blocks)

time: 141 us -> 137 us (0.972)
  waiting for transfers between devices: 21.2 us -> 15.5 us
  starting transfers between devices: 83.8 us -> 85.7 us
    all_to_all x0 -> x1, starting transfers between devices: none -> 5.57 us  [on_device(): lax.all_to_all(operand2, 'tm', 0, 0, axis_index_groups=YZ_GROUPS, tiled=T...]
    all_to_all x2 -> x1, starting transfers between devices: 14.8 us -> 10.3 us  [spread(): lax.all_to_all(operand, axis, 0, 0, axis_index_groups=groups, tiled=True)]
    all_to_all x2 -> x1, waiting for transfers between devices: 4.42 us -> 0.01 us  [spread(): lax.all_to_all(operand, axis, 0, 0, axis_index_groups=groups, tiled=True)]
    all_to_all x1, starting transfers between devices: 4.41 us -> 7.56 us  [on_device(): lax.all_to_all(sum_terms(total), 'tm', 0, 0, axis_index_groups=YZ_GROUPS,...]
    ppermute x6, waiting for transfers between devices: 4.82 us -> 2.2 us  [along_x(): return [block] + [lax.ppermute(block, 'tm', route) for route in routes]]
    ppermute x7, starting transfers between devices: 19.3 us -> 17 us  [swap_cores(): lax.ppermute(block, 'rows', [(i, i ^ 1) for i in range(lax.axis_size('row...]
  transfers between devices with their start and end apart: 21 -> 21, of which waited for: 6 -> 5; matrix products, arithmetic and copies ran while one was open for 3% -> 2% of each run, Pallas kernels for 15% -> 16%
where the time goes in v9:
time: 137 us; the launch traced here: 135 us
  starting transfers between devices  85.7 us (63%)
  Pallas kernels  24.1 us (18%)
  waiting for transfers between devices  15.5 us (11%)
  local copies, waits for them, and re-layouts  8.57 us (6%)
    ppermute x6, starting transfers between devices, along_x(): return [block] + [lax.ppermute(block, 'tm', route) for route in routes]  19.1 us
    ppermute x7, starting transfers between devices, swap_cores(): lax.ppermute(block, 'rows', [(i, i ^ 1) for i in range(lax.axis_size('row...  17 us
    pallas_call x8, Pallas kernels, call(): pl.pallas_call(kernel, out_shape=out_shape, in_specs=smem + [VMEM] * (len...  13.2 us
    pallas_call x1, Pallas kernels, backward(): pl.pallas_call(backward_kernel, out_shape=jax.ShapeDtypeStruct((4, 2, W,...  10.9 us
    all_to_all x1, starting transfers between devices, spread(): lax.all_to_all(operand, axis, 0, 0, axis_index_groups=groups, tiled=True)  10.3 us
    all_to_all x1, starting transfers between devices, on_device(): lax.all_to_all(operand, 'tm', 0, 0, axis_index_groups=YZ_GROUPS, tiled=True)  9.56 us
    ppermute x2, waiting for transfers between devices, shift(): return lax.ppermute(block, axis, route)  8.78 us
    all_to_all x1, starting transfers between devices, on_device(): lax.all_to_all(sum_terms(total), 'tm', 0, 0, axis_index_groups=YZ_GROUPS,...  7.56 us
  transfers between devices with their start and end apart: 21, of which 5 were waited for; matrix products, arithmetic and copies ran while one was open for 2% of the time, Pallas kernels for 16%

profile of v9, /device:TPU:1, one launch (start us, length us, event | category | flops | bytes accessed | tf_op | source)
XLA Modules:
  0.0 135.4 jit_solution(3966152953974439939)
XLA Ops:
  0.6 0.0 copy-start
  0.7 0.8 copy-done
  1.5 0.1 fusion
  1.6 0.8 broadcast_in_dim.6
  2.4 9.6 %all-to-all-start = ((bf16[16,108,128]{2,1,0:T(8,128)(2,1)}), bf16[16,108,128]{2,1,0:T(8,128)(2,1)S(1)}, u32[]{:S(2)}, u32[]{:S(2)}) async-start(bf16[16,108,128]{2,1,0:T(8,128)(2,1)} %broadcast_in_dim.6), calls=%async_computation | async-start | bytes 917504 | tf_op jit(solution)/shard_map/all_to_all | solution.py:350
  12.0 0.9 fusion.2
  12.9 1.3 collective-permute-start.3
  14.2 4.0 %collective-permute-start.4 = (bf16[2,2,32,256]{3,2,1,0:T(8,128)(2,1)S(1)}, bf16[2,2,32,256]{3,2,1,0:T(8,128)(2,1)S(1)}, u32[]{:S(2)}, u32[]{:S(2)}) collective-permute-start(bf16[2,2,32,256]{3,2,1,0:T(8,128)(2,1)S(1)} %get-tuple-element.42), channel_id=1, source_target_pairs={{0,8},{8,16},{16,24},{24,32},{32,40},{40,48},{48,56},{56,64},{64,7... | collective-permute-start | bytes 196616 | tf_op jit(solution)/shard_map/ppermute | solution.py:38
  18.3 0.1 stack.31.flags
  18.3 0.0 copy-start.7
  18.4 0.7 gains.1
  19.0 1.5 %collective-permute-done.4 = bf16[2,2,32,256]{3,2,1,0:T(8,128)(2,1)S(1)} collective-permute-done((bf16[2,2,32,256]{3,2,1,0:T(8,128)(2,1)S(1)}, bf16[2,2,32,256]{3,2,1,0:T(8,128)(2,1)S(1)}, u32[]{:S(2)}, u32[]{:S(2)}) %collective-permute-start.4) | collective-permute-done | bytes 65568 | tf_op jit(solution)/shard_map/ppermute | solution.py:38
  20.6 7.2 %collective-permute-done.3 = bf16[6,2,32,256]{3,2,1,0:T(8,128)(2,1)S(1)} collective-permute-done((bf16[6,2,32,256]{3,2,1,0:T(8,128)(2,1)S(1)}, bf16[6,2,32,256]{3,2,1,0:T(8,128)(2,1)S(1)}, u32[]{:S(2)}, u32[]{:S(2)}) %collective-permute-start.3) | collective-permute-done | bytes 196640 | tf_op jit(solution)/shard_map/ppermute | solution.py:38
  27.9 0.0 copy-start.8
  27.9 7.3 %collective-permute-start.5 = (bf16[16,2,32,256]{3,2,1,0:T(8,128)(2,1)S(1)}, bf16[16,2,32,256]{3,2,1,0:T(8,128)(2,1)S(1)}, u32[]{:S(2)}, u32[]{:S(2)}) collective-permute-start(bf16[16,2,32,256]{3,2,1,0:T(8,128)(2,1)S(1)} %slice_dynamic-update-slice_fusion.mid), channel_id=1, source_target_pairs={{1,2},{3,4},{5,6},{2,1},{4,3},{6,5},{9,10},{11,12},{13,14},{10,9},... | collective-permute-start | bytes 1572872 | tf_op jit(solution)/shard_map/ppermute | solution.py:50
  35.2 0.0 all-to-all-done.block
  35.2 0.1 unpack.2.a
  35.3 3.1 %collective-permute-start = (bf16[1728,128]{1,0:T(8,128)(2,1)S(1)}, bf16[1728,128]{1,0:T(8,128)(2,1)}, u32[]{:S(2)}, u32[]{:S(2)}) collective-permute-start(bf16[1728,128]{1,0:T(8,128)(2,1)S(1)} %unpack.2.a), channel_id=1, source_target_pairs={{0,128},{8,136},{16,144},{24,152},{32,160},{40,168},{48,176},{56,1... | collective-permute-start | bytes 1327112 | tf_op jit(solution)/shard_map/ppermute | solution.py:44
  38.4 3.7 %collective-permute-start.1 = (bf16[1728,128]{1,0:T(8,128)(2,1)S(1)}, bf16[1728,128]{1,0:T(8,128)(2,1)}, u32[]{:S(2)}, u32[]{:S(2)}) collective-permute-start(bf16[1728,128]{1,0:T(8,128)(2,1)S(1)} %unpack.2.a), channel_id=1, source_target_pairs={{0,384},{8,392},{16,400},{24,408},{32,416},{40,424},{48,432},{56,4... | collective-permute-start | bytes 1327112 | tf_op jit(solution)/shard_map/ppermute | solution.py:44
  42.1 2.7 %collective-permute-start.2 = (bf16[1728,128]{1,0:T(8,128)(2,1)S(1)}, bf16[1728,128]{1,0:T(8,128)(2,1)}, u32[]{:S(2)}, u32[]{:S(2)}) collective-permute-start(bf16[1728,128]{1,0:T(8,128)(2,1)S(1)} %unpack.2.a), channel_id=1, source_target_pairs={{0,256},{8,264},{16,272},{24,280},{32,288},{40,296},{48,304},{56,3... | collective-permute-start | bytes 1327112 | tf_op jit(solution)/shard_map/ppermute | solution.py:44
  44.9 3.2 %collective-permute-done.5.edge = bf16[16,2,32,256]{3,2,1,0:T(8,128)(2,1)S(1)} collective-permute-done((bf16[16,2,32,256]{3,2,1,0:T(8,128)(2,1)S(1)}, bf16[16,2,32,256]{3,2,1,0:T(8,128)(2,1)S(1)}, u32[]{:S(2)}, u32[]{:S(2)}) %collective-permute-start.5) | collective-permute-done | bytes 524320 | tf_op jit(solution)/shard_map/ppermute | solution.py:50
  48.1 0.8 broadcast_in_dim.7
  48.9 5.6 %all-to-all-start.1 = ((bf16[16,108,128]{2,1,0:T(8,128)(2,1)}), bf16[16,108,128]{2,1,0:T(8,128)(2,1)S(1)}, u32[]{:S(2)}, u32[]{:S(2)}) async-start(bf16[16,108,128]{2,1,0:T(8,128)(2,1)} %broadcast_in_dim.7), calls=%async_computation.1 | async-start | bytes 917504 | tf_op jit(solution)/shard_map/all_to_all | solution.py:366
  54.5 0.1 pad_maximum_fusion
  54.6 1.9 %collective-permute-start.6 = (bf16[16,3,32,256]{3,2,1,0:T(8,128)(2,1)S(1)}, bf16[16,3,32,256]{3,2,1,0:T(8,128)(2,1)S(1)}, u32[]{:S(2)}, u32[]{:S(2)}) collective-permute-start(bf16[16,3,32,256]{3,2,1,0:T(8,128)(2,1)S(1)} %pad_maximum_fusion), channel_id=1, source_target_pairs={{0,1},{1,0},{2,3},{3,2},{4,5},{5,4},{6,7},{7,6},{8,9},{9,8},{10,11... | collective-permute-start | bytes 2359304 | tf_op jit(solution)/shard_map/ppermute | solution.py:32
  56.5 0.0 collective-permute-done.b
  56.5 2.2 %collective-permute-done.1.c = bf16[1728,128]{1,0:T(8,128)(2,1)} collective-permute-done((bf16[1728,128]{1,0:T(8,128)(2,1)S(1)}, bf16[1728,128]{1,0:T(8,128)(2,1)}, u32[]{:S(2)}, u32[]{:S(2)}) %collective-permute-start.1) | collective-permute-done | bytes 442400 | tf_op jit(solution)/shard_map/ppermute | solution.py:44
  58.7 0.0 collective-permute-done.2.d
  58.7 0.0 collective-permute-done.6.other.others
  58.8 3.8 %forward_half.1 = (f32[512,128]{1,0:T(8,128)S(1)}, f32[512,128]{1,0:T(8,128)S(1)}, bf16[6912,128]{1,0:T(8,128)(2,1)}) custom-call(s32[9]{0:T(128)S(1)} %stack.31.flags, f32[1,256]{1,0:T(1,128)S(1)} %gate.1.gated, bf16[16,2,32,256]{3,2,1,0:T(8,128)(2,1)S(1)} %slice_dynamic-update-slice_fusion.mid, bf16[16,2,32,256]{3,2,1,0:T(8,128)(2,1)S(1)} %collective-permute-done.5.edge, ...), custom_call_target="tpu_custom_call" | custom-call | flops 1811939328 | bytes 1048576 | tf_op jit(solution)/shard_map/forward_half/pallas_call | solution.py:248
  62.6 0.7 copy-done.4
  63.3 2.0 %collective-permute-start.7 = (f32[512,128]{1,0:T(8,128)S(1)}, f32[512,128]{1,0:T(8,128)S(1)}, u32[]{:S(2)}, u32[]{:S(2)}) collective-permute-start(f32[512,128]{1,0:T(8,128)S(1)} %get-tuple-element.32.own), channel_id=1, source_target_pairs={{0,1},{1,0},{2,3},{3,2},{4,5},{5,4},{6,7},{7,6},{8,9},{9,8},{10,11... | collective-permute-start | bytes 786440 | tf_op jit(solution)/shard_map/ppermute | solution.py:32
  65.3 0.0 all-to-all-done.1.block
  65.3 0.1 unpack.3.a
  65.4 1.3 collective-permute-done.7.others
  66.7 0.9 copy-done.5
  67.6 2.4 %local_terms.1 = bf16[3456,128]{1,0:T(8,128)(2,1)} custom-call(s32[9]{0:T(128)S(1)} %stack.31.flags, f32[512,128]{1,0:T(8,128)S(1)} %copy-done.5, f32[512,128]{1,0:T(8,128)S(1)} %get-tuple-element.32.own, f32[512,128]{1,0:T(8,128)S(1)} %collective-permute-done.7.others, f32[1,128]{1,0:T(1,128)S(1)} %get-tuple-element.26.gain, ...), custom_call_target="tpu_custom_call" | custom-call | flops 1811939328 | bytes 1048576 | tf_op jit(solution)/shard_map/local_terms/pallas_call | solution.py:248
  70.1 2.0 %collective-permute-start.8 = (bf16[6912,128]{1,0:T(8,128)(2,1)}, bf16[6912,128]{1,0:T(8,128)(2,1)}, u32[]{:S(2)}, u32[]{:S(2)}) collective-permute-start(bf16[6912,128]{1,0:T(8,128)(2,1)} %get-tuple-element.35.own.w1_own), channel_id=1, source_target_pairs={{0,1},{1,0},{2,3},{3,2},{4,5},{5,4},{6,7},{7,6},{8,9},{9,8},{10,11... | collective-permute-start | bytes 5308424 | tf_op jit(solution)/shard_map/ppermute | solution.py:32
  72.1 4.0 %all-to-all-start.2 = ((bf16[4,864,128]{2,1,0:T(8,128)(2,1)}), bf16[4,864,128]{2,1,0:T(8,128)(2,1)S(1)}, u32[]{:S(2)}, u32[]{:S(2)}) async-start(bf16[4,864,128]{2,1,0:T(8,128)(2,1)} %bitcast.9), calls=%async_computation.2 | async-start | bytes 1769472 | tf_op jit(solution)/shard_map/all_to_all | solution.py:375
  76.2 3.4 %collective-permute-start.9 = (bf16[1728,128]{1,0:T(8,128)(2,1)S(1)}, bf16[1728,128]{1,0:T(8,128)(2,1)}, u32[]{:S(2)}, u32[]{:S(2)}) collective-permute-start(bf16[1728,128]{1,0:T(8,128)(2,1)S(1)} %unpack.3.a), channel_id=1, source_target_pairs={{0,128},{8,136},{16,144},{24,152},{32,160},{40,168},{48,176},{56,1... | collective-permute-start | bytes 1327112 | tf_op jit(solution)/shard_map/ppermute | solution.py:44
  79.5 3.7 %collective-permute-start.10 = (bf16[1728,128]{1,0:T(8,128)(2,1)S(1)}, bf16[1728,128]{1,0:T(8,128)(2,1)}, u32[]{:S(2)}, u32[]{:S(2)}) collective-permute-start(bf16[1728,128]{1,0:T(8,128)(2,1)S(1)} %unpack.3.a), channel_id=1, source_target_pairs={{0,384},{8,392},{16,400},{24,408},{32,416},{40,424},{48,432},{56,4... | collective-permute-start | bytes 1327112 | tf_op jit(solution)/shard_map/ppermute | solution.py:44
  83.2 2.5 %collective-permute-start.11 = (bf16[1728,128]{1,0:T(8,128)(2,1)S(1)}, bf16[1728,128]{1,0:T(8,128)(2,1)}, u32[]{:S(2)}, u32[]{:S(2)}) collective-permute-start(bf16[1728,128]{1,0:T(8,128)(2,1)S(1)} %unpack.3.a), channel_id=1, source_target_pairs={{0,256},{8,264},{16,272},{24,280},{32,288},{40,296},{48,304},{56,3... | collective-permute-start | bytes 1327112 | tf_op jit(solution)/shard_map/ppermute | solution.py:44
  85.8 0.0 collective-permute-done.8.other.w1_other
  85.8 5.3 %forward_all.1.pre_in = f32[768,256]{1,0:T(8,128)S(1)} custom-call(s32[9]{0:T(128)S(1)} %stack.31.flags, bf16[16,2,32,256]{3,2,1,0:T(8,128)(2,1)S(1)} %slice_dynamic-update-slice_fusion.mid, bf16[16,2,32,256]{3,2,1,0:T(8,128)(2,1)S(1)} %collective-permute-done.5.edge, bf16[16,3,32,256]{3,2,1,0:T(8,128)(2,1)S(1)} %collective-permute-done.6.other.others, ...), custom_call_target="tpu_custom_call" | custom-call | flops 2717908992 | bytes 1048576 | tf_op jit(solution)/shard_map/forward_all/pallas_call | solution.py:248
  91.1 0.9 copy-done.2
  92.0 0.0 all-to-all-done.2.terms
  92.0 0.9 sum_terms.1
  92.8 7.6 %all-to-all-start.3 = ((bf16[16,54,128]{2,1,0:T(8,128)(2,1)}), bf16[16,54,128]{2,1,0:T(8,128)(2,1)S(1)}, u32[]{:S(2)}, u32[]{:S(2)}) async-start(bf16[16,54,128]{2,1,0:T(8,128)(2,1)} %sum_terms.1), calls=%async_computation.3 | async-start | bytes 458752 | tf_op jit(solution)/shard_map/all_to_all | solution.py:383
  100.4 3.7 %collective-permute-start.12 = (bf16[1728,128]{1,0:T(8,128)(2,1)S(1)}, bf16[1728,128]{1,0:T(8,128)(2,1)S(1)}, u32[]{:S(2)}, u32[]{:S(2)}) collective-permute-start(bf16[1728,128]{1,0:T(8,128)(2,1)S(1)} %unpack.3.a), channel_id=1, source_target_pairs={{0,1},{1,0},{2,3},{3,2},{4,5},{5,4},{6,7},{7,6},{8,9},{9,8},{10,11... | collective-permute-start | bytes 1327112 | tf_op jit(solution)/shard_map/ppermute | solution.py:32
  104.1 0.0 collective-permute-done.9.b
  104.1 1.9 %collective-permute-start.13 = (bf16[1728,128]{1,0:T(8,128)(2,1)}, bf16[1728,128]{1,0:T(8,128)(2,1)S(1)}, u32[]{:S(2)}, u32[]{:S(2)}) collective-permute-start(bf16[1728,128]{1,0:T(8,128)(2,1)} %collective-permute-done.9.b), channel_id=1, source_target_pairs={{0,1},{1,0},{2,3},{3,2},{4,5},{5,4},{6,7},{7,6},{8,9},{9,8},{10,11... | collective-permute-start | bytes 1327112 | tf_op jit(solution)/shard_map/ppermute | solution.py:32
  106.0 0.0 collective-permute-done.10.c
  106.0 2.4 %collective-permute-start.14 = (bf16[1728,128]{1,0:T(8,128)(2,1)}, bf16[1728,128]{1,0:T(8,128)(2,1)}, u32[]{:S(2)}, u32[]{:S(2)}) collective-permute-start(bf16[1728,128]{1,0:T(8,128)(2,1)} %collective-permute-done.10.c), channel_id=1, source_target_pairs={{0,1},{1,0},{2,3},{3,2},{4,5},{5,4},{6,7},{7,6},{8,9},{9,8},{10,11... | collective-permute-start | bytes 1327112 | tf_op jit(solution)/shard_map/ppermute | solution.py:32
  108.5 3.0 %collective-permute-start.15 = (bf16[1728,128]{1,0:T(8,128)(2,1)}, bf16[1728,128]{1,0:T(8,128)(2,1)}, u32[]{:S(2)}, u32[]{:S(2)}) collective-permute-start(bf16[1728,128]{1,0:T(8,128)(2,1)} %collective-permute-done.11.d), channel_id=1, source_target_pairs={{0,1},{1,0},{2,3},{3,2},{4,5},{5,4},{6,7},{7,6},{8,9},{9,8},{10,11... | collective-permute-start | bytes 1327112 | tf_op jit(solution)/shard_map/ppermute | solution.py:32
  111.5 0.0 all-to-all-done.3
  111.5 0.7 broadcast_in_dim.8
  112.2 10.3 %all-to-all-start.4 = ((f32[8,54,128]{2,1,0:T(8,128)}), f32[8,54,128]{2,1,0:T(8,128)S(1)}, u32[]{:S(2)}, u32[]{:S(2)}) async-start(f32[8,54,128]{2,1,0:T(8,128)} %broadcast_in_dim.8), calls=%async_computation.4 | async-start | bytes 458752 | tf_op jit(solution)/shard_map/all_to_all | solution.py:28
  122.6 0.0 collective-permute-done.12.far_a
  122.6 0.0 collective-permute-done.13.far_b
  122.6 0.0 collective-permute-done.15.far_d
  122.6 1.1 copy-done.3
  123.7 10.9 %backward.1 = bf16[4,2,32,256]{3,2,1,0:T(8,128)(2,1)} custom-call(s32[9]{0:T(128)S(1)} %stack.31.flags, bf16[16,2,32,256]{3,2,1,0:T(8,128)(2,1)S(1)} %slice_dynamic-update-slice_fusion.mid, bf16[16,2,32,256]{3,2,1,0:T(8,128)(2,1)S(1)} %collective-permute-done.5.edge, bf16[16,3,32,256]{3,2,1,0:T(8,128)(2,1)S(1)} %collective-permute-done.6.other.others, ...), custom_call_target="tpu_custom_call" | custom-call | flops 3623878656 | bytes 10485760 | tf_op jit(solution)/shard_map/backward/pallas_call | solution.py:315
  134.7 0.0 all-to-all-done.4
  134.7 0.7 reshape.22
  (25 shorter events, 0.2 us)
Async XLA Ops:
  0.6 0.8 copy-start
  0.6 12.3 %copy-start.6 = (bf16[4,2,32,256]{3,2,1,0:T(8,128)(2,1)S(1)}, bf16[4,2,32,256]{3,2,1,0:T(8,128)(2,1)}, u32[]{:S(2)}) copy-start(bf16[4,2,32,256]{3,2,1,0:T(8,128)(2,1)} %param.6) | copy-start | bytes 393220
  0.7 17.7 %copy-start.1 = (f32[256]{0:T(256)S(1)}, f32[256]{0:T(256)}, u32[]{:S(2)}) copy-start(f32[256]{0:T(256)} %param.7) | copy-start | bytes 3076
  2.4 32.8 %all-to-all-start = ((bf16[16,108,128]{2,1,0:T(8,128)(2,1)}), bf16[16,108,128]{2,1,0:T(8,128)(2,1)S(1)}, u32[]{:S(2)}, u32[]{:S(2)}) async-start(bf16[16,108,128]{2,1,0:T(8,128)(2,1)} %broadcast_in_dim.6), calls=%async_computation | async-start | bytes 917504 | tf_op jit(solution)/shard_map/all_to_all | solution.py:350
  12.9 14.9 %collective-permute-start.3 = (bf16[6,2,32,256]{3,2,1,0:T(8,128)(2,1)S(1)}, bf16[6,2,32,256]{3,2,1,0:T(8,128)(2,1)S(1)}, u32[]{:S(2)}, u32[]{:S(2)}) collective-permute-start(bf16[6,2,32,256]{3,2,1,0:T(8,128)(2,1)S(1)} %pad_maximum_fusion.1), channel_id=1, source_target_pairs={{8,0},{16,8},{24,16},{32,24},{40,32},{48,40},{56,48},{64,56},{72,6... | collective-permute-start | bytes 589832 | tf_op jit(solution)/shard_map/ppermute | solution.py:38
  14.2 6.3 %collective-permute-start.4 = (bf16[2,2,32,256]{3,2,1,0:T(8,128)(2,1)S(1)}, bf16[2,2,32,256]{3,2,1,0:T(8,128)(2,1)S(1)}, u32[]{:S(2)}, u32[]{:S(2)}) collective-permute-start(bf16[2,2,32,256]{3,2,1,0:T(8,128)(2,1)S(1)} %get-tuple-element.42), channel_id=1, source_target_pairs={{0,8},{8,16},{16,24},{24,32},{32,40},{40,48},{48,56},{56,64},{64,7... | collective-permute-start | bytes 196616 | tf_op jit(solution)/shard_map/ppermute | solution.py:38
  18.3 9.5 %copy-start.7 = (bf16[4,2,32,256]{3,2,1,0:T(8,128)(2,1)S(1)}, bf16[4,2,32,256]{3,2,1,0:T(8,128)(2,1)}, u32[]{:S(2)}) copy-start(bf16[4,2,32,256]{3,2,1,0:T(8,128)(2,1)} %param.5) | copy-start | bytes 393220
  27.9 17.0 %copy-start.8 = (bf16[108,256]{1,0:T(8,128)(2,1)S(1)}, bf16[108,256]{1,0:T(8,128)(2,1)}, u32[]{:S(2)}) copy-start(bf16[108,256]{1,0:T(8,128)(2,1)} %param.9) | copy-start | bytes 165892
  27.9 20.2 %collective-permute-start.5 = (bf16[16,2,32,256]{3,2,1,0:T(8,128)(2,1)S(1)}, bf16[16,2,32,256]{3,2,1,0:T(8,128)(2,1)S(1)}, u32[]{:S(2)}, u32[]{:S(2)}) collective-permute-start(bf16[16,2,32,256]{3,2,1,0:T(8,128)(2,1)S(1)} %slice_dynamic-update-slice_fusion.mid), channel_id=1, source_target_pairs={{1,2},{3,4},{5,6},{2,1},{4,3},{6,5},{9,10},{11,12},{13,14},{10,9},... | collective-permute-start | bytes 1572872 | tf_op jit(solution)/shard_map/ppermute | solution.py:50
  35.3 21.3 %collective-permute-start = (bf16[1728,128]{1,0:T(8,128)(2,1)S(1)}, bf16[1728,128]{1,0:T(8,128)(2,1)}, u32[]{:S(2)}, u32[]{:S(2)}) collective-permute-start(bf16[1728,128]{1,0:T(8,128)(2,1)S(1)} %unpack.2.a), channel_id=1, source_target_pairs={{0,128},{8,136},{16,144},{24,152},{32,160},{40,168},{48,176},{56,1... | collective-permute-start | bytes 1327112 | tf_op jit(solution)/shard_map/ppermute | solution.py:44
  38.4 20.3 %collective-permute-start.1 = (bf16[1728,128]{1,0:T(8,128)(2,1)S(1)}, bf16[1728,128]{1,0:T(8,128)(2,1)}, u32[]{:S(2)}, u32[]{:S(2)}) collective-permute-start(bf16[1728,128]{1,0:T(8,128)(2,1)S(1)} %unpack.2.a), channel_id=1, source_target_pairs={{0,384},{8,392},{16,400},{24,408},{32,416},{40,424},{48,432},{56,4... | collective-permute-start | bytes 1327112 | tf_op jit(solution)/shard_map/ppermute | solution.py:44
  42.1 16.6 %collective-permute-start.2 = (bf16[1728,128]{1,0:T(8,128)(2,1)S(1)}, bf16[1728,128]{1,0:T(8,128)(2,1)}, u32[]{:S(2)}, u32[]{:S(2)}) collective-permute-start(bf16[1728,128]{1,0:T(8,128)(2,1)S(1)} %unpack.2.a), channel_id=1, source_target_pairs={{0,256},{8,264},{16,272},{24,280},{32,288},{40,296},{48,304},{56,3... | collective-permute-start | bytes 1327112 | tf_op jit(solution)/shard_map/ppermute | solution.py:44
  48.9 16.4 %all-to-all-start.1 = ((bf16[16,108,128]{2,1,0:T(8,128)(2,1)}), bf16[16,108,128]{2,1,0:T(8,128)(2,1)S(1)}, u32[]{:S(2)}, u32[]{:S(2)}) async-start(bf16[16,108,128]{2,1,0:T(8,128)(2,1)} %broadcast_in_dim.7), calls=%async_computation.1 | async-start | bytes 917504 | tf_op jit(solution)/shard_map/all_to_all | solution.py:366
  54.6 4.2 %collective-permute-start.6 = (bf16[16,3,32,256]{3,2,1,0:T(8,128)(2,1)S(1)}, bf16[16,3,32,256]{3,2,1,0:T(8,128)(2,1)S(1)}, u32[]{:S(2)}, u32[]{:S(2)}) collective-permute-start(bf16[16,3,32,256]{3,2,1,0:T(8,128)(2,1)S(1)} %pad_maximum_fusion), channel_id=1, source_target_pairs={{0,1},{1,0},{2,3},{3,2},{4,5},{5,4},{6,7},{7,6},{8,9},{9,8},{10,11... | collective-permute-start | bytes 2359304 | tf_op jit(solution)/shard_map/ppermute | solution.py:32
  62.6 0.7 copy-start.4
  63.3 3.4 %collective-permute-start.7 = (f32[512,128]{1,0:T(8,128)S(1)}, f32[512,128]{1,0:T(8,128)S(1)}, u32[]{:S(2)}, u32[]{:S(2)}) collective-permute-start(f32[512,128]{1,0:T(8,128)S(1)} %get-tuple-element.32.own), channel_id=1, source_target_pairs={{0,1},{1,0},{2,3},{3,2},{4,5},{5,4},{6,7},{7,6},{8,9},{9,8},{10,11... | collective-permute-start | bytes 786440 | tf_op jit(solution)/shard_map/ppermute | solution.py:32
  66.7 1.0 copy-start.5
  70.1 15.7 %collective-permute-start.8 = (bf16[6912,128]{1,0:T(8,128)(2,1)}, bf16[6912,128]{1,0:T(8,128)(2,1)}, u32[]{:S(2)}, u32[]{:S(2)}) collective-permute-start(bf16[6912,128]{1,0:T(8,128)(2,1)} %get-tuple-element.35.own.w1_own), channel_id=1, source_target_pairs={{0,1},{1,0},{2,3},{3,2},{4,5},{5,4},{6,7},{7,6},{8,9},{9,8},{10,11... | collective-permute-start | bytes 5308424 | tf_op jit(solution)/shard_map/ppermute | solution.py:32
  72.1 19.9 %all-to-all-start.2 = ((bf16[4,864,128]{2,1,0:T(8,128)(2,1)}), bf16[4,864,128]{2,1,0:T(8,128)(2,1)S(1)}, u32[]{:S(2)}, u32[]{:S(2)}) async-start(bf16[4,864,128]{2,1,0:T(8,128)(2,1)} %bitcast.9), calls=%async_computation.2 | async-start | bytes 1769472 | tf_op jit(solution)/shard_map/all_to_all | solution.py:375
  76.2 27.9 %collective-permute-start.9 = (bf16[1728,128]{1,0:T(8,128)(2,1)S(1)}, bf16[1728,128]{1,0:T(8,128)(2,1)}, u32[]{:S(2)}, u32[]{:S(2)}) collective-permute-start(bf16[1728,128]{1,0:T(8,128)(2,1)S(1)} %unpack.3.a), channel_id=1, source_target_pairs={{0,128},{8,136},{16,144},{24,152},{32,160},{40,168},{48,176},{56,1... | collective-permute-start | bytes 1327112 | tf_op jit(solution)/shard_map/ppermute | solution.py:44
  79.5 26.5 %collective-permute-start.10 = (bf16[1728,128]{1,0:T(8,128)(2,1)S(1)}, bf16[1728,128]{1,0:T(8,128)(2,1)}, u32[]{:S(2)}, u32[]{:S(2)}) collective-permute-start(bf16[1728,128]{1,0:T(8,128)(2,1)S(1)} %unpack.3.a), channel_id=1, source_target_pairs={{0,384},{8,392},{16,400},{24,408},{32,416},{40,424},{48,432},{56,4... | collective-permute-start | bytes 1327112 | tf_op jit(solution)/shard_map/ppermute | solution.py:44
  83.2 25.2 %collective-permute-start.11 = (bf16[1728,128]{1,0:T(8,128)(2,1)S(1)}, bf16[1728,128]{1,0:T(8,128)(2,1)}, u32[]{:S(2)}, u32[]{:S(2)}) collective-permute-start(bf16[1728,128]{1,0:T(8,128)(2,1)S(1)} %unpack.3.a), channel_id=1, source_target_pairs={{0,256},{8,264},{16,272},{24,280},{32,288},{40,296},{48,304},{56,3... | collective-permute-start | bytes 1327112 | tf_op jit(solution)/shard_map/ppermute | solution.py:44
  91.1 0.9 copy-start.2
  92.8 18.6 %all-to-all-start.3 = ((bf16[16,54,128]{2,1,0:T(8,128)(2,1)}), bf16[16,54,128]{2,1,0:T(8,128)(2,1)S(1)}, u32[]{:S(2)}, u32[]{:S(2)}) async-start(bf16[16,54,128]{2,1,0:T(8,128)(2,1)} %sum_terms.1), calls=%async_computation.3 | async-start | bytes 458752 | tf_op jit(solution)/shard_map/all_to_all | solution.py:383
  100.4 22.2 %collective-permute-start.12 = (bf16[1728,128]{1,0:T(8,128)(2,1)S(1)}, bf16[1728,128]{1,0:T(8,128)(2,1)S(1)}, u32[]{:S(2)}, u32[]{:S(2)}) collective-permute-start(bf16[1728,128]{1,0:T(8,128)(2,1)S(1)} %unpack.3.a), channel_id=1, source_target_pairs={{0,1},{1,0},{2,3},{3,2},{4,5},{5,4},{6,7},{7,6},{8,9},{9,8},{10,11... | collective-permute-start | bytes 1327112 | tf_op jit(solution)/shard_map/ppermute | solution.py:32
  104.1 18.5 %collective-permute-start.13 = (bf16[1728,128]{1,0:T(8,128)(2,1)}, bf16[1728,128]{1,0:T(8,128)(2,1)S(1)}, u32[]{:S(2)}, u32[]{:S(2)}) collective-permute-start(bf16[1728,128]{1,0:T(8,128)(2,1)} %collective-permute-done.9.b), channel_id=1, source_target_pairs={{0,1},{1,0},{2,3},{3,2},{4,5},{5,4},{6,7},{7,6},{8,9},{9,8},{10,11... | collective-permute-start | bytes 1327112 | tf_op jit(solution)/shard_map/ppermute | solution.py:32
  106.0 16.5 %collective-permute-start.14 = (bf16[1728,128]{1,0:T(8,128)(2,1)}, bf16[1728,128]{1,0:T(8,128)(2,1)}, u32[]{:S(2)}, u32[]{:S(2)}) collective-permute-start(bf16[1728,128]{1,0:T(8,128)(2,1)} %collective-permute-done.10.c), channel_id=1, source_target_pairs={{0,1},{1,0},{2,3},{3,2},{4,5},{5,4},{6,7},{7,6},{8,9},{9,8},{10,11... | collective-permute-start | bytes 1327112 | tf_op jit(solution)/shard_map/ppermute | solution.py:32
  108.5 14.1 %collective-permute-start.15 = (bf16[1728,128]{1,0:T(8,128)(2,1)}, bf16[1728,128]{1,0:T(8,128)(2,1)}, u32[]{:S(2)}, u32[]{:S(2)}) collective-permute-start(bf16[1728,128]{1,0:T(8,128)(2,1)} %collective-permute-done.11.d), channel_id=1, source_target_pairs={{0,1},{1,0},{2,3},{3,2},{4,5},{5,4},{6,7},{7,6},{8,9},{9,8},{10,11... | collective-permute-start | bytes 1327112 | tf_op jit(solution)/shard_map/ppermute | solution.py:32
  112.2 22.4 %all-to-all-start.4 = ((f32[8,54,128]{2,1,0:T(8,128)}), f32[8,54,128]{2,1,0:T(8,128)S(1)}, u32[]{:S(2)}, u32[]{:S(2)}) async-start(f32[8,54,128]{2,1,0:T(8,128)} %broadcast_in_dim.8), calls=%async_computation.4 | async-start | bytes 458752 | tf_op jit(solution)/shard_map/all_to_all | solution.py:28
  122.6 1.1 copy-start.3
